TPU v7x, 32 devices: a whole 2x2x4 slice. The times are simulated.
32 devices in a mesh: groups: 2 (over x), sky: 16 (over z, y, core).
Axes of the slice: x: 2, y: 2, z: 4, core: 2. Of those that a mesh axis runs over, the one named last changes fastest.
Arguments:
- potential: float32 [8, 128, 1024], P('groups', 'sky'), parts along dimension 0, may hold values from -6 to 6
- lens_weight: float32 [4], replicated, may hold values from 0.08 to 0.25
- ray_start: float32 [4096, 2, 256], P(('groups', 'sky')), parts along dimension 0, may hold values from 0 to 32
- patch_index: int32 [8, 2048], P('groups', 'sky'), parts along dimension 0, may hold values from 0 to 127
- destination: int32 [4096, 1], P(('groups', 'sky')), parts along dimension 0, may hold values from 0 to 15; in each aligned block of 128 rows (0 to 127, 128 to 255, ...) at most 16 rows name the same one
Outputs:
- ray_shift: float32 [8192, 2, 256], P(('groups', 'sky')), parts along dimension 0
- distortion: float32 [8192, 4, 256], P(('groups', 'sky')), parts along dimension 0
There are 2 independent parts, one for each index of `groups`. A program takes and returns all parts, laid end to end along the dimension named above; an argument that names none is the same for every part. Nothing has to cross between parts.
Inputs may be any that keep to these rules, and one draw needn't show every extreme that they name: Among the 128 bundles of one owner at most 16 name one destination, and in every draw some owner sends exactly 16 to one destination.
All inputs are finite; a program needn't handle non-finite values.
Results may differ from a plain program's by a relative error of at most 0.0003.
Values sent between devices are 32-bit elements; how exact they have to be, the bound alone decides.
No kernel may reach another device: no remote copies, remote signals or barrier semaphores. Data moves between devices by JAX's collectives and lax.ppermute only.
A program may use at most 64 MiB of HBM per device.

v0:
```python
import math

import jax
import jax.numpy as jnp
from jax import lax
from jax.sharding import PartitionSpec as P


def hat_weights(pos, side):
    grid = jnp.arange(side).astype(pos.dtype)
    dist = jnp.mod(pos[..., None] - grid + side / 2.0, side) - side / 2.0
    return jnp.maximum(0.0, 1.0 - jnp.abs(dist))


def derive_fields(patch):
    east = jnp.roll(patch, -1, axis=2)
    west = jnp.roll(patch, 1, axis=2)
    north = jnp.roll(patch, -1, axis=1)
    south = jnp.roll(patch, 1, axis=1)
    grad_x = (east - west) * 0.5
    grad_y = (north - south) * 0.5
    curv_xx = east - 2.0 * patch + west
    curv_yy = north - 2.0 * patch + south
    cross = (
        jnp.roll(east, -1, axis=1)
        - jnp.roll(west, -1, axis=1)
        - jnp.roll(east, 1, axis=1)
        + jnp.roll(west, 1, axis=1)
    ) * 0.25
    return jnp.concatenate([grad_x, grad_y, curv_xx, cross, curv_yy], axis=2)


def sample_fields(fields, pos_x, pos_y):
    side = fields.shape[1]
    weight_x = hat_weights(pos_x, side)
    weight_y = hat_weights(pos_y, side)
    rows = jnp.einsum("nrg,ngk->nrk", weight_y, fields, precision=lax.Precision.HIGHEST)
    rows = rows.reshape(rows.shape[0], rows.shape[1], 5, side)
    return jnp.sum(rows * weight_x[:, :, None, :], axis=-1)


def select_tiles(potential, ids):
    piece = lax.all_gather(potential, "sky", axis=1, tiled=True)
    columns = lax.iota(jnp.int32, piece.shape[1])
    onehot = (ids[:, :, None] == columns[None, None, :]).astype(jnp.float32)
    chosen = jnp.einsum("pnm,pmk->pnk", onehot, piece, precision=lax.Precision.HIGHEST)
    return jnp.transpose(chosen, (1, 0, 2))


def trace_rays(start, lens_weight, tiles):
    pos_x = start[:, 0]
    pos_y = start[:, 1]
    a_one = jnp.ones_like(pos_x)
    a_zero = jnp.zeros_like(pos_x)
    m11, m12, m21, m22 = (a_one, a_zero, a_zero, a_one)
    for plane in range(lens_weight.shape[0]):
        patch = tiles[:, plane]
        side = math.isqrt(patch.shape[1])
        fields = derive_fields(patch.reshape(patch.shape[0], side, side))
        vals = sample_fields(fields, pos_x, pos_y)
        strength = lens_weight[plane]
        hxx, hxy, hyy = (vals[:, :, 2], vals[:, :, 3], vals[:, :, 4])
        n11 = m11 - strength * (hxx * m11 + hxy * m21)
        n12 = m12 - strength * (hxx * m12 + hxy * m22)
        n21 = m21 - strength * (hxy * m11 + hyy * m21)
        n22 = m22 - strength * (hxy * m12 + hyy * m22)
        m11, m12, m21, m22 = (n11, n12, n21, n22)
        pos_x = pos_x - strength * vals[:, :, 0]
        pos_y = pos_y - strength * vals[:, :, 1]
    shift = jnp.stack([pos_x - start[:, 0], pos_y - start[:, 1]], axis=1)
    matrix = jnp.stack([m11, m12, m21, m22], axis=1)
    return (shift, matrix)


def trace_blocks(start, lens_weight, tiles):
    count = start.shape[0]
    rays = start.shape[2]
    block = 16
    blocks = count // block
    start_blocks = start.reshape(blocks, block, 2, rays)
    tile_blocks = tiles.reshape(blocks, block, tiles.shape[1], tiles.shape[2])

    def one_block(item):
        return trace_rays(item[0], lens_weight, item[1])

    shift, matrix = lax.map(one_block, (start_blocks, tile_blocks))
    return (shift.reshape(count, 2, rays), matrix.reshape(count, 4, rays))


def shards(potential, lens_weight, ray_start, patch_index, destination):
    n_sky = lax.axis_size("sky")
    bundles = ray_start.shape[0]
    rays = ray_start.shape[2]
    slots_each = max(2, 2 * bundles // n_sky)
    recv_slots = n_sky * slots_each
    dest = destination[:, 0]
    same = dest[:, None] == dest[None, :]
    earlier = jnp.arange(bundles)[None, :] < jnp.arange(bundles)[:, None]
    rank = jnp.sum((same & earlier).astype(jnp.int32), axis=1)
    slot = dest * slots_each + rank
    placing = (lax.iota(jnp.int32, recv_slots)[:, None] == slot[None, :]).astype(jnp.float32)
    tiles = select_tiles(potential, patch_index)
    shift, matrix = trace_blocks(ray_start, lens_weight, tiles)
    state = jnp.concatenate([shift, matrix], axis=1).reshape(bundles, 6 * rays)
    sent = jnp.dot(placing, state, precision=lax.Precision.HIGHEST).reshape(recv_slots, 6, rays)
    got = lax.all_to_all(sent, "sky", split_axis=0, concat_axis=0, tiled=True)
    return (got[:, 0:2], got[:, 2:6])


def solution(mesh):
    in_specs = (
        P("groups", "sky", None),
        P(),
        P(("groups", "sky"), None, None),
        P("groups", "sky"),
        P(("groups", "sky"), None),
    )
    out_specs = (P(("groups", "sky"), None, None), P(("groups", "sky"), None, None))
    return jax.shard_map(shards, mesh=mesh, in_specs=in_specs, out_specs=out_specs, check_vma=False)
```

profile of v0, /device:TPU:0, one launch (start us, length us, event | category | flops | bytes accessed | tf_op | source)
XLA Modules:
  0.0 383.2 jit_solution(13947057077665217202)
XLA Ops:
  9.5 44.9 %all-gather.2.cloned.1.call-done = f32[4,128,1024]{2,1,0:T(8,128)} async-done(((f32[4,8,1024]{2,1,0:T(8,128)}), f32[4,128,1024]{2,1,0:T(8,128)}) %all-gather.2.cloned.1.call-update) | async-done | bytes 2097168 | tf_op jit(solution)/shard_map/all_gather | solution.py:43
  54.4 4.1 %fusion.156 = f32[4,128,1024]{2,1,0:T(8,128)} fusion(f32[4,128,1024]{2,1,0:T(8,128)} %all-gather.2.cloned.1.call-done, s32[4,128]{1,0:T(4,128)} %param.10), kind=kOutput, calls=%fused_computation.313 | convolution fusion | flops 805371904 | bytes 4196352 | tf_op jit(solution)/shard_map/pnm,pmk->pnk/dot_general | solution.py:46
  58.5 262.0 %while.15 = (s32[]{:T(128)}, f32[8,16,2,256]{3,1,0,2:T(8,128)}, f32[8,16,4,256]{3,1,0,2:T(8,128)S(1)}, f32[8,16,2,256]{3,2,1,0:T(2,128)}, f32[4]{0:T(128)S(1)}, /*index=5*/f32[8,16,4,1024]{3,1,0,2:T(8,128)}, s32[]{:T(128)}) while((s32[]{:T(128)}, f32[8,16,2,256]{3,1,0,2:T(8,128)}, f32[8,16,4,256]{3,1,0,2:T(8,128)S(1)}, ...), condition=%wide.region_6.7_spmd, body=%wide.region_1.6_spmd.sunk | while | flops 1026535424 | bytes 40899352 | solution.py:86
  63.7 2.5 fusion.254
  68.6 2.5 fusion.263
  72.2 1.4 multiply_subtract_fusion.23
  76.1 2.5 fusion.272
  82.1 2.5 fusion.275
  85.6 2.7 fusion.277
  96.5 2.5 fusion.254
  101.4 2.5 fusion.263
  105.0 1.4 multiply_subtract_fusion.23
  108.8 2.5 fusion.272
  114.8 2.5 fusion.275
  118.4 2.7 fusion.277
  129.2 2.5 fusion.254
  134.1 2.5 fusion.263
  137.7 1.4 multiply_subtract_fusion.23
  141.6 2.5 fusion.272
  147.6 2.5 fusion.275
  151.1 2.7 fusion.277
  162.0 2.5 fusion.254
  166.9 2.5 fusion.263
  170.5 1.4 multiply_subtract_fusion.23
  174.3 2.5 fusion.272
  180.3 2.5 fusion.275
  183.9 2.7 fusion.277
  194.7 2.5 fusion.254
  199.6 2.5 fusion.263
  207.1 2.5 fusion.272
  213.1 2.5 fusion.275
  216.6 2.7 fusion.277
  227.5 2.5 fusion.254
  232.4 2.5 fusion.263
  239.8 2.5 fusion.272
  245.8 2.5 fusion.275
  249.4 2.7 fusion.277
  260.2 2.5 fusion.254
  265.1 2.5 fusion.263
  272.6 2.5 fusion.272
  278.6 2.5 fusion.275
  282.1 2.7 fusion.277
  293.0 2.5 fusion.254
  297.9 2.5 fusion.263
  305.3 2.5 fusion.272
  311.3 2.5 fusion.275
  314.9 2.7 fusion.277
  323.5 50.6 %all_to_all.5 = f32[256,6,256]{2,1,0:T(8,128)S(1)} all-to-all(f32[256,6,256]{2,1,0:T(8,128)S(1)} %copy.38), channel_id=1, replica_groups=mesh['groups'=2,'sky'=16] {'sky'}, dimensions={0} | all-to-all | bytes 3145728 | tf_op jit(solution)/shard_map/all_to_all | solution.py:106
  (578 shorter events, 157.4 us)
Async XLA Ops:
  7.2 51.3 %copy-start = (f32[4]{0:T(128)S(1)}, f32[4]{0:T(128)}, u32[]{:S(2)}) copy-start(f32[4]{0:T(128)} %param.8) | copy-start | bytes 52
  7.2 47.2 %all-gather.2.cloned.1.call-start = ((), (), s32[]{:S(2)}) async-start(), calls=%async_computation.1 | async-start | bytes 2228224 | tf_op jit(solution)/shard_map/all_gather | solution.py:43
Sparse Core Ops, SparseCore 0:
  10.2 44.1 all-gather.1
where the time goes:
time: 385 us; the launch traced here: 383 us
  other arithmetic  131 us (34%)
  matrix products  86.2 us (22%)
  local copies, waits for them, and re-layouts  52.3 us (14%)
  blocking collectives  50.6 us (13%)
  waiting for transfers between devices  45.5 us (12%)
  between operations  14.1 us (4%)
    dot_general x32, matrix products, sample_fields(): jnp.einsum('nrg,ngk->nrk', weight_y, fields, precision=lax.Precision.HIGH...  81.3 us
    all_to_all x1, blocking collectives, shards(): got = lax.all_to_all(sent, 'sky', split_axis=0, concat_axis=0, tiled=True)  50.6 us
    all_gather x1, waiting for transfers between devices, select_tiles(): piece = lax.all_gather(potential, 'sky', axis=1, tiled=True)  44.9 us
    sub x8, other arithmetic, trace_rays(): shift = jnp.stack([pos_x - start[:, 0], pos_y - start[:, 1]], axis=1)  21.8 us
    reduce_sum x32, other arithmetic, sample_fields(): return jnp.sum(rows * weight_x[:, :, None, :], axis=-1)  18 us
    sub x16, other arithmetic, trace_rays(): n21 = m21 - strength * (hxy * m11 + hyy * m21)  16.6 us
    sub x24, other arithmetic, trace_rays(): pos_x = pos_x - strength * vals[:, :, 0]  16.4 us
    concatenate x64, other arithmetic, derive_fields(): west = jnp.roll(patch, 1, axis=2)  15.3 us
  transfers between devices with their start and end apart: 1, of which 1 were waited for; matrix products, arithmetic and copies ran while one was open for 0% of the time, Pallas kernels for 0%

commit v1 on v0

v1 whole, which is shorter than its diff:
```python
import functools

import jax
import jax.numpy as jnp
from jax import lax
from jax.experimental import pallas as pl
from jax.experimental.pallas import tpu as pltpu
from jax.sharding import PartitionSpec as P

LANES = 128
SUB = 8
SIDE = 32
CHUNKS = 8


def lane_gather(table, idx):
    dims = lax.GatherDimensionNumbers(
        offset_dims=(),
        collapsed_slice_dims=(1,),
        start_index_map=(1,),
        operand_batching_dims=(0,),
        start_indices_batching_dims=(0,),
    )
    return lax.gather(
        table,
        idx[..., None],
        dims,
        slice_sizes=(1, 1),
        mode=lax.GatherScatterMode.PROMISE_IN_BOUNDS,
    )


def split3(value):
    high = value.astype(jnp.bfloat16)
    rest = value - high.astype(jnp.float32)
    middle = rest.astype(jnp.bfloat16)
    low = (rest - middle.astype(jnp.float32)).astype(jnp.bfloat16)
    return high, middle, low


def regroup_kernel(src_ref, dst_ref):
    planes, tiles, _ = src_ref.shape
    lane = lax.broadcasted_iota(jnp.int32, (SUB, LANES), 1)
    source = (lane & 96) + ((lane & 15) << 1) + ((lane >> 4) & 1)
    for plane in range(planes):
        for base in range(0, tiles, SUB):
            rows = pl.ds(base, SUB)
            parts = [
                lane_gather(src_ref[plane, rows, pl.ds(c * LANES, LANES)], source)
                for c in range(CHUNKS)
            ]
            for step in (1, 2, 4):
                keep = ((lane >> 4) & step) == 0
                for c in range(CHUNKS):
                    if c & step:
                        continue
                    one, two = parts[c], parts[c + step]
                    parts[c] = jnp.where(keep, one, pltpu.roll(two, step * 16, 1))
                    parts[c + step] = jnp.where(keep, pltpu.roll(one, LANES - step * 16, 1), two)
            for c in range(CHUNKS):
                dst_ref[plane, rows, pl.ds(c * LANES, LANES)] = parts[c]


def regroup(potential):
    return pl.pallas_call(
        regroup_kernel,
        out_shape=jax.ShapeDtypeStruct(potential.shape, potential.dtype),
        in_specs=[pl.BlockSpec(memory_space=pltpu.VMEM)],
        out_specs=pl.BlockSpec(memory_space=pltpu.VMEM),
        name="regroup",
    )(potential)


def pack_kernel(n_sky, each, dest_ref, ids_ref, rays_ref, out_ref):
    bundles = dest_ref.shape[1]
    slots = n_sky * each
    dest_row = jnp.broadcast_to(dest_ref[...], (bundles, bundles))
    dest_col = jnp.transpose(dest_row)
    row = lax.broadcasted_iota(jnp.int32, (bundles, bundles), 0)
    col = lax.broadcasted_iota(jnp.int32, (bundles, bundles), 1)
    hits = jnp.where((dest_row == dest_col) & (row < col), 1.0, 0.0)
    rank = jnp.sum(hits, axis=0, keepdims=True).astype(jnp.int32)
    slot = dest_ref[...] * each + rank
    place = lax.broadcasted_iota(jnp.int32, (slots, bundles), 0) == slot
    place = jnp.where(place, 1.0, 0.0)
    place3 = jnp.concatenate([place] * 3, axis=1).astype(jnp.bfloat16)
    for part in range(4):
        rays = rays_ref[pl.ds(part, bundles, stride=4), :]
        terms = jnp.concatenate(split3(rays), axis=0)
        sent = jnp.dot(place3, terms, preferred_element_type=jnp.float32)
        for o in range(n_sky):
            out_ref[o, pl.ds(part, each, stride=4), :] = sent[o * each:(o + 1) * each]
    ids = ids_ref[...] + 1
    pad = jnp.zeros((SUB - ids.shape[0], bundles), jnp.float32)
    fine = jnp.concatenate([(ids & 15).astype(jnp.float32), pad], axis=0)
    coarse = jnp.concatenate([(ids >> 4).astype(jnp.float32), pad], axis=0)
    place = place.astype(jnp.bfloat16)
    contract = (((1,), (1,)), ((), ()))
    fine = lax.dot_general(fine.astype(jnp.bfloat16), place, contract, preferred_element_type=jnp.float32)
    coarse = lax.dot_general(coarse.astype(jnp.bfloat16), place, contract, preferred_element_type=jnp.float32)
    numbers = coarse * 16.0 + fine
    lane = lax.broadcasted_iota(jnp.int32, (SUB, LANES), 1)
    for o in range(n_sky):
        first = o * each
        block = numbers[:, first // LANES * LANES:first // LANES * LANES + LANES]
        turn = (LANES - first % LANES) % LANES
        if turn:
            block = pltpu.roll(block, turn, 1)
        out_ref[o, pl.ds(4 * each, SUB), :] = jnp.where(lane < each, block, 0.0)


def pack(n_sky, each, dest, ids, rays):
    return pl.pallas_call(
        functools.partial(pack_kernel, n_sky, each),
        out_shape=jax.ShapeDtypeStruct((n_sky, 4 * each + SUB, LANES), jnp.float32),
        in_specs=[pl.BlockSpec(memory_space=pltpu.VMEM)] * 3,
        out_specs=pl.BlockSpec(memory_space=pltpu.VMEM),
        name="pack",
    )(dest, ids, rays)


def bilinear(f00, f01, f10, f11, u, v):
    one = f00 + u * (f01 - f00)
    two = f10 + u * (f11 - f10)
    return one + v * (two - one)


def lerp(one, two, t):
    return one + t * (two - one)


def window(tables, pos_x, pos_y):
    ix = (pos_x + float(SIDE)).astype(jnp.int32)
    iy = (pos_y + float(SIDE)).astype(jnp.int32)
    u = pos_x - (ix.astype(jnp.float32) - float(SIDE))
    v = pos_y - (iy.astype(jnp.float32) - float(SIDE))
    odd = (ix - 1) >> 1
    even = ix >> 1
    columns = (((even & 15), ((even + 1) & 15)), ((odd & 15), ((odd + 1) & 15)))
    odd_first = (ix & 1) == 0
    by_two = ((iy - 1) & 2) != 0
    by_one = (iy & 1) == 0
    sorted_columns = []
    for a in range(4):
        line = ((iy + (2 - a)) & 28) << 2
        e0, e1 = [lane_gather(tables[2 * a], line + c) for c in columns[0]]
        o0, o1 = [lane_gather(tables[2 * a + 1], line + c) for c in columns[1]]
        sorted_columns.append((
            jnp.where(odd_first, o0, e0),
            jnp.where(odd_first, e0, o0),
            jnp.where(odd_first, o1, e1),
            jnp.where(odd_first, e1, o1),
        ))
    w = [[None] * 4 for _ in range(4)]
    for k in range(4):
        half = [jnp.where(by_two, sorted_columns[(r + 2) & 3][k], sorted_columns[r][k]) for r in range(4)]
        for r in range(4):
            w[r][k] = jnp.where(by_one, half[(r + 1) & 3], half[r])
    return w, u, v


def trace_step(tables, strength, pos_x, pos_y, matrix):
    w, u, v = window(tables, pos_x, pos_y)
    gx = [lerp(w[1][k + 1] - w[1][k], w[2][k + 1] - w[2][k], v) for k in range(3)]
    gy = [lerp(w[r + 1][1] - w[r][1], w[r + 1][2] - w[r][2], u) for r in range(3)]
    fx2 = lerp(gx[0] + gx[1], gx[1] + gx[2], u)
    fxx = lerp(gx[1] - gx[0], gx[2] - gx[1], u)
    fy2 = lerp(gy[0] + gy[1], gy[1] + gy[2], v)
    fyy = lerp(gy[1] - gy[0], gy[2] - gy[1], v)
    wide = [[w[r][k + 2] - w[r][k] for k in range(2)] for r in range(4)]
    fxy4 = bilinear(
        wide[2][0] - wide[0][0], wide[2][1] - wide[0][1],
        wide[3][0] - wide[1][0], wide[3][1] - wide[1][1], u, v)
    half = 0.5 * strength
    hxx, hxy, hyy = strength * fxx, (0.25 * strength) * fxy4, strength * fyy
    m11, m12, m21, m22 = matrix
    matrix = (
        m11 - (hxx * m11 + hxy * m21),
        m12 - (hxx * m12 + hxy * m22),
        m21 - (hxy * m11 + hyy * m21),
        m22 - (hxy * m12 + hyy * m22),
    )
    return pos_x - half * fx2, pos_y - half * fy2, matrix


def trace_kernel(each, lens_ref, tiles_ref, got_ref, shift_ref, matrix_ref, chosen, rays, taken):
    planes, patches, pixels = tiles_ref.shape
    n_sky = got_ref.shape[0]
    slots = n_sky * each
    groups = LANES // each
    for d in range(n_sky):
        rays[pl.ds(d * 4 * each, 4 * each), :] = got_ref[d, pl.ds(0, 4 * each), :]
    numbers = []
    for first in range(0, n_sky, groups):
        total = None
        for d in range(first, min(first + groups, n_sky)):
            block = got_ref[d, pl.ds(4 * each, SUB), :]
            turn = (d - first) * each
            if turn:
                block = pltpu.roll(block, turn, 1)
            total = block if total is None else total + block
        numbers.append(total)
    tile_row = lax.broadcasted_iota(jnp.int32, (patches, LANES), 0).astype(jnp.float32) + 1.0
    for plane in range(planes):
        terms = split3(tiles_ref[plane])
        for part, number in enumerate(numbers):
            match = jnp.where(tile_row == number[plane:plane + 1, :], 1.0, 0.0)
            match = jnp.transpose(match)
            if plane == 0:
                found = jnp.sum(match, axis=1, keepdims=True)
                taken[pl.ds(part * LANES, LANES), :] = jnp.broadcast_to(found, (LANES, LANES))
            match = match.astype(jnp.bfloat16)
            total = None
            for term in terms:
                piece = jnp.dot(match, term, preferred_element_type=jnp.float32)
                total = piece if total is None else total + piece
            chosen[plane, pl.ds(part * LANES, LANES), :] = total

    def body(group, carry):
        base = pl.multiple_of(group * SUB, SUB)
        used = taken[pl.ds(base, SUB), :]
        start, state = [], []
        for h in range(2):
            x0 = rays[pl.ds(base * 4 + 2 * h, SUB, stride=4), :]
            y0 = rays[pl.ds(base * 4 + 2 * h + 1, SUB, stride=4), :]
            start.append((x0, y0))
            state.append((x0, y0, (used, jnp.zeros_like(used), jnp.zeros_like(used), used)))
        for plane in range(planes):
            tables = [chosen[plane, pl.ds(base, SUB), pl.ds(c * LANES, LANES)] for c in range(CHUNKS)]
            strength = lens_ref[plane]
            state = [trace_step(tables, strength, *one) for one in state]
        for h in range(2):
            x, y, matrix = state[h]
            shift_ref[pl.ds(base * 4 + 2 * h, SUB, stride=4), :] = x - start[h][0]
            shift_ref[pl.ds(base * 4 + 2 * h + 1, SUB, stride=4), :] = y - start[h][1]
            for e in range(4):
                matrix_ref[pl.ds(base * 8 + 4 * h + e, SUB, stride=8), :] = matrix[e]
        return carry

    lax.fori_loop(0, slots // SUB, body, 0)


def trace(each, lens_weight, tiles, got):
    slots = got.shape[0] * each
    planes, _, pixels = tiles.shape
    return pl.pallas_call(
        functools.partial(trace_kernel, each),
        out_shape=(
            jax.ShapeDtypeStruct((slots * 4, LANES), jnp.float32),
            jax.ShapeDtypeStruct((slots * 8, LANES), jnp.float32),
        ),
        in_specs=[
            pl.BlockSpec(memory_space=pltpu.SMEM),
            pl.BlockSpec(memory_space=pltpu.VMEM),
            pl.BlockSpec(memory_space=pltpu.VMEM),
        ],
        out_specs=(
            pl.BlockSpec(memory_space=pltpu.VMEM),
            pl.BlockSpec(memory_space=pltpu.VMEM),
        ),
        scratch_shapes=[
            pltpu.VMEM((planes, slots, pixels), jnp.float32),
            pltpu.VMEM((slots * 4, LANES), jnp.float32),
            pltpu.VMEM((slots, LANES), jnp.float32),
        ],
        compiler_params=pltpu.CompilerParams(vmem_limit_bytes=48 * 1024 * 1024),
        name="trace",
    )(lens_weight, tiles, got)


def shards(potential, lens_weight, ray_start, patch_index, destination):
    n_sky = lax.axis_size("sky")
    bundles, _, rays = ray_start.shape
    each = max(2, 2 * bundles // n_sky)
    slots = n_sky * each
    halves = rays // LANES
    tiles = lax.all_gather(regroup(potential), "sky", axis=1, tiled=True)
    flat = ray_start.reshape(bundles, 2, halves, LANES).transpose(0, 2, 1, 3).reshape(bundles * 2 * halves, LANES)
    sent = pack(n_sky, each, destination.reshape(1, bundles), patch_index, flat)
    got = lax.all_to_all(sent, "sky", split_axis=0, concat_axis=0, tiled=True)
    shift, matrix = trace(each, lens_weight, tiles, got)
    shift = shift.reshape(slots, halves, 2, LANES).transpose(0, 2, 1, 3).reshape(slots, 2, rays)
    matrix = matrix.reshape(slots, halves, 4, LANES).transpose(0, 2, 1, 3).reshape(slots, 4, rays)
    return shift, matrix


def solution(mesh):
    in_specs = (
        P("groups", "sky", None),
        P(),
        P(("groups", "sky"), None, None),
        P("groups", "sky"),
        P(("groups", "sky"), None),
    )
    out_specs = (P(("groups", "sky"), None, None), P(("groups", "sky"), None, None))
    return jax.shard_map(shards, mesh=mesh, in_specs=in_specs, out_specs=out_specs, check_vma=False)
```

time: 385 us -> 93 us (0.24)
  other arithmetic: 131 us -> 0 us
  matrix products: 86.2 us -> 0 us
  local copies, waits for them, and re-layouts: 52.3 us -> 1.6 us
  Pallas kernels: 0 us -> 29.8 us
  waiting for transfers between devices: 45.5 us -> 18.4 us
  blocking collectives: 50.6 us -> 28.9 us
    dot_general x34 -> x0, matrix products: 86.2 us -> none  [the longest x32 81.3 us: sample_fields(): jnp.einsum('nrg,ngk->nrk', weight_y, fields, precision=lax.Precision.HIGH...]
    sub x56 -> x0, other arithmetic: 66.3 us -> none  [the longest x8 21.8 us: trace_rays(): shift = jnp.stack([pos_x - start[:, 0], pos_y - start[:, 1]], axis=1)]
    pallas_call x0 -> x3, Pallas kernels: none -> 29.8 us  [the longest x1 25.5 us: trace(): pl.pallas_call(functools.partial(trace_kernel, each), out_shape=(jax.Shap...]
    all_gather x1, waiting for transfers between devices: 44.9 us -> 18.4 us  [shards(): tiles = lax.all_gather(regroup(potential), 'sky', axis=1, tiled=True)]
    all_to_all x1, blocking collectives: 50.6 us -> 28.9 us  [shards(): got = lax.all_to_all(sent, 'sky', split_axis=0, concat_axis=0, tiled=True)]
    reduce_sum x33 -> x0, other arithmetic: 18.9 us -> none  [the longest x32 18 us: sample_fields(): return jnp.sum(rows * weight_x[:, :, None, :], axis=-1)]
    slice x154 -> x0, local copies, waits for them, and re-layouts: 18.4 us -> none  [the longest x64 8.78 us: derive_fields(): east = jnp.roll(patch, -1, axis=2)]
    squeeze x48 -> x0, local copies, waits for them, and re-layouts: 17.5 us -> none  [the longest x16 13.9 us: trace_blocks(): shift, matrix = lax.map(one_block, (start_blocks, tile_blocks))]
  transfers between devices with their start and end apart: 1 -> 1, of which waited for: 1 -> 1; matrix products, arithmetic and copies ran while one was open for 0% -> 0% of each run, Pallas kernels for 0% -> 3%
where the time goes in v1:
time: 93 us; the launch traced here: 92.8 us
  Pallas kernels  29.8 us (32%)
  blocking collectives  28.9 us (31%)
  waiting for transfers between devices  18.4 us (20%)
  between operations  14 us (15%)
  local copies, waits for them, and re-layouts  1.6 us (2%)
    all_to_all x1, blocking collectives, shards(): got = lax.all_to_all(sent, 'sky', split_axis=0, concat_axis=0, tiled=True)  28.9 us
    pallas_call x1, Pallas kernels, trace(): pl.pallas_call(functools.partial(trace_kernel, each), out_shape=(jax.Shap...  25.5 us
    all_gather x1, waiting for transfers between devices, shards(): tiles = lax.all_gather(regroup(potential), 'sky', axis=1, tiled=True)  18.4 us
    pallas_call x1, Pallas kernels, pack(): pl.pallas_call(functools.partial(pack_kernel, n_sky, each), out_shape=jax...  2.36 us
    pallas_call x1, Pallas kernels, regroup(): pl.pallas_call(regroup_kernel, out_shape=jax.ShapeDtypeStruct(potential.s...  1.88 us
  transfers between devices with their start and end apart: 1, of which 1 were waited for; matrix products, arithmetic and copies ran while one was open for 0% of the time, Pallas kernels for 3%

profile of v1, /device:TPU:0, one launch (start us, length us, event | category | flops | bytes accessed | tf_op | source)
XLA Modules:
  0.0 92.8 jit_solution(6765079904658984088)
XLA Ops:
  7.2 0.0 copy-start.1
  7.2 0.0 all-gather.2.cloned.1.call-start
  7.2 1.9 %regroup.1 = f32[4,8,1024]{2,1,0:T(8,128)} custom-call(f32[4,8,1024]{2,1,0:T(8,128)} %src_ref.1), custom_call_target="tpu_custom_call" | custom-call | tf_op jit(solution)/shard_map/regroup/pallas_call | solution.py:65
  9.1 0.0 all-gather.2.cloned.1.call-update
  9.1 2.4 %pack.1 = f32[16,72,128]{2,1,0:T(8,128)} custom-call(s32[1,128]{1,0:T(1,128)} %bitcast.17, s32[4,128]{1,0:T(4,128)} %ids_ref.1, f32[512,128]{1,0:T(8,128)} %bitcast.16), custom_call_target="tpu_custom_call" | custom-call | tf_op jit(solution)/shard_map/pack/pallas_call | solution.py:113
  11.5 28.9 %all_to_all.5.got_ref = f32[16,72,128]{2,1,0:T(8,128)S(1)} all-to-all(f32[16,72,128]{2,1,0:T(8,128)} %pack.1), channel_id=1, replica_groups=mesh['groups'=2,'sky'=16] {'sky'}, dimensions={0} | all-to-all | bytes 1179648 | tf_op jit(solution)/shard_map/all_to_all | solution.py:280
  40.4 18.4 %all-gather.2.cloned.1.call-done.tiles_ref = f32[4,128,1024]{2,1,0:T(8,128)} async-done(((f32[4,8,1024]{2,1,0:T(8,128)}), f32[4,128,1024]{2,1,0:T(8,128)}) %all-gather.2.cloned.1.call-update) | async-done | bytes 2097168 | tf_op jit(solution)/shard_map/all_gather | solution.py:277
  58.8 0.0 copy-done.1
  58.8 0.0 copy-start
  58.8 1.6 %copy-done = f32[4,128,1024]{2,1,0:T(8,128)S(1)} copy-done((f32[4,128,1024]{2,1,0:T(8,128)S(1)}, f32[4,128,1024]{2,1,0:T(8,128)}, u32[]{:S(2)}) %copy-start) | copy-done | bytes 2097176
  60.4 25.5 %trace.1 = (f32[1024,128]{1,0:T(8,128)}, f32[2048,128]{1,0:T(8,128)}) custom-call(f32[4]{0:T(128)S(1)} %copy-done.1, f32[4,128,1024]{2,1,0:T(8,128)S(1)} %copy-done, f32[16,72,128]{2,1,0:T(8,128)S(1)} %all_to_all.5.got_ref), custom_call_target="tpu_custom_call" | custom-call | tf_op jit(solution)/shard_map/trace/pallas_call | solution.py:246
Async XLA Ops:
  7.2 51.6 %copy-start.1 = (f32[4]{0:T(128)S(1)}, f32[4]{0:T(128)}, u32[]{:S(2)}) copy-start(f32[4]{0:T(128)} %lens_ref.1) | copy-start | bytes 52
  7.2 51.6 %all-gather.2.cloned.1.call-start = ((), (), s32[]{:S(2)}) async-start(), calls=%async_computation.1 | async-start | bytes 2228224 | tf_op jit(solution)/shard_map/all_gather | solution.py:277
  58.8 1.6 %copy-start = (f32[4,128,1024]{2,1,0:T(8,128)S(1)}, f32[4,128,1024]{2,1,0:T(8,128)}, u32[]{:S(2)}) copy-start(f32[4,128,1024]{2,1,0:T(8,128)} %all-gather.2.cloned.1.call-done.tiles_ref) | copy-start | bytes 6291460
Sparse Core Ops, SparseCore 0:
  10.8 47.9 all-gather.1

commit v2 on v1

v2 whole, which is shorter than its diff:
```python
import functools

import jax
import jax.numpy as jnp
from jax import lax
from jax.experimental import pallas as pl
from jax.experimental.pallas import tpu as pltpu
from jax.sharding import PartitionSpec as P

LANES = 128
SUB = 8
SIDE = 32
CHUNKS = 8
EMPTY = -1024.0


def lane_gather(table, idx):
    dims = lax.GatherDimensionNumbers(
        offset_dims=(),
        collapsed_slice_dims=(1,),
        start_index_map=(1,),
        operand_batching_dims=(0,),
        start_indices_batching_dims=(0,),
    )
    return lax.gather(
        table,
        idx[..., None],
        dims,
        slice_sizes=(1, 1),
        mode=lax.GatherScatterMode.PROMISE_IN_BOUNDS,
    )


def split3(value):
    high = value.astype(jnp.bfloat16)
    rest = value - high.astype(jnp.float32)
    middle = rest.astype(jnp.bfloat16)
    low = (rest - middle.astype(jnp.float32)).astype(jnp.bfloat16)
    return high, middle, low


def regroup_kernel(src_ref, dst_ref):
    planes, tiles, _ = src_ref.shape
    lane = lax.broadcasted_iota(jnp.int32, (SUB, LANES), 1)
    source = (lane & 96) + ((lane & 15) << 1) + ((lane >> 4) & 1)
    for plane in range(planes):
        for base in range(0, tiles, SUB):
            parts = [
                lane_gather(src_ref[plane, pl.ds(base, SUB), pl.ds(c * LANES, LANES)], source)
                for c in range(CHUNKS)
            ]
            for step in (1, 2, 4):
                keep = ((lane >> 4) & step) == 0
                for c in range(CHUNKS):
                    if c & step:
                        continue
                    one, two = parts[c], parts[c + step]
                    parts[c] = jnp.where(keep, one, pltpu.roll(two, step * 16, 1))
                    parts[c + step] = jnp.where(keep, pltpu.roll(one, LANES - step * 16, 1), two)
            for c in range(CHUNKS):
                rows = pl.ds((plane * tiles + base) * CHUNKS + c, SUB, stride=CHUNKS)
                dst_ref[rows, :] = parts[c]


def regroup(potential):
    planes, tiles, pixels = potential.shape
    rows = planes * tiles * pixels // LANES
    return pl.pallas_call(
        regroup_kernel,
        out_shape=jax.ShapeDtypeStruct((rows, LANES), potential.dtype),
        in_specs=[pl.BlockSpec(memory_space=pltpu.VMEM)],
        out_specs=pl.BlockSpec(memory_space=pltpu.VMEM),
        name="regroup",
    )(potential)


def pack_kernel(n_sky, each, per_owner, me_ref, dest_ref, ids_ref, rays_ref, *out_refs):
    me = me_ref[0]
    bundles = dest_ref.shape[1]
    planes = ids_ref.shape[0]
    slots = n_sky * each
    dest_row = jnp.broadcast_to(dest_ref[...], (bundles, bundles))
    dest_col = jnp.transpose(dest_row)
    row = lax.broadcasted_iota(jnp.int32, (bundles, bundles), 0)
    col = lax.broadcasted_iota(jnp.int32, (bundles, bundles), 1)
    hits = jnp.where((dest_row == dest_col) & (row < col), 1.0, 0.0)
    rank = jnp.sum(hits, axis=0, keepdims=True).astype(jnp.int32)
    turned = dest_ref[...] ^ me
    slot = turned * each + rank
    place = lax.broadcasted_iota(jnp.int32, (slots, bundles), 0) == slot
    place = jnp.where(place, 1.0, 0.0)
    found = jnp.dot(
        place.astype(jnp.bfloat16),
        jnp.ones((bundles, LANES), jnp.bfloat16),
        preferred_element_type=jnp.float32,
    )
    place3 = jnp.concatenate([place] * 3, axis=1).astype(jnp.bfloat16)
    for part in range(4):
        rays = rays_ref[pl.ds(part, bundles, stride=4), :]
        terms = jnp.concatenate(split3(rays), axis=0)
        sent = jnp.dot(place3, terms, preferred_element_type=jnp.float32)
        if part % 2 == 0:
            sent = jnp.where(found > 0.5, sent, EMPTY)
        for s in range(n_sky):
            out_refs[s][pl.ds(part, each, stride=4), :] = sent[s * each:(s + 1) * each]
    ids = ids_ref[...]
    plane = lax.broadcasted_iota(jnp.int32, ids.shape, 0)
    owner = (ids // per_owner) ^ dest_ref[...]
    spot = (owner * planes + plane) * per_owner + ids % per_owner
    pad = jnp.zeros((SUB - planes, bundles), jnp.float32)
    fine = jnp.concatenate([(spot & 15).astype(jnp.float32), pad], axis=0)
    coarse = jnp.concatenate([(spot >> 4).astype(jnp.float32), pad], axis=0)
    place = place.astype(jnp.bfloat16)
    contract = (((1,), (1,)), ((), ()))
    fine = lax.dot_general(fine.astype(jnp.bfloat16), place, contract, preferred_element_type=jnp.float32)
    coarse = lax.dot_general(coarse.astype(jnp.bfloat16), place, contract, preferred_element_type=jnp.float32)
    numbers = coarse * 16.0 + fine
    for s in range(n_sky):
        first = s * each
        block = numbers[:, first // LANES * LANES:first // LANES * LANES + LANES]
        turn = (LANES - first % LANES) % LANES
        if turn:
            block = pltpu.roll(block, turn, 1)
        out_refs[s][pl.ds(4 * each, SUB), :] = block


def pack(n_sky, each, per_owner, me, dest, ids, rays):
    block = jax.ShapeDtypeStruct((4 * each + SUB, LANES), jnp.float32)
    return pl.pallas_call(
        functools.partial(pack_kernel, n_sky, each, per_owner),
        out_shape=[block] * n_sky,
        in_specs=[pl.BlockSpec(memory_space=pltpu.SMEM)] + [pl.BlockSpec(memory_space=pltpu.VMEM)] * 3,
        out_specs=[pl.BlockSpec(memory_space=pltpu.VMEM)] * n_sky,
        name="pack",
    )(me, dest, ids, rays)


def bilinear(f00, f01, f10, f11, u, v):
    one = f00 + u * (f01 - f00)
    two = f10 + u * (f11 - f10)
    return one + v * (two - one)


def lerp(one, two, t):
    return one + t * (two - one)


def window(tables, pos_x, pos_y):
    ix = (pos_x + float(SIDE)).astype(jnp.int32)
    iy = (pos_y + float(SIDE)).astype(jnp.int32)
    u = pos_x - (ix.astype(jnp.float32) - float(SIDE))
    v = pos_y - (iy.astype(jnp.float32) - float(SIDE))
    odd = (ix - 1) >> 1
    even = ix >> 1
    columns = (((even & 15), ((even + 1) & 15)), ((odd & 15), ((odd + 1) & 15)))
    odd_first = (ix & 1) == 0
    by_two = ((iy - 1) & 2) != 0
    by_one = (iy & 1) == 0
    sorted_columns = []
    for a in range(4):
        line = ((iy + (2 - a)) & 28) << 2
        e0, e1 = [lane_gather(tables[2 * a], line + c) for c in columns[0]]
        o0, o1 = [lane_gather(tables[2 * a + 1], line + c) for c in columns[1]]
        sorted_columns.append((
            jnp.where(odd_first, o0, e0),
            jnp.where(odd_first, e0, o0),
            jnp.where(odd_first, o1, e1),
            jnp.where(odd_first, e1, o1),
        ))
    w = [[None] * 4 for _ in range(4)]
    for k in range(4):
        half = [jnp.where(by_two, sorted_columns[(r + 2) & 3][k], sorted_columns[r][k]) for r in range(4)]
        for r in range(4):
            w[r][k] = jnp.where(by_one, half[(r + 1) & 3], half[r])
    return w, u, v


def trace_step(tables, strength, pos_x, pos_y, matrix):
    w, u, v = window(tables, pos_x, pos_y)
    gx = [lerp(w[1][k + 1] - w[1][k], w[2][k + 1] - w[2][k], v) for k in range(3)]
    gy = [lerp(w[r + 1][1] - w[r][1], w[r + 1][2] - w[r][2], u) for r in range(3)]
    fx2 = lerp(gx[0] + gx[1], gx[1] + gx[2], u)
    fxx = lerp(gx[1] - gx[0], gx[2] - gx[1], u)
    fy2 = lerp(gy[0] + gy[1], gy[1] + gy[2], v)
    fyy = lerp(gy[1] - gy[0], gy[2] - gy[1], v)
    wide = [[w[r][k + 2] - w[r][k] for k in range(2)] for r in range(4)]
    fxy4 = bilinear(
        wide[2][0] - wide[0][0], wide[2][1] - wide[0][1],
        wide[3][0] - wide[1][0], wide[3][1] - wide[1][1], u, v)
    half = 0.5 * strength
    hxx, hxy, hyy = strength * fxx, (0.25 * strength) * fxy4, strength * fyy
    m11, m12, m21, m22 = matrix
    matrix = (
        m11 - (hxx * m11 + hxy * m21),
        m12 - (hxx * m12 + hxy * m22),
        m21 - (hxy * m11 + hyy * m21),
        m22 - (hxy * m12 + hyy * m22),
    )
    return pos_x - half * fx2, pos_y - half * fy2, matrix


def trace_kernel(n_sky, each, planes, together, me_ref, lens_ref, *refs):
    tile_refs, got_refs = refs[:n_sky], refs[n_sky:2 * n_sky]
    shift_ref, matrix_ref, tiles, chosen, rays, places, sems = refs[2 * n_sky:]
    me = me_ref[0]
    slots = n_sky * each
    rows = tile_refs[0].shape[0]
    copies = []
    for s in range(n_sky):
        source = me ^ s
        copies.append((
            pltpu.make_async_copy(
                got_refs[s].at[pl.ds(4 * each, SUB), :],
                places.at[pl.ds(source * SUB, SUB), :],
                sems.at[0, s]),
            pltpu.make_async_copy(tile_refs[s], tiles.at[pl.ds(s * rows, rows), :], sems.at[1, s]),
            pltpu.make_async_copy(
                got_refs[s].at[pl.ds(0, 4 * each), :],
                rays.at[pl.ds(source * 4 * each, 4 * each), :],
                sems.at[2, s]),
        ))
    for kind in range(3):
        for s in range(n_sky):
            copies[s][kind].start()
    for kind in range(3):
        for s in range(n_sky):
            copies[s][kind].wait()

    def choose(slot, carry):
        source = slot // each
        k = slot % each
        for plane in range(planes):
            spot = places[source * SUB + plane, k].astype(jnp.int32)
            tile = tiles[pl.ds(pl.multiple_of(spot * CHUNKS, CHUNKS), CHUNKS), :]
            chosen[pl.ds(plane * CHUNKS * slots + slot, CHUNKS, stride=slots), :] = tile
        return carry

    lax.fori_loop(0, slots, choose, 0, unroll=8)

    def body(step, carry):
        chains = []
        for part in range(together):
            base = pl.multiple_of((step * together + part) * SUB, SUB)
            for h in range(2):
                x0 = rays[pl.ds(base * 4 + 2 * h, SUB, stride=4), :]
                y0 = rays[pl.ds(base * 4 + 2 * h + 1, SUB, stride=4), :]
                one = jnp.ones_like(x0)
                zero = jnp.zeros_like(x0)
                chains.append((base, h, x0, y0, (x0, y0, (one, zero, zero, one))))
        for plane in range(planes):
            strength = lens_ref[plane]
            later = []
            for base, h, x0, y0, state in chains:
                tables = [chosen[pl.ds((plane * CHUNKS + c) * slots + base, SUB), :] for c in range(CHUNKS)]
                later.append((base, h, x0, y0, trace_step(tables, strength, *state)))
            chains = later
        for base, h, x0, y0, (x, y, matrix) in chains:
            used = x0 > EMPTY * 0.5
            shift_ref[pl.ds(base * 4 + 2 * h, SUB, stride=4), :] = jnp.where(used, x - x0, 0.0)
            shift_ref[pl.ds(base * 4 + 2 * h + 1, SUB, stride=4), :] = jnp.where(used, y - y0, 0.0)
            for e in range(4):
                matrix_ref[pl.ds(base * 8 + 4 * h + e, SUB, stride=8), :] = jnp.where(used, matrix[e], 0.0)
        return carry

    lax.fori_loop(0, slots // (SUB * together), body, 0)


def trace(each, planes, me, lens_weight, tiles, got):
    n_sky = len(tiles)
    slots = n_sky * each
    rows = tiles[0].shape[0]
    return pl.pallas_call(
        functools.partial(trace_kernel, n_sky, each, planes, 2),
        out_shape=(
            jax.ShapeDtypeStruct((slots * 4, LANES), jnp.float32),
            jax.ShapeDtypeStruct((slots * 8, LANES), jnp.float32),
        ),
        in_specs=[pl.BlockSpec(memory_space=pltpu.SMEM)] * 2 + [pl.BlockSpec(memory_space=pl.ANY)] * (2 * n_sky),
        out_specs=(
            pl.BlockSpec(memory_space=pltpu.VMEM),
            pl.BlockSpec(memory_space=pltpu.VMEM),
        ),
        scratch_shapes=[
            pltpu.VMEM((n_sky * rows, LANES), jnp.float32),
            pltpu.VMEM((planes * CHUNKS * slots, LANES), jnp.float32),
            pltpu.VMEM((slots * 4, LANES), jnp.float32),
            pltpu.SMEM((n_sky * SUB, LANES), jnp.float32),
            pltpu.SemaphoreType.DMA((3, n_sky)),
        ],
        compiler_params=pltpu.CompilerParams(vmem_limit_bytes=40 * 1024 * 1024),
        name="trace",
    )(me, lens_weight, *tiles, *got)


def flipped(value, n_sky, bits):
    return lax.ppermute(value, "sky", [(i, i ^ bits) for i in range(n_sky)])


def everyone(own, n_sky):
    held = {0: own}
    bit = n_sky // 2
    while bit:
        for s in list(held):
            held[s ^ bit] = flipped(held[s], n_sky, bit)
        bit //= 2
    return [held[s] for s in range(n_sky)]


def shards(potential, lens_weight, ray_start, patch_index, destination):
    n_sky = lax.axis_size("sky")
    me = lax.axis_index("sky").reshape(1)
    planes, per_owner, _ = potential.shape
    bundles, _, rays = ray_start.shape
    each = max(2, 2 * bundles // n_sky)
    slots = n_sky * each
    halves = rays // LANES
    tiles = everyone(regroup(potential), n_sky)
    flat = ray_start.reshape(bundles, 2, halves, LANES).transpose(0, 2, 1, 3).reshape(bundles * 2 * halves, LANES)
    sent = pack(n_sky, each, per_owner, me, destination.reshape(1, bundles), patch_index, flat)
    got = [sent[0]] + [flipped(sent[s], n_sky, s) for s in range(1, n_sky)]
    shift, matrix = trace(each, planes, me, lens_weight, tiles, got)
    shift = shift.reshape(slots, halves, 2, LANES).transpose(0, 2, 1, 3).reshape(slots, 2, rays)
    matrix = matrix.reshape(slots, halves, 4, LANES).transpose(0, 2, 1, 3).reshape(slots, 4, rays)
    return shift, matrix


def solution(mesh):
    in_specs = (
        P("groups", "sky", None),
        P(),
        P(("groups", "sky"), None, None),
        P("groups", "sky"),
        P(("groups", "sky"), None),
    )
    out_specs = (P(("groups", "sky"), None, None), P(("groups", "sky"), None, None))
    return jax.shard_map(shards, mesh=mesh, in_specs=in_specs, out_specs=out_specs, check_vma=False)
```

time: 93 us -> 87.5 us (0.941)
  blocking collectives: 28.9 us -> 0 us
  starting transfers between devices: 0.04 us -> 25.7 us
  between operations: 14 us -> 0.7 us
  waiting for transfers between devices: 18.4 us -> 30.1 us
    ppermute x0 -> x30, waiting for transfers between devices: none -> 30.1 us  [flipped(): return lax.ppermute(value, 'sky', [(i, i ^ bits) for i in range(n_sky)])]
    all_to_all x1 -> x0, blocking collectives: 28.9 us -> none  [shards(): got = lax.all_to_all(sent, 'sky', split_axis=0, concat_axis=0, tiled=True)]
    ppermute x0 -> x30, starting transfers between devices: none -> 25.7 us  [flipped(): return lax.ppermute(value, 'sky', [(i, i ^ bits) for i in range(n_sky)])]
    all_gather x1 -> x0, waiting for transfers between devices: 18.4 us -> none  [shards(): tiles = lax.all_gather(regroup(potential), 'sky', axis=1, tiled=True)]
  transfers between devices with their start and end apart: 1 -> 30, of which waited for: 1 -> 13; matrix products, arithmetic and copies ran while one was open for 0% -> 0% of each run, Pallas kernels for 3% -> 3%
where the time goes in v2:
time: 87.5 us; the launch traced here: 87.3 us
  waiting for transfers between devices  30.1 us (34%)
  Pallas kernels  30 us (34%)
  starting transfers between devices  25.7 us (29%)
    ppermute x30, waiting for transfers between devices, flipped(): return lax.ppermute(value, 'sky', [(i, i ^ bits) for i in range(n_sky)])  30.1 us
    pallas_call x1, Pallas kernels, trace(): pl.pallas_call(functools.partial(trace_kernel, n_sky, each, planes, 2), o...  25.8 us
    ppermute x30, starting transfers between devices, flipped(): return lax.ppermute(value, 'sky', [(i, i ^ bits) for i in range(n_sky)])  25.7 us
    pallas_call x1, Pallas kernels, pack(): pl.pallas_call(functools.partial(pack_kernel, n_sky, each, per_owner), ou...  2.36 us
    pallas_call x1, Pallas kernels, regroup(): pl.pallas_call(regroup_kernel, out_shape=jax.ShapeDtypeStruct((rows, LANE...  1.88 us
  transfers between devices with their start and end apart: 30, of which 13 were waited for; matrix products, arithmetic and copies ran while one was open for 0% of the time, Pallas kernels for 3%

profile of v2, /device:TPU:0, one launch (start us, length us, event | category | flops | bytes accessed | tf_op | source)
XLA Modules:
  0.0 87.3 jit_solution(14932397097967080323)
XLA Ops:
  0.6 1.9 %regroup.1.refs_0_ = f32[256,128]{1,0:T(8,128)} custom-call(f32[4,8,1024]{2,1,0:T(8,128)} %src_ref.1), custom_call_target="tpu_custom_call" | custom-call | tf_op jit(solution)/shard_map/regroup/pallas_call | solution.py:68
  2.5 4.0 %collective-permute-start.7 = (f32[256,128]{1,0:T(8,128)}, f32[256,128]{1,0:T(8,128)S(1)}, u32[]{:S(2)}, u32[]{:S(2)}) collective-permute-start(f32[256,128]{1,0:T(8,128)} %regroup.1.refs_0_), channel_id=1, source_target_pairs={{0,8},{1,9},{2,10},{3,11},{4,12},{5,13},{6,14},{7,15},{8,0},{9,1},... | collective-permute-start | bytes 393224 | tf_op jit(solution)/shard_map/ppermute | solution.py:296
  6.5 2.4 %pack.1 = (f32[72,128]{1,0:T(8,128)}, f32[72,128]{1,0:T(8,128)}, f32[72,128]{1,0:T(8,128)}, f32[72,128]{1,0:T(8,128)}, f32[72,128]{1,0:T(8,128)}, /*index=5*/f32...) custom-call(s32[1]{0:T(128)} %bitcast.me_ref, ...), custom_call_target="tpu_custom_call" | custom-call | tf_op jit(solution)/shard_map/pack/pallas_call | solution.py:129
  8.9 0.0 collective-permute-start.15
  9.0 1.6 %collective-permute-start.16 = (f32[72,128]{1,0:T(8,128)}, f32[72,128]{1,0:T(8,128)S(1)}, u32[]{:S(2)}, u32[]{:S(2)}) collective-permute-start(f32[72,128]{1,0:T(8,128)} %get-tuple-element.22), channel_id=1, source_target_pairs={{0,2},{1,3},{2,0},{3,1},{4,6},{5,7},{6,4},{7,5},{8,10},{9,11},{10,... | collective-permute-start | bytes 110600 | tf_op jit(solution)/shard_map/ppermute | solution.py:296
  10.5 0.3 collective-permute-start.17
  10.8 1.6 %collective-permute-start.18 = (f32[72,128]{1,0:T(8,128)}, f32[72,128]{1,0:T(8,128)S(1)}, u32[]{:S(2)}, u32[]{:S(2)}) collective-permute-start(f32[72,128]{1,0:T(8,128)} %get-tuple-element.24), channel_id=1, source_target_pairs={{0,4},{1,5},{2,6},{3,7},{4,0},{5,1},{6,2},{7,3},{8,12},{9,13},{10,... | collective-permute-start | bytes 110600 | tf_op jit(solution)/shard_map/ppermute | solution.py:296
  12.4 0.1 collective-permute-start.19
  12.5 0.7 collective-permute-done.16.refs_18_
  13.2 2.9 %collective-permute-start.20 = (f32[72,128]{1,0:T(8,128)}, f32[72,128]{1,0:T(8,128)S(1)}, u32[]{:S(2)}, u32[]{:S(2)}) collective-permute-start(f32[72,128]{1,0:T(8,128)} %get-tuple-element.26), channel_id=1, source_target_pairs={{0,6},{1,7},{2,4},{3,5},{4,2},{5,3},{6,0},{7,1},{8,14},{9,15},{10,... | collective-permute-start | bytes 110600 | tf_op jit(solution)/shard_map/ppermute | solution.py:296
  16.0 0.0 collective-permute-done.17.refs_19_
  16.1 0.0 collective-permute-start.21
  16.1 0.0 collective-permute-done.18.refs_20_
  16.1 0.4 collective-permute-start.22
  16.5 2.0 %collective-permute-start.23 = (f32[72,128]{1,0:T(8,128)}, f32[72,128]{1,0:T(8,128)S(1)}, u32[]{:S(2)}, u32[]{:S(2)}) collective-permute-start(f32[72,128]{1,0:T(8,128)} %get-tuple-element.29), channel_id=1, source_target_pairs={{0,9},{1,8},{2,11},{3,10},{4,13},{5,12},{6,15},{7,14},{8,1},{9,0},... | collective-permute-start | bytes 110600 | tf_op jit(solution)/shard_map/ppermute | solution.py:296
  18.5 1.6 %collective-permute-start.24 = (f32[72,128]{1,0:T(8,128)}, f32[72,128]{1,0:T(8,128)S(1)}, u32[]{:S(2)}, u32[]{:S(2)}) collective-permute-start(f32[72,128]{1,0:T(8,128)} %get-tuple-element.30), channel_id=1, source_target_pairs={{0,10},{1,11},{2,8},{3,9},{4,14},{5,15},{6,12},{7,13},{8,2},{9,3},... | collective-permute-start | bytes 110600 | tf_op jit(solution)/shard_map/ppermute | solution.py:296
  20.1 0.4 collective-permute-done.21.refs_23_
  20.5 1.8 %collective-permute-start.25 = (f32[72,128]{1,0:T(8,128)}, f32[72,128]{1,0:T(8,128)S(1)}, u32[]{:S(2)}, u32[]{:S(2)}) collective-permute-start(f32[72,128]{1,0:T(8,128)} %get-tuple-element.31), channel_id=1, source_target_pairs={{0,11},{1,10},{2,9},{3,8},{4,15},{5,14},{6,13},{7,12},{8,3},{9,2},... | collective-permute-start | bytes 110600 | tf_op jit(solution)/shard_map/ppermute | solution.py:296
  22.4 0.6 collective-permute-done.22.refs_24_
  23.0 0.9 collective-permute-start.26
  23.8 0.0 collective-permute-done.23.refs_25_
  23.9 2.3 %collective-permute-done.24.refs_26_ = f32[72,128]{1,0:T(8,128)S(1)} collective-permute-done((f32[72,128]{1,0:T(8,128)}, f32[72,128]{1,0:T(8,128)S(1)}, u32[]{:S(2)}, u32[]{:S(2)}) %collective-permute-start.24) | collective-permute-done | bytes 36896 | tf_op jit(solution)/shard_map/ppermute | solution.py:296
  26.1 1.8 %collective-permute-start.1 = (f32[256,128]{1,0:T(8,128)S(1)}, f32[256,128]{1,0:T(8,128)S(1)}, u32[]{:S(2)}, u32[]{:S(2)}) collective-permute-start(f32[256,128]{1,0:T(8,128)S(1)} %copy-done), channel_id=1, source_target_pairs={{0,2},{1,3},{2,0},{3,1},{4,6},{5,7},{6,4},{7,5},{8,10},{9,11},{10,... | collective-permute-start | bytes 393224 | tf_op jit(solution)/shard_map/ppermute | solution.py:296
  28.0 0.1 collective-permute-start.11
  28.1 1.3 %collective-permute-done.26.refs_28_ = f32[72,128]{1,0:T(8,128)S(1)} collective-permute-done((f32[72,128]{1,0:T(8,128)}, f32[72,128]{1,0:T(8,128)S(1)}, u32[]{:S(2)}, u32[]{:S(2)}) %collective-permute-start.26) | collective-permute-done | bytes 36896 | tf_op jit(solution)/shard_map/ppermute | solution.py:296
  29.3 1.7 %collective-permute-start.27 = (f32[72,128]{1,0:T(8,128)}, f32[72,128]{1,0:T(8,128)S(1)}, u32[]{:S(2)}, u32[]{:S(2)}) collective-permute-start(f32[72,128]{1,0:T(8,128)} %get-tuple-element.33), channel_id=1, source_target_pairs={{0,13},{1,12},{2,15},{3,14},{4,9},{5,8},{6,11},{7,10},{8,5},{9,4},... | collective-permute-start | bytes 110600 | tf_op jit(solution)/shard_map/ppermute | solution.py:296
  31.0 4.6 %collective-permute-done.27.refs_29_ = f32[72,128]{1,0:T(8,128)S(1)} collective-permute-done((f32[72,128]{1,0:T(8,128)}, f32[72,128]{1,0:T(8,128)S(1)}, u32[]{:S(2)}, u32[]{:S(2)}) %collective-permute-start.27) | collective-permute-done | bytes 36896 | tf_op jit(solution)/shard_map/ppermute | solution.py:296
  35.6 1.2 %collective-permute-start.28 = (f32[72,128]{1,0:T(8,128)}, f32[72,128]{1,0:T(8,128)S(1)}, u32[]{:S(2)}, u32[]{:S(2)}) collective-permute-start(f32[72,128]{1,0:T(8,128)} %get-tuple-element.34), channel_id=1, source_target_pairs={{0,14},{1,15},{2,12},{3,13},{4,10},{5,11},{6,8},{7,9},{8,6},{9,7},... | collective-permute-start | bytes 110600 | tf_op jit(solution)/shard_map/ppermute | solution.py:296
  36.8 5.7 %collective-permute-done.28.refs_30_ = f32[72,128]{1,0:T(8,128)S(1)} collective-permute-done((f32[72,128]{1,0:T(8,128)}, f32[72,128]{1,0:T(8,128)S(1)}, u32[]{:S(2)}, u32[]{:S(2)}) %collective-permute-start.28) | collective-permute-done | bytes 36896 | tf_op jit(solution)/shard_map/ppermute | solution.py:296
  42.6 0.0 collective-permute-start.29
  42.6 6.3 %collective-permute-done.29.refs_31_ = f32[72,128]{1,0:T(8,128)S(1)} collective-permute-done((f32[72,128]{1,0:T(8,128)}, f32[72,128]{1,0:T(8,128)S(1)}, u32[]{:S(2)}, u32[]{:S(2)}) %collective-permute-start.29) | collective-permute-done | bytes 36896 | tf_op jit(solution)/shard_map/ppermute | solution.py:296
  48.9 0.4 collective-permute-start.9
  49.3 0.0 collective-permute-done.3.refs_4_
  49.3 1.7 %collective-permute-start.5 = (f32[256,128]{1,0:T(8,128)S(1)}, f32[256,128]{1,0:T(8,128)S(1)}, u32[]{:S(2)}, u32[]{:S(2)}) collective-permute-start(f32[256,128]{1,0:T(8,128)S(1)} %collective-permute-done.3.refs_4_), channel_id=1, source_target_pairs={{0,2},{1,3},{2,0},{3,1},{4,6},{5,7},{6,4},{7,5},{8,10},{9,11},{10,... | collective-permute-start | bytes 393224 | tf_op jit(solution)/shard_map/ppermute | solution.py:296
  51.0 0.2 collective-permute-start.4
  51.1 0.4 collective-permute-start.13
  51.5 3.7 %collective-permute-done.9.refs_10_ = f32[256,128]{1,0:T(8,128)S(1)} collective-permute-done((f32[256,128]{1,0:T(8,128)S(1)}, f32[256,128]{1,0:T(8,128)S(1)}, u32[]{:S(2)}, u32[]{:S(2)}) %collective-permute-start.9) | collective-permute-done | bytes 131104 | tf_op jit(solution)/shard_map/ppermute | solution.py:296
  55.2 0.0 collective-permute-done.8.refs_9_
  55.2 0.5 collective-permute-start.12
  55.8 2.2 %collective-permute-done.5.refs_6_ = f32[256,128]{1,0:T(8,128)S(1)} collective-permute-done((f32[256,128]{1,0:T(8,128)S(1)}, f32[256,128]{1,0:T(8,128)S(1)}, u32[]{:S(2)}, u32[]{:S(2)}) %collective-permute-start.5) | collective-permute-done | bytes 131104 | tf_op jit(solution)/shard_map/ppermute | solution.py:296
  58.0 0.5 collective-permute-start.6
  58.5 0.9 %collective-permute-done.13.refs_14_ = f32[256,128]{1,0:T(8,128)S(1)} collective-permute-done((f32[256,128]{1,0:T(8,128)S(1)}, f32[256,128]{1,0:T(8,128)S(1)}, u32[]{:S(2)}, u32[]{:S(2)}) %collective-permute-start.13) | collective-permute-done | bytes 131104 | tf_op jit(solution)/shard_map/ppermute | solution.py:296
  59.4 0.0 collective-permute-start.14
  59.4 0.0 collective-permute-done.2.refs_3_
  59.4 0.1 collective-permute-done.6.refs_7_
  59.5 1.2 %collective-permute-done.14.refs_15_ = f32[256,128]{1,0:T(8,128)S(1)} collective-permute-done((f32[256,128]{1,0:T(8,128)S(1)}, f32[256,128]{1,0:T(8,128)S(1)}, u32[]{:S(2)}, u32[]{:S(2)}) %collective-permute-start.14) | collective-permute-done | bytes 131104 | tf_op jit(solution)/shard_map/ppermute | solution.py:296
  60.7 0.8 copy-done.1
  61.5 25.8 %trace.1 = (f32[1024,128]{1,0:T(8,128)}, f32[2048,128]{1,0:T(8,128)}) custom-call(s32[1]{0:T(128)} %bitcast.me_ref, f32[4]{0:T(128)S(1)} %copy-done.2, f32[256,128]{1,0:T(8,128)S(1)} %copy-done, f32[256,128]{1,0:T(8,128)S(1)} %collective-permute-done.refs_1_, f32[256,128]{1,0:T(8,128)S(1)} %collective-permute-done.1.refs_2_, ...), custom_call_target="tpu_custom_call" | custom-call | tf_op jit(solution)/shard_map/trace/pallas_call | solution.py:272
  (21 shorter events, 0.1 us)
Async XLA Ops:
  2.5 25.5 %collective-permute-start.7 = (f32[256,128]{1,0:T(8,128)}, f32[256,128]{1,0:T(8,128)S(1)}, u32[]{:S(2)}, u32[]{:S(2)}) collective-permute-start(f32[256,128]{1,0:T(8,128)} %regroup.1.refs_0_), channel_id=1, source_target_pairs={{0,8},{1,9},{2,10},{3,11},{4,12},{5,13},{6,14},{7,15},{8,0},{9,1},... | collective-permute-start | bytes 393224 | tf_op jit(solution)/shard_map/ppermute | solution.py:296
  6.5 17.3 %copy-start = (f32[256,128]{1,0:T(8,128)S(1)}, f32[256,128]{1,0:T(8,128)}, u32[]{:S(2)}) copy-start(f32[256,128]{1,0:T(8,128)} %regroup.1.refs_0_) | copy-start | bytes 393220
  8.9 3.5 %collective-permute-start.15 = (f32[72,128]{1,0:T(8,128)}, f32[72,128]{1,0:T(8,128)S(1)}, u32[]{:S(2)}, u32[]{:S(2)}) collective-permute-start(f32[72,128]{1,0:T(8,128)} %get-tuple-element.21), channel_id=1, source_target_pairs={{0,1},{1,0},{2,3},{3,2},{4,5},{5,4},{6,7},{7,6},{8,9},{9,8},{10,11... | collective-permute-start | bytes 110600 | tf_op jit(solution)/shard_map/ppermute | solution.py:296
  9.0 4.2 %collective-permute-start.16 = (f32[72,128]{1,0:T(8,128)}, f32[72,128]{1,0:T(8,128)S(1)}, u32[]{:S(2)}, u32[]{:S(2)}) collective-permute-start(f32[72,128]{1,0:T(8,128)} %get-tuple-element.22), channel_id=1, source_target_pairs={{0,2},{1,3},{2,0},{3,1},{4,6},{5,7},{6,4},{7,5},{8,10},{9,11},{10,... | collective-permute-start | bytes 110600 | tf_op jit(solution)/shard_map/ppermute | solution.py:296
  10.5 5.5 %collective-permute-start.17 = (f32[72,128]{1,0:T(8,128)}, f32[72,128]{1,0:T(8,128)S(1)}, u32[]{:S(2)}, u32[]{:S(2)}) collective-permute-start(f32[72,128]{1,0:T(8,128)} %get-tuple-element.23), channel_id=1, source_target_pairs={{0,3},{1,2},{2,1},{3,0},{4,7},{5,6},{6,5},{7,4},{8,11},{9,10},{10,... | collective-permute-start | bytes 110600 | tf_op jit(solution)/shard_map/ppermute | solution.py:296
  10.8 5.2 %collective-permute-start.18 = (f32[72,128]{1,0:T(8,128)}, f32[72,128]{1,0:T(8,128)S(1)}, u32[]{:S(2)}, u32[]{:S(2)}) collective-permute-start(f32[72,128]{1,0:T(8,128)} %get-tuple-element.24), channel_id=1, source_target_pairs={{0,4},{1,5},{2,6},{3,7},{4,0},{5,1},{6,2},{7,3},{8,12},{9,13},{10,... | collective-permute-start | bytes 110600 | tf_op jit(solution)/shard_map/ppermute | solution.py:296
  12.4 4.1 %collective-permute-start.19 = (f32[72,128]{1,0:T(8,128)}, f32[72,128]{1,0:T(8,128)S(1)}, u32[]{:S(2)}, u32[]{:S(2)}) collective-permute-start(f32[72,128]{1,0:T(8,128)} %get-tuple-element.25), channel_id=1, source_target_pairs={{0,5},{1,4},{2,7},{3,6},{4,1},{5,0},{6,3},{7,2},{8,13},{9,12},{10,... | collective-permute-start | bytes 110600 | tf_op jit(solution)/shard_map/ppermute | solution.py:296
  13.2 5.3 %collective-permute-start.20 = (f32[72,128]{1,0:T(8,128)}, f32[72,128]{1,0:T(8,128)S(1)}, u32[]{:S(2)}, u32[]{:S(2)}) collective-permute-start(f32[72,128]{1,0:T(8,128)} %get-tuple-element.26), channel_id=1, source_target_pairs={{0,6},{1,7},{2,4},{3,5},{4,2},{5,3},{6,0},{7,1},{8,14},{9,15},{10,... | collective-permute-start | bytes 110600 | tf_op jit(solution)/shard_map/ppermute | solution.py:296
  16.1 4.5 %collective-permute-start.21 = (f32[72,128]{1,0:T(8,128)}, f32[72,128]{1,0:T(8,128)S(1)}, u32[]{:S(2)}, u32[]{:S(2)}) collective-permute-start(f32[72,128]{1,0:T(8,128)} %get-tuple-element.27), channel_id=1, source_target_pairs={{0,7},{1,6},{2,5},{3,4},{4,3},{5,2},{6,1},{7,0},{8,15},{9,14},{10,... | collective-permute-start | bytes 110600 | tf_op jit(solution)/shard_map/ppermute | solution.py:296
  16.1 6.9 %collective-permute-start.22 = (f32[72,128]{1,0:T(8,128)}, f32[72,128]{1,0:T(8,128)S(1)}, u32[]{:S(2)}, u32[]{:S(2)}) collective-permute-start(f32[72,128]{1,0:T(8,128)} %get-tuple-element.28), channel_id=1, source_target_pairs={{0,8},{1,9},{2,10},{3,11},{4,12},{5,13},{6,14},{7,15},{8,0},{9,1},... | collective-permute-start | bytes 110600 | tf_op jit(solution)/shard_map/ppermute | solution.py:296
  16.5 7.3 %collective-permute-start.23 = (f32[72,128]{1,0:T(8,128)}, f32[72,128]{1,0:T(8,128)S(1)}, u32[]{:S(2)}, u32[]{:S(2)}) collective-permute-start(f32[72,128]{1,0:T(8,128)} %get-tuple-element.29), channel_id=1, source_target_pairs={{0,9},{1,8},{2,11},{3,10},{4,13},{5,12},{6,15},{7,14},{8,1},{9,0},... | collective-permute-start | bytes 110600 | tf_op jit(solution)/shard_map/ppermute | solution.py:296
  18.5 7.6 %collective-permute-start.24 = (f32[72,128]{1,0:T(8,128)}, f32[72,128]{1,0:T(8,128)S(1)}, u32[]{:S(2)}, u32[]{:S(2)}) collective-permute-start(f32[72,128]{1,0:T(8,128)} %get-tuple-element.30), channel_id=1, source_target_pairs={{0,10},{1,11},{2,8},{3,9},{4,14},{5,15},{6,12},{7,13},{8,2},{9,3},... | collective-permute-start | bytes 110600 | tf_op jit(solution)/shard_map/ppermute | solution.py:296
  20.5 7.4 %collective-permute-start.25 = (f32[72,128]{1,0:T(8,128)}, f32[72,128]{1,0:T(8,128)S(1)}, u32[]{:S(2)}, u32[]{:S(2)}) collective-permute-start(f32[72,128]{1,0:T(8,128)} %get-tuple-element.31), channel_id=1, source_target_pairs={{0,11},{1,10},{2,9},{3,8},{4,15},{5,14},{6,13},{7,12},{8,3},{9,2},... | collective-permute-start | bytes 110600 | tf_op jit(solution)/shard_map/ppermute | solution.py:296
  23.0 6.4 %collective-permute-start.26 = (f32[72,128]{1,0:T(8,128)}, f32[72,128]{1,0:T(8,128)S(1)}, u32[]{:S(2)}, u32[]{:S(2)}) collective-permute-start(f32[72,128]{1,0:T(8,128)} %get-tuple-element.32), channel_id=1, source_target_pairs={{0,12},{1,13},{2,14},{3,15},{4,8},{5,9},{6,10},{7,11},{8,4},{9,5},... | collective-permute-start | bytes 110600 | tf_op jit(solution)/shard_map/ppermute | solution.py:296
  23.8 25.4 %collective-permute-start.3 = (f32[256,128]{1,0:T(8,128)S(1)}, f32[256,128]{1,0:T(8,128)S(1)}, u32[]{:S(2)}, u32[]{:S(2)}) collective-permute-start(f32[256,128]{1,0:T(8,128)S(1)} %copy-done), channel_id=1, source_target_pairs={{0,4},{1,5},{2,6},{3,7},{4,0},{5,1},{6,2},{7,3},{8,12},{9,13},{10,... | collective-permute-start | bytes 393224 | tf_op jit(solution)/shard_map/ppermute | solution.py:296
  26.1 23.1 %collective-permute-start.1 = (f32[256,128]{1,0:T(8,128)S(1)}, f32[256,128]{1,0:T(8,128)S(1)}, u32[]{:S(2)}, u32[]{:S(2)}) collective-permute-start(f32[256,128]{1,0:T(8,128)S(1)} %copy-done), channel_id=1, source_target_pairs={{0,2},{1,3},{2,0},{3,1},{4,6},{5,7},{6,4},{7,5},{8,10},{9,11},{10,... | collective-permute-start | bytes 393224 | tf_op jit(solution)/shard_map/ppermute | solution.py:296
  28.0 23.0 %collective-permute-start = (f32[256,128]{1,0:T(8,128)S(1)}, f32[256,128]{1,0:T(8,128)S(1)}, u32[]{:S(2)}, u32[]{:S(2)}) collective-permute-start(f32[256,128]{1,0:T(8,128)S(1)} %copy-done), channel_id=1, source_target_pairs={{0,1},{1,0},{2,3},{3,2},{4,5},{5,4},{6,7},{7,6},{8,9},{9,8},{10,11... | collective-permute-start | bytes 393224 | tf_op jit(solution)/shard_map/ppermute | solution.py:296
  28.0 23.2 %collective-permute-start.11 = (f32[256,128]{1,0:T(8,128)S(1)}, f32[256,128]{1,0:T(8,128)S(1)}, u32[]{:S(2)}, u32[]{:S(2)}) collective-permute-start(f32[256,128]{1,0:T(8,128)S(1)} %collective-permute-done.7.refs_8_), channel_id=1, source_target_pairs={{0,4},{1,5},{2,6},{3,7},{4,0},{5,1},{6,2},{7,3},{8,12},{9,13},{10,... | collective-permute-start | bytes 393224 | tf_op jit(solution)/shard_map/ppermute | solution.py:296
  29.3 6.3 %collective-permute-start.27 = (f32[72,128]{1,0:T(8,128)}, f32[72,128]{1,0:T(8,128)S(1)}, u32[]{:S(2)}, u32[]{:S(2)}) collective-permute-start(f32[72,128]{1,0:T(8,128)} %get-tuple-element.33), channel_id=1, source_target_pairs={{0,13},{1,12},{2,15},{3,14},{4,9},{5,8},{6,11},{7,10},{8,5},{9,4},... | collective-permute-start | bytes 110600 | tf_op jit(solution)/shard_map/ppermute | solution.py:296
  35.6 7.0 %collective-permute-start.28 = (f32[72,128]{1,0:T(8,128)}, f32[72,128]{1,0:T(8,128)S(1)}, u32[]{:S(2)}, u32[]{:S(2)}) collective-permute-start(f32[72,128]{1,0:T(8,128)} %get-tuple-element.34), channel_id=1, source_target_pairs={{0,14},{1,15},{2,12},{3,13},{4,10},{5,11},{6,8},{7,9},{8,6},{9,7},... | collective-permute-start | bytes 110600 | tf_op jit(solution)/shard_map/ppermute | solution.py:296
  42.6 18.2 %copy-start.2 = (f32[4]{0:T(128)S(1)}, f32[4]{0:T(128)}, u32[]{:S(2)}) copy-start(f32[4]{0:T(128)} %lens_ref.1) | copy-start | bytes 52
  42.6 6.3 %collective-permute-start.29 = (f32[72,128]{1,0:T(8,128)}, f32[72,128]{1,0:T(8,128)S(1)}, u32[]{:S(2)}, u32[]{:S(2)}) collective-permute-start(f32[72,128]{1,0:T(8,128)} %get-tuple-element.35), channel_id=1, source_target_pairs={{0,15},{1,14},{2,13},{3,12},{4,11},{5,10},{6,9},{7,8},{8,7},{9,6},... | collective-permute-start | bytes 110600 | tf_op jit(solution)/shard_map/ppermute | solution.py:296
  48.9 6.4 %collective-permute-start.9 = (f32[256,128]{1,0:T(8,128)S(1)}, f32[256,128]{1,0:T(8,128)S(1)}, u32[]{:S(2)}, u32[]{:S(2)}) collective-permute-start(f32[256,128]{1,0:T(8,128)S(1)} %collective-permute-done.7.refs_8_), channel_id=1, source_target_pairs={{0,2},{1,3},{2,0},{3,1},{4,6},{5,7},{6,4},{7,5},{8,10},{9,11},{10,... | collective-permute-start | bytes 393224 | tf_op jit(solution)/shard_map/ppermute | solution.py:296
  49.3 6.0 %collective-permute-start.8 = (f32[256,128]{1,0:T(8,128)S(1)}, f32[256,128]{1,0:T(8,128)S(1)}, u32[]{:S(2)}, u32[]{:S(2)}) collective-permute-start(f32[256,128]{1,0:T(8,128)S(1)} %collective-permute-done.7.refs_8_), channel_id=1, source_target_pairs={{0,1},{1,0},{2,3},{3,2},{4,5},{5,4},{6,7},{7,6},{8,9},{9,8},{10,11... | collective-permute-start | bytes 393224 | tf_op jit(solution)/shard_map/ppermute | solution.py:296
  49.3 8.7 %collective-permute-start.5 = (f32[256,128]{1,0:T(8,128)S(1)}, f32[256,128]{1,0:T(8,128)S(1)}, u32[]{:S(2)}, u32[]{:S(2)}) collective-permute-start(f32[256,128]{1,0:T(8,128)S(1)} %collective-permute-done.3.refs_4_), channel_id=1, source_target_pairs={{0,2},{1,3},{2,0},{3,1},{4,6},{5,7},{6,4},{7,5},{8,10},{9,11},{10,... | collective-permute-start | bytes 393224 | tf_op jit(solution)/shard_map/ppermute | solution.py:296
  51.0 7.0 %collective-permute-start.4 = (f32[256,128]{1,0:T(8,128)S(1)}, f32[256,128]{1,0:T(8,128)S(1)}, u32[]{:S(2)}, u32[]{:S(2)}) collective-permute-start(f32[256,128]{1,0:T(8,128)S(1)} %collective-permute-done.3.refs_4_), channel_id=1, source_target_pairs={{0,1},{1,0},{2,3},{3,2},{4,5},{5,4},{6,7},{7,6},{8,9},{9,8},{10,11... | collective-permute-start | bytes 393224 | tf_op jit(solution)/shard_map/ppermute | solution.py:296
  51.1 8.2 %collective-permute-start.13 = (f32[256,128]{1,0:T(8,128)S(1)}, f32[256,128]{1,0:T(8,128)S(1)}, u32[]{:S(2)}, u32[]{:S(2)}) collective-permute-start(f32[256,128]{1,0:T(8,128)S(1)} %collective-permute-done.11.refs_12_), channel_id=1, source_target_pairs={{0,2},{1,3},{2,0},{3,1},{4,6},{5,7},{6,4},{7,5},{8,10},{9,11},{10,... | collective-permute-start | bytes 393224 | tf_op jit(solution)/shard_map/ppermute | solution.py:296
  55.2 4.2 %collective-permute-start.2 = (f32[256,128]{1,0:T(8,128)S(1)}, f32[256,128]{1,0:T(8,128)S(1)}, u32[]{:S(2)}, u32[]{:S(2)}) collective-permute-start(f32[256,128]{1,0:T(8,128)S(1)} %collective-permute-done.1.refs_2_), channel_id=1, source_target_pairs={{0,1},{1,0},{2,3},{3,2},{4,5},{5,4},{6,7},{7,6},{8,9},{9,8},{10,11... | collective-permute-start | bytes 393224 | tf_op jit(solution)/shard_map/ppermute | solution.py:296
  55.2 4.2 %collective-permute-start.12 = (f32[256,128]{1,0:T(8,128)S(1)}, f32[256,128]{1,0:T(8,128)S(1)}, u32[]{:S(2)}, u32[]{:S(2)}) collective-permute-start(f32[256,128]{1,0:T(8,128)S(1)} %collective-permute-done.11.refs_12_), channel_id=1, source_target_pairs={{0,1},{1,0},{2,3},{3,2},{4,5},{5,4},{6,7},{7,6},{8,9},{9,8},{10,11... | collective-permute-start | bytes 393224 | tf_op jit(solution)/shard_map/ppermute | solution.py:296
  58.0 1.4 %collective-permute-start.10 = (f32[256,128]{1,0:T(8,128)S(1)}, f32[256,128]{1,0:T(8,128)S(1)}, u32[]{:S(2)}, u32[]{:S(2)}) collective-permute-start(f32[256,128]{1,0:T(8,128)S(1)} %collective-permute-done.9.refs_10_), channel_id=1, source_target_pairs={{0,1},{1,0},{2,3},{3,2},{4,5},{5,4},{6,7},{7,6},{8,9},{9,8},{10,11... | collective-permute-start | bytes 393224 | tf_op jit(solution)/shard_map/ppermute | solution.py:296
  58.0 1.5 %collective-permute-start.6 = (f32[256,128]{1,0:T(8,128)S(1)}, f32[256,128]{1,0:T(8,128)S(1)}, u32[]{:S(2)}, u32[]{:S(2)}) collective-permute-start(f32[256,128]{1,0:T(8,128)S(1)} %collective-permute-done.5.refs_6_), channel_id=1, source_target_pairs={{0,1},{1,0},{2,3},{3,2},{4,5},{5,4},{6,7},{7,6},{8,9},{9,8},{10,11... | collective-permute-start | bytes 393224 | tf_op jit(solution)/shard_map/ppermute | solution.py:296
  59.4 1.3 %collective-permute-start.14 = (f32[256,128]{1,0:T(8,128)S(1)}, f32[256,128]{1,0:T(8,128)S(1)}, u32[]{:S(2)}, u32[]{:S(2)}) collective-permute-start(f32[256,128]{1,0:T(8,128)S(1)} %collective-permute-done.13.refs_14_), channel_id=1, source_target_pairs={{0,1},{1,0},{2,3},{3,2},{4,5},{5,4},{6,7},{7,6},{8,9},{9,8},{10,11... | collective-permute-start | bytes 393224 | tf_op jit(solution)/shard_map/ppermute | solution.py:296
  60.7 0.8 copy-start.1

commit v3 on v2

--- a/solution.py
+++ b/solution.py
@@ -74,8 +74,7 @@
     )(potential)
 
 
-def pack_kernel(n_sky, each, per_owner, me_ref, dest_ref, ids_ref, rays_ref, *out_refs):
-    me = me_ref[0]
+def pack_kernel(n_sky, each, per_owner, dest_ref, ids_ref, rays_ref, out_ref):
     bundles = dest_ref.shape[1]
     planes = ids_ref.shape[0]
     slots = n_sky * each
@@ -85,8 +84,7 @@
     col = lax.broadcasted_iota(jnp.int32, (bundles, bundles), 1)
     hits = jnp.where((dest_row == dest_col) & (row < col), 1.0, 0.0)
     rank = jnp.sum(hits, axis=0, keepdims=True).astype(jnp.int32)
-    turned = dest_ref[...] ^ me
-    slot = turned * each + rank
+    slot = dest_ref[...] * each + rank
     place = lax.broadcasted_iota(jnp.int32, (slots, bundles), 0) == slot
     place = jnp.where(place, 1.0, 0.0)
     found = jnp.dot(
@@ -101,8 +99,8 @@
         sent = jnp.dot(place3, terms, preferred_element_type=jnp.float32)
         if part % 2 == 0:
             sent = jnp.where(found > 0.5, sent, EMPTY)
-        for s in range(n_sky):
-            out_refs[s][pl.ds(part, each, stride=4), :] = sent[s * each:(s + 1) * each]
+        for o in range(n_sky):
+            out_ref[o, pl.ds(part, each, stride=4), :] = sent[o * each:(o + 1) * each]
     ids = ids_ref[...]
     plane = lax.broadcasted_iota(jnp.int32, ids.shape, 0)
     owner = (ids // per_owner) ^ dest_ref[...]
@@ -115,24 +113,23 @@
     fine = lax.dot_general(fine.astype(jnp.bfloat16), place, contract, preferred_element_type=jnp.float32)
     coarse = lax.dot_general(coarse.astype(jnp.bfloat16), place, contract, preferred_element_type=jnp.float32)
     numbers = coarse * 16.0 + fine
-    for s in range(n_sky):
-        first = s * each
+    for o in range(n_sky):
+        first = o * each
         block = numbers[:, first // LANES * LANES:first // LANES * LANES + LANES]
         turn = (LANES - first % LANES) % LANES
         if turn:
             block = pltpu.roll(block, turn, 1)
-        out_refs[s][pl.ds(4 * each, SUB), :] = block
-
-
-def pack(n_sky, each, per_owner, me, dest, ids, rays):
-    block = jax.ShapeDtypeStruct((4 * each + SUB, LANES), jnp.float32)
+        out_ref[o, pl.ds(4 * each, SUB), :] = block
+
+
+def pack(n_sky, each, per_owner, dest, ids, rays):
     return pl.pallas_call(
         functools.partial(pack_kernel, n_sky, each, per_owner),
-        out_shape=[block] * n_sky,
-        in_specs=[pl.BlockSpec(memory_space=pltpu.SMEM)] + [pl.BlockSpec(memory_space=pltpu.VMEM)] * 3,
-        out_specs=[pl.BlockSpec(memory_space=pltpu.VMEM)] * n_sky,
+        out_shape=jax.ShapeDtypeStruct((n_sky, 4 * each + SUB, LANES), jnp.float32),
+        in_specs=[pl.BlockSpec(memory_space=pltpu.VMEM)] * 3,
+        out_specs=pl.BlockSpec(memory_space=pltpu.VMEM),
         name="pack",
-    )(me, dest, ids, rays)
+    )(dest, ids, rays)
 
 
 def bilinear(f00, f01, f10, f11, u, v):
@@ -199,24 +196,22 @@
     return pos_x - half * fx2, pos_y - half * fy2, matrix
 
 
-def trace_kernel(n_sky, each, planes, together, me_ref, lens_ref, *refs):
-    tile_refs, got_refs = refs[:n_sky], refs[n_sky:2 * n_sky]
-    shift_ref, matrix_ref, tiles, chosen, rays, places, sems = refs[2 * n_sky:]
-    me = me_ref[0]
+def trace_kernel(n_sky, each, planes, together, lens_ref, got_ref, *refs):
+    tile_refs = refs[:n_sky]
+    shift_ref, matrix_ref, tiles, chosen, rays, places, sems = refs[n_sky:]
     slots = n_sky * each
     rows = tile_refs[0].shape[0]
     copies = []
     for s in range(n_sky):
-        source = me ^ s
         copies.append((
             pltpu.make_async_copy(
-                got_refs[s].at[pl.ds(4 * each, SUB), :],
-                places.at[pl.ds(source * SUB, SUB), :],
+                got_ref.at[s, pl.ds(4 * each, SUB), :],
+                places.at[pl.ds(s * SUB, SUB), :],
                 sems.at[0, s]),
             pltpu.make_async_copy(tile_refs[s], tiles.at[pl.ds(s * rows, rows), :], sems.at[1, s]),
             pltpu.make_async_copy(
-                got_refs[s].at[pl.ds(0, 4 * each), :],
-                rays.at[pl.ds(source * 4 * each, 4 * each), :],
+                got_ref.at[s, pl.ds(0, 4 * each), :],
+                rays.at[pl.ds(s * 4 * each, 4 * each), :],
                 sems.at[2, s]),
         ))
     for kind in range(3):
@@ -226,35 +221,36 @@
         for s in range(n_sky):
             copies[s][kind].wait()
 
-    def choose(slot, carry):
-        source = slot // each
-        k = slot % each
-        for plane in range(planes):
-            spot = places[source * SUB + plane, k].astype(jnp.int32)
-            tile = tiles[pl.ds(pl.multiple_of(spot * CHUNKS, CHUNKS), CHUNKS), :]
-            chosen[pl.ds(plane * CHUNKS * slots + slot, CHUNKS, stride=slots), :] = tile
-        return carry
-
-    lax.fori_loop(0, slots, choose, 0, unroll=8)
-
     def body(step, carry):
         chains = []
+        first = pl.multiple_of(step * (together * SUB), together * SUB)
+        for plane in range(planes):
+            for part in range(together):
+                for k in range(SUB):
+                    slot = first + (part * SUB + k)
+                    spot = places[slot // each * SUB + plane, slot % each].astype(jnp.int32)
+                    tile = tiles[pl.ds(pl.multiple_of(spot * CHUNKS, CHUNKS), CHUNKS), :]
+                    chosen[pl.ds((plane * together + part) * CHUNKS * SUB + k, CHUNKS, stride=SUB), :] = tile
         for part in range(together):
-            base = pl.multiple_of((step * together + part) * SUB, SUB)
+            base = first + part * SUB
             for h in range(2):
                 x0 = rays[pl.ds(base * 4 + 2 * h, SUB, stride=4), :]
                 y0 = rays[pl.ds(base * 4 + 2 * h + 1, SUB, stride=4), :]
                 one = jnp.ones_like(x0)
                 zero = jnp.zeros_like(x0)
-                chains.append((base, h, x0, y0, (x0, y0, (one, zero, zero, one))))
+                chains.append((part, h, x0, y0, (x0, y0, (one, zero, zero, one))))
         for plane in range(planes):
             strength = lens_ref[plane]
             later = []
-            for base, h, x0, y0, state in chains:
-                tables = [chosen[pl.ds((plane * CHUNKS + c) * slots + base, SUB), :] for c in range(CHUNKS)]
-                later.append((base, h, x0, y0, trace_step(tables, strength, *state)))
+            for part, h, x0, y0, state in chains:
+                tables = [
+                    chosen[pl.ds(((plane * together + part) * CHUNKS + c) * SUB, SUB), :]
+                    for c in range(CHUNKS)
+                ]
+                later.append((part, h, x0, y0, trace_step(tables, strength, *state)))
             chains = later
-        for base, h, x0, y0, (x, y, matrix) in chains:
+        for part, h, x0, y0, (x, y, matrix) in chains:
+            base = first + part * SUB
             used = x0 > EMPTY * 0.5
             shift_ref[pl.ds(base * 4 + 2 * h, SUB, stride=4), :] = jnp.where(used, x - x0, 0.0)
             shift_ref[pl.ds(base * 4 + 2 * h + 1, SUB, stride=4), :] = jnp.where(used, y - y0, 0.0)
@@ -265,60 +261,67 @@
     lax.fori_loop(0, slots // (SUB * together), body, 0)
 
 
-def trace(each, planes, me, lens_weight, tiles, got):
+def trace(each, planes, lens_weight, got, tiles):
     n_sky = len(tiles)
     slots = n_sky * each
     rows = tiles[0].shape[0]
+    together = 2
     return pl.pallas_call(
-        functools.partial(trace_kernel, n_sky, each, planes, 2),
+        functools.partial(trace_kernel, n_sky, each, planes, together),
         out_shape=(
             jax.ShapeDtypeStruct((slots * 4, LANES), jnp.float32),
             jax.ShapeDtypeStruct((slots * 8, LANES), jnp.float32),
         ),
-        in_specs=[pl.BlockSpec(memory_space=pltpu.SMEM)] * 2 + [pl.BlockSpec(memory_space=pl.ANY)] * (2 * n_sky),
+        in_specs=[pl.BlockSpec(memory_space=pltpu.SMEM)] + [pl.BlockSpec(memory_space=pl.ANY)] * (1 + n_sky),
         out_specs=(
             pl.BlockSpec(memory_space=pltpu.VMEM),
             pl.BlockSpec(memory_space=pltpu.VMEM),
         ),
         scratch_shapes=[
             pltpu.VMEM((n_sky * rows, LANES), jnp.float32),
-            pltpu.VMEM((planes * CHUNKS * slots, LANES), jnp.float32),
+            pltpu.VMEM((planes * together * CHUNKS * SUB, LANES), jnp.float32),
             pltpu.VMEM((slots * 4, LANES), jnp.float32),
             pltpu.SMEM((n_sky * SUB, LANES), jnp.float32),
             pltpu.SemaphoreType.DMA((3, n_sky)),
         ],
         compiler_params=pltpu.CompilerParams(vmem_limit_bytes=40 * 1024 * 1024),
         name="trace",
-    )(me, lens_weight, *tiles, *got)
+    )(lens_weight, got, *tiles)
 
 
 def flipped(value, n_sky, bits):
     return lax.ppermute(value, "sky", [(i, i ^ bits) for i in range(n_sky)])
 
 
-def everyone(own, n_sky):
-    held = {0: own}
-    bit = n_sky // 2
-    while bit:
-        for s in list(held):
-            held[s ^ bit] = flipped(held[s], n_sky, bit)
-        bit //= 2
-    return [held[s] for s in range(n_sky)]
+def level(held, n_sky, bit):
+    for s in list(held):
+        held[s ^ bit] = flipped(held[s], n_sky, bit)
 
 
 def shards(potential, lens_weight, ray_start, patch_index, destination):
     n_sky = lax.axis_size("sky")
-    me = lax.axis_index("sky").reshape(1)
     planes, per_owner, _ = potential.shape
     bundles, _, rays = ray_start.shape
     each = max(2, 2 * bundles // n_sky)
     slots = n_sky * each
     halves = rays // LANES
-    tiles = everyone(regroup(potential), n_sky)
+    bits = [1 << k for k in reversed(range((n_sky - 1).bit_length()))]
+    held = {0: regroup(potential)}
     flat = ray_start.reshape(bundles, 2, halves, LANES).transpose(0, 2, 1, 3).reshape(bundles * 2 * halves, LANES)
-    sent = pack(n_sky, each, per_owner, me, destination.reshape(1, bundles), patch_index, flat)
-    got = [sent[0]] + [flipped(sent[s], n_sky, s) for s in range(1, n_sky)]
-    shift, matrix = trace(each, planes, me, lens_weight, tiles, got)
+    sent = pack(n_sky, each, per_owner, destination.reshape(1, bundles), patch_index, flat)
+    level(held, n_sky, bits[0])
+    sent, held[bits[0]] = lax.optimization_barrier((sent, held[bits[0]]))
+    level(held, n_sky, bits[1])
+    last = bits[0] ^ bits[1]
+    sent, held[last] = lax.optimization_barrier((sent, held[last]))
+    got = lax.all_to_all(sent, "sky", split_axis=0, concat_axis=0, tiled=True)
+    for bit in bits[2:-1]:
+        level(held, n_sky, bit)
+    late = sorted(s for s in held if s == last or s & (bits[1] - 1))
+    got, *tied = lax.optimization_barrier((got, *[held[s] for s in late]))
+    held.update(zip(late, tied))
+    level(held, n_sky, bits[-1])
+    shift, matrix = trace(each, planes, lens_weight, got, [held[s] for s in range(n_sky)])
     shift = shift.reshape(slots, halves, 2, LANES).transpose(0, 2, 1, 3).reshape(slots, 2, rays)
     matrix = matrix.reshape(slots, halves, 4, LANES).transpose(0, 2, 1, 3).reshape(slots, 4, rays)
     return shift, matrix

time: 87.5 us -> 72.1 us (0.82)
  starting transfers between devices: 25.7 us -> 19.7 us
  Pallas kernels: 30 us -> 24.5 us
  waiting for transfers between devices: 30.1 us -> 26.9 us
    ppermute x30 -> x15, starting transfers between devices: 25.7 us -> 13.4 us  [flipped(): return lax.ppermute(value, 'sky', [(i, i ^ bits) for i in range(n_sky)])]
    all_to_all x0 -> x1, starting transfers between devices: none -> 6.33 us  [shards(): got = lax.all_to_all(sent, 'sky', split_axis=0, concat_axis=0, tiled=True)]
    pallas_call x1, Pallas kernels: 25.8 us -> 20.2 us  [trace(): pl.pallas_call(functools.partial(trace_kernel, n_sky, each, planes, toget...]
    ppermute x30 -> x15, waiting for transfers between devices: 30.1 us -> 26.9 us  [flipped(): return lax.ppermute(value, 'sky', [(i, i ^ bits) for i in range(n_sky)])]
  transfers between devices with their start and end apart: 30 -> 16, of which waited for: 13 -> 11; matrix products, arithmetic and copies ran while one was open for 0% -> 0% of each run, Pallas kernels for 3% -> 3%
where the time goes in v3:
time: 72.1 us; the launch traced here: 71.7 us
  waiting for transfers between devices  26.9 us (37%)
  Pallas kernels  24.5 us (34%)
  starting transfers between devices  19.7 us (27%)
    ppermute x15, waiting for transfers between devices, flipped(): return lax.ppermute(value, 'sky', [(i, i ^ bits) for i in range(n_sky)])  26.9 us
    pallas_call x1, Pallas kernels, trace(): pl.pallas_call(functools.partial(trace_kernel, n_sky, each, planes, toget...  20.2 us
    ppermute x15, starting transfers between devices, flipped(): return lax.ppermute(value, 'sky', [(i, i ^ bits) for i in range(n_sky)])  13.4 us
    all_to_all x1, starting transfers between devices, shards(): got = lax.all_to_all(sent, 'sky', split_axis=0, concat_axis=0, tiled=True)  6.33 us
    pallas_call x1, Pallas kernels, pack(): pl.pallas_call(functools.partial(pack_kernel, n_sky, each, per_owner), ou...  2.37 us
    pallas_call x1, Pallas kernels, regroup(): pl.pallas_call(regroup_kernel, out_shape=jax.ShapeDtypeStruct((rows, LANE...  1.88 us
  transfers between devices with their start and end apart: 16, of which 11 were waited for; matrix products, arithmetic and copies ran while one was open for 0% of the time, Pallas kernels for 3%

profile of v3, /device:TPU:0, one launch (start us, length us, event | category | flops | bytes accessed | tf_op | source)
XLA Modules:
  0.0 71.7 jit_solution(10169813543224864371)
XLA Ops:
  0.6 1.9 %regroup.1.refs_0_ = f32[256,128]{1,0:T(8,128)} custom-call(f32[4,8,1024]{2,1,0:T(8,128)} %src_ref.1), custom_call_target="tpu_custom_call" | custom-call | tf_op jit(solution)/shard_map/regroup/pallas_call | solution.py:68
  2.5 4.0 %collective-permute-start = (f32[256,128]{1,0:T(8,128)}, f32[256,128]{1,0:T(8,128)S(1)}, u32[]{:S(2)}, u32[]{:S(2)}) collective-permute-start(f32[256,128]{1,0:T(8,128)} %regroup.1.refs_0_), channel_id=1, source_target_pairs={{0,8},{1,9},{2,10},{3,11},{4,12},{5,13},{6,14},{7,15},{8,0},{9,1},... | collective-permute-start | bytes 393224 | tf_op jit(solution)/shard_map/ppermute | solution.py:293
  6.5 2.4 %pack.1 = f32[16,72,128]{2,1,0:T(8,128)} custom-call(s32[1,128]{1,0:T(1,128)} %bitcast.17, s32[4,128]{1,0:T(4,128)} %ids_ref.1, f32[512,128]{1,0:T(8,128)} %bitcast.16), custom_call_target="tpu_custom_call" | custom-call | tf_op jit(solution)/shard_map/pack/pallas_call | solution.py:126
  8.9 0.0 copy-start
  8.9 0.0 copy-start.1
  8.9 4.1 %collective-permute-done.refs_8_ = f32[256,128]{1,0:T(8,128)S(1)} collective-permute-done((f32[256,128]{1,0:T(8,128)}, f32[256,128]{1,0:T(8,128)S(1)}, u32[]{:S(2)}, u32[]{:S(2)}) %collective-permute-start) | collective-permute-done | bytes 131104 | tf_op jit(solution)/shard_map/ppermute | solution.py:293
  13.1 0.8 %collective-permute-start.1 = (f32[256,128]{1,0:T(8,128)S(1)}, f32[256,128]{1,0:T(8,128)S(1)}, u32[]{:S(2)}, u32[]{:S(2)}) collective-permute-start(f32[256,128]{1,0:T(8,128)S(1)} %collective-permute-done.refs_8_), channel_id=1, source_target_pairs={{0,4},{1,5},{2,6},{3,7},{4,0},{5,1},{6,2},{7,3},{8,12},{9,13},{10,... | collective-permute-start | bytes 393224 | tf_op jit(solution)/shard_map/ppermute | solution.py:293
  13.9 4.1 %collective-permute-done.1.refs_12_ = f32[256,128]{1,0:T(8,128)S(1)} collective-permute-done((f32[256,128]{1,0:T(8,128)S(1)}, f32[256,128]{1,0:T(8,128)S(1)}, u32[]{:S(2)}, u32[]{:S(2)}) %collective-permute-start.1) | collective-permute-done | bytes 131104 | tf_op jit(solution)/shard_map/ppermute | solution.py:293
  18.0 6.3 %all-to-all-start = ((f32[16,72,128]{2,1,0:T(8,128)}), f32[16,72,128]{2,1,0:T(8,128)S(1)}, u32[]{:S(2)}, u32[]{:S(2)}) async-start(f32[16,72,128]{2,1,0:T(8,128)} %pack.1), calls=%async_computation | async-start | bytes 1179648 | tf_op jit(solution)/shard_map/all_to_all | solution.py:317
  24.4 0.0 copy-done
  24.4 2.0 %collective-permute-start.3 = (f32[256,128]{1,0:T(8,128)S(1)}, f32[256,128]{1,0:T(8,128)S(1)}, u32[]{:S(2)}, u32[]{:S(2)}) collective-permute-start(f32[256,128]{1,0:T(8,128)S(1)} %copy-done), channel_id=1, source_target_pairs={{0,4},{1,5},{2,6},{3,7},{4,0},{5,1},{6,2},{7,3},{8,12},{9,13},{10,... | collective-permute-start | bytes 393224 | tf_op jit(solution)/shard_map/ppermute | solution.py:293
  26.4 1.5 %collective-permute-start.2 = (f32[256,128]{1,0:T(8,128)S(1)}, f32[256,128]{1,0:T(8,128)S(1)}, u32[]{:S(2)}, u32[]{:S(2)}) collective-permute-start(f32[256,128]{1,0:T(8,128)S(1)} %copy-done), channel_id=1, source_target_pairs={{0,2},{1,3},{2,0},{3,1},{4,6},{5,7},{6,4},{7,5},{8,10},{9,11},{10,... | collective-permute-start | bytes 393224 | tf_op jit(solution)/shard_map/ppermute | solution.py:293
  27.8 11.8 %collective-permute-done.3.refs_4_ = f32[256,128]{1,0:T(8,128)S(1)} collective-permute-done((f32[256,128]{1,0:T(8,128)S(1)}, f32[256,128]{1,0:T(8,128)S(1)}, u32[]{:S(2)}, u32[]{:S(2)}) %collective-permute-start.3) | collective-permute-done | bytes 131104 | tf_op jit(solution)/shard_map/ppermute | solution.py:293
  39.6 1.4 %collective-permute-start.4 = (f32[256,128]{1,0:T(8,128)S(1)}, f32[256,128]{1,0:T(8,128)S(1)}, u32[]{:S(2)}, u32[]{:S(2)}) collective-permute-start(f32[256,128]{1,0:T(8,128)S(1)} %collective-permute-done.3.refs_4_), channel_id=1, source_target_pairs={{0,2},{1,3},{2,0},{3,1},{4,6},{5,7},{6,4},{7,5},{8,10},{9,11},{10,... | collective-permute-start | bytes 393224 | tf_op jit(solution)/shard_map/ppermute | solution.py:293
  41.0 0.6 collective-permute-start.5
  41.6 1.4 %collective-permute-start.6 = (f32[256,128]{1,0:T(8,128)S(1)}, f32[256,128]{1,0:T(8,128)S(1)}, u32[]{:S(2)}, u32[]{:S(2)}) collective-permute-start(f32[256,128]{1,0:T(8,128)S(1)} %collective-permute-done.1.refs_12_), channel_id=1, source_target_pairs={{0,2},{1,3},{2,0},{3,1},{4,6},{5,7},{6,4},{7,5},{8,10},{9,11},{10,... | collective-permute-start | bytes 393224 | tf_op jit(solution)/shard_map/ppermute | solution.py:293
  43.0 0.0 collective-permute-start.7
  43.0 0.0 collective-permute-done.2.refs_2_
  43.0 0.5 collective-permute-start.9
  43.5 2.5 %collective-permute-done.4.refs_6_ = f32[256,128]{1,0:T(8,128)S(1)} collective-permute-done((f32[256,128]{1,0:T(8,128)S(1)}, f32[256,128]{1,0:T(8,128)S(1)}, u32[]{:S(2)}, u32[]{:S(2)}) %collective-permute-start.4) | collective-permute-done | bytes 131104 | tf_op jit(solution)/shard_map/ppermute | solution.py:293
  46.0 0.0 collective-permute-start.11
  46.0 1.7 %collective-permute-done.5.refs_10_ = f32[256,128]{1,0:T(8,128)S(1)} collective-permute-done((f32[256,128]{1,0:T(8,128)S(1)}, f32[256,128]{1,0:T(8,128)S(1)}, u32[]{:S(2)}, u32[]{:S(2)}) %collective-permute-start.5) | collective-permute-done | bytes 131104 | tf_op jit(solution)/shard_map/ppermute | solution.py:293
  47.7 1.4 %collective-permute-done.6.refs_14_ = f32[256,128]{1,0:T(8,128)S(1)} collective-permute-done((f32[256,128]{1,0:T(8,128)S(1)}, f32[256,128]{1,0:T(8,128)S(1)}, u32[]{:S(2)}, u32[]{:S(2)}) %collective-permute-start.6) | collective-permute-done | bytes 131104 | tf_op jit(solution)/shard_map/ppermute | solution.py:293
  49.1 0.0 all-to-all-done.got_ref
  49.1 0.0 collective-permute-start.8
  49.1 0.5 collective-permute-start.10
  49.6 0.0 collective-permute-done.7.refs_1_
  49.7 0.0 collective-permute-start.12
  49.7 0.0 collective-permute-done.9.refs_5_
  49.7 0.5 collective-permute-start.13
  50.2 0.0 collective-permute-done.11.refs_9_
  50.2 0.1 collective-permute-start.14
  50.2 0.2 collective-permute-done.8.refs_3_
  50.5 0.2 collective-permute-done.10.refs_7_
  50.7 0.3 collective-permute-done.12.refs_11_
  51.0 0.2 collective-permute-done.13.refs_13_
  51.2 0.3 collective-permute-done.14.refs_15_
  51.5 0.0 copy-done.1
  51.5 20.2 %trace.1 = (f32[1024,128]{1,0:T(8,128)}, f32[2048,128]{1,0:T(8,128)}) custom-call(f32[4]{0:T(128)S(1)} %copy-done.1, f32[16,72,128]{2,1,0:T(8,128)S(1)} %all-to-all-done.got_ref, f32[256,128]{1,0:T(8,128)S(1)} %copy-done, f32[256,128]{1,0:T(8,128)S(1)} %collective-permute-done.7.refs_1_, f32[256,128]{1,0:T(8,128)S(1)} %collective-permute-done.2.refs_2_, ...), custom_call_target="tpu_custom_call" | custom-call | tf_op jit(solution)/shard_map/trace/pallas_call | solution.py:269
Async XLA Ops:
  2.5 10.5 %collective-permute-start = (f32[256,128]{1,0:T(8,128)}, f32[256,128]{1,0:T(8,128)S(1)}, u32[]{:S(2)}, u32[]{:S(2)}) collective-permute-start(f32[256,128]{1,0:T(8,128)} %regroup.1.refs_0_), channel_id=1, source_target_pairs={{0,8},{1,9},{2,10},{3,11},{4,12},{5,13},{6,14},{7,15},{8,0},{9,1},... | collective-permute-start | bytes 393224 | tf_op jit(solution)/shard_map/ppermute | solution.py:293
  8.9 15.4 %copy-start = (f32[256,128]{1,0:T(8,128)S(1)}, f32[256,128]{1,0:T(8,128)}, u32[]{:S(2)}) copy-start(f32[256,128]{1,0:T(8,128)} %regroup.1.refs_0_) | copy-start | bytes 393220
  8.9 42.6 %copy-start.1 = (f32[4]{0:T(128)S(1)}, f32[4]{0:T(128)}, u32[]{:S(2)}) copy-start(f32[4]{0:T(128)} %lens_ref.1) | copy-start | bytes 52
  13.1 5.0 %collective-permute-start.1 = (f32[256,128]{1,0:T(8,128)S(1)}, f32[256,128]{1,0:T(8,128)S(1)}, u32[]{:S(2)}, u32[]{:S(2)}) collective-permute-start(f32[256,128]{1,0:T(8,128)S(1)} %collective-permute-done.refs_8_), channel_id=1, source_target_pairs={{0,4},{1,5},{2,6},{3,7},{4,0},{5,1},{6,2},{7,3},{8,12},{9,13},{10,... | collective-permute-start | bytes 393224 | tf_op jit(solution)/shard_map/ppermute | solution.py:293
  18.0 31.1 %all-to-all-start = ((f32[16,72,128]{2,1,0:T(8,128)}), f32[16,72,128]{2,1,0:T(8,128)S(1)}, u32[]{:S(2)}, u32[]{:S(2)}) async-start(f32[16,72,128]{2,1,0:T(8,128)} %pack.1), calls=%async_computation | async-start | bytes 1179648 | tf_op jit(solution)/shard_map/all_to_all | solution.py:317
  24.4 15.2 %collective-permute-start.3 = (f32[256,128]{1,0:T(8,128)S(1)}, f32[256,128]{1,0:T(8,128)S(1)}, u32[]{:S(2)}, u32[]{:S(2)}) collective-permute-start(f32[256,128]{1,0:T(8,128)S(1)} %copy-done), channel_id=1, source_target_pairs={{0,4},{1,5},{2,6},{3,7},{4,0},{5,1},{6,2},{7,3},{8,12},{9,13},{10,... | collective-permute-start | bytes 393224 | tf_op jit(solution)/shard_map/ppermute | solution.py:293
  26.4 16.7 %collective-permute-start.2 = (f32[256,128]{1,0:T(8,128)S(1)}, f32[256,128]{1,0:T(8,128)S(1)}, u32[]{:S(2)}, u32[]{:S(2)}) collective-permute-start(f32[256,128]{1,0:T(8,128)S(1)} %copy-done), channel_id=1, source_target_pairs={{0,2},{1,3},{2,0},{3,1},{4,6},{5,7},{6,4},{7,5},{8,10},{9,11},{10,... | collective-permute-start | bytes 393224 | tf_op jit(solution)/shard_map/ppermute | solution.py:293
  39.6 6.4 %collective-permute-start.4 = (f32[256,128]{1,0:T(8,128)S(1)}, f32[256,128]{1,0:T(8,128)S(1)}, u32[]{:S(2)}, u32[]{:S(2)}) collective-permute-start(f32[256,128]{1,0:T(8,128)S(1)} %collective-permute-done.3.refs_4_), channel_id=1, source_target_pairs={{0,2},{1,3},{2,0},{3,1},{4,6},{5,7},{6,4},{7,5},{8,10},{9,11},{10,... | collective-permute-start | bytes 393224 | tf_op jit(solution)/shard_map/ppermute | solution.py:293
  41.0 6.7 %collective-permute-start.5 = (f32[256,128]{1,0:T(8,128)S(1)}, f32[256,128]{1,0:T(8,128)S(1)}, u32[]{:S(2)}, u32[]{:S(2)}) collective-permute-start(f32[256,128]{1,0:T(8,128)S(1)} %collective-permute-done.refs_8_), channel_id=1, source_target_pairs={{0,2},{1,3},{2,0},{3,1},{4,6},{5,7},{6,4},{7,5},{8,10},{9,11},{10,... | collective-permute-start | bytes 393224 | tf_op jit(solution)/shard_map/ppermute | solution.py:293
  41.6 7.5 %collective-permute-start.6 = (f32[256,128]{1,0:T(8,128)S(1)}, f32[256,128]{1,0:T(8,128)S(1)}, u32[]{:S(2)}, u32[]{:S(2)}) collective-permute-start(f32[256,128]{1,0:T(8,128)S(1)} %collective-permute-done.1.refs_12_), channel_id=1, source_target_pairs={{0,2},{1,3},{2,0},{3,1},{4,6},{5,7},{6,4},{7,5},{8,10},{9,11},{10,... | collective-permute-start | bytes 393224 | tf_op jit(solution)/shard_map/ppermute | solution.py:293
  43.0 6.6 %collective-permute-start.7 = (f32[256,128]{1,0:T(8,128)S(1)}, f32[256,128]{1,0:T(8,128)S(1)}, u32[]{:S(2)}, u32[]{:S(2)}) collective-permute-start(f32[256,128]{1,0:T(8,128)S(1)} %copy-done), channel_id=1, source_target_pairs={{0,1},{1,0},{2,3},{3,2},{4,5},{5,4},{6,7},{7,6},{8,9},{9,8},{10,11... | collective-permute-start | bytes 393224 | tf_op jit(solution)/shard_map/ppermute | solution.py:293
  43.0 6.6 %collective-permute-start.9 = (f32[256,128]{1,0:T(8,128)S(1)}, f32[256,128]{1,0:T(8,128)S(1)}, u32[]{:S(2)}, u32[]{:S(2)}) collective-permute-start(f32[256,128]{1,0:T(8,128)S(1)} %collective-permute-done.3.refs_4_), channel_id=1, source_target_pairs={{0,1},{1,0},{2,3},{3,2},{4,5},{5,4},{6,7},{7,6},{8,9},{9,8},{10,11... | collective-permute-start | bytes 393224 | tf_op jit(solution)/shard_map/ppermute | solution.py:293
  46.0 4.2 %collective-permute-start.11 = (f32[256,128]{1,0:T(8,128)S(1)}, f32[256,128]{1,0:T(8,128)S(1)}, u32[]{:S(2)}, u32[]{:S(2)}) collective-permute-start(f32[256,128]{1,0:T(8,128)S(1)} %collective-permute-done.refs_8_), channel_id=1, source_target_pairs={{0,1},{1,0},{2,3},{3,2},{4,5},{5,4},{6,7},{7,6},{8,9},{9,8},{10,11... | collective-permute-start | bytes 393224 | tf_op jit(solution)/shard_map/ppermute | solution.py:293
  49.1 1.3 %collective-permute-start.8 = (f32[256,128]{1,0:T(8,128)S(1)}, f32[256,128]{1,0:T(8,128)S(1)}, u32[]{:S(2)}, u32[]{:S(2)}) collective-permute-start(f32[256,128]{1,0:T(8,128)S(1)} %collective-permute-done.2.refs_2_), channel_id=1, source_target_pairs={{0,1},{1,0},{2,3},{3,2},{4,5},{5,4},{6,7},{7,6},{8,9},{9,8},{10,11... | collective-permute-start | bytes 393224 | tf_op jit(solution)/shard_map/ppermute | solution.py:293
  49.1 1.5 %collective-permute-start.10 = (f32[256,128]{1,0:T(8,128)S(1)}, f32[256,128]{1,0:T(8,128)S(1)}, u32[]{:S(2)}, u32[]{:S(2)}) collective-permute-start(f32[256,128]{1,0:T(8,128)S(1)} %collective-permute-done.4.refs_6_), channel_id=1, source_target_pairs={{0,1},{1,0},{2,3},{3,2},{4,5},{5,4},{6,7},{7,6},{8,9},{9,8},{10,11... | collective-permute-start | bytes 393224 | tf_op jit(solution)/shard_map/ppermute | solution.py:293
  49.7 1.3 %collective-permute-start.12 = (f32[256,128]{1,0:T(8,128)S(1)}, f32[256,128]{1,0:T(8,128)S(1)}, u32[]{:S(2)}, u32[]{:S(2)}) collective-permute-start(f32[256,128]{1,0:T(8,128)S(1)} %collective-permute-done.5.refs_10_), channel_id=1, source_target_pairs={{0,1},{1,0},{2,3},{3,2},{4,5},{5,4},{6,7},{7,6},{8,9},{9,8},{10,11... | collective-permute-start | bytes 393224 | tf_op jit(solution)/shard_map/ppermute | solution.py:293
  49.7 1.5 %collective-permute-start.13 = (f32[256,128]{1,0:T(8,128)S(1)}, f32[256,128]{1,0:T(8,128)S(1)}, u32[]{:S(2)}, u32[]{:S(2)}) collective-permute-start(f32[256,128]{1,0:T(8,128)S(1)} %collective-permute-done.1.refs_12_), channel_id=1, source_target_pairs={{0,1},{1,0},{2,3},{3,2},{4,5},{5,4},{6,7},{7,6},{8,9},{9,8},{10,11... | collective-permute-start | bytes 393224 | tf_op jit(solution)/shard_map/ppermute | solution.py:293
  50.2 1.3 %collective-permute-start.14 = (f32[256,128]{1,0:T(8,128)S(1)}, f32[256,128]{1,0:T(8,128)S(1)}, u32[]{:S(2)}, u32[]{:S(2)}) collective-permute-start(f32[256,128]{1,0:T(8,128)S(1)} %collective-permute-done.6.refs_14_), channel_id=1, source_target_pairs={{0,1},{1,0},{2,3},{3,2},{4,5},{5,4},{6,7},{7,6},{8,9},{9,8},{10,11... | collective-permute-start | bytes 393224 | tf_op jit(solution)/shard_map/ppermute | solution.py:293

commit v4 on v3

--- a/solution.py
+++ b/solution.py
@@ -265,7 +265,7 @@
     n_sky = len(tiles)
     slots = n_sky * each
     rows = tiles[0].shape[0]
-    together = 2
+    together = 1
     return pl.pallas_call(
         functools.partial(trace_kernel, n_sky, each, planes, together),
         out_shape=(
@@ -293,9 +293,11 @@
     return lax.ppermute(value, "sky", [(i, i ^ bits) for i in range(n_sky)])
 
 
-def level(held, n_sky, bit):
-    for s in list(held):
-        held[s ^ bit] = flipped(held[s], n_sky, bit)
+def spread(held, n_sky, bits):
+    for bit in bits:
+        for s in [s for s in held if s & (2 * bit - 1) == 0]:
+            if s ^ bit not in held:
+                held[s ^ bit] = flipped(held[s], n_sky, bit)
 
 
 def shards(potential, lens_weight, ray_start, patch_index, destination):
@@ -309,18 +311,13 @@
     held = {0: regroup(potential)}
     flat = ray_start.reshape(bundles, 2, halves, LANES).transpose(0, 2, 1, 3).reshape(bundles * 2 * halves, LANES)
     sent = pack(n_sky, each, per_owner, destination.reshape(1, bundles), patch_index, flat)
-    level(held, n_sky, bits[0])
-    sent, held[bits[0]] = lax.optimization_barrier((sent, held[bits[0]]))
-    level(held, n_sky, bits[1])
-    last = bits[0] ^ bits[1]
-    sent, held[last] = lax.optimization_barrier((sent, held[last]))
+    near = [bit for bit in bits[:3] if bit > 1]
+    for bit in near:
+        held[bit] = flipped(held[0], n_sky, bit)
+    sent, *first = lax.optimization_barrier((sent, *[held[bit] for bit in near]))
+    held.update(zip(near, first))
     got = lax.all_to_all(sent, "sky", split_axis=0, concat_axis=0, tiled=True)
-    for bit in bits[2:-1]:
-        level(held, n_sky, bit)
-    late = sorted(s for s in held if s == last or s & (bits[1] - 1))
-    got, *tied = lax.optimization_barrier((got, *[held[s] for s in late]))
-    held.update(zip(late, tied))
-    level(held, n_sky, bits[-1])
+    spread(held, n_sky, bits)
     shift, matrix = trace(each, planes, lens_weight, got, [held[s] for s in range(n_sky)])
     shift = shift.reshape(slots, halves, 2, LANES).transpose(0, 2, 1, 3).reshape(slots, 2, rays)
     matrix = matrix.reshape(slots, halves, 4, LANES).transpose(0, 2, 1, 3).reshape(slots, 4, rays)

time: 72.1 us -> 71.6 us (level)
  Pallas kernels: 24.5 us -> 34.5 us
  waiting for transfers between devices: 26.9 us -> 18.3 us
  starting transfers between devices: 19.7 us -> 17.8 us
    pallas_call x1, Pallas kernels: 20.2 us -> 30.2 us  [trace(): pl.pallas_call(functools.partial(trace_kernel, n_sky, each, planes, toget...]
    ppermute x15, waiting for transfers between devices: 26.9 us -> 18.3 us  [flipped(): return lax.ppermute(value, 'sky', [(i, i ^ bits) for i in range(n_sky)])]
    all_to_all x1, starting transfers between devices: 6.33 us -> 3.84 us  [shards(): got = lax.all_to_all(sent, 'sky', split_axis=0, concat_axis=0, tiled=True)]
  transfers between devices with their start and end apart: 16 -> 16, of which waited for: 11 -> 5; matrix products, arithmetic and copies ran while one was open for 0% -> 0% of each run, Pallas kernels for 3% -> 3%
where the time goes in v4:
time: 71.6 us; the launch traced here: 71.3 us
  Pallas kernels  34.5 us (48%)
  waiting for transfers between devices  18.3 us (26%)
  starting transfers between devices  17.8 us (25%)
    pallas_call x1, Pallas kernels, trace(): pl.pallas_call(functools.partial(trace_kernel, n_sky, each, planes, toget...  30.2 us
    ppermute x15, waiting for transfers between devices, flipped(): return lax.ppermute(value, 'sky', [(i, i ^ bits) for i in range(n_sky)])  18.3 us
    ppermute x15, starting transfers between devices, flipped(): return lax.ppermute(value, 'sky', [(i, i ^ bits) for i in range(n_sky)])  14 us
    all_to_all x1, starting transfers between devices, shards(): got = lax.all_to_all(sent, 'sky', split_axis=0, concat_axis=0, tiled=True)  3.84 us
    pallas_call x1, Pallas kernels, pack(): pl.pallas_call(functools.partial(pack_kernel, n_sky, each, per_owner), ou...  2.37 us
    pallas_call x1, Pallas kernels, regroup(): pl.pallas_call(regroup_kernel, out_shape=jax.ShapeDtypeStruct((rows, LANE...  1.88 us
  transfers between devices with their start and end apart: 16, of which 5 were waited for; matrix products, arithmetic and copies ran while one was open for 0% of the time, Pallas kernels for 3%

profile of v4, /device:TPU:0, one launch (start us, length us, event | category | flops | bytes accessed | tf_op | source)
XLA Modules:
  0.0 71.3 jit_solution(3009783163922156910)
XLA Ops:
  0.6 1.9 %regroup.1.refs_0_ = f32[256,128]{1,0:T(8,128)} custom-call(f32[4,8,1024]{2,1,0:T(8,128)} %src_ref.1), custom_call_target="tpu_custom_call" | custom-call | tf_op jit(solution)/shard_map/regroup/pallas_call | solution.py:68
  2.5 3.0 %collective-permute-start.2 = (f32[256,128]{1,0:T(8,128)}, f32[256,128]{1,0:T(8,128)S(1)}, u32[]{:S(2)}, u32[]{:S(2)}) collective-permute-start(f32[256,128]{1,0:T(8,128)} %regroup.1.refs_0_), channel_id=1, source_target_pairs={{0,2},{1,3},{2,0},{3,1},{4,6},{5,7},{6,4},{7,5},{8,10},{9,11},{10,... | collective-permute-start | bytes 393224 | tf_op jit(solution)/shard_map/ppermute | solution.py:293
  5.5 1.6 %collective-permute-start.1 = (f32[256,128]{1,0:T(8,128)}, f32[256,128]{1,0:T(8,128)S(1)}, u32[]{:S(2)}, u32[]{:S(2)}) collective-permute-start(f32[256,128]{1,0:T(8,128)} %regroup.1.refs_0_), channel_id=1, source_target_pairs={{0,4},{1,5},{2,6},{3,7},{4,0},{5,1},{6,2},{7,3},{8,12},{9,13},{10,... | collective-permute-start | bytes 393224 | tf_op jit(solution)/shard_map/ppermute | solution.py:293
  7.1 2.6 %collective-permute-start = (f32[256,128]{1,0:T(8,128)}, f32[256,128]{1,0:T(8,128)S(1)}, u32[]{:S(2)}, u32[]{:S(2)}) collective-permute-start(f32[256,128]{1,0:T(8,128)} %regroup.1.refs_0_), channel_id=1, source_target_pairs={{0,8},{1,9},{2,10},{3,11},{4,12},{5,13},{6,14},{7,15},{8,0},{9,1},... | collective-permute-start | bytes 393224 | tf_op jit(solution)/shard_map/ppermute | solution.py:293
  9.6 2.4 %pack.1 = f32[16,72,128]{2,1,0:T(8,128)} custom-call(s32[1,128]{1,0:T(1,128)} %bitcast.17, s32[4,128]{1,0:T(4,128)} %ids_ref.1, f32[512,128]{1,0:T(8,128)} %bitcast.16), custom_call_target="tpu_custom_call" | custom-call | tf_op jit(solution)/shard_map/pack/pallas_call | solution.py:126
  12.0 0.0 copy-start
  12.0 0.0 copy-start.1
  12.0 0.0 collective-permute-done.2.refs_2_
  12.0 0.3 collective-permute-done.1.refs_4_
  12.3 3.4 %collective-permute-done.refs_8_ = f32[256,128]{1,0:T(8,128)S(1)} collective-permute-done((f32[256,128]{1,0:T(8,128)}, f32[256,128]{1,0:T(8,128)S(1)}, u32[]{:S(2)}, u32[]{:S(2)}) %collective-permute-start) | collective-permute-done | bytes 131104 | tf_op jit(solution)/shard_map/ppermute | solution.py:293
  15.7 3.8 %all-to-all-start = ((f32[16,72,128]{2,1,0:T(8,128)}), f32[16,72,128]{2,1,0:T(8,128)S(1)}, u32[]{:S(2)}, u32[]{:S(2)}) async-start(f32[16,72,128]{2,1,0:T(8,128)} %pack.1), calls=%async_computation | async-start | bytes 1179648 | tf_op jit(solution)/shard_map/all_to_all | solution.py:319
  19.6 0.0 copy-done
  19.6 0.5 collective-permute-start.3
  20.0 1.7 %collective-permute-start.11 = (f32[256,128]{1,0:T(8,128)S(1)}, f32[256,128]{1,0:T(8,128)S(1)}, u32[]{:S(2)}, u32[]{:S(2)}) collective-permute-start(f32[256,128]{1,0:T(8,128)S(1)} %collective-permute-done.refs_8_), channel_id=1, source_target_pairs={{0,4},{1,5},{2,6},{3,7},{4,0},{5,1},{6,2},{7,3},{8,12},{9,13},{10,... | collective-permute-start | bytes 393224 | tf_op jit(solution)/shard_map/ppermute | solution.py:293
  21.7 0.1 collective-permute-start.4
  21.8 1.5 %collective-permute-start.6 = (f32[256,128]{1,0:T(8,128)S(1)}, f32[256,128]{1,0:T(8,128)S(1)}, u32[]{:S(2)}, u32[]{:S(2)}) collective-permute-start(f32[256,128]{1,0:T(8,128)S(1)} %collective-permute-done.1.refs_4_), channel_id=1, source_target_pairs={{0,2},{1,3},{2,0},{3,1},{4,6},{5,7},{6,4},{7,5},{8,10},{9,11},{10,... | collective-permute-start | bytes 393224 | tf_op jit(solution)/shard_map/ppermute | solution.py:293
  23.2 0.2 collective-permute-start.5
  23.4 0.0 collective-permute-done.3.refs_1_
  23.4 0.6 collective-permute-start.9
  24.0 10.8 %collective-permute-done.11.refs_12_ = f32[256,128]{1,0:T(8,128)S(1)} collective-permute-done((f32[256,128]{1,0:T(8,128)S(1)}, f32[256,128]{1,0:T(8,128)S(1)}, u32[]{:S(2)}, u32[]{:S(2)}) %collective-permute-start.11) | collective-permute-done | bytes 131104 | tf_op jit(solution)/shard_map/ppermute | solution.py:293
  34.8 1.4 %collective-permute-start.13 = (f32[256,128]{1,0:T(8,128)S(1)}, f32[256,128]{1,0:T(8,128)S(1)}, u32[]{:S(2)}, u32[]{:S(2)}) collective-permute-start(f32[256,128]{1,0:T(8,128)S(1)} %collective-permute-done.11.refs_12_), channel_id=1, source_target_pairs={{0,2},{1,3},{2,0},{3,1},{4,6},{5,7},{6,4},{7,5},{8,10},{9,11},{10,... | collective-permute-start | bytes 393224 | tf_op jit(solution)/shard_map/ppermute | solution.py:293
  36.2 0.0 collective-permute-done.4.refs_3_
  36.2 0.0 collective-permute-start.8
  36.2 0.0 collective-permute-done.6.refs_6_
  36.2 0.5 collective-permute-start.12
  36.7 0.0 collective-permute-done.5.refs_5_
  36.7 0.1 collective-permute-start.7
  36.8 0.0 collective-permute-done.9.refs_10_
  36.8 0.4 collective-permute-start.10
  37.2 2.5 %collective-permute-done.13.refs_14_ = f32[256,128]{1,0:T(8,128)S(1)} collective-permute-done((f32[256,128]{1,0:T(8,128)S(1)}, f32[256,128]{1,0:T(8,128)S(1)}, u32[]{:S(2)}, u32[]{:S(2)}) %collective-permute-start.13) | collective-permute-done | bytes 131104 | tf_op jit(solution)/shard_map/ppermute | solution.py:293
  39.7 0.0 collective-permute-start.14
  39.7 0.0 collective-permute-done.8.refs_9_
  39.8 0.0 collective-permute-done.7.refs_7_
  39.8 0.0 collective-permute-done.12.refs_13_
  39.8 0.0 collective-permute-done.10.refs_11_
  39.8 1.3 %collective-permute-done.14.refs_15_ = f32[256,128]{1,0:T(8,128)S(1)} collective-permute-done((f32[256,128]{1,0:T(8,128)S(1)}, f32[256,128]{1,0:T(8,128)S(1)}, u32[]{:S(2)}, u32[]{:S(2)}) %collective-permute-start.14) | collective-permute-done | bytes 131104 | tf_op jit(solution)/shard_map/ppermute | solution.py:293
  41.1 0.0 all-to-all-done.got_ref
  41.1 0.0 copy-done.1
  41.1 30.2 %trace.1 = (f32[1024,128]{1,0:T(8,128)}, f32[2048,128]{1,0:T(8,128)}) custom-call(f32[4]{0:T(128)S(1)} %copy-done.1, f32[16,72,128]{2,1,0:T(8,128)S(1)} %all-to-all-done.got_ref, f32[256,128]{1,0:T(8,128)S(1)} %copy-done, f32[256,128]{1,0:T(8,128)S(1)} %collective-permute-done.3.refs_1_, f32[256,128]{1,0:T(8,128)S(1)} %collective-permute-done.2.refs_2_, ...), custom_call_target="tpu_custom_call" | custom-call | tf_op jit(solution)/shard_map/trace/pallas_call | solution.py:269
Async XLA Ops:
  2.5 9.5 %collective-permute-start.2 = (f32[256,128]{1,0:T(8,128)}, f32[256,128]{1,0:T(8,128)S(1)}, u32[]{:S(2)}, u32[]{:S(2)}) collective-permute-start(f32[256,128]{1,0:T(8,128)} %regroup.1.refs_0_), channel_id=1, source_target_pairs={{0,2},{1,3},{2,0},{3,1},{4,6},{5,7},{6,4},{7,5},{8,10},{9,11},{10,... | collective-permute-start | bytes 393224 | tf_op jit(solution)/shard_map/ppermute | solution.py:293
  5.5 6.8 %collective-permute-start.1 = (f32[256,128]{1,0:T(8,128)}, f32[256,128]{1,0:T(8,128)S(1)}, u32[]{:S(2)}, u32[]{:S(2)}) collective-permute-start(f32[256,128]{1,0:T(8,128)} %regroup.1.refs_0_), channel_id=1, source_target_pairs={{0,4},{1,5},{2,6},{3,7},{4,0},{5,1},{6,2},{7,3},{8,12},{9,13},{10,... | collective-permute-start | bytes 393224 | tf_op jit(solution)/shard_map/ppermute | solution.py:293
  7.1 8.7 %collective-permute-start = (f32[256,128]{1,0:T(8,128)}, f32[256,128]{1,0:T(8,128)S(1)}, u32[]{:S(2)}, u32[]{:S(2)}) collective-permute-start(f32[256,128]{1,0:T(8,128)} %regroup.1.refs_0_), channel_id=1, source_target_pairs={{0,8},{1,9},{2,10},{3,11},{4,12},{5,13},{6,14},{7,15},{8,0},{9,1},... | collective-permute-start | bytes 393224 | tf_op jit(solution)/shard_map/ppermute | solution.py:293
  12.0 7.5 %copy-start = (f32[256,128]{1,0:T(8,128)S(1)}, f32[256,128]{1,0:T(8,128)}, u32[]{:S(2)}) copy-start(f32[256,128]{1,0:T(8,128)} %regroup.1.refs_0_) | copy-start | bytes 393220
  12.0 29.1 %copy-start.1 = (f32[4]{0:T(128)S(1)}, f32[4]{0:T(128)}, u32[]{:S(2)}) copy-start(f32[4]{0:T(128)} %lens_ref.1) | copy-start | bytes 52
  15.7 25.4 %all-to-all-start = ((f32[16,72,128]{2,1,0:T(8,128)}), f32[16,72,128]{2,1,0:T(8,128)S(1)}, u32[]{:S(2)}, u32[]{:S(2)}) async-start(f32[16,72,128]{2,1,0:T(8,128)} %pack.1), calls=%async_computation | async-start | bytes 1179648 | tf_op jit(solution)/shard_map/all_to_all | solution.py:319
  19.6 3.9 %collective-permute-start.3 = (f32[256,128]{1,0:T(8,128)S(1)}, f32[256,128]{1,0:T(8,128)S(1)}, u32[]{:S(2)}, u32[]{:S(2)}) collective-permute-start(f32[256,128]{1,0:T(8,128)S(1)} %copy-done), channel_id=1, source_target_pairs={{0,1},{1,0},{2,3},{3,2},{4,5},{5,4},{6,7},{7,6},{8,9},{9,8},{10,11... | collective-permute-start | bytes 393224 | tf_op jit(solution)/shard_map/ppermute | solution.py:293
  20.0 14.7 %collective-permute-start.11 = (f32[256,128]{1,0:T(8,128)S(1)}, f32[256,128]{1,0:T(8,128)S(1)}, u32[]{:S(2)}, u32[]{:S(2)}) collective-permute-start(f32[256,128]{1,0:T(8,128)S(1)} %collective-permute-done.refs_8_), channel_id=1, source_target_pairs={{0,4},{1,5},{2,6},{3,7},{4,0},{5,1},{6,2},{7,3},{8,12},{9,13},{10,... | collective-permute-start | bytes 393224 | tf_op jit(solution)/shard_map/ppermute | solution.py:293
  21.7 14.5 %collective-permute-start.4 = (f32[256,128]{1,0:T(8,128)S(1)}, f32[256,128]{1,0:T(8,128)S(1)}, u32[]{:S(2)}, u32[]{:S(2)}) collective-permute-start(f32[256,128]{1,0:T(8,128)S(1)} %collective-permute-done.2.refs_2_), channel_id=1, source_target_pairs={{0,1},{1,0},{2,3},{3,2},{4,5},{5,4},{6,7},{7,6},{8,9},{9,8},{10,11... | collective-permute-start | bytes 393224 | tf_op jit(solution)/shard_map/ppermute | solution.py:293
  21.8 14.4 %collective-permute-start.6 = (f32[256,128]{1,0:T(8,128)S(1)}, f32[256,128]{1,0:T(8,128)S(1)}, u32[]{:S(2)}, u32[]{:S(2)}) collective-permute-start(f32[256,128]{1,0:T(8,128)S(1)} %collective-permute-done.1.refs_4_), channel_id=1, source_target_pairs={{0,2},{1,3},{2,0},{3,1},{4,6},{5,7},{6,4},{7,5},{8,10},{9,11},{10,... | collective-permute-start | bytes 393224 | tf_op jit(solution)/shard_map/ppermute | solution.py:293
  23.2 13.5 %collective-permute-start.5 = (f32[256,128]{1,0:T(8,128)S(1)}, f32[256,128]{1,0:T(8,128)S(1)}, u32[]{:S(2)}, u32[]{:S(2)}) collective-permute-start(f32[256,128]{1,0:T(8,128)S(1)} %collective-permute-done.1.refs_4_), channel_id=1, source_target_pairs={{0,1},{1,0},{2,3},{3,2},{4,5},{5,4},{6,7},{7,6},{8,9},{9,8},{10,11... | collective-permute-start | bytes 393224 | tf_op jit(solution)/shard_map/ppermute | solution.py:293
  23.4 13.4 %collective-permute-start.9 = (f32[256,128]{1,0:T(8,128)S(1)}, f32[256,128]{1,0:T(8,128)S(1)}, u32[]{:S(2)}, u32[]{:S(2)}) collective-permute-start(f32[256,128]{1,0:T(8,128)S(1)} %collective-permute-done.refs_8_), channel_id=1, source_target_pairs={{0,2},{1,3},{2,0},{3,1},{4,6},{5,7},{6,4},{7,5},{8,10},{9,11},{10,... | collective-permute-start | bytes 393224 | tf_op jit(solution)/shard_map/ppermute | solution.py:293
  34.8 5.0 %collective-permute-start.13 = (f32[256,128]{1,0:T(8,128)S(1)}, f32[256,128]{1,0:T(8,128)S(1)}, u32[]{:S(2)}, u32[]{:S(2)}) collective-permute-start(f32[256,128]{1,0:T(8,128)S(1)} %collective-permute-done.11.refs_12_), channel_id=1, source_target_pairs={{0,2},{1,3},{2,0},{3,1},{4,6},{5,7},{6,4},{7,5},{8,10},{9,11},{10,... | collective-permute-start | bytes 393224 | tf_op jit(solution)/shard_map/ppermute | solution.py:293
  36.2 3.6 %collective-permute-start.8 = (f32[256,128]{1,0:T(8,128)S(1)}, f32[256,128]{1,0:T(8,128)S(1)}, u32[]{:S(2)}, u32[]{:S(2)}) collective-permute-start(f32[256,128]{1,0:T(8,128)S(1)} %collective-permute-done.refs_8_), channel_id=1, source_target_pairs={{0,1},{1,0},{2,3},{3,2},{4,5},{5,4},{6,7},{7,6},{8,9},{9,8},{10,11... | collective-permute-start | bytes 393224 | tf_op jit(solution)/shard_map/ppermute | solution.py:293
  36.2 3.6 %collective-permute-start.12 = (f32[256,128]{1,0:T(8,128)S(1)}, f32[256,128]{1,0:T(8,128)S(1)}, u32[]{:S(2)}, u32[]{:S(2)}) collective-permute-start(f32[256,128]{1,0:T(8,128)S(1)} %collective-permute-done.11.refs_12_), channel_id=1, source_target_pairs={{0,1},{1,0},{2,3},{3,2},{4,5},{5,4},{6,7},{7,6},{8,9},{9,8},{10,11... | collective-permute-start | bytes 393224 | tf_op jit(solution)/shard_map/ppermute | solution.py:293
  36.7 3.0 %collective-permute-start.7 = (f32[256,128]{1,0:T(8,128)S(1)}, f32[256,128]{1,0:T(8,128)S(1)}, u32[]{:S(2)}, u32[]{:S(2)}) collective-permute-start(f32[256,128]{1,0:T(8,128)S(1)} %collective-permute-done.6.refs_6_), channel_id=1, source_target_pairs={{0,1},{1,0},{2,3},{3,2},{4,5},{5,4},{6,7},{7,6},{8,9},{9,8},{10,11... | collective-permute-start | bytes 393224 | tf_op jit(solution)/shard_map/ppermute | solution.py:293
  36.8 3.0 %collective-permute-start.10 = (f32[256,128]{1,0:T(8,128)S(1)}, f32[256,128]{1,0:T(8,128)S(1)}, u32[]{:S(2)}, u32[]{:S(2)}) collective-permute-start(f32[256,128]{1,0:T(8,128)S(1)} %collective-permute-done.9.refs_10_), channel_id=1, source_target_pairs={{0,1},{1,0},{2,3},{3,2},{4,5},{5,4},{6,7},{7,6},{8,9},{9,8},{10,11... | collective-permute-start | bytes 393224 | tf_op jit(solution)/shard_map/ppermute | solution.py:293
  39.7 1.3 %collective-permute-start.14 = (f32[256,128]{1,0:T(8,128)S(1)}, f32[256,128]{1,0:T(8,128)S(1)}, u32[]{:S(2)}, u32[]{:S(2)}) collective-permute-start(f32[256,128]{1,0:T(8,128)S(1)} %collective-permute-done.13.refs_14_), channel_id=1, source_target_pairs={{0,1},{1,0},{2,3},{3,2},{4,5},{5,4},{6,7},{7,6},{8,9},{9,8},{10,11... | collective-permute-start | bytes 393224 | tf_op jit(solution)/shard_map/ppermute | solution.py:293

commit v5 on v4

--- a/solution.py
+++ b/solution.py
@@ -265,7 +265,7 @@
     n_sky = len(tiles)
     slots = n_sky * each
     rows = tiles[0].shape[0]
-    together = 1
+    together = 4
     return pl.pallas_call(
         functools.partial(trace_kernel, n_sky, each, planes, together),
         out_shape=(
@@ -311,7 +311,7 @@
     held = {0: regroup(potential)}
     flat = ray_start.reshape(bundles, 2, halves, LANES).transpose(0, 2, 1, 3).reshape(bundles * 2 * halves, LANES)
     sent = pack(n_sky, each, per_owner, destination.reshape(1, bundles), patch_index, flat)
-    near = [bit for bit in bits[:3] if bit > 1]
+    near = [bit for bit in bits[1:3] if bit > 1]
     for bit in near:
         held[bit] = flipped(held[0], n_sky, bit)
     sent, *first = lax.optimization_barrier((sent, *[held[bit] for bit in near]))

time: 71.6 us -> 69.6 us (0.972)
  Pallas kernels: 34.5 us -> 23.6 us
  waiting for transfers between devices: 18.3 us -> 28.1 us
  starting transfers between devices: 17.8 us -> 17 us
    pallas_call x1, Pallas kernels: 30.2 us -> 19.3 us  [trace(): pl.pallas_call(functools.partial(trace_kernel, n_sky, each, planes, toget...]
    ppermute x15, waiting for transfers between devices: 18.3 us -> 28 us  [flipped(): return lax.ppermute(value, 'sky', [(i, i ^ bits) for i in range(n_sky)])]
    ppermute x15, starting transfers between devices: 14 us -> 12 us  [flipped(): return lax.ppermute(value, 'sky', [(i, i ^ bits) for i in range(n_sky)])]
    all_to_all x1, starting transfers between devices: 3.84 us -> 4.98 us  [shards(): got = lax.all_to_all(sent, 'sky', split_axis=0, concat_axis=0, tiled=True)]
  transfers between devices with their start and end apart: 16 -> 16, of which waited for: 5 -> 6; matrix products, arithmetic and copies ran while one was open for 0% -> 0% of each run, Pallas kernels for 3% -> 3%
where the time goes in v5:
time: 69.6 us; the launch traced here: 69.3 us
  waiting for transfers between devices  28.1 us (40%)
  Pallas kernels  23.6 us (34%)
  starting transfers between devices  17 us (24%)
    ppermute x15, waiting for transfers between devices, flipped(): return lax.ppermute(value, 'sky', [(i, i ^ bits) for i in range(n_sky)])  28 us
    pallas_call x1, Pallas kernels, trace(): pl.pallas_call(functools.partial(trace_kernel, n_sky, each, planes, toget...  19.3 us
    ppermute x15, starting transfers between devices, flipped(): return lax.ppermute(value, 'sky', [(i, i ^ bits) for i in range(n_sky)])  12 us
    all_to_all x1, starting transfers between devices, shards(): got = lax.all_to_all(sent, 'sky', split_axis=0, concat_axis=0, tiled=True)  4.98 us
    pallas_call x1, Pallas kernels, pack(): pl.pallas_call(functools.partial(pack_kernel, n_sky, each, per_owner), ou...  2.37 us
    pallas_call x1, Pallas kernels, regroup(): pl.pallas_call(regroup_kernel, out_shape=jax.ShapeDtypeStruct((rows, LANE...  1.88 us
  transfers between devices with their start and end apart: 16, of which 6 were waited for; matrix products, arithmetic and copies ran while one was open for 0% of the time, Pallas kernels for 3%

profile of v5, /device:TPU:0, one launch (start us, length us, event | category | flops | bytes accessed | tf_op | source)
XLA Modules:
  0.0 69.3 jit_solution(4158587016381731728)
XLA Ops:
  0.6 1.9 %regroup.1.refs_0_ = f32[256,128]{1,0:T(8,128)} custom-call(f32[4,8,1024]{2,1,0:T(8,128)} %src_ref.1), custom_call_target="tpu_custom_call" | custom-call | tf_op jit(solution)/shard_map/regroup/pallas_call | solution.py:68
  2.5 3.0 %collective-permute-start.1 = (f32[256,128]{1,0:T(8,128)}, f32[256,128]{1,0:T(8,128)S(1)}, u32[]{:S(2)}, u32[]{:S(2)}) collective-permute-start(f32[256,128]{1,0:T(8,128)} %regroup.1.refs_0_), channel_id=1, source_target_pairs={{0,2},{1,3},{2,0},{3,1},{4,6},{5,7},{6,4},{7,5},{8,10},{9,11},{10,... | collective-permute-start | bytes 393224 | tf_op jit(solution)/shard_map/ppermute | solution.py:293
  5.5 1.6 %collective-permute-start = (f32[256,128]{1,0:T(8,128)}, f32[256,128]{1,0:T(8,128)S(1)}, u32[]{:S(2)}, u32[]{:S(2)}) collective-permute-start(f32[256,128]{1,0:T(8,128)} %regroup.1.refs_0_), channel_id=1, source_target_pairs={{0,4},{1,5},{2,6},{3,7},{4,0},{5,1},{6,2},{7,3},{8,12},{9,13},{10,... | collective-permute-start | bytes 393224 | tf_op jit(solution)/shard_map/ppermute | solution.py:293
  7.1 2.4 %pack.1 = f32[16,72,128]{2,1,0:T(8,128)} custom-call(s32[1,128]{1,0:T(1,128)} %bitcast.17, s32[4,128]{1,0:T(4,128)} %ids_ref.1, f32[512,128]{1,0:T(8,128)} %bitcast.16), custom_call_target="tpu_custom_call" | custom-call | tf_op jit(solution)/shard_map/pack/pallas_call | solution.py:126
  9.4 0.0 copy-start
  9.4 0.0 copy-start.1
  9.4 0.0 collective-permute-done.1.refs_2_
  9.4 1.2 %collective-permute-done.refs_4_ = f32[256,128]{1,0:T(8,128)S(1)} collective-permute-done((f32[256,128]{1,0:T(8,128)}, f32[256,128]{1,0:T(8,128)S(1)}, u32[]{:S(2)}, u32[]{:S(2)}) %collective-permute-start) | collective-permute-done | bytes 131104 | tf_op jit(solution)/shard_map/ppermute | solution.py:293
  10.7 5.0 %all-to-all-start = ((f32[16,72,128]{2,1,0:T(8,128)}), f32[16,72,128]{2,1,0:T(8,128)S(1)}, u32[]{:S(2)}, u32[]{:S(2)}) async-start(f32[16,72,128]{2,1,0:T(8,128)} %pack.1), calls=%async_computation | async-start | bytes 1179648 | tf_op jit(solution)/shard_map/all_to_all | solution.py:319
  15.6 0.0 copy-done
  15.7 2.9 %collective-permute-start.7 = (f32[256,128]{1,0:T(8,128)S(1)}, f32[256,128]{1,0:T(8,128)S(1)}, u32[]{:S(2)}, u32[]{:S(2)}) collective-permute-start(f32[256,128]{1,0:T(8,128)S(1)} %copy-done), channel_id=1, source_target_pairs={{0,8},{1,9},{2,10},{3,11},{4,12},{5,13},{6,14},{7,15},{8,0},{9,1},... | collective-permute-start | bytes 393224 | tf_op jit(solution)/shard_map/ppermute | solution.py:293
  18.5 0.0 collective-permute-start.2
  18.5 19.4 %collective-permute-done.7.refs_8_ = f32[256,128]{1,0:T(8,128)S(1)} collective-permute-done((f32[256,128]{1,0:T(8,128)S(1)}, f32[256,128]{1,0:T(8,128)S(1)}, u32[]{:S(2)}, u32[]{:S(2)}) %collective-permute-start.7) | collective-permute-done | bytes 131104 | tf_op jit(solution)/shard_map/ppermute | solution.py:293
  38.0 0.0 collective-permute-start.11
  38.0 1.5 %collective-permute-start.9 = (f32[256,128]{1,0:T(8,128)S(1)}, f32[256,128]{1,0:T(8,128)S(1)}, u32[]{:S(2)}, u32[]{:S(2)}) collective-permute-start(f32[256,128]{1,0:T(8,128)S(1)} %collective-permute-done.7.refs_8_), channel_id=1, source_target_pairs={{0,2},{1,3},{2,0},{3,1},{4,6},{5,7},{6,4},{7,5},{8,10},{9,11},{10,... | collective-permute-start | bytes 393224 | tf_op jit(solution)/shard_map/ppermute | solution.py:293
  39.4 0.0 collective-permute-start.8
  39.5 0.5 collective-permute-start.3
  40.0 0.0 collective-permute-done.2.refs_1_
  40.0 0.6 collective-permute-start.5
  40.5 2.5 %collective-permute-done.11.refs_12_ = f32[256,128]{1,0:T(8,128)S(1)} collective-permute-done((f32[256,128]{1,0:T(8,128)S(1)}, f32[256,128]{1,0:T(8,128)S(1)}, u32[]{:S(2)}, u32[]{:S(2)}) %collective-permute-start.11) | collective-permute-done | bytes 131104 | tf_op jit(solution)/shard_map/ppermute | solution.py:293
  43.0 1.5 %collective-permute-start.13 = (f32[256,128]{1,0:T(8,128)S(1)}, f32[256,128]{1,0:T(8,128)S(1)}, u32[]{:S(2)}, u32[]{:S(2)}) collective-permute-start(f32[256,128]{1,0:T(8,128)S(1)} %collective-permute-done.11.refs_12_), channel_id=1, source_target_pairs={{0,2},{1,3},{2,0},{3,1},{4,6},{5,7},{6,4},{7,5},{8,10},{9,11},{10,... | collective-permute-start | bytes 393224 | tf_op jit(solution)/shard_map/ppermute | solution.py:293
  44.5 0.0 collective-permute-done.9.refs_10_
  44.5 0.0 collective-permute-start.4
  44.5 0.0 collective-permute-done.8.refs_9_
  44.5 0.5 collective-permute-start.12
  45.0 0.0 collective-permute-done.3.refs_3_
  45.0 0.1 collective-permute-start.10
  45.1 1.2 %collective-permute-done.5.refs_6_ = f32[256,128]{1,0:T(8,128)S(1)} collective-permute-done((f32[256,128]{1,0:T(8,128)S(1)}, f32[256,128]{1,0:T(8,128)S(1)}, u32[]{:S(2)}, u32[]{:S(2)}) %collective-permute-start.5) | collective-permute-done | bytes 131104 | tf_op jit(solution)/shard_map/ppermute | solution.py:293
  46.3 0.0 collective-permute-start.6
  46.3 2.3 %collective-permute-done.13.refs_14_ = f32[256,128]{1,0:T(8,128)S(1)} collective-permute-done((f32[256,128]{1,0:T(8,128)S(1)}, f32[256,128]{1,0:T(8,128)S(1)}, u32[]{:S(2)}, u32[]{:S(2)}) %collective-permute-start.13) | collective-permute-done | bytes 131104 | tf_op jit(solution)/shard_map/ppermute | solution.py:293
  48.6 0.0 collective-permute-start.14
  48.6 0.0 collective-permute-done.4.refs_5_
  48.6 0.0 collective-permute-done.12.refs_13_
  48.7 0.0 collective-permute-done.10.refs_11_
  48.7 0.0 collective-permute-done.6.refs_7_
  48.7 1.3 %collective-permute-done.14.refs_15_ = f32[256,128]{1,0:T(8,128)S(1)} collective-permute-done((f32[256,128]{1,0:T(8,128)S(1)}, f32[256,128]{1,0:T(8,128)S(1)}, u32[]{:S(2)}, u32[]{:S(2)}) %collective-permute-start.14) | collective-permute-done | bytes 131104 | tf_op jit(solution)/shard_map/ppermute | solution.py:293
  50.0 0.0 all-to-all-done.got_ref
  50.0 0.0 copy-done.1
  50.0 19.3 %trace.1 = (f32[1024,128]{1,0:T(8,128)}, f32[2048,128]{1,0:T(8,128)}) custom-call(f32[4]{0:T(128)S(1)} %copy-done.1, f32[16,72,128]{2,1,0:T(8,128)S(1)} %all-to-all-done.got_ref, f32[256,128]{1,0:T(8,128)S(1)} %copy-done, f32[256,128]{1,0:T(8,128)S(1)} %collective-permute-done.2.refs_1_, f32[256,128]{1,0:T(8,128)S(1)} %collective-permute-done.1.refs_2_, ...), custom_call_target="tpu_custom_call" | custom-call | tf_op jit(solution)/shard_map/trace/pallas_call | solution.py:269
Async XLA Ops:
  2.5 6.9 %collective-permute-start.1 = (f32[256,128]{1,0:T(8,128)}, f32[256,128]{1,0:T(8,128)S(1)}, u32[]{:S(2)}, u32[]{:S(2)}) collective-permute-start(f32[256,128]{1,0:T(8,128)} %regroup.1.refs_0_), channel_id=1, source_target_pairs={{0,2},{1,3},{2,0},{3,1},{4,6},{5,7},{6,4},{7,5},{8,10},{9,11},{10,... | collective-permute-start | bytes 393224 | tf_op jit(solution)/shard_map/ppermute | solution.py:293
  5.5 5.2 %collective-permute-start = (f32[256,128]{1,0:T(8,128)}, f32[256,128]{1,0:T(8,128)S(1)}, u32[]{:S(2)}, u32[]{:S(2)}) collective-permute-start(f32[256,128]{1,0:T(8,128)} %regroup.1.refs_0_), channel_id=1, source_target_pairs={{0,4},{1,5},{2,6},{3,7},{4,0},{5,1},{6,2},{7,3},{8,12},{9,13},{10,... | collective-permute-start | bytes 393224 | tf_op jit(solution)/shard_map/ppermute | solution.py:293
  9.4 6.2 %copy-start = (f32[256,128]{1,0:T(8,128)S(1)}, f32[256,128]{1,0:T(8,128)}, u32[]{:S(2)}) copy-start(f32[256,128]{1,0:T(8,128)} %regroup.1.refs_0_) | copy-start | bytes 393220
  9.4 40.6 %copy-start.1 = (f32[4]{0:T(128)S(1)}, f32[4]{0:T(128)}, u32[]{:S(2)}) copy-start(f32[4]{0:T(128)} %lens_ref.1) | copy-start | bytes 52
  10.7 39.3 %all-to-all-start = ((f32[16,72,128]{2,1,0:T(8,128)}), f32[16,72,128]{2,1,0:T(8,128)S(1)}, u32[]{:S(2)}, u32[]{:S(2)}) async-start(f32[16,72,128]{2,1,0:T(8,128)} %pack.1), calls=%async_computation | async-start | bytes 1179648 | tf_op jit(solution)/shard_map/all_to_all | solution.py:319
  15.7 22.3 %collective-permute-start.7 = (f32[256,128]{1,0:T(8,128)S(1)}, f32[256,128]{1,0:T(8,128)S(1)}, u32[]{:S(2)}, u32[]{:S(2)}) collective-permute-start(f32[256,128]{1,0:T(8,128)S(1)} %copy-done), channel_id=1, source_target_pairs={{0,8},{1,9},{2,10},{3,11},{4,12},{5,13},{6,14},{7,15},{8,0},{9,1},... | collective-permute-start | bytes 393224 | tf_op jit(solution)/shard_map/ppermute | solution.py:293
  18.5 21.4 %collective-permute-start.2 = (f32[256,128]{1,0:T(8,128)S(1)}, f32[256,128]{1,0:T(8,128)S(1)}, u32[]{:S(2)}, u32[]{:S(2)}) collective-permute-start(f32[256,128]{1,0:T(8,128)S(1)} %copy-done), channel_id=1, source_target_pairs={{0,1},{1,0},{2,3},{3,2},{4,5},{5,4},{6,7},{7,6},{8,9},{9,8},{10,11... | collective-permute-start | bytes 393224 | tf_op jit(solution)/shard_map/ppermute | solution.py:293
  38.0 5.0 %collective-permute-start.11 = (f32[256,128]{1,0:T(8,128)S(1)}, f32[256,128]{1,0:T(8,128)S(1)}, u32[]{:S(2)}, u32[]{:S(2)}) collective-permute-start(f32[256,128]{1,0:T(8,128)S(1)} %collective-permute-done.7.refs_8_), channel_id=1, source_target_pairs={{0,4},{1,5},{2,6},{3,7},{4,0},{5,1},{6,2},{7,3},{8,12},{9,13},{10,... | collective-permute-start | bytes 393224 | tf_op jit(solution)/shard_map/ppermute | solution.py:293
  38.0 6.5 %collective-permute-start.9 = (f32[256,128]{1,0:T(8,128)S(1)}, f32[256,128]{1,0:T(8,128)S(1)}, u32[]{:S(2)}, u32[]{:S(2)}) collective-permute-start(f32[256,128]{1,0:T(8,128)S(1)} %collective-permute-done.7.refs_8_), channel_id=1, source_target_pairs={{0,2},{1,3},{2,0},{3,1},{4,6},{5,7},{6,4},{7,5},{8,10},{9,11},{10,... | collective-permute-start | bytes 393224 | tf_op jit(solution)/shard_map/ppermute | solution.py:293
  39.4 5.0 %collective-permute-start.8 = (f32[256,128]{1,0:T(8,128)S(1)}, f32[256,128]{1,0:T(8,128)S(1)}, u32[]{:S(2)}, u32[]{:S(2)}) collective-permute-start(f32[256,128]{1,0:T(8,128)S(1)} %collective-permute-done.7.refs_8_), channel_id=1, source_target_pairs={{0,1},{1,0},{2,3},{3,2},{4,5},{5,4},{6,7},{7,6},{8,9},{9,8},{10,11... | collective-permute-start | bytes 393224 | tf_op jit(solution)/shard_map/ppermute | solution.py:293
  39.5 5.6 %collective-permute-start.3 = (f32[256,128]{1,0:T(8,128)S(1)}, f32[256,128]{1,0:T(8,128)S(1)}, u32[]{:S(2)}, u32[]{:S(2)}) collective-permute-start(f32[256,128]{1,0:T(8,128)S(1)} %collective-permute-done.1.refs_2_), channel_id=1, source_target_pairs={{0,1},{1,0},{2,3},{3,2},{4,5},{5,4},{6,7},{7,6},{8,9},{9,8},{10,11... | collective-permute-start | bytes 393224 | tf_op jit(solution)/shard_map/ppermute | solution.py:293
  40.0 6.4 %collective-permute-start.5 = (f32[256,128]{1,0:T(8,128)S(1)}, f32[256,128]{1,0:T(8,128)S(1)}, u32[]{:S(2)}, u32[]{:S(2)}) collective-permute-start(f32[256,128]{1,0:T(8,128)S(1)} %collective-permute-done.refs_4_), channel_id=1, source_target_pairs={{0,2},{1,3},{2,0},{3,1},{4,6},{5,7},{6,4},{7,5},{8,10},{9,11},{10,... | collective-permute-start | bytes 393224 | tf_op jit(solution)/shard_map/ppermute | solution.py:293
  43.0 5.6 %collective-permute-start.13 = (f32[256,128]{1,0:T(8,128)S(1)}, f32[256,128]{1,0:T(8,128)S(1)}, u32[]{:S(2)}, u32[]{:S(2)}) collective-permute-start(f32[256,128]{1,0:T(8,128)S(1)} %collective-permute-done.11.refs_12_), channel_id=1, source_target_pairs={{0,2},{1,3},{2,0},{3,1},{4,6},{5,7},{6,4},{7,5},{8,10},{9,11},{10,... | collective-permute-start | bytes 393224 | tf_op jit(solution)/shard_map/ppermute | solution.py:293
  44.5 4.2 %collective-permute-start.4 = (f32[256,128]{1,0:T(8,128)S(1)}, f32[256,128]{1,0:T(8,128)S(1)}, u32[]{:S(2)}, u32[]{:S(2)}) collective-permute-start(f32[256,128]{1,0:T(8,128)S(1)} %collective-permute-done.refs_4_), channel_id=1, source_target_pairs={{0,1},{1,0},{2,3},{3,2},{4,5},{5,4},{6,7},{7,6},{8,9},{9,8},{10,11... | collective-permute-start | bytes 393224 | tf_op jit(solution)/shard_map/ppermute | solution.py:293
  44.5 4.2 %collective-permute-start.12 = (f32[256,128]{1,0:T(8,128)S(1)}, f32[256,128]{1,0:T(8,128)S(1)}, u32[]{:S(2)}, u32[]{:S(2)}) collective-permute-start(f32[256,128]{1,0:T(8,128)S(1)} %collective-permute-done.11.refs_12_), channel_id=1, source_target_pairs={{0,1},{1,0},{2,3},{3,2},{4,5},{5,4},{6,7},{7,6},{8,9},{9,8},{10,11... | collective-permute-start | bytes 393224 | tf_op jit(solution)/shard_map/ppermute | solution.py:293
  45.0 3.7 %collective-permute-start.10 = (f32[256,128]{1,0:T(8,128)S(1)}, f32[256,128]{1,0:T(8,128)S(1)}, u32[]{:S(2)}, u32[]{:S(2)}) collective-permute-start(f32[256,128]{1,0:T(8,128)S(1)} %collective-permute-done.9.refs_10_), channel_id=1, source_target_pairs={{0,1},{1,0},{2,3},{3,2},{4,5},{5,4},{6,7},{7,6},{8,9},{9,8},{10,11... | collective-permute-start | bytes 393224 | tf_op jit(solution)/shard_map/ppermute | solution.py:293
  46.3 2.3 %collective-permute-start.6 = (f32[256,128]{1,0:T(8,128)S(1)}, f32[256,128]{1,0:T(8,128)S(1)}, u32[]{:S(2)}, u32[]{:S(2)}) collective-permute-start(f32[256,128]{1,0:T(8,128)S(1)} %collective-permute-done.5.refs_6_), channel_id=1, source_target_pairs={{0,1},{1,0},{2,3},{3,2},{4,5},{5,4},{6,7},{7,6},{8,9},{9,8},{10,11... | collective-permute-start | bytes 393224 | tf_op jit(solution)/shard_map/ppermute | solution.py:293
  48.6 1.3 %collective-permute-start.14 = (f32[256,128]{1,0:T(8,128)S(1)}, f32[256,128]{1,0:T(8,128)S(1)}, u32[]{:S(2)}, u32[]{:S(2)}) collective-permute-start(f32[256,128]{1,0:T(8,128)S(1)} %collective-permute-done.13.refs_14_), channel_id=1, source_target_pairs={{0,1},{1,0},{2,3},{3,2},{4,5},{5,4},{6,7},{7,6},{8,9},{9,8},{10,11... | collective-permute-start | bytes 393224 | tf_op jit(solution)/shard_map/ppermute | solution.py:293

commit v6 on v5

--- a/solution.py
+++ b/solution.py
@@ -12,6 +12,7 @@
 SIDE = 32
 CHUNKS = 8
 EMPTY = -1024.0
+NEAR = 4
 
 
 def lane_gather(table, idx):
@@ -74,17 +75,19 @@
     )(potential)
 
 
-def pack_kernel(n_sky, each, per_owner, dest_ref, ids_ref, rays_ref, out_ref):
+def pack_kernel(n_sky, each, per_owner, me_ref, dest_ref, ids_ref, rays_ref, *out_refs):
+    me = me_ref[0]
     bundles = dest_ref.shape[1]
     planes = ids_ref.shape[0]
     slots = n_sky * each
+    size = 4 * each + SUB
     dest_row = jnp.broadcast_to(dest_ref[...], (bundles, bundles))
     dest_col = jnp.transpose(dest_row)
     row = lax.broadcasted_iota(jnp.int32, (bundles, bundles), 0)
     col = lax.broadcasted_iota(jnp.int32, (bundles, bundles), 1)
     hits = jnp.where((dest_row == dest_col) & (row < col), 1.0, 0.0)
     rank = jnp.sum(hits, axis=0, keepdims=True).astype(jnp.int32)
-    slot = dest_ref[...] * each + rank
+    slot = (dest_ref[...] ^ me) * each + rank
     place = lax.broadcasted_iota(jnp.int32, (slots, bundles), 0) == slot
     place = jnp.where(place, 1.0, 0.0)
     found = jnp.dot(
@@ -99,8 +102,9 @@
         sent = jnp.dot(place3, terms, preferred_element_type=jnp.float32)
         if part % 2 == 0:
             sent = jnp.where(found > 0.5, sent, EMPTY)
-        for o in range(n_sky):
-            out_ref[o, pl.ds(part, each, stride=4), :] = sent[o * each:(o + 1) * each]
+        for s in range(n_sky):
+            rows = pl.ds(s // NEAR * size + part, each, stride=4)
+            out_refs[s % NEAR][rows, :] = sent[s * each:(s + 1) * each]
     ids = ids_ref[...]
     plane = lax.broadcasted_iota(jnp.int32, ids.shape, 0)
     owner = (ids // per_owner) ^ dest_ref[...]
@@ -113,23 +117,43 @@
     fine = lax.dot_general(fine.astype(jnp.bfloat16), place, contract, preferred_element_type=jnp.float32)
     coarse = lax.dot_general(coarse.astype(jnp.bfloat16), place, contract, preferred_element_type=jnp.float32)
     numbers = coarse * 16.0 + fine
-    for o in range(n_sky):
-        first = o * each
+    for s in range(n_sky):
+        first = s * each
         block = numbers[:, first // LANES * LANES:first // LANES * LANES + LANES]
         turn = (LANES - first % LANES) % LANES
         if turn:
             block = pltpu.roll(block, turn, 1)
-        out_ref[o, pl.ds(4 * each, SUB), :] = block
-
-
-def pack(n_sky, each, per_owner, dest, ids, rays):
+        out_refs[s % NEAR][pl.ds(s // NEAR * size + 4 * each, SUB), :] = block
+
+
+def pack(n_sky, each, per_owner, me, dest, ids, rays):
+    part = jax.ShapeDtypeStruct((n_sky // NEAR * (4 * each + SUB), LANES), jnp.float32)
     return pl.pallas_call(
         functools.partial(pack_kernel, n_sky, each, per_owner),
-        out_shape=jax.ShapeDtypeStruct((n_sky, 4 * each + SUB, LANES), jnp.float32),
-        in_specs=[pl.BlockSpec(memory_space=pltpu.VMEM)] * 3,
-        out_specs=pl.BlockSpec(memory_space=pltpu.VMEM),
+        out_shape=[part] * NEAR,
+        in_specs=[pl.BlockSpec(memory_space=pltpu.SMEM)] + [pl.BlockSpec(memory_space=pltpu.VMEM)] * 3,
+        out_specs=[pl.BlockSpec(memory_space=pltpu.VMEM)] * NEAR,
         name="pack",
-    )(dest, ids, rays)
+    )(me, dest, ids, rays)
+
+
+def turn_kernel(size, *refs):
+    far = len(refs) - NEAR
+    for f in range(far):
+        for c in range(NEAR):
+            refs[NEAR + f][pl.ds(c * size, size), :] = refs[c][pl.ds(f * size, size), :]
+
+
+def turn(size, parts):
+    far = parts[0].shape[0] // size
+    block = jax.ShapeDtypeStruct((NEAR * size, LANES), jnp.float32)
+    return pl.pallas_call(
+        functools.partial(turn_kernel, size),
+        out_shape=[block] * far,
+        in_specs=[pl.BlockSpec(memory_space=pltpu.VMEM)] * NEAR,
+        out_specs=[pl.BlockSpec(memory_space=pltpu.VMEM)] * far,
+        name="turn",
+    )(*parts)
 
 
 def bilinear(f00, f01, f10, f11, u, v):
@@ -196,22 +220,27 @@
     return pos_x - half * fx2, pos_y - half * fy2, matrix
 
 
-def trace_kernel(n_sky, each, planes, together, lens_ref, got_ref, *refs):
-    tile_refs = refs[:n_sky]
-    shift_ref, matrix_ref, tiles, chosen, rays, places, sems = refs[n_sky:]
+def trace_kernel(n_sky, each, planes, together, me_ref, lens_ref, *refs):
+    far = n_sky // NEAR
+    size = 4 * each + SUB
+    tile_refs, got_refs = refs[:n_sky], refs[n_sky:n_sky + far]
+    shift_ref, matrix_ref, tiles, chosen, rays, places, sems = refs[n_sky + far:]
+    me = me_ref[0]
     slots = n_sky * each
     rows = tile_refs[0].shape[0]
     copies = []
     for s in range(n_sky):
+        source = me ^ s
+        got_ref, first = got_refs[s // NEAR], s % NEAR * size
         copies.append((
             pltpu.make_async_copy(
-                got_ref.at[s, pl.ds(4 * each, SUB), :],
-                places.at[pl.ds(s * SUB, SUB), :],
+                got_ref.at[pl.ds(first + 4 * each, SUB), :],
+                places.at[pl.ds(source * SUB, SUB), :],
                 sems.at[0, s]),
             pltpu.make_async_copy(tile_refs[s], tiles.at[pl.ds(s * rows, rows), :], sems.at[1, s]),
             pltpu.make_async_copy(
-                got_ref.at[s, pl.ds(0, 4 * each), :],
-                rays.at[pl.ds(s * 4 * each, 4 * each), :],
+                got_ref.at[pl.ds(first, 4 * each), :],
+                rays.at[pl.ds(source * 4 * each, 4 * each), :],
                 sems.at[2, s]),
         ))
     for kind in range(3):
@@ -261,7 +290,7 @@
     lax.fori_loop(0, slots // (SUB * together), body, 0)
 
 
-def trace(each, planes, lens_weight, got, tiles):
+def trace(each, planes, me, lens_weight, tiles, got):
     n_sky = len(tiles)
     slots = n_sky * each
     rows = tiles[0].shape[0]
@@ -272,7 +301,7 @@
             jax.ShapeDtypeStruct((slots * 4, LANES), jnp.float32),
             jax.ShapeDtypeStruct((slots * 8, LANES), jnp.float32),
         ),
-        in_specs=[pl.BlockSpec(memory_space=pltpu.SMEM)] + [pl.BlockSpec(memory_space=pl.ANY)] * (1 + n_sky),
+        in_specs=[pl.BlockSpec(memory_space=pltpu.SMEM)] * 2 + [pl.BlockSpec(memory_space=pl.ANY)] * (n_sky + len(got)),
         out_specs=(
             pl.BlockSpec(memory_space=pltpu.VMEM),
             pl.BlockSpec(memory_space=pltpu.VMEM),
@@ -286,7 +315,7 @@
         ],
         compiler_params=pltpu.CompilerParams(vmem_limit_bytes=40 * 1024 * 1024),
         name="trace",
-    )(lens_weight, got, *tiles)
+    )(me, lens_weight, *tiles, *got)
 
 
 def flipped(value, n_sky, bits):
@@ -302,23 +331,33 @@
 
 def shards(potential, lens_weight, ray_start, patch_index, destination):
     n_sky = lax.axis_size("sky")
+    me = lax.axis_index("sky").reshape(1)
     planes, per_owner, _ = potential.shape
     bundles, _, rays = ray_start.shape
     each = max(2, 2 * bundles // n_sky)
     slots = n_sky * each
     halves = rays // LANES
     bits = [1 << k for k in reversed(range((n_sky - 1).bit_length()))]
-    held = {0: regroup(potential)}
     flat = ray_start.reshape(bundles, 2, halves, LANES).transpose(0, 2, 1, 3).reshape(bundles * 2 * halves, LANES)
-    sent = pack(n_sky, each, per_owner, destination.reshape(1, bundles), patch_index, flat)
-    near = [bit for bit in bits[1:3] if bit > 1]
-    for bit in near:
-        held[bit] = flipped(held[0], n_sky, bit)
-    sent, *first = lax.optimization_barrier((sent, *[held[bit] for bit in near]))
-    held.update(zip(near, first))
-    got = lax.all_to_all(sent, "sky", split_axis=0, concat_axis=0, tiled=True)
+    own = regroup(potential)
+    held = {0: own}
+    for bit in bits[:2]:
+        held[bit] = flipped(own, n_sky, bit)
+    own, flat = lax.optimization_barrier((own, flat))
+    sent = pack(n_sky, each, per_owner, me, destination.reshape(1, bundles), patch_index, flat)
+    sent = [sent[0]] + [flipped(sent[s], n_sky, s) for s in range(1, NEAR)]
+    held[bits[0] ^ bits[1]] = flipped(held[bits[0]], n_sky, bits[1])
+    got = turn(4 * each + SUB, sent)
+    early = [0, bits[0], bits[1]]
+    *got, a, b, c = lax.optimization_barrier((*got, *[held[s] for s in early]))
+    held.update(zip(early, (a, b, c)))
+    got = [got[0]] + [flipped(got[f], n_sky, f * NEAR) for f in range(1, len(got))]
+    spread(held, n_sky, bits[:-1])
+    mid, *evens = lax.optimization_barrier((got[len(got) // 2], *[held[s] for s in range(0, n_sky, 2)]))
+    got[len(got) // 2] = mid
+    held.update(zip(range(0, n_sky, 2), evens))
     spread(held, n_sky, bits)
-    shift, matrix = trace(each, planes, lens_weight, got, [held[s] for s in range(n_sky)])
+    shift, matrix = trace(each, planes, me, lens_weight, [held[s] for s in range(n_sky)], got)
     shift = shift.reshape(slots, halves, 2, LANES).transpose(0, 2, 1, 3).reshape(slots, 2, rays)
     matrix = matrix.reshape(slots, halves, 4, LANES).transpose(0, 2, 1, 3).reshape(slots, 4, rays)
     return shift, matrix

time: 69.6 us -> 60.5 us (0.87)
  waiting for transfers between devices: 28.1 us -> 15.3 us
  Pallas kernels: 23.6 us -> 25.6 us
  local copies, waits for them, and re-layouts: 0.01 us -> 1.56 us
    ppermute x15 -> x21, waiting for transfers between devices: 28 us -> 15.3 us  [flipped(): return lax.ppermute(value, 'sky', [(i, i ^ bits) for i in range(n_sky)])]
    ppermute x15 -> x21, starting transfers between devices: 12 us -> 17.2 us  [flipped(): return lax.ppermute(value, 'sky', [(i, i ^ bits) for i in range(n_sky)])]
    all_to_all x1 -> x0, starting transfers between devices: 4.98 us -> none  [shards(): got = lax.all_to_all(sent, 'sky', split_axis=0, concat_axis=0, tiled=True)]
    pallas_call x0 -> x1, Pallas kernels: none -> 1.96 us  [turn(): pl.pallas_call(functools.partial(turn_kernel, size), out_shape=[block] *...]
    unnamed x4 -> x12, local copies, waits for them, and re-layouts: 0.01 us -> 1.56 us
  transfers between devices with their start and end apart: 16 -> 21, of which waited for: 6 -> 14; matrix products, arithmetic and copies ran while one was open for 0% -> 0% of each run, Pallas kernels for 3% -> 7%
where the time goes in v6:
time: 60.5 us; the launch traced here: 60.3 us
  Pallas kernels  25.6 us (42%)
  starting transfers between devices  17.2 us (28%)
  waiting for transfers between devices  15.3 us (25%)
  local copies, waits for them, and re-layouts  1.56 us (3%)
  between operations  0.66 us (1%)
    pallas_call x1, Pallas kernels, trace(): pl.pallas_call(functools.partial(trace_kernel, n_sky, each, planes, toget...  19.4 us
    ppermute x21, starting transfers between devices, flipped(): return lax.ppermute(value, 'sky', [(i, i ^ bits) for i in range(n_sky)])  17.2 us
    ppermute x21, waiting for transfers between devices, flipped(): return lax.ppermute(value, 'sky', [(i, i ^ bits) for i in range(n_sky)])  15.3 us
    pallas_call x1, Pallas kernels, pack(): pl.pallas_call(functools.partial(pack_kernel, n_sky, each, per_owner), ou...  2.37 us
    pallas_call x1, Pallas kernels, turn(): pl.pallas_call(functools.partial(turn_kernel, size), out_shape=[block] *...  1.96 us
    pallas_call x1, Pallas kernels, regroup(): pl.pallas_call(regroup_kernel, out_shape=jax.ShapeDtypeStruct((rows, LANE...  1.87 us
    unnamed x12, local copies, waits for them, and re-layouts  1.56 us
  transfers between devices with their start and end apart: 21, of which 14 were waited for; matrix products, arithmetic and copies ran while one was open for 0% of the time, Pallas kernels for 7%

profile of v6, /device:TPU:0, one launch (start us, length us, event | category | flops | bytes accessed | tf_op | source)
XLA Modules:
  0.0 60.3 jit_solution(9021934817905802331)
XLA Ops:
  0.6 1.9 %regroup.1.refs_0_ = f32[256,128]{1,0:T(8,128)} custom-call(f32[4,8,1024]{2,1,0:T(8,128)} %src_ref.1), custom_call_target="tpu_custom_call" | custom-call | tf_op jit(solution)/shard_map/regroup/pallas_call | solution.py:69
  2.5 4.0 %collective-permute-start.3 = (f32[256,128]{1,0:T(8,128)}, f32[256,128]{1,0:T(8,128)S(1)}, u32[]{:S(2)}, u32[]{:S(2)}) collective-permute-start(f32[256,128]{1,0:T(8,128)} %regroup.1.refs_0_), channel_id=1, source_target_pairs={{0,8},{1,9},{2,10},{3,11},{4,12},{5,13},{6,14},{7,15},{8,0},{9,1},... | collective-permute-start | bytes 393224 | tf_op jit(solution)/shard_map/ppermute | solution.py:322
  6.5 2.4 %pack.1 = (f32[288,128]{1,0:T(8,128)}, f32[288,128]{1,0:T(8,128)}, f32[288,128]{1,0:T(8,128)}, f32[288,128]{1,0:T(8,128)}) custom-call(s32[1]{0:T(128)} %bitcast.me_ref, s32[1,128]{1,0:T(1,128)} %bitcast.18, s32[4,128]{1,0:T(4,128)} %ids_ref.1, f32[512,128]{1,0:T(8,128)} %bitcast.17), custom_call_target="tpu_custom_call" | custom-call | tf_op jit(solution)/shard_map/pack/pallas_call | solution.py:131
  8.9 0.0 collective-permute-start
  8.9 1.5 %collective-permute-start.1 = (f32[288,128]{1,0:T(8,128)}, f32[288,128]{1,0:T(8,128)S(1)}, u32[]{:S(2)}, u32[]{:S(2)}) collective-permute-start(f32[288,128]{1,0:T(8,128)} %get-tuple-element.32), channel_id=1, source_target_pairs={{0,2},{1,3},{2,0},{3,1},{4,6},{5,7},{6,4},{7,5},{8,10},{9,11},{10,... | collective-permute-start | bytes 442376 | tf_op jit(solution)/shard_map/ppermute | solution.py:322
  10.4 0.3 collective-permute-start.2
  10.8 1.6 %collective-permute-start.4 = (f32[256,128]{1,0:T(8,128)S(1)}, f32[256,128]{1,0:T(8,128)S(1)}, u32[]{:S(2)}, u32[]{:S(2)}) collective-permute-start(f32[256,128]{1,0:T(8,128)S(1)} %copy-done), channel_id=1, source_target_pairs={{0,4},{1,5},{2,6},{3,7},{4,0},{5,1},{6,2},{7,3},{8,12},{9,13},{10,... | collective-permute-start | bytes 393224 | tf_op jit(solution)/shard_map/ppermute | solution.py:322
  12.4 0.7 %collective-permute-done.3.refs_8_ = f32[256,128]{1,0:T(8,128)S(1)} collective-permute-done((f32[256,128]{1,0:T(8,128)}, f32[256,128]{1,0:T(8,128)S(1)}, u32[]{:S(2)}, u32[]{:S(2)}) %collective-permute-start.3) | collective-permute-done | bytes 131104 | tf_op jit(solution)/shard_map/ppermute | solution.py:322
  13.1 0.8 %collective-permute-start.9 = (f32[256,128]{1,0:T(8,128)S(1)}, f32[256,128]{1,0:T(8,128)S(1)}, u32[]{:S(2)}, u32[]{:S(2)}) collective-permute-start(f32[256,128]{1,0:T(8,128)S(1)} %collective-permute-done.3.refs_8_), channel_id=1, source_target_pairs={{0,4},{1,5},{2,6},{3,7},{4,0},{5,1},{6,2},{7,3},{8,12},{9,13},{10,... | collective-permute-start | bytes 393224 | tf_op jit(solution)/shard_map/ppermute | solution.py:322
  13.9 0.0 collective-permute-done.refs_1_
  13.9 1.9 %collective-permute-done.1.refs_2_ = f32[288,128]{1,0:T(8,128)S(1)} collective-permute-done((f32[288,128]{1,0:T(8,128)}, f32[288,128]{1,0:T(8,128)S(1)}, u32[]{:S(2)}, u32[]{:S(2)}) %collective-permute-start.1) | collective-permute-done | bytes 147488 | tf_op jit(solution)/shard_map/ppermute | solution.py:322
  15.8 2.4 %collective-permute-done.2.refs_3_ = f32[288,128]{1,0:T(8,128)S(1)} collective-permute-done((f32[288,128]{1,0:T(8,128)}, f32[288,128]{1,0:T(8,128)S(1)}, u32[]{:S(2)}, u32[]{:S(2)}) %collective-permute-start.2) | collective-permute-done | bytes 147488 | tf_op jit(solution)/shard_map/ppermute | solution.py:322
  18.2 0.6 %copy-done.5 = f32[288,128]{1,0:T(8,128)} copy-done((f32[288,128]{1,0:T(8,128)}, f32[288,128]{1,0:T(8,128)S(1)}, u32[]{:S(2)}) %copy-start.5) | copy-done | bytes 147480
  18.8 2.0 %turn.1 = (f32[288,128]{1,0:T(8,128)}, f32[288,128]{1,0:T(8,128)}, f32[288,128]{1,0:T(8,128)}, f32[288,128]{1,0:T(8,128)}) custom-call(f32[288,128]{1,0:T(8,128)} %get-tuple-element.30.refs_0_, f32[288,128]{1,0:T(8,128)} %copy-done.3, f32[288,128]{1,0:T(8,128)} %copy-done.4, f32[288,128]{1,0:T(8,128)} %copy-done.5), custom_call_target="tpu_custom_call" | custom-call | tf_op jit(solution)/shard_map/turn/pallas_call | solution.py:150
  20.8 0.0 collective-permute-done.4.refs_4_
  20.8 1.6 %collective-permute-start.6 = (f32[256,128]{1,0:T(8,128)S(1)}, f32[256,128]{1,0:T(8,128)S(1)}, u32[]{:S(2)}, u32[]{:S(2)}) collective-permute-start(f32[256,128]{1,0:T(8,128)S(1)} %copy-done), channel_id=1, source_target_pairs={{0,2},{1,3},{2,0},{3,1},{4,6},{5,7},{6,4},{7,5},{8,10},{9,11},{10,... | collective-permute-start | bytes 393224 | tf_op jit(solution)/shard_map/ppermute | solution.py:322
  22.4 0.5 collective-permute-start.7
  22.9 0.2 collective-permute-start.5
  23.1 1.6 %collective-permute-start.8 = (f32[256,128]{1,0:T(8,128)S(1)}, f32[256,128]{1,0:T(8,128)S(1)}, u32[]{:S(2)}, u32[]{:S(2)}) collective-permute-start(f32[256,128]{1,0:T(8,128)S(1)} %collective-permute-done.3.refs_8_), channel_id=1, source_target_pairs={{0,2},{1,3},{2,0},{3,1},{4,6},{5,7},{6,4},{7,5},{8,10},{9,11},{10,... | collective-permute-start | bytes 393224 | tf_op jit(solution)/shard_map/ppermute | solution.py:322
  24.7 0.0 collective-permute-done.9.refs_12_
  24.7 0.4 collective-permute-start.10
  25.1 2.0 %collective-permute-done.6.refs_2_ = f32[256,128]{1,0:T(8,128)S(1)} collective-permute-done((f32[256,128]{1,0:T(8,128)S(1)}, f32[256,128]{1,0:T(8,128)S(1)}, u32[]{:S(2)}, u32[]{:S(2)}) %collective-permute-start.6) | collective-permute-done | bytes 131104 | tf_op jit(solution)/shard_map/ppermute | solution.py:322
  27.1 1.6 %collective-permute-start.19 = (f32[288,128]{1,0:T(8,128)}, f32[288,128]{1,0:T(8,128)S(1)}, u32[]{:S(2)}, u32[]{:S(2)}) collective-permute-start(f32[288,128]{1,0:T(8,128)} %get-tuple-element.51), channel_id=1, source_target_pairs={{0,4},{1,5},{2,6},{3,7},{4,0},{5,1},{6,2},{7,3},{8,12},{9,13},{10,... | collective-permute-start | bytes 442376 | tf_op jit(solution)/shard_map/ppermute | solution.py:322
  28.7 1.2 %collective-permute-done.7.refs_6_ = f32[256,128]{1,0:T(8,128)S(1)} collective-permute-done((f32[256,128]{1,0:T(8,128)S(1)}, f32[256,128]{1,0:T(8,128)S(1)}, u32[]{:S(2)}, u32[]{:S(2)}) %collective-permute-start.7) | collective-permute-done | bytes 131104 | tf_op jit(solution)/shard_map/ppermute | solution.py:322
  29.9 1.4 %collective-permute-start.20 = (f32[288,128]{1,0:T(8,128)}, f32[288,128]{1,0:T(8,128)S(1)}, u32[]{:S(2)}, u32[]{:S(2)}) collective-permute-start(f32[288,128]{1,0:T(8,128)} %get-tuple-element.53), channel_id=1, source_target_pairs={{0,12},{1,13},{2,14},{3,15},{4,8},{5,9},{6,10},{7,11},{8,4},{9,5},... | collective-permute-start | bytes 442376 | tf_op jit(solution)/shard_map/ppermute | solution.py:322
  31.3 1.4 %collective-permute-done.8.refs_10_ = f32[256,128]{1,0:T(8,128)S(1)} collective-permute-done((f32[256,128]{1,0:T(8,128)S(1)}, f32[256,128]{1,0:T(8,128)S(1)}, u32[]{:S(2)}, u32[]{:S(2)}) %collective-permute-start.8) | collective-permute-done | bytes 131104 | tf_op jit(solution)/shard_map/ppermute | solution.py:322
  32.7 0.2 collective-permute-done.5.refs_18_
  32.9 2.2 %collective-permute-done.10.refs_14_ = f32[256,128]{1,0:T(8,128)S(1)} collective-permute-done((f32[256,128]{1,0:T(8,128)S(1)}, f32[256,128]{1,0:T(8,128)S(1)}, u32[]{:S(2)}, u32[]{:S(2)}) %collective-permute-start.10) | collective-permute-done | bytes 131104 | tf_op jit(solution)/shard_map/ppermute | solution.py:322
  35.2 0.0 collective-permute-start.11
  35.2 0.5 collective-permute-start.12
  35.7 0.0 collective-permute-start.13
  35.7 2.0 %collective-permute-done.19.refs_17_ = f32[288,128]{1,0:T(8,128)S(1)} collective-permute-done((f32[288,128]{1,0:T(8,128)}, f32[288,128]{1,0:T(8,128)S(1)}, u32[]{:S(2)}, u32[]{:S(2)}) %collective-permute-start.19) | collective-permute-done | bytes 147488 | tf_op jit(solution)/shard_map/ppermute | solution.py:322
  37.6 0.0 collective-permute-start.14
  37.6 0.0 collective-permute-done.20.refs_19_
  37.6 0.5 collective-permute-start.15
  38.2 0.0 collective-permute-done.11.refs_1_
  38.2 0.1 collective-permute-start.16
  38.2 0.0 collective-permute-done.12.refs_3_
  38.2 0.4 collective-permute-start.17
  38.7 0.0 collective-permute-done.13.refs_5_
  38.7 0.1 collective-permute-start.18
  38.7 0.2 collective-permute-done.14.refs_7_
  39.0 0.2 collective-permute-done.15.refs_9_
  39.2 0.3 collective-permute-done.16.refs_11_
  39.5 0.2 collective-permute-done.17.refs_13_
  39.7 0.3 collective-permute-done.18.refs_15_
  40.0 0.9 %copy-done.1 = f32[288,128]{1,0:T(8,128)S(1)} copy-done((f32[288,128]{1,0:T(8,128)S(1)}, f32[288,128]{1,0:T(8,128)}, u32[]{:S(2)}) %copy-start.1) | copy-done | bytes 147480
  40.9 19.4 %trace.1 = (f32[1024,128]{1,0:T(8,128)}, f32[2048,128]{1,0:T(8,128)}) custom-call(s32[1]{0:T(128)} %bitcast.me_ref, f32[4]{0:T(128)S(1)} %copy-done.2, f32[256,128]{1,0:T(8,128)S(1)} %copy-done, f32[256,128]{1,0:T(8,128)S(1)} %collective-permute-done.11.refs_1_, f32[256,128]{1,0:T(8,128)S(1)} %collective-permute-done.6.refs_2_, ...), custom_call_target="tpu_custom_call" | custom-call | tf_op jit(solution)/shard_map/trace/pallas_call | solution.py:298
  (10 shorter events, 0.0 us)
Async XLA Ops:
  2.5 10.5 %collective-permute-start.3 = (f32[256,128]{1,0:T(8,128)}, f32[256,128]{1,0:T(8,128)S(1)}, u32[]{:S(2)}, u32[]{:S(2)}) collective-permute-start(f32[256,128]{1,0:T(8,128)} %regroup.1.refs_0_), channel_id=1, source_target_pairs={{0,8},{1,9},{2,10},{3,11},{4,12},{5,13},{6,14},{7,15},{8,0},{9,1},... | collective-permute-start | bytes 393224 | tf_op jit(solution)/shard_map/ppermute | solution.py:322
  6.5 4.2 %copy-start = (f32[256,128]{1,0:T(8,128)S(1)}, f32[256,128]{1,0:T(8,128)}, u32[]{:S(2)}) copy-start(f32[256,128]{1,0:T(8,128)} %regroup.1.refs_0_) | copy-start | bytes 393220
  8.9 5.0 %collective-permute-start = (f32[288,128]{1,0:T(8,128)}, f32[288,128]{1,0:T(8,128)S(1)}, u32[]{:S(2)}, u32[]{:S(2)}) collective-permute-start(f32[288,128]{1,0:T(8,128)} %get-tuple-element.31), channel_id=1, source_target_pairs={{0,1},{1,0},{2,3},{3,2},{4,5},{5,4},{6,7},{7,6},{8,9},{9,8},{10,11... | collective-permute-start | bytes 442376 | tf_op jit(solution)/shard_map/ppermute | solution.py:322
  8.9 6.9 %collective-permute-start.1 = (f32[288,128]{1,0:T(8,128)}, f32[288,128]{1,0:T(8,128)S(1)}, u32[]{:S(2)}, u32[]{:S(2)}) collective-permute-start(f32[288,128]{1,0:T(8,128)} %get-tuple-element.32), channel_id=1, source_target_pairs={{0,2},{1,3},{2,0},{3,1},{4,6},{5,7},{6,4},{7,5},{8,10},{9,11},{10,... | collective-permute-start | bytes 442376 | tf_op jit(solution)/shard_map/ppermute | solution.py:322
  10.4 7.7 %collective-permute-start.2 = (f32[288,128]{1,0:T(8,128)}, f32[288,128]{1,0:T(8,128)S(1)}, u32[]{:S(2)}, u32[]{:S(2)}) collective-permute-start(f32[288,128]{1,0:T(8,128)} %get-tuple-element.33), channel_id=1, source_target_pairs={{0,3},{1,2},{2,1},{3,0},{4,7},{5,6},{6,5},{7,4},{8,11},{9,10},{10,... | collective-permute-start | bytes 442376 | tf_op jit(solution)/shard_map/ppermute | solution.py:322
  10.8 10.0 %collective-permute-start.4 = (f32[256,128]{1,0:T(8,128)S(1)}, f32[256,128]{1,0:T(8,128)S(1)}, u32[]{:S(2)}, u32[]{:S(2)}) collective-permute-start(f32[256,128]{1,0:T(8,128)S(1)} %copy-done), channel_id=1, source_target_pairs={{0,4},{1,5},{2,6},{3,7},{4,0},{5,1},{6,2},{7,3},{8,12},{9,13},{10,... | collective-permute-start | bytes 393224 | tf_op jit(solution)/shard_map/ppermute | solution.py:322
  13.1 11.7 %collective-permute-start.9 = (f32[256,128]{1,0:T(8,128)S(1)}, f32[256,128]{1,0:T(8,128)S(1)}, u32[]{:S(2)}, u32[]{:S(2)}) collective-permute-start(f32[256,128]{1,0:T(8,128)S(1)} %collective-permute-done.3.refs_8_), channel_id=1, source_target_pairs={{0,4},{1,5},{2,6},{3,7},{4,0},{5,1},{6,2},{7,3},{8,12},{9,13},{10,... | collective-permute-start | bytes 393224 | tf_op jit(solution)/shard_map/ppermute | solution.py:322
  13.9 4.3 %copy-start.3 = (f32[288,128]{1,0:T(8,128)}, f32[288,128]{1,0:T(8,128)S(1)}, u32[]{:S(2)}) copy-start(f32[288,128]{1,0:T(8,128)S(1)} %collective-permute-done.refs_1_) | copy-start | bytes 442372
  15.8 2.4 %copy-start.4 = (f32[288,128]{1,0:T(8,128)}, f32[288,128]{1,0:T(8,128)S(1)}, u32[]{:S(2)}) copy-start(f32[288,128]{1,0:T(8,128)S(1)} %collective-permute-done.1.refs_2_) | copy-start | bytes 442372
  18.2 0.6 %copy-start.5 = (f32[288,128]{1,0:T(8,128)}, f32[288,128]{1,0:T(8,128)S(1)}, u32[]{:S(2)}) copy-start(f32[288,128]{1,0:T(8,128)S(1)} %collective-permute-done.2.refs_3_) | copy-start | bytes 442372
  20.8 19.3 %copy-start.2 = (f32[4]{0:T(128)S(1)}, f32[4]{0:T(128)}, u32[]{:S(2)}) copy-start(f32[4]{0:T(128)} %lens_ref.1) | copy-start | bytes 52
  20.8 6.4 %collective-permute-start.6 = (f32[256,128]{1,0:T(8,128)S(1)}, f32[256,128]{1,0:T(8,128)S(1)}, u32[]{:S(2)}, u32[]{:S(2)}) collective-permute-start(f32[256,128]{1,0:T(8,128)S(1)} %copy-done), channel_id=1, source_target_pairs={{0,2},{1,3},{2,0},{3,1},{4,6},{5,7},{6,4},{7,5},{8,10},{9,11},{10,... | collective-permute-start | bytes 393224 | tf_op jit(solution)/shard_map/ppermute | solution.py:322
  22.4 7.6 %collective-permute-start.7 = (f32[256,128]{1,0:T(8,128)S(1)}, f32[256,128]{1,0:T(8,128)S(1)}, u32[]{:S(2)}, u32[]{:S(2)}) collective-permute-start(f32[256,128]{1,0:T(8,128)S(1)} %collective-permute-done.4.refs_4_), channel_id=1, source_target_pairs={{0,2},{1,3},{2,0},{3,1},{4,6},{5,7},{6,4},{7,5},{8,10},{9,11},{10,... | collective-permute-start | bytes 393224 | tf_op jit(solution)/shard_map/ppermute | solution.py:322
  22.9 10.1 %collective-permute-start.5 = (f32[288,128]{1,0:T(8,128)}, f32[288,128]{1,0:T(8,128)S(1)}, u32[]{:S(2)}, u32[]{:S(2)}) collective-permute-start(f32[288,128]{1,0:T(8,128)} %get-tuple-element.38), channel_id=1, source_target_pairs={{0,8},{1,9},{2,10},{3,11},{4,12},{5,13},{6,14},{7,15},{8,0},{9,1},... | collective-permute-start | bytes 442376 | tf_op jit(solution)/shard_map/ppermute | solution.py:322
  23.1 9.6 %collective-permute-start.8 = (f32[256,128]{1,0:T(8,128)S(1)}, f32[256,128]{1,0:T(8,128)S(1)}, u32[]{:S(2)}, u32[]{:S(2)}) collective-permute-start(f32[256,128]{1,0:T(8,128)S(1)} %collective-permute-done.3.refs_8_), channel_id=1, source_target_pairs={{0,2},{1,3},{2,0},{3,1},{4,6},{5,7},{6,4},{7,5},{8,10},{9,11},{10,... | collective-permute-start | bytes 393224 | tf_op jit(solution)/shard_map/ppermute | solution.py:322
  24.7 10.4 %collective-permute-start.10 = (f32[256,128]{1,0:T(8,128)S(1)}, f32[256,128]{1,0:T(8,128)S(1)}, u32[]{:S(2)}, u32[]{:S(2)}) collective-permute-start(f32[256,128]{1,0:T(8,128)S(1)} %collective-permute-done.9.refs_12_), channel_id=1, source_target_pairs={{0,2},{1,3},{2,0},{3,1},{4,6},{5,7},{6,4},{7,5},{8,10},{9,11},{10,... | collective-permute-start | bytes 393224 | tf_op jit(solution)/shard_map/ppermute | solution.py:322
  27.1 10.5 %collective-permute-start.19 = (f32[288,128]{1,0:T(8,128)}, f32[288,128]{1,0:T(8,128)S(1)}, u32[]{:S(2)}, u32[]{:S(2)}) collective-permute-start(f32[288,128]{1,0:T(8,128)} %get-tuple-element.51), channel_id=1, source_target_pairs={{0,4},{1,5},{2,6},{3,7},{4,0},{5,1},{6,2},{7,3},{8,12},{9,13},{10,... | collective-permute-start | bytes 442376 | tf_op jit(solution)/shard_map/ppermute | solution.py:322
  29.9 7.7 %collective-permute-start.20 = (f32[288,128]{1,0:T(8,128)}, f32[288,128]{1,0:T(8,128)S(1)}, u32[]{:S(2)}, u32[]{:S(2)}) collective-permute-start(f32[288,128]{1,0:T(8,128)} %get-tuple-element.53), channel_id=1, source_target_pairs={{0,12},{1,13},{2,14},{3,15},{4,8},{5,9},{6,10},{7,11},{8,4},{9,5},... | collective-permute-start | bytes 442376 | tf_op jit(solution)/shard_map/ppermute | solution.py:322
  35.2 3.0 %collective-permute-start.11 = (f32[256,128]{1,0:T(8,128)S(1)}, f32[256,128]{1,0:T(8,128)S(1)}, u32[]{:S(2)}, u32[]{:S(2)}) collective-permute-start(f32[256,128]{1,0:T(8,128)S(1)} %copy-done), channel_id=1, source_target_pairs={{0,1},{1,0},{2,3},{3,2},{4,5},{5,4},{6,7},{7,6},{8,9},{9,8},{10,11... | collective-permute-start | bytes 393224 | tf_op jit(solution)/shard_map/ppermute | solution.py:322
  35.2 3.1 %collective-permute-start.12 = (f32[256,128]{1,0:T(8,128)S(1)}, f32[256,128]{1,0:T(8,128)S(1)}, u32[]{:S(2)}, u32[]{:S(2)}) collective-permute-start(f32[256,128]{1,0:T(8,128)S(1)} %collective-permute-done.6.refs_2_), channel_id=1, source_target_pairs={{0,1},{1,0},{2,3},{3,2},{4,5},{5,4},{6,7},{7,6},{8,9},{9,8},{10,11... | collective-permute-start | bytes 393224 | tf_op jit(solution)/shard_map/ppermute | solution.py:322
  35.7 3.0 %collective-permute-start.13 = (f32[256,128]{1,0:T(8,128)S(1)}, f32[256,128]{1,0:T(8,128)S(1)}, u32[]{:S(2)}, u32[]{:S(2)}) collective-permute-start(f32[256,128]{1,0:T(8,128)S(1)} %collective-permute-done.4.refs_4_), channel_id=1, source_target_pairs={{0,1},{1,0},{2,3},{3,2},{4,5},{5,4},{6,7},{7,6},{8,9},{9,8},{10,11... | collective-permute-start | bytes 393224 | tf_op jit(solution)/shard_map/ppermute | solution.py:322
  37.6 1.3 %collective-permute-start.14 = (f32[256,128]{1,0:T(8,128)S(1)}, f32[256,128]{1,0:T(8,128)S(1)}, u32[]{:S(2)}, u32[]{:S(2)}) collective-permute-start(f32[256,128]{1,0:T(8,128)S(1)} %collective-permute-done.7.refs_6_), channel_id=1, source_target_pairs={{0,1},{1,0},{2,3},{3,2},{4,5},{5,4},{6,7},{7,6},{8,9},{9,8},{10,11... | collective-permute-start | bytes 393224 | tf_op jit(solution)/shard_map/ppermute | solution.py:322
  37.6 1.5 %collective-permute-start.15 = (f32[256,128]{1,0:T(8,128)S(1)}, f32[256,128]{1,0:T(8,128)S(1)}, u32[]{:S(2)}, u32[]{:S(2)}) collective-permute-start(f32[256,128]{1,0:T(8,128)S(1)} %collective-permute-done.3.refs_8_), channel_id=1, source_target_pairs={{0,1},{1,0},{2,3},{3,2},{4,5},{5,4},{6,7},{7,6},{8,9},{9,8},{10,11... | collective-permute-start | bytes 393224 | tf_op jit(solution)/shard_map/ppermute | solution.py:322
  38.2 1.3 %collective-permute-start.16 = (f32[256,128]{1,0:T(8,128)S(1)}, f32[256,128]{1,0:T(8,128)S(1)}, u32[]{:S(2)}, u32[]{:S(2)}) collective-permute-start(f32[256,128]{1,0:T(8,128)S(1)} %collective-permute-done.8.refs_10_), channel_id=1, source_target_pairs={{0,1},{1,0},{2,3},{3,2},{4,5},{5,4},{6,7},{7,6},{8,9},{9,8},{10,11... | collective-permute-start | bytes 393224 | tf_op jit(solution)/shard_map/ppermute | solution.py:322
  38.2 1.5 %collective-permute-start.17 = (f32[256,128]{1,0:T(8,128)S(1)}, f32[256,128]{1,0:T(8,128)S(1)}, u32[]{:S(2)}, u32[]{:S(2)}) collective-permute-start(f32[256,128]{1,0:T(8,128)S(1)} %collective-permute-done.9.refs_12_), channel_id=1, source_target_pairs={{0,1},{1,0},{2,3},{3,2},{4,5},{5,4},{6,7},{7,6},{8,9},{9,8},{10,11... | collective-permute-start | bytes 393224 | tf_op jit(solution)/shard_map/ppermute | solution.py:322
  38.7 1.3 %collective-permute-start.18 = (f32[256,128]{1,0:T(8,128)S(1)}, f32[256,128]{1,0:T(8,128)S(1)}, u32[]{:S(2)}, u32[]{:S(2)}) collective-permute-start(f32[256,128]{1,0:T(8,128)S(1)} %collective-permute-done.10.refs_14_), channel_id=1, source_target_pairs={{0,1},{1,0},{2,3},{3,2},{4,5},{5,4},{6,7},{7,6},{8,9},{9,8},{10,11... | collective-permute-start | bytes 393224 | tf_op jit(solution)/shard_map/ppermute | solution.py:322
  40.0 0.9 %copy-start.1 = (f32[288,128]{1,0:T(8,128)S(1)}, f32[288,128]{1,0:T(8,128)}, u32[]{:S(2)}) copy-start(f32[288,128]{1,0:T(8,128)} %get-tuple-element.50.refs_16_) | copy-start | bytes 442372

commit v7 on v6

--- a/solution.py
+++ b/solution.py
@@ -61,18 +61,6 @@
             for c in range(CHUNKS):
                 rows = pl.ds((plane * tiles + base) * CHUNKS + c, SUB, stride=CHUNKS)
                 dst_ref[rows, :] = parts[c]
-
-
-def regroup(potential):
-    planes, tiles, pixels = potential.shape
-    rows = planes * tiles * pixels // LANES
-    return pl.pallas_call(
-        regroup_kernel,
-        out_shape=jax.ShapeDtypeStruct((rows, LANES), potential.dtype),
-        in_specs=[pl.BlockSpec(memory_space=pltpu.VMEM)],
-        out_specs=pl.BlockSpec(memory_space=pltpu.VMEM),
-        name="regroup",
-    )(potential)
 
 
 def pack_kernel(n_sky, each, per_owner, me_ref, dest_ref, ids_ref, rays_ref, *out_refs):
@@ -126,15 +114,23 @@
         out_refs[s % NEAR][pl.ds(s // NEAR * size + 4 * each, SUB), :] = block
 
 
-def pack(n_sky, each, per_owner, me, dest, ids, rays):
+def prepare_kernel(n_sky, each, me_ref, dest_ref, ids_ref, rays_ref, src_ref, dst_ref, *out_refs):
+    regroup_kernel(src_ref, dst_ref)
+    pack_kernel(n_sky, each, src_ref.shape[1], me_ref, dest_ref, ids_ref, rays_ref, *out_refs)
+
+
+def prepare(n_sky, each, me, dest, ids, rays, potential):
+    planes, tiles, pixels = potential.shape
     part = jax.ShapeDtypeStruct((n_sky // NEAR * (4 * each + SUB), LANES), jnp.float32)
-    return pl.pallas_call(
-        functools.partial(pack_kernel, n_sky, each, per_owner),
-        out_shape=[part] * NEAR,
-        in_specs=[pl.BlockSpec(memory_space=pltpu.SMEM)] + [pl.BlockSpec(memory_space=pltpu.VMEM)] * 3,
-        out_specs=[pl.BlockSpec(memory_space=pltpu.VMEM)] * NEAR,
-        name="pack",
-    )(me, dest, ids, rays)
+    own = jax.ShapeDtypeStruct((planes * tiles * pixels // LANES, LANES), jnp.float32)
+    own, *sent = pl.pallas_call(
+        functools.partial(prepare_kernel, n_sky, each),
+        out_shape=[own] + [part] * NEAR,
+        in_specs=[pl.BlockSpec(memory_space=pltpu.SMEM)] + [pl.BlockSpec(memory_space=pltpu.VMEM)] * 4,
+        out_specs=[pl.BlockSpec(memory_space=pltpu.VMEM)] * (1 + NEAR),
+        name="prepare",
+    )(me, dest, ids, rays, potential)
+    return own, sent
 
 
 def turn_kernel(size, *refs):
@@ -332,20 +328,18 @@
 def shards(potential, lens_weight, ray_start, patch_index, destination):
     n_sky = lax.axis_size("sky")
     me = lax.axis_index("sky").reshape(1)
-    planes, per_owner, _ = potential.shape
+    planes = potential.shape[0]
     bundles, _, rays = ray_start.shape
     each = max(2, 2 * bundles // n_sky)
     slots = n_sky * each
     halves = rays // LANES
     bits = [1 << k for k in reversed(range((n_sky - 1).bit_length()))]
     flat = ray_start.reshape(bundles, 2, halves, LANES).transpose(0, 2, 1, 3).reshape(bundles * 2 * halves, LANES)
-    own = regroup(potential)
+    own, sent = prepare(n_sky, each, me, destination.reshape(1, bundles), patch_index, flat, potential)
+    sent = [sent[0]] + [flipped(sent[s], n_sky, s) for s in range(1, NEAR)]
     held = {0: own}
     for bit in bits[:2]:
         held[bit] = flipped(own, n_sky, bit)
-    own, flat = lax.optimization_barrier((own, flat))
-    sent = pack(n_sky, each, per_owner, me, destination.reshape(1, bundles), patch_index, flat)
-    sent = [sent[0]] + [flipped(sent[s], n_sky, s) for s in range(1, NEAR)]
     held[bits[0] ^ bits[1]] = flipped(held[bits[0]], n_sky, bits[1])
     got = turn(4 * each + SUB, sent)
     early = [0, bits[0], bits[1]]
@@ -353,9 +347,11 @@
     held.update(zip(early, (a, b, c)))
     got = [got[0]] + [flipped(got[f], n_sky, f * NEAR) for f in range(1, len(got))]
     spread(held, n_sky, bits[:-1])
-    mid, *evens = lax.optimization_barrier((got[len(got) // 2], *[held[s] for s in range(0, n_sky, 2)]))
-    got[len(got) // 2] = mid
-    held.update(zip(range(0, n_sky, 2), evens))
+    half = len(got) // 2
+    for mid, low in ((half, 0), (half + 1, n_sky // 2)):
+        some = range(low, low + n_sky // 2, 2)
+        got[mid], *evens = lax.optimization_barrier((got[mid], *[held[s] for s in some]))
+        held.update(zip(some, evens))
     spread(held, n_sky, bits)
     shift, matrix = trace(each, planes, me, lens_weight, [held[s] for s in range(n_sky)], got)
     shift = shift.reshape(slots, halves, 2, LANES).transpose(0, 2, 1, 3).reshape(slots, 2, rays)

time: 60.5 us -> 58.9 us (0.974)
  Pallas kernels: 25.6 us -> 23.7 us
  starting transfers between devices: 17.2 us -> 18.3 us
  waiting for transfers between devices: 15.3 us -> 14.5 us
    pallas_call x2 -> x1, Pallas kernels: 4.25 us -> 2.37 us  [prepare(): pl.pallas_call(functools.partial(prepare_kernel, n_sky, each), out_shape=...]
    ppermute x21, starting transfers between devices: 17.2 us -> 18.3 us  [flipped(): return lax.ppermute(value, 'sky', [(i, i ^ bits) for i in range(n_sky)])]
    ppermute x21, waiting for transfers between devices: 15.3 us -> 14.5 us  [flipped(): return lax.ppermute(value, 'sky', [(i, i ^ bits) for i in range(n_sky)])]
  transfers between devices with their start and end apart: 21 -> 21, of which waited for: 14 -> 10; matrix products, arithmetic and copies ran while one was open for 0% -> 0% of each run, Pallas kernels for 7% -> 3%
where the time goes in v7:
time: 58.9 us; the launch traced here: 58.7 us
  Pallas kernels  23.7 us (40%)
  starting transfers between devices  18.3 us (31%)
  waiting for transfers between devices  14.5 us (25%)
  local copies, waits for them, and re-layouts  1.58 us (3%)
  between operations  0.68 us (1%)
    pallas_call x1, Pallas kernels, trace(): pl.pallas_call(functools.partial(trace_kernel, n_sky, each, planes, toget...  19.4 us
    ppermute x21, starting transfers between devices, flipped(): return lax.ppermute(value, 'sky', [(i, i ^ bits) for i in range(n_sky)])  18.3 us
    ppermute x21, waiting for transfers between devices, flipped(): return lax.ppermute(value, 'sky', [(i, i ^ bits) for i in range(n_sky)])  14.5 us
    pallas_call x1, Pallas kernels, prepare(): pl.pallas_call(functools.partial(prepare_kernel, n_sky, each), out_shape=...  2.37 us
    pallas_call x1, Pallas kernels, turn(): pl.pallas_call(functools.partial(turn_kernel, size), out_shape=[block] *...  1.98 us
    unnamed x12, local copies, waits for them, and re-layouts  1.58 us
  transfers between devices with their start and end apart: 21, of which 10 were waited for; matrix products, arithmetic and copies ran while one was open for 0% of the time, Pallas kernels for 3%

profile of v7, /device:TPU:0, one launch (start us, length us, event | category | flops | bytes accessed | tf_op | source)
XLA Modules:
  0.0 58.7 jit_solution(3668250128427838552)
XLA Ops:
  0.6 2.4 %prepare.1 = (f32[256,128]{1,0:T(8,128)}, f32[288,128]{1,0:T(8,128)}, f32[288,128]{1,0:T(8,128)}, f32[288,128]{1,0:T(8,128)}, f32[288,128]{1,0:T(8,128)}) custom-call(s32[1]{0:T(128)} %bitcast.me_ref, s32[1,128]{1,0:T(1,128)} %bitcast.18, s32[4,128]{1,0:T(4,128)} %ids_ref.1, f32[512,128]{1,0:T(8,128)} %bitcast.17, f32[4,8,1024]{2,1,0:T(8,128)} %src_ref.1), custom_call_target="tpu_custom_call" | custom-call | tf_op jit(solution)/shard_map/prepare/pallas_call | solution.py:126
  3.0 4.0 %collective-permute-start.3 = (f32[256,128]{1,0:T(8,128)}, f32[256,128]{1,0:T(8,128)S(1)}, u32[]{:S(2)}, u32[]{:S(2)}) collective-permute-start(f32[256,128]{1,0:T(8,128)} %get-tuple-element.42.refs_0_), channel_id=1, source_target_pairs={{0,8},{1,9},{2,10},{3,11},{4,12},{5,13},{6,14},{7,15},{8,0},{9,1},... | collective-permute-start | bytes 393224 | tf_op jit(solution)/shard_map/ppermute | solution.py:318
  7.0 0.0 collective-permute-start
  7.0 1.5 %collective-permute-start.1 = (f32[288,128]{1,0:T(8,128)}, f32[288,128]{1,0:T(8,128)S(1)}, u32[]{:S(2)}, u32[]{:S(2)}) collective-permute-start(f32[288,128]{1,0:T(8,128)} %get-tuple-element.32), channel_id=1, source_target_pairs={{0,2},{1,3},{2,0},{3,1},{4,6},{5,7},{6,4},{7,5},{8,10},{9,11},{10,... | collective-permute-start | bytes 442376 | tf_op jit(solution)/shard_map/ppermute | solution.py:318
  8.6 0.3 collective-permute-start.2
  8.9 1.6 %collective-permute-start.4 = (f32[256,128]{1,0:T(8,128)}, f32[256,128]{1,0:T(8,128)S(1)}, u32[]{:S(2)}, u32[]{:S(2)}) collective-permute-start(f32[256,128]{1,0:T(8,128)} %get-tuple-element.42.refs_0_), channel_id=1, source_target_pairs={{0,4},{1,5},{2,6},{3,7},{4,0},{5,1},{6,2},{7,3},{8,12},{9,13},{10,... | collective-permute-start | bytes 393224 | tf_op jit(solution)/shard_map/ppermute | solution.py:318
  10.5 3.2 %collective-permute-done.3.refs_8_ = f32[256,128]{1,0:T(8,128)S(1)} collective-permute-done((f32[256,128]{1,0:T(8,128)}, f32[256,128]{1,0:T(8,128)S(1)}, u32[]{:S(2)}, u32[]{:S(2)}) %collective-permute-start.3) | collective-permute-done | bytes 131104 | tf_op jit(solution)/shard_map/ppermute | solution.py:318
  13.7 0.8 %collective-permute-start.14 = (f32[256,128]{1,0:T(8,128)S(1)}, f32[256,128]{1,0:T(8,128)S(1)}, u32[]{:S(2)}, u32[]{:S(2)}) collective-permute-start(f32[256,128]{1,0:T(8,128)S(1)} %collective-permute-done.3.refs_8_), channel_id=1, source_target_pairs={{0,4},{1,5},{2,6},{3,7},{4,0},{5,1},{6,2},{7,3},{8,12},{9,13},{10,... | collective-permute-start | bytes 393224 | tf_op jit(solution)/shard_map/ppermute | solution.py:318
  14.4 0.0 collective-permute-done.refs_1_
  14.4 0.0 collective-permute-done.1.refs_2_
  14.4 1.8 %collective-permute-done.2.refs_3_ = f32[288,128]{1,0:T(8,128)S(1)} collective-permute-done((f32[288,128]{1,0:T(8,128)}, f32[288,128]{1,0:T(8,128)S(1)}, u32[]{:S(2)}, u32[]{:S(2)}) %collective-permute-start.2) | collective-permute-done | bytes 147488 | tf_op jit(solution)/shard_map/ppermute | solution.py:318
  16.3 0.0 copy-done.3
  16.3 0.6 %copy-done.5 = f32[288,128]{1,0:T(8,128)} copy-done((f32[288,128]{1,0:T(8,128)}, f32[288,128]{1,0:T(8,128)S(1)}, u32[]{:S(2)}) %copy-start.5) | copy-done | bytes 147480
  16.9 2.0 %turn.1 = (f32[288,128]{1,0:T(8,128)}, f32[288,128]{1,0:T(8,128)}, f32[288,128]{1,0:T(8,128)}, f32[288,128]{1,0:T(8,128)}) custom-call(f32[288,128]{1,0:T(8,128)} %get-tuple-element.30.refs_0_, f32[288,128]{1,0:T(8,128)} %copy-done.3, f32[288,128]{1,0:T(8,128)} %copy-done.4, f32[288,128]{1,0:T(8,128)} %copy-done.5), custom_call_target="tpu_custom_call" | custom-call | tf_op jit(solution)/shard_map/turn/pallas_call | solution.py:146
  18.9 0.0 collective-permute-done.4.refs_4_
  18.9 1.6 %collective-permute-start.6 = (f32[256,128]{1,0:T(8,128)S(1)}, f32[256,128]{1,0:T(8,128)S(1)}, u32[]{:S(2)}, u32[]{:S(2)}) collective-permute-start(f32[256,128]{1,0:T(8,128)S(1)} %copy-done.1), channel_id=1, source_target_pairs={{0,2},{1,3},{2,0},{3,1},{4,6},{5,7},{6,4},{7,5},{8,10},{9,11},{10,... | collective-permute-start | bytes 393224 | tf_op jit(solution)/shard_map/ppermute | solution.py:318
  20.5 1.6 %collective-permute-start.5 = (f32[288,128]{1,0:T(8,128)}, f32[288,128]{1,0:T(8,128)S(1)}, u32[]{:S(2)}, u32[]{:S(2)}) collective-permute-start(f32[288,128]{1,0:T(8,128)} %get-tuple-element.39), channel_id=1, source_target_pairs={{0,8},{1,9},{2,10},{3,11},{4,12},{5,13},{6,14},{7,15},{8,0},{9,1},... | collective-permute-start | bytes 442376 | tf_op jit(solution)/shard_map/ppermute | solution.py:318
  22.1 2.4 %collective-permute-start.12 = (f32[288,128]{1,0:T(8,128)}, f32[288,128]{1,0:T(8,128)S(1)}, u32[]{:S(2)}, u32[]{:S(2)}) collective-permute-start(f32[288,128]{1,0:T(8,128)} %get-tuple-element.46), channel_id=1, source_target_pairs={{0,12},{1,13},{2,14},{3,15},{4,8},{5,9},{6,10},{7,11},{8,4},{9,5},... | collective-permute-start | bytes 442376 | tf_op jit(solution)/shard_map/ppermute | solution.py:318
  24.5 0.5 collective-permute-start.7
  25.0 0.0 collective-permute-done.14.refs_12_
  25.0 1.5 %collective-permute-start.13 = (f32[256,128]{1,0:T(8,128)S(1)}, f32[256,128]{1,0:T(8,128)S(1)}, u32[]{:S(2)}, u32[]{:S(2)}) collective-permute-start(f32[256,128]{1,0:T(8,128)S(1)} %collective-permute-done.3.refs_8_), channel_id=1, source_target_pairs={{0,2},{1,3},{2,0},{3,1},{4,6},{5,7},{6,4},{7,5},{8,10},{9,11},{10,... | collective-permute-start | bytes 393224 | tf_op jit(solution)/shard_map/ppermute | solution.py:318
  26.5 0.0 collective-permute-done.6.refs_2_
  26.5 0.4 collective-permute-start.20
  26.9 4.0 %collective-permute-done.7.refs_6_ = f32[256,128]{1,0:T(8,128)S(1)} collective-permute-done((f32[256,128]{1,0:T(8,128)S(1)}, f32[256,128]{1,0:T(8,128)S(1)}, u32[]{:S(2)}, u32[]{:S(2)}) %collective-permute-start.7) | collective-permute-done | bytes 131104 | tf_op jit(solution)/shard_map/ppermute | solution.py:318
  30.9 0.5 collective-permute-start.15
  31.4 3.3 %collective-permute-done.5.refs_18_ = f32[288,128]{1,0:T(8,128)S(1)} collective-permute-done((f32[288,128]{1,0:T(8,128)}, f32[288,128]{1,0:T(8,128)S(1)}, u32[]{:S(2)}, u32[]{:S(2)}) %collective-permute-start.5) | collective-permute-done | bytes 147488 | tf_op jit(solution)/shard_map/ppermute | solution.py:318
  34.7 0.0 collective-permute-start.8
  34.7 0.0 collective-permute-done.13.refs_10_
  34.7 0.5 collective-permute-start.9
  35.2 0.0 collective-permute-done.12.refs_19_
  35.2 0.1 collective-permute-start.10
  35.3 0.5 collective-permute-done.15.refs_14_
  35.8 0.0 collective-permute-start.11
  35.8 0.5 collective-permute-done.20.refs_17_
  36.4 0.0 collective-permute-start.16
  36.4 0.0 collective-permute-done.8.refs_1_
  36.4 0.5 collective-permute-start.17
  36.9 0.0 collective-permute-done.9.refs_3_
  36.9 0.1 collective-permute-start.18
  37.0 0.0 collective-permute-done.10.refs_5_
  37.0 0.4 collective-permute-start.19
  37.4 0.0 collective-permute-done.11.refs_7_
  37.4 0.3 collective-permute-done.16.refs_9_
  37.7 0.2 collective-permute-done.17.refs_11_
  37.9 0.3 collective-permute-done.18.refs_13_
  38.2 0.2 collective-permute-done.19.refs_15_
  38.4 0.9 %copy-done = f32[288,128]{1,0:T(8,128)S(1)} copy-done((f32[288,128]{1,0:T(8,128)S(1)}, f32[288,128]{1,0:T(8,128)}, u32[]{:S(2)}) %copy-start) | copy-done | bytes 147480
  39.3 19.4 %trace.1 = (f32[1024,128]{1,0:T(8,128)}, f32[2048,128]{1,0:T(8,128)}) custom-call(s32[1]{0:T(128)} %bitcast.me_ref, f32[4]{0:T(128)S(1)} %copy-done.2, f32[256,128]{1,0:T(8,128)S(1)} %copy-done.1, f32[256,128]{1,0:T(8,128)S(1)} %collective-permute-done.8.refs_1_, f32[256,128]{1,0:T(8,128)S(1)} %collective-permute-done.6.refs_2_, ...), custom_call_target="tpu_custom_call" | custom-call | tf_op jit(solution)/shard_map/trace/pallas_call | solution.py:294
  (9 shorter events, 0.0 us)
Async XLA Ops:
  3.0 10.7 %collective-permute-start.3 = (f32[256,128]{1,0:T(8,128)}, f32[256,128]{1,0:T(8,128)S(1)}, u32[]{:S(2)}, u32[]{:S(2)}) collective-permute-start(f32[256,128]{1,0:T(8,128)} %get-tuple-element.42.refs_0_), channel_id=1, source_target_pairs={{0,8},{1,9},{2,10},{3,11},{4,12},{5,13},{6,14},{7,15},{8,0},{9,1},... | collective-permute-start | bytes 393224 | tf_op jit(solution)/shard_map/ppermute | solution.py:318
  7.0 7.4 %collective-permute-start = (f32[288,128]{1,0:T(8,128)}, f32[288,128]{1,0:T(8,128)S(1)}, u32[]{:S(2)}, u32[]{:S(2)}) collective-permute-start(f32[288,128]{1,0:T(8,128)} %get-tuple-element.31), channel_id=1, source_target_pairs={{0,1},{1,0},{2,3},{3,2},{4,5},{5,4},{6,7},{7,6},{8,9},{9,8},{10,11... | collective-permute-start | bytes 442376 | tf_op jit(solution)/shard_map/ppermute | solution.py:318
  7.0 7.4 %collective-permute-start.1 = (f32[288,128]{1,0:T(8,128)}, f32[288,128]{1,0:T(8,128)S(1)}, u32[]{:S(2)}, u32[]{:S(2)}) collective-permute-start(f32[288,128]{1,0:T(8,128)} %get-tuple-element.32), channel_id=1, source_target_pairs={{0,2},{1,3},{2,0},{3,1},{4,6},{5,7},{6,4},{7,5},{8,10},{9,11},{10,... | collective-permute-start | bytes 442376 | tf_op jit(solution)/shard_map/ppermute | solution.py:318
  8.6 7.7 %collective-permute-start.2 = (f32[288,128]{1,0:T(8,128)}, f32[288,128]{1,0:T(8,128)S(1)}, u32[]{:S(2)}, u32[]{:S(2)}) collective-permute-start(f32[288,128]{1,0:T(8,128)} %get-tuple-element.33), channel_id=1, source_target_pairs={{0,3},{1,2},{2,1},{3,0},{4,7},{5,6},{6,5},{7,4},{8,11},{9,10},{10,... | collective-permute-start | bytes 442376 | tf_op jit(solution)/shard_map/ppermute | solution.py:318
  8.9 10.0 %collective-permute-start.4 = (f32[256,128]{1,0:T(8,128)}, f32[256,128]{1,0:T(8,128)S(1)}, u32[]{:S(2)}, u32[]{:S(2)}) collective-permute-start(f32[256,128]{1,0:T(8,128)} %get-tuple-element.42.refs_0_), channel_id=1, source_target_pairs={{0,4},{1,5},{2,6},{3,7},{4,0},{5,1},{6,2},{7,3},{8,12},{9,13},{10,... | collective-permute-start | bytes 393224 | tf_op jit(solution)/shard_map/ppermute | solution.py:318
  13.7 11.3 %collective-permute-start.14 = (f32[256,128]{1,0:T(8,128)S(1)}, f32[256,128]{1,0:T(8,128)S(1)}, u32[]{:S(2)}, u32[]{:S(2)}) collective-permute-start(f32[256,128]{1,0:T(8,128)S(1)} %collective-permute-done.3.refs_8_), channel_id=1, source_target_pairs={{0,4},{1,5},{2,6},{3,7},{4,0},{5,1},{6,2},{7,3},{8,12},{9,13},{10,... | collective-permute-start | bytes 393224 | tf_op jit(solution)/shard_map/ppermute | solution.py:318
  14.4 1.9 %copy-start.3 = (f32[288,128]{1,0:T(8,128)}, f32[288,128]{1,0:T(8,128)S(1)}, u32[]{:S(2)}) copy-start(f32[288,128]{1,0:T(8,128)S(1)} %collective-permute-done.refs_1_) | copy-start | bytes 442372
  14.4 1.9 %copy-start.4 = (f32[288,128]{1,0:T(8,128)}, f32[288,128]{1,0:T(8,128)S(1)}, u32[]{:S(2)}) copy-start(f32[288,128]{1,0:T(8,128)S(1)} %collective-permute-done.1.refs_2_) | copy-start | bytes 442372
  16.3 0.7 %copy-start.5 = (f32[288,128]{1,0:T(8,128)}, f32[288,128]{1,0:T(8,128)S(1)}, u32[]{:S(2)}) copy-start(f32[288,128]{1,0:T(8,128)S(1)} %collective-permute-done.2.refs_3_) | copy-start | bytes 442372
  16.9 2.0 %copy-start.1 = (f32[256,128]{1,0:T(8,128)S(1)}, f32[256,128]{1,0:T(8,128)}, u32[]{:S(2)}) copy-start(f32[256,128]{1,0:T(8,128)} %get-tuple-element.42.refs_0_) | copy-start | bytes 393220
  18.9 19.5 %copy-start.2 = (f32[4]{0:T(128)S(1)}, f32[4]{0:T(128)}, u32[]{:S(2)}) copy-start(f32[4]{0:T(128)} %lens_ref.1) | copy-start | bytes 52
  18.9 7.6 %collective-permute-start.6 = (f32[256,128]{1,0:T(8,128)S(1)}, f32[256,128]{1,0:T(8,128)S(1)}, u32[]{:S(2)}, u32[]{:S(2)}) collective-permute-start(f32[256,128]{1,0:T(8,128)S(1)} %copy-done.1), channel_id=1, source_target_pairs={{0,2},{1,3},{2,0},{3,1},{4,6},{5,7},{6,4},{7,5},{8,10},{9,11},{10,... | collective-permute-start | bytes 393224 | tf_op jit(solution)/shard_map/ppermute | solution.py:318
  20.5 14.2 %collective-permute-start.5 = (f32[288,128]{1,0:T(8,128)}, f32[288,128]{1,0:T(8,128)S(1)}, u32[]{:S(2)}, u32[]{:S(2)}) collective-permute-start(f32[288,128]{1,0:T(8,128)} %get-tuple-element.39), channel_id=1, source_target_pairs={{0,8},{1,9},{2,10},{3,11},{4,12},{5,13},{6,14},{7,15},{8,0},{9,1},... | collective-permute-start | bytes 442376 | tf_op jit(solution)/shard_map/ppermute | solution.py:318
  22.1 13.1 %collective-permute-start.12 = (f32[288,128]{1,0:T(8,128)}, f32[288,128]{1,0:T(8,128)S(1)}, u32[]{:S(2)}, u32[]{:S(2)}) collective-permute-start(f32[288,128]{1,0:T(8,128)} %get-tuple-element.46), channel_id=1, source_target_pairs={{0,12},{1,13},{2,14},{3,15},{4,8},{5,9},{6,10},{7,11},{8,4},{9,5},... | collective-permute-start | bytes 442376 | tf_op jit(solution)/shard_map/ppermute | solution.py:318
  24.5 6.4 %collective-permute-start.7 = (f32[256,128]{1,0:T(8,128)S(1)}, f32[256,128]{1,0:T(8,128)S(1)}, u32[]{:S(2)}, u32[]{:S(2)}) collective-permute-start(f32[256,128]{1,0:T(8,128)S(1)} %collective-permute-done.4.refs_4_), channel_id=1, source_target_pairs={{0,2},{1,3},{2,0},{3,1},{4,6},{5,7},{6,4},{7,5},{8,10},{9,11},{10,... | collective-permute-start | bytes 393224 | tf_op jit(solution)/shard_map/ppermute | solution.py:318
  25.0 9.7 %collective-permute-start.13 = (f32[256,128]{1,0:T(8,128)S(1)}, f32[256,128]{1,0:T(8,128)S(1)}, u32[]{:S(2)}, u32[]{:S(2)}) collective-permute-start(f32[256,128]{1,0:T(8,128)S(1)} %collective-permute-done.3.refs_8_), channel_id=1, source_target_pairs={{0,2},{1,3},{2,0},{3,1},{4,6},{5,7},{6,4},{7,5},{8,10},{9,11},{10,... | collective-permute-start | bytes 393224 | tf_op jit(solution)/shard_map/ppermute | solution.py:318
  26.5 9.9 %collective-permute-start.20 = (f32[288,128]{1,0:T(8,128)}, f32[288,128]{1,0:T(8,128)S(1)}, u32[]{:S(2)}, u32[]{:S(2)}) collective-permute-start(f32[288,128]{1,0:T(8,128)} %get-tuple-element.53), channel_id=1, source_target_pairs={{0,4},{1,5},{2,6},{3,7},{4,0},{5,1},{6,2},{7,3},{8,12},{9,13},{10,... | collective-permute-start | bytes 442376 | tf_op jit(solution)/shard_map/ppermute | solution.py:318
  30.9 5.0 %collective-permute-start.15 = (f32[256,128]{1,0:T(8,128)S(1)}, f32[256,128]{1,0:T(8,128)S(1)}, u32[]{:S(2)}, u32[]{:S(2)}) collective-permute-start(f32[256,128]{1,0:T(8,128)S(1)} %collective-permute-done.14.refs_12_), channel_id=1, source_target_pairs={{0,2},{1,3},{2,0},{3,1},{4,6},{5,7},{6,4},{7,5},{8,10},{9,11},{10,... | collective-permute-start | bytes 393224 | tf_op jit(solution)/shard_map/ppermute | solution.py:318
  34.7 1.7 %collective-permute-start.8 = (f32[256,128]{1,0:T(8,128)S(1)}, f32[256,128]{1,0:T(8,128)S(1)}, u32[]{:S(2)}, u32[]{:S(2)}) collective-permute-start(f32[256,128]{1,0:T(8,128)S(1)} %copy-done.1), channel_id=1, source_target_pairs={{0,1},{1,0},{2,3},{3,2},{4,5},{5,4},{6,7},{7,6},{8,9},{9,8},{10,11... | collective-permute-start | bytes 393224 | tf_op jit(solution)/shard_map/ppermute | solution.py:318
  34.7 2.2 %collective-permute-start.9 = (f32[256,128]{1,0:T(8,128)S(1)}, f32[256,128]{1,0:T(8,128)S(1)}, u32[]{:S(2)}, u32[]{:S(2)}) collective-permute-start(f32[256,128]{1,0:T(8,128)S(1)} %collective-permute-done.6.refs_2_), channel_id=1, source_target_pairs={{0,1},{1,0},{2,3},{3,2},{4,5},{5,4},{6,7},{7,6},{8,9},{9,8},{10,11... | collective-permute-start | bytes 393224 | tf_op jit(solution)/shard_map/ppermute | solution.py:318
  35.2 1.7 %collective-permute-start.10 = (f32[256,128]{1,0:T(8,128)S(1)}, f32[256,128]{1,0:T(8,128)S(1)}, u32[]{:S(2)}, u32[]{:S(2)}) collective-permute-start(f32[256,128]{1,0:T(8,128)S(1)} %collective-permute-done.4.refs_4_), channel_id=1, source_target_pairs={{0,1},{1,0},{2,3},{3,2},{4,5},{5,4},{6,7},{7,6},{8,9},{9,8},{10,11... | collective-permute-start | bytes 393224 | tf_op jit(solution)/shard_map/ppermute | solution.py:318
  35.8 1.6 %collective-permute-start.11 = (f32[256,128]{1,0:T(8,128)S(1)}, f32[256,128]{1,0:T(8,128)S(1)}, u32[]{:S(2)}, u32[]{:S(2)}) collective-permute-start(f32[256,128]{1,0:T(8,128)S(1)} %collective-permute-done.7.refs_6_), channel_id=1, source_target_pairs={{0,1},{1,0},{2,3},{3,2},{4,5},{5,4},{6,7},{7,6},{8,9},{9,8},{10,11... | collective-permute-start | bytes 393224 | tf_op jit(solution)/shard_map/ppermute | solution.py:318
  36.4 1.3 %collective-permute-start.16 = (f32[256,128]{1,0:T(8,128)S(1)}, f32[256,128]{1,0:T(8,128)S(1)}, u32[]{:S(2)}, u32[]{:S(2)}) collective-permute-start(f32[256,128]{1,0:T(8,128)S(1)} %collective-permute-done.3.refs_8_), channel_id=1, source_target_pairs={{0,1},{1,0},{2,3},{3,2},{4,5},{5,4},{6,7},{7,6},{8,9},{9,8},{10,11... | collective-permute-start | bytes 393224 | tf_op jit(solution)/shard_map/ppermute | solution.py:318
  36.4 1.5 %collective-permute-start.17 = (f32[256,128]{1,0:T(8,128)S(1)}, f32[256,128]{1,0:T(8,128)S(1)}, u32[]{:S(2)}, u32[]{:S(2)}) collective-permute-start(f32[256,128]{1,0:T(8,128)S(1)} %collective-permute-done.13.refs_10_), channel_id=1, source_target_pairs={{0,1},{1,0},{2,3},{3,2},{4,5},{5,4},{6,7},{7,6},{8,9},{9,8},{10,11... | collective-permute-start | bytes 393224 | tf_op jit(solution)/shard_map/ppermute | solution.py:318
  36.9 1.3 %collective-permute-start.18 = (f32[256,128]{1,0:T(8,128)S(1)}, f32[256,128]{1,0:T(8,128)S(1)}, u32[]{:S(2)}, u32[]{:S(2)}) collective-permute-start(f32[256,128]{1,0:T(8,128)S(1)} %collective-permute-done.14.refs_12_), channel_id=1, source_target_pairs={{0,1},{1,0},{2,3},{3,2},{4,5},{5,4},{6,7},{7,6},{8,9},{9,8},{10,11... | collective-permute-start | bytes 393224 | tf_op jit(solution)/shard_map/ppermute | solution.py:318
  37.0 1.5 %collective-permute-start.19 = (f32[256,128]{1,0:T(8,128)S(1)}, f32[256,128]{1,0:T(8,128)S(1)}, u32[]{:S(2)}, u32[]{:S(2)}) collective-permute-start(f32[256,128]{1,0:T(8,128)S(1)} %collective-permute-done.15.refs_14_), channel_id=1, source_target_pairs={{0,1},{1,0},{2,3},{3,2},{4,5},{5,4},{6,7},{7,6},{8,9},{9,8},{10,11... | collective-permute-start | bytes 393224 | tf_op jit(solution)/shard_map/ppermute | solution.py:318
  38.4 0.9 %copy-start = (f32[288,128]{1,0:T(8,128)S(1)}, f32[288,128]{1,0:T(8,128)}, u32[]{:S(2)}) copy-start(f32[288,128]{1,0:T(8,128)} %get-tuple-element.52.refs_16_) | copy-start | bytes 442372

commit v8 on v7

--- a/solution.py
+++ b/solution.py
@@ -216,35 +216,50 @@
     return pos_x - half * fx2, pos_y - half * fy2, matrix
 
 
-def trace_kernel(n_sky, each, planes, together, me_ref, lens_ref, *refs):
-    far = n_sky // NEAR
+def store_kernel(*refs):
+    *tile_refs, store_ref, sems = refs
+    rows = tile_refs[0].shape[0]
+    copies = [
+        pltpu.make_async_copy(tile_ref, store_ref.at[pl.ds(s * rows, rows), :], sems.at[s])
+        for s, tile_ref in enumerate(tile_refs)
+    ]
+    for copy in copies:
+        copy.start()
+    for copy in copies:
+        copy.wait()
+
+
+def store(tiles):
+    rows = tiles[0].shape[0]
+    return pl.pallas_call(
+        store_kernel,
+        out_shape=jax.ShapeDtypeStruct((len(tiles) * rows, LANES), jnp.float32),
+        in_specs=[pl.BlockSpec(memory_space=pl.ANY)] * len(tiles),
+        out_specs=pl.BlockSpec(memory_space=pltpu.VMEM),
+        scratch_shapes=[pltpu.SemaphoreType.DMA((len(tiles),))],
+        compiler_params=pltpu.CompilerParams(vmem_limit_bytes=40 * 1024 * 1024),
+        name="store",
+    )(*tiles)
+
+
+def trace_kernel(f, each, planes, together, me_ref, lens_ref, tiles, got_ref, *refs):
+    shift_ref, matrix_ref, chosen, rays, places, shift, matrix, sems = refs[-8:]
+    me = me_ref[0]
+    slots = NEAR * each
     size = 4 * each + SUB
-    tile_refs, got_refs = refs[:n_sky], refs[n_sky:n_sky + far]
-    shift_ref, matrix_ref, tiles, chosen, rays, places, sems = refs[n_sky + far:]
-    me = me_ref[0]
-    slots = n_sky * each
-    rows = tile_refs[0].shape[0]
-    copies = []
-    for s in range(n_sky):
-        source = me ^ s
-        got_ref, first = got_refs[s // NEAR], s % NEAR * size
-        copies.append((
-            pltpu.make_async_copy(
-                got_ref.at[pl.ds(first + 4 * each, SUB), :],
-                places.at[pl.ds(source * SUB, SUB), :],
-                sems.at[0, s]),
-            pltpu.make_async_copy(tile_refs[s], tiles.at[pl.ds(s * rows, rows), :], sems.at[1, s]),
-            pltpu.make_async_copy(
-                got_ref.at[pl.ds(first, 4 * each), :],
-                rays.at[pl.ds(source * 4 * each, 4 * each), :],
-                sems.at[2, s]),
-        ))
-    for kind in range(3):
-        for s in range(n_sky):
-            copies[s][kind].start()
-    for kind in range(3):
-        for s in range(n_sky):
-            copies[s][kind].wait()
+    numbers = [
+        pltpu.make_async_copy(
+            got_ref.at[pl.ds(c * size + 4 * each, SUB), :],
+            places.at[pl.ds(c * SUB, SUB), :],
+            sems.at[0, c])
+        for c in range(NEAR)
+    ]
+    for copy in numbers:
+        copy.start()
+    for c in range(NEAR):
+        rays[pl.ds(c * 4 * each, 4 * each), :] = got_ref[pl.ds(c * size, 4 * each), :]
+    for copy in numbers:
+        copy.wait()
 
     def body(step, carry):
         chains = []
@@ -274,44 +289,60 @@
                 ]
                 later.append((part, h, x0, y0, trace_step(tables, strength, *state)))
             chains = later
-        for part, h, x0, y0, (x, y, matrix) in chains:
+        for part, h, x0, y0, (x, y, entries) in chains:
             base = first + part * SUB
             used = x0 > EMPTY * 0.5
-            shift_ref[pl.ds(base * 4 + 2 * h, SUB, stride=4), :] = jnp.where(used, x - x0, 0.0)
-            shift_ref[pl.ds(base * 4 + 2 * h + 1, SUB, stride=4), :] = jnp.where(used, y - y0, 0.0)
+            shift[pl.ds(base * 4 + 2 * h, SUB, stride=4), :] = jnp.where(used, x - x0, 0.0)
+            shift[pl.ds(base * 4 + 2 * h + 1, SUB, stride=4), :] = jnp.where(used, y - y0, 0.0)
             for e in range(4):
-                matrix_ref[pl.ds(base * 8 + 4 * h + e, SUB, stride=8), :] = jnp.where(used, matrix[e], 0.0)
+                matrix[pl.ds(base * 8 + 4 * h + e, SUB, stride=8), :] = jnp.where(used, entries[e], 0.0)
         return carry
 
     lax.fori_loop(0, slots // (SUB * together), body, 0)
-
-
-def trace(each, planes, me, lens_weight, tiles, got):
-    n_sky = len(tiles)
-    slots = n_sky * each
-    rows = tiles[0].shape[0]
-    together = 4
+    copies = []
+    for c in range(NEAR):
+        source = me ^ (f * NEAR + c)
+        for kind, (block, out_ref, rows) in enumerate(((shift, shift_ref, 4 * each), (matrix, matrix_ref, 8 * each))):
+            copies.append(pltpu.make_async_copy(
+                block.at[pl.ds(c * rows, rows), :],
+                out_ref.at[pl.ds(source * rows, rows), :],
+                sems.at[1 + kind, c]))
+    for copy in copies:
+        copy.start()
+    for copy in copies:
+        copy.wait()
+
+
+def trace(f, each, planes, me, lens_weight, tiles, got, n_sky, outs):
+    slots = NEAR * each
+    together = min(4, slots // SUB)
     return pl.pallas_call(
-        functools.partial(trace_kernel, n_sky, each, planes, together),
+        functools.partial(trace_kernel, f, each, planes, together),
         out_shape=(
-            jax.ShapeDtypeStruct((slots * 4, LANES), jnp.float32),
-            jax.ShapeDtypeStruct((slots * 8, LANES), jnp.float32),
+            jax.ShapeDtypeStruct((n_sky * each * 4, LANES), jnp.float32),
+            jax.ShapeDtypeStruct((n_sky * each * 8, LANES), jnp.float32),
         ),
-        in_specs=[pl.BlockSpec(memory_space=pltpu.SMEM)] * 2 + [pl.BlockSpec(memory_space=pl.ANY)] * (n_sky + len(got)),
+        in_specs=(
+            [pl.BlockSpec(memory_space=pltpu.SMEM)] * 2
+            + [pl.BlockSpec(memory_space=pltpu.VMEM)] * 2
+            + [pl.BlockSpec(memory_space=pl.ANY)] * len(outs)
+        ),
         out_specs=(
-            pl.BlockSpec(memory_space=pltpu.VMEM),
-            pl.BlockSpec(memory_space=pltpu.VMEM),
+            pl.BlockSpec(memory_space=pl.ANY),
+            pl.BlockSpec(memory_space=pl.ANY),
         ),
         scratch_shapes=[
-            pltpu.VMEM((n_sky * rows, LANES), jnp.float32),
             pltpu.VMEM((planes * together * CHUNKS * SUB, LANES), jnp.float32),
             pltpu.VMEM((slots * 4, LANES), jnp.float32),
-            pltpu.SMEM((n_sky * SUB, LANES), jnp.float32),
-            pltpu.SemaphoreType.DMA((3, n_sky)),
+            pltpu.SMEM((NEAR * SUB, LANES), jnp.float32),
+            pltpu.VMEM((slots * 4, LANES), jnp.float32),
+            pltpu.VMEM((slots * 8, LANES), jnp.float32),
+            pltpu.SemaphoreType.DMA((3, NEAR)),
         ],
+        input_output_aliases={4 + k: k for k in range(len(outs))},
         compiler_params=pltpu.CompilerParams(vmem_limit_bytes=40 * 1024 * 1024),
         name="trace",
-    )(me, lens_weight, *tiles, *got)
+    )(me, lens_weight, tiles, got, *outs)
 
 
 def flipped(value, n_sky, bits):
@@ -346,14 +377,12 @@
     *got, a, b, c = lax.optimization_barrier((*got, *[held[s] for s in early]))
     held.update(zip(early, (a, b, c)))
     got = [got[0]] + [flipped(got[f], n_sky, f * NEAR) for f in range(1, len(got))]
-    spread(held, n_sky, bits[:-1])
-    half = len(got) // 2
-    for mid, low in ((half, 0), (half + 1, n_sky // 2)):
-        some = range(low, low + n_sky // 2, 2)
-        got[mid], *evens = lax.optimization_barrier((got[mid], *[held[s] for s in some]))
-        held.update(zip(some, evens))
     spread(held, n_sky, bits)
-    shift, matrix = trace(each, planes, me, lens_weight, [held[s] for s in range(n_sky)], got)
+    tiles = store([held[s] for s in range(n_sky)])
+    outs = ()
+    for f in range(len(got)):
+        outs = trace(f, each, planes, me, lens_weight, tiles, got[f], n_sky, outs)
+    shift, matrix = outs
     shift = shift.reshape(slots, halves, 2, LANES).transpose(0, 2, 1, 3).reshape(slots, 2, rays)
     matrix = matrix.reshape(slots, halves, 4, LANES).transpose(0, 2, 1, 3).reshape(slots, 4, rays)
     return shift, matrix

time: 58.9 us -> 65.2 us (1.11)
  Pallas kernels: 23.7 us -> 29.4 us
  starting transfers between devices: 18.3 us -> 20.3 us
  waiting for transfers between devices: 14.5 us -> 13 us
    pallas_call x1 -> x5, Pallas kernels: 19.4 us -> 25 us  [the longest x4 22.1 us: trace(): pl.pallas_call(functools.partial(trace_kernel, f, each, planes, together)...]
    ppermute x21, starting transfers between devices: 18.3 us -> 20.3 us  [flipped(): return lax.ppermute(value, 'sky', [(i, i ^ bits) for i in range(n_sky)])]
    ppermute x21, waiting for transfers between devices: 14.5 us -> 13 us  [flipped(): return lax.ppermute(value, 'sky', [(i, i ^ bits) for i in range(n_sky)])]
  transfers between devices with their start and end apart: 21 -> 21, of which waited for: 10 -> 8; matrix products, arithmetic and copies ran while one was open for 0% -> 0% of each run, Pallas kernels for 3% -> 33%
where the time goes in v8:
time: 65.2 us; the launch traced here: 65 us
  Pallas kernels  29.4 us (45%)
  starting transfers between devices  20.3 us (31%)
  waiting for transfers between devices  13 us (20%)
  local copies, waits for them, and re-layouts  1.58 us (2%)
  between operations  0.75 us (1%)
    pallas_call x4, Pallas kernels, trace(): pl.pallas_call(functools.partial(trace_kernel, f, each, planes, together)...  22.1 us
    ppermute x21, starting transfers between devices, flipped(): return lax.ppermute(value, 'sky', [(i, i ^ bits) for i in range(n_sky)])  20.3 us
    ppermute x21, waiting for transfers between devices, flipped(): return lax.ppermute(value, 'sky', [(i, i ^ bits) for i in range(n_sky)])  13 us
    pallas_call x1, Pallas kernels, store(): pl.pallas_call(store_kernel, out_shape=jax.ShapeDtypeStruct((len(tiles) *...  2.93 us
    pallas_call x1, Pallas kernels, prepare(): pl.pallas_call(functools.partial(prepare_kernel, n_sky, each), out_shape=...  2.37 us
    pallas_call x1, Pallas kernels, turn(): pl.pallas_call(functools.partial(turn_kernel, size), out_shape=[block] *...  1.96 us
    unnamed x12, local copies, waits for them, and re-layouts  1.58 us
  transfers between devices with their start and end apart: 21, of which 8 were waited for; matrix products, arithmetic and copies ran while one was open for 0% of the time, Pallas kernels for 33%

profile of v8, /device:TPU:0, one launch (start us, length us, event | category | flops | bytes accessed | tf_op | source)
XLA Modules:
  0.0 65.0 jit_solution(15879467152075704986)
XLA Ops:
  0.6 2.4 %prepare.1 = (f32[256,128]{1,0:T(8,128)}, f32[288,128]{1,0:T(8,128)}, f32[288,128]{1,0:T(8,128)}, f32[288,128]{1,0:T(8,128)}, f32[288,128]{1,0:T(8,128)}) custom-call(s32[1]{0:T(128)} %bitcast.me_ref, s32[1,128]{1,0:T(1,128)} %bitcast.20, s32[4,128]{1,0:T(4,128)} %ids_ref.1, f32[512,128]{1,0:T(8,128)} %bitcast.19, f32[4,8,1024]{2,1,0:T(8,128)} %src_ref.1), custom_call_target="tpu_custom_call" | custom-call | tf_op jit(solution)/shard_map/prepare/pallas_call | solution.py:126
  3.0 4.0 %collective-permute-start.3 = (f32[256,128]{1,0:T(8,128)}, f32[256,128]{1,0:T(8,128)S(1)}, u32[]{:S(2)}, u32[]{:S(2)}) collective-permute-start(f32[256,128]{1,0:T(8,128)} %get-tuple-element.35.refs_0_), channel_id=1, source_target_pairs={{0,8},{1,9},{2,10},{3,11},{4,12},{5,13},{6,14},{7,15},{8,0},{9,1},... | collective-permute-start | bytes 393224 | tf_op jit(solution)/shard_map/ppermute | solution.py:349
  7.0 0.0 collective-permute-start
  7.0 1.5 %collective-permute-start.1 = (f32[288,128]{1,0:T(8,128)}, f32[288,128]{1,0:T(8,128)S(1)}, u32[]{:S(2)}, u32[]{:S(2)}) collective-permute-start(f32[288,128]{1,0:T(8,128)} %get-tuple-element.28), channel_id=1, source_target_pairs={{0,2},{1,3},{2,0},{3,1},{4,6},{5,7},{6,4},{7,5},{8,10},{9,11},{10,... | collective-permute-start | bytes 442376 | tf_op jit(solution)/shard_map/ppermute | solution.py:349
  8.6 0.3 collective-permute-start.2
  8.9 1.6 %collective-permute-start.4 = (f32[256,128]{1,0:T(8,128)}, f32[256,128]{1,0:T(8,128)S(1)}, u32[]{:S(2)}, u32[]{:S(2)}) collective-permute-start(f32[256,128]{1,0:T(8,128)} %get-tuple-element.35.refs_0_), channel_id=1, source_target_pairs={{0,4},{1,5},{2,6},{3,7},{4,0},{5,1},{6,2},{7,3},{8,12},{9,13},{10,... | collective-permute-start | bytes 393224 | tf_op jit(solution)/shard_map/ppermute | solution.py:349
  10.5 3.2 %collective-permute-done.3.refs_8_ = f32[256,128]{1,0:T(8,128)S(1)} collective-permute-done((f32[256,128]{1,0:T(8,128)}, f32[256,128]{1,0:T(8,128)S(1)}, u32[]{:S(2)}, u32[]{:S(2)}) %collective-permute-start.3) | collective-permute-done | bytes 131104 | tf_op jit(solution)/shard_map/ppermute | solution.py:349
  13.7 0.8 %collective-permute-start.14 = (f32[256,128]{1,0:T(8,128)S(1)}, f32[256,128]{1,0:T(8,128)S(1)}, u32[]{:S(2)}, u32[]{:S(2)}) collective-permute-start(f32[256,128]{1,0:T(8,128)S(1)} %collective-permute-done.3.refs_8_), channel_id=1, source_target_pairs={{0,4},{1,5},{2,6},{3,7},{4,0},{5,1},{6,2},{7,3},{8,12},{9,13},{10,... | collective-permute-start | bytes 393224 | tf_op jit(solution)/shard_map/ppermute | solution.py:349
  14.4 0.0 collective-permute-done.refs_1_
  14.4 0.0 collective-permute-done.1.refs_2_
  14.5 1.8 %collective-permute-done.2.refs_3_ = f32[288,128]{1,0:T(8,128)S(1)} collective-permute-done((f32[288,128]{1,0:T(8,128)}, f32[288,128]{1,0:T(8,128)S(1)}, u32[]{:S(2)}, u32[]{:S(2)}) %collective-permute-start.2) | collective-permute-done | bytes 147488 | tf_op jit(solution)/shard_map/ppermute | solution.py:349
  16.3 0.7 %copy-done.5 = f32[288,128]{1,0:T(8,128)} copy-done((f32[288,128]{1,0:T(8,128)}, f32[288,128]{1,0:T(8,128)S(1)}, u32[]{:S(2)}) %copy-start.5) | copy-done | bytes 147480
  17.0 2.0 %turn.1 = (f32[288,128]{1,0:T(8,128)}, f32[288,128]{1,0:T(8,128)}, f32[288,128]{1,0:T(8,128)}, f32[288,128]{1,0:T(8,128)}) custom-call(f32[288,128]{1,0:T(8,128)} %get-tuple-element.26.refs_0_, f32[288,128]{1,0:T(8,128)} %copy-done.3, f32[288,128]{1,0:T(8,128)} %copy-done.4, f32[288,128]{1,0:T(8,128)} %copy-done.5), custom_call_target="tpu_custom_call" | custom-call | tf_op jit(solution)/shard_map/turn/pallas_call | solution.py:146
  18.9 0.0 collective-permute-done.4.refs_4_
  18.9 1.6 %collective-permute-start.6 = (f32[256,128]{1,0:T(8,128)}, f32[256,128]{1,0:T(8,128)S(1)}, u32[]{:S(2)}, u32[]{:S(2)}) collective-permute-start(f32[256,128]{1,0:T(8,128)} %get-tuple-element.35.refs_0_), channel_id=1, source_target_pairs={{0,2},{1,3},{2,0},{3,1},{4,6},{5,7},{6,4},{7,5},{8,10},{9,11},{10,... | collective-permute-start | bytes 393224 | tf_op jit(solution)/shard_map/ppermute | solution.py:349
  20.5 0.0 collective-permute-start.5
  20.5 0.5 collective-permute-start.9
  21.0 0.2 collective-permute-start.8
  21.2 0.0 collective-permute-done.14.refs_12_
  21.2 1.5 %collective-permute-start.12 = (f32[256,128]{1,0:T(8,128)S(1)}, f32[256,128]{1,0:T(8,128)S(1)}, u32[]{:S(2)}, u32[]{:S(2)}) collective-permute-start(f32[256,128]{1,0:T(8,128)S(1)} %collective-permute-done.3.refs_8_), channel_id=1, source_target_pairs={{0,2},{1,3},{2,0},{3,1},{4,6},{5,7},{6,4},{7,5},{8,10},{9,11},{10,... | collective-permute-start | bytes 393224 | tf_op jit(solution)/shard_map/ppermute | solution.py:349
  22.8 2.7 %collective-permute-done.6.refs_2_ = f32[256,128]{1,0:T(8,128)S(1)} collective-permute-done((f32[256,128]{1,0:T(8,128)}, f32[256,128]{1,0:T(8,128)S(1)}, u32[]{:S(2)}, u32[]{:S(2)}) %collective-permute-start.6) | collective-permute-done | bytes 131104 | tf_op jit(solution)/shard_map/ppermute | solution.py:349
  25.5 0.0 collective-permute-start.11
  25.5 0.0 collective-permute-done.5.refs_1_
  25.5 1.5 %collective-permute-start.16 = (f32[256,128]{1,0:T(8,128)S(1)}, f32[256,128]{1,0:T(8,128)S(1)}, u32[]{:S(2)}, u32[]{:S(2)}) collective-permute-start(f32[256,128]{1,0:T(8,128)S(1)} %collective-permute-done.14.refs_12_), channel_id=1, source_target_pairs={{0,2},{1,3},{2,0},{3,1},{4,6},{5,7},{6,4},{7,5},{8,10},{9,11},{10,... | collective-permute-start | bytes 393224 | tf_op jit(solution)/shard_map/ppermute | solution.py:349
  27.0 1.3 %collective-permute-done.9.refs_6_ = f32[256,128]{1,0:T(8,128)S(1)} collective-permute-done((f32[256,128]{1,0:T(8,128)S(1)}, f32[256,128]{1,0:T(8,128)S(1)}, u32[]{:S(2)}, u32[]{:S(2)}) %collective-permute-start.9) | collective-permute-done | bytes 131104 | tf_op jit(solution)/shard_map/ppermute | solution.py:349
  28.3 0.0 collective-permute-start.15
  28.3 0.0 collective-permute-done.8.refs_5_
  28.3 0.5 collective-permute-start.7
  28.8 2.3 %collective-permute-done.12.refs_10_ = f32[256,128]{1,0:T(8,128)S(1)} collective-permute-done((f32[256,128]{1,0:T(8,128)S(1)}, f32[256,128]{1,0:T(8,128)S(1)}, u32[]{:S(2)}, u32[]{:S(2)}) %collective-permute-start.12) | collective-permute-done | bytes 131104 | tf_op jit(solution)/shard_map/ppermute | solution.py:349
  31.1 0.0 collective-permute-start.10
  31.1 0.0 collective-permute-done.11.refs_9_
  31.1 1.6 %collective-permute-start.20 = (f32[288,128]{1,0:T(8,128)}, f32[288,128]{1,0:T(8,128)S(1)}, u32[]{:S(2)}, u32[]{:S(2)}) collective-permute-start(f32[288,128]{1,0:T(8,128)} %get-tuple-element.40), channel_id=1, source_target_pairs={{0,4},{1,5},{2,6},{3,7},{4,0},{5,1},{6,2},{7,3},{8,12},{9,13},{10,... | collective-permute-start | bytes 442376 | tf_op jit(solution)/shard_map/ppermute | solution.py:349
  32.7 0.6 collective-permute-done.16.refs_14_
  33.3 1.0 %collective-permute-start.19 = (f32[288,128]{1,0:T(8,128)}, f32[288,128]{1,0:T(8,128)S(1)}, u32[]{:S(2)}, u32[]{:S(2)}) collective-permute-start(f32[288,128]{1,0:T(8,128)} %get-tuple-element.39), channel_id=1, source_target_pairs={{0,8},{1,9},{2,10},{3,11},{4,12},{5,13},{6,14},{7,15},{8,0},{9,1},... | collective-permute-start | bytes 442376 | tf_op jit(solution)/shard_map/ppermute | solution.py:349
  34.3 0.0 collective-permute-done.15.refs_13_
  34.3 3.2 %collective-permute-start.18 = (f32[288,128]{1,0:T(8,128)}, f32[288,128]{1,0:T(8,128)S(1)}, u32[]{:S(2)}, u32[]{:S(2)}) collective-permute-start(f32[288,128]{1,0:T(8,128)} %get-tuple-element.38), channel_id=1, source_target_pairs={{0,12},{1,13},{2,14},{3,15},{4,8},{5,9},{6,10},{7,11},{8,4},{9,5},... | collective-permute-start | bytes 442376 | tf_op jit(solution)/shard_map/ppermute | solution.py:349
  37.5 0.0 collective-permute-done.7.refs_3_
  37.5 0.0 collective-permute-done.10.refs_7_
  37.5 0.5 collective-permute-start.17
  38.0 0.8 %collective-permute-done.13.refs_11_ = f32[256,128]{1,0:T(8,128)S(1)} collective-permute-done((f32[256,128]{1,0:T(8,128)S(1)}, f32[256,128]{1,0:T(8,128)S(1)}, u32[]{:S(2)}, u32[]{:S(2)}) %collective-permute-start.13) | collective-permute-done | bytes 131104 | tf_op jit(solution)/shard_map/ppermute | solution.py:349
  38.8 0.2 collective-permute-done.17.refs_15_
  39.0 0.9 %copy-done.1 = f32[256,128]{1,0:T(8,128)S(1)} copy-done((f32[256,128]{1,0:T(8,128)S(1)}, f32[256,128]{1,0:T(8,128)}, u32[]{:S(2)}) %copy-start.1) | copy-done | bytes 131096
  39.9 2.9 %store.1.tiles = f32[4096,128]{1,0:T(8,128)S(1)} custom-call(f32[256,128]{1,0:T(8,128)S(1)} %copy-done.1, f32[256,128]{1,0:T(8,128)S(1)} %collective-permute-done.5.refs_1_, f32[256,128]{1,0:T(8,128)S(1)} %collective-permute-done.6.refs_2_, f32[256,128]{1,0:T(8,128)S(1)} %collective-permute-done.7.refs_3_, f32[256,128]{1,0:T(8,128)S(1)} %collective-permute-done.4.refs_4_, ...), custom_call_target="tpu_custom_call" | custom-call | tf_op jit(solution)/shard_map/store/pallas_call | solution.py:234
  42.9 5.5 %trace.4 = (f32[1024,128]{1,0:T(8,128)}, f32[2048,128]{1,0:T(8,128)}) custom-call(s32[1]{0:T(128)} %bitcast.me_ref, f32[4]{0:T(128)S(1)} %copy-done.2, f32[4096,128]{1,0:T(8,128)S(1)} %store.1.tiles, f32[288,128]{1,0:T(8,128)S(1)} %copy-done), custom_call_target="tpu_custom_call" | custom-call | tf_op jit(solution)/shard_map/trace/pallas_call | solution.py:319
  48.4 5.5 %trace.5 = (f32[1024,128]{1,0:T(8,128)}, f32[2048,128]{1,0:T(8,128)}) custom-call(s32[1]{0:T(128)} %bitcast.me_ref, f32[4]{0:T(128)S(1)} %copy-done.2, f32[4096,128]{1,0:T(8,128)S(1)} %store.1.tiles, f32[288,128]{1,0:T(8,128)S(1)} %collective-permute-done.20.got_ref, ...), custom_call_target="tpu_custom_call", output_to_operand_aliasing={{0}: (4, {}), {1}: (5, {})} | custom-call | tf_op jit(solution)/shard_map/trace/pallas_call | solution.py:319
  54.0 5.5 %trace.6 = (f32[1024,128]{1,0:T(8,128)}, f32[2048,128]{1,0:T(8,128)}) custom-call(s32[1]{0:T(128)} %bitcast.me_ref, f32[4]{0:T(128)S(1)} %copy-done.2, f32[4096,128]{1,0:T(8,128)S(1)} %store.1.tiles, f32[288,128]{1,0:T(8,128)S(1)} %collective-permute-done.19.got_ref, ...), custom_call_target="tpu_custom_call", output_to_operand_aliasing={{0}: (4, {}), {1}: (5, {})} | custom-call | tf_op jit(solution)/shard_map/trace/pallas_call | solution.py:319
  59.5 0.0 collective-permute-done.18.got_ref
  59.5 5.5 %trace.7 = (f32[1024,128]{1,0:T(8,128)}, f32[2048,128]{1,0:T(8,128)}) custom-call(s32[1]{0:T(128)} %bitcast.me_ref, f32[4]{0:T(128)S(1)} %copy-done.2, f32[4096,128]{1,0:T(8,128)S(1)} %store.1.tiles, f32[288,128]{1,0:T(8,128)S(1)} %collective-permute-done.18.got_ref, ...), custom_call_target="tpu_custom_call", output_to_operand_aliasing={{0}: (4, {}), {1}: (5, {})} | custom-call | tf_op jit(solution)/shard_map/trace/pallas_call | solution.py:319
  (13 shorter events, 0.0 us)
Async XLA Ops:
  3.0 10.7 %collective-permute-start.3 = (f32[256,128]{1,0:T(8,128)}, f32[256,128]{1,0:T(8,128)S(1)}, u32[]{:S(2)}, u32[]{:S(2)}) collective-permute-start(f32[256,128]{1,0:T(8,128)} %get-tuple-element.35.refs_0_), channel_id=1, source_target_pairs={{0,8},{1,9},{2,10},{3,11},{4,12},{5,13},{6,14},{7,15},{8,0},{9,1},... | collective-permute-start | bytes 393224 | tf_op jit(solution)/shard_map/ppermute | solution.py:349
  7.0 7.4 %collective-permute-start = (f32[288,128]{1,0:T(8,128)}, f32[288,128]{1,0:T(8,128)S(1)}, u32[]{:S(2)}, u32[]{:S(2)}) collective-permute-start(f32[288,128]{1,0:T(8,128)} %get-tuple-element.27), channel_id=1, source_target_pairs={{0,1},{1,0},{2,3},{3,2},{4,5},{5,4},{6,7},{7,6},{8,9},{9,8},{10,11... | collective-permute-start | bytes 442376 | tf_op jit(solution)/shard_map/ppermute | solution.py:349
  7.0 7.4 %collective-permute-start.1 = (f32[288,128]{1,0:T(8,128)}, f32[288,128]{1,0:T(8,128)S(1)}, u32[]{:S(2)}, u32[]{:S(2)}) collective-permute-start(f32[288,128]{1,0:T(8,128)} %get-tuple-element.28), channel_id=1, source_target_pairs={{0,2},{1,3},{2,0},{3,1},{4,6},{5,7},{6,4},{7,5},{8,10},{9,11},{10,... | collective-permute-start | bytes 442376 | tf_op jit(solution)/shard_map/ppermute | solution.py:349
  8.6 7.7 %collective-permute-start.2 = (f32[288,128]{1,0:T(8,128)}, f32[288,128]{1,0:T(8,128)S(1)}, u32[]{:S(2)}, u32[]{:S(2)}) collective-permute-start(f32[288,128]{1,0:T(8,128)} %get-tuple-element.29), channel_id=1, source_target_pairs={{0,3},{1,2},{2,1},{3,0},{4,7},{5,6},{6,5},{7,4},{8,11},{9,10},{10,... | collective-permute-start | bytes 442376 | tf_op jit(solution)/shard_map/ppermute | solution.py:349
  8.9 10.0 %collective-permute-start.4 = (f32[256,128]{1,0:T(8,128)}, f32[256,128]{1,0:T(8,128)S(1)}, u32[]{:S(2)}, u32[]{:S(2)}) collective-permute-start(f32[256,128]{1,0:T(8,128)} %get-tuple-element.35.refs_0_), channel_id=1, source_target_pairs={{0,4},{1,5},{2,6},{3,7},{4,0},{5,1},{6,2},{7,3},{8,12},{9,13},{10,... | collective-permute-start | bytes 393224 | tf_op jit(solution)/shard_map/ppermute | solution.py:349
  13.7 7.6 %collective-permute-start.14 = (f32[256,128]{1,0:T(8,128)S(1)}, f32[256,128]{1,0:T(8,128)S(1)}, u32[]{:S(2)}, u32[]{:S(2)}) collective-permute-start(f32[256,128]{1,0:T(8,128)S(1)} %collective-permute-done.3.refs_8_), channel_id=1, source_target_pairs={{0,4},{1,5},{2,6},{3,7},{4,0},{5,1},{6,2},{7,3},{8,12},{9,13},{10,... | collective-permute-start | bytes 393224 | tf_op jit(solution)/shard_map/ppermute | solution.py:349
  14.4 1.9 %copy-start.3 = (f32[288,128]{1,0:T(8,128)}, f32[288,128]{1,0:T(8,128)S(1)}, u32[]{:S(2)}) copy-start(f32[288,128]{1,0:T(8,128)S(1)} %collective-permute-done.refs_1_) | copy-start | bytes 442372
  14.4 1.9 %copy-start.4 = (f32[288,128]{1,0:T(8,128)}, f32[288,128]{1,0:T(8,128)S(1)}, u32[]{:S(2)}) copy-start(f32[288,128]{1,0:T(8,128)S(1)} %collective-permute-done.1.refs_2_) | copy-start | bytes 442372
  16.3 0.7 %copy-start.5 = (f32[288,128]{1,0:T(8,128)}, f32[288,128]{1,0:T(8,128)S(1)}, u32[]{:S(2)}) copy-start(f32[288,128]{1,0:T(8,128)S(1)} %collective-permute-done.2.refs_3_) | copy-start | bytes 442372
  18.9 23.9 %copy-start.2 = (f32[4]{0:T(128)S(1)}, f32[4]{0:T(128)}, u32[]{:S(2)}) copy-start(f32[4]{0:T(128)} %lens_ref.7) | copy-start | bytes 52
  18.9 24.0 %copy-start = (f32[288,128]{1,0:T(8,128)S(1)}, f32[288,128]{1,0:T(8,128)}, u32[]{:S(2)}) copy-start(f32[288,128]{1,0:T(8,128)} %get-tuple-element.41.got_ref) | copy-start | bytes 442372
  18.9 6.6 %collective-permute-start.6 = (f32[256,128]{1,0:T(8,128)}, f32[256,128]{1,0:T(8,128)S(1)}, u32[]{:S(2)}, u32[]{:S(2)}) collective-permute-start(f32[256,128]{1,0:T(8,128)} %get-tuple-element.35.refs_0_), channel_id=1, source_target_pairs={{0,2},{1,3},{2,0},{3,1},{4,6},{5,7},{6,4},{7,5},{8,10},{9,11},{10,... | collective-permute-start | bytes 393224 | tf_op jit(solution)/shard_map/ppermute | solution.py:349
  20.5 5.0 %collective-permute-start.5 = (f32[256,128]{1,0:T(8,128)}, f32[256,128]{1,0:T(8,128)S(1)}, u32[]{:S(2)}, u32[]{:S(2)}) collective-permute-start(f32[256,128]{1,0:T(8,128)} %get-tuple-element.35.refs_0_), channel_id=1, source_target_pairs={{0,1},{1,0},{2,3},{3,2},{4,5},{5,4},{6,7},{7,6},{8,9},{9,8},{10,11... | collective-permute-start | bytes 393224 | tf_op jit(solution)/shard_map/ppermute | solution.py:349
  20.5 7.8 %collective-permute-start.9 = (f32[256,128]{1,0:T(8,128)S(1)}, f32[256,128]{1,0:T(8,128)S(1)}, u32[]{:S(2)}, u32[]{:S(2)}) collective-permute-start(f32[256,128]{1,0:T(8,128)S(1)} %collective-permute-done.4.refs_4_), channel_id=1, source_target_pairs={{0,2},{1,3},{2,0},{3,1},{4,6},{5,7},{6,4},{7,5},{8,10},{9,11},{10,... | collective-permute-start | bytes 393224 | tf_op jit(solution)/shard_map/ppermute | solution.py:349
  21.0 7.3 %collective-permute-start.8 = (f32[256,128]{1,0:T(8,128)S(1)}, f32[256,128]{1,0:T(8,128)S(1)}, u32[]{:S(2)}, u32[]{:S(2)}) collective-permute-start(f32[256,128]{1,0:T(8,128)S(1)} %collective-permute-done.4.refs_4_), channel_id=1, source_target_pairs={{0,1},{1,0},{2,3},{3,2},{4,5},{5,4},{6,7},{7,6},{8,9},{9,8},{10,11... | collective-permute-start | bytes 393224 | tf_op jit(solution)/shard_map/ppermute | solution.py:349
  21.2 9.9 %collective-permute-start.12 = (f32[256,128]{1,0:T(8,128)S(1)}, f32[256,128]{1,0:T(8,128)S(1)}, u32[]{:S(2)}, u32[]{:S(2)}) collective-permute-start(f32[256,128]{1,0:T(8,128)S(1)} %collective-permute-done.3.refs_8_), channel_id=1, source_target_pairs={{0,2},{1,3},{2,0},{3,1},{4,6},{5,7},{6,4},{7,5},{8,10},{9,11},{10,... | collective-permute-start | bytes 393224 | tf_op jit(solution)/shard_map/ppermute | solution.py:349
  25.5 5.6 %collective-permute-start.11 = (f32[256,128]{1,0:T(8,128)S(1)}, f32[256,128]{1,0:T(8,128)S(1)}, u32[]{:S(2)}, u32[]{:S(2)}) collective-permute-start(f32[256,128]{1,0:T(8,128)S(1)} %collective-permute-done.3.refs_8_), channel_id=1, source_target_pairs={{0,1},{1,0},{2,3},{3,2},{4,5},{5,4},{6,7},{7,6},{8,9},{9,8},{10,11... | collective-permute-start | bytes 393224 | tf_op jit(solution)/shard_map/ppermute | solution.py:349
  25.5 7.8 %collective-permute-start.16 = (f32[256,128]{1,0:T(8,128)S(1)}, f32[256,128]{1,0:T(8,128)S(1)}, u32[]{:S(2)}, u32[]{:S(2)}) collective-permute-start(f32[256,128]{1,0:T(8,128)S(1)} %collective-permute-done.14.refs_12_), channel_id=1, source_target_pairs={{0,2},{1,3},{2,0},{3,1},{4,6},{5,7},{6,4},{7,5},{8,10},{9,11},{10,... | collective-permute-start | bytes 393224 | tf_op jit(solution)/shard_map/ppermute | solution.py:349
  28.3 6.0 %collective-permute-start.15 = (f32[256,128]{1,0:T(8,128)S(1)}, f32[256,128]{1,0:T(8,128)S(1)}, u32[]{:S(2)}, u32[]{:S(2)}) collective-permute-start(f32[256,128]{1,0:T(8,128)S(1)} %collective-permute-done.14.refs_12_), channel_id=1, source_target_pairs={{0,1},{1,0},{2,3},{3,2},{4,5},{5,4},{6,7},{7,6},{8,9},{9,8},{10,11... | collective-permute-start | bytes 393224 | tf_op jit(solution)/shard_map/ppermute | solution.py:349
  28.3 9.1 %collective-permute-start.7 = (f32[256,128]{1,0:T(8,128)S(1)}, f32[256,128]{1,0:T(8,128)S(1)}, u32[]{:S(2)}, u32[]{:S(2)}) collective-permute-start(f32[256,128]{1,0:T(8,128)S(1)} %collective-permute-done.6.refs_2_), channel_id=1, source_target_pairs={{0,1},{1,0},{2,3},{3,2},{4,5},{5,4},{6,7},{7,6},{8,9},{9,8},{10,11... | collective-permute-start | bytes 393224 | tf_op jit(solution)/shard_map/ppermute | solution.py:349
  31.1 6.3 %collective-permute-start.10 = (f32[256,128]{1,0:T(8,128)S(1)}, f32[256,128]{1,0:T(8,128)S(1)}, u32[]{:S(2)}, u32[]{:S(2)}) collective-permute-start(f32[256,128]{1,0:T(8,128)S(1)} %collective-permute-done.9.refs_6_), channel_id=1, source_target_pairs={{0,1},{1,0},{2,3},{3,2},{4,5},{5,4},{6,7},{7,6},{8,9},{9,8},{10,11... | collective-permute-start | bytes 393224 | tf_op jit(solution)/shard_map/ppermute | solution.py:349
  31.1 17.3 %collective-permute-start.20 = (f32[288,128]{1,0:T(8,128)}, f32[288,128]{1,0:T(8,128)S(1)}, u32[]{:S(2)}, u32[]{:S(2)}) collective-permute-start(f32[288,128]{1,0:T(8,128)} %get-tuple-element.40), channel_id=1, source_target_pairs={{0,4},{1,5},{2,6},{3,7},{4,0},{5,1},{6,2},{7,3},{8,12},{9,13},{10,... | collective-permute-start | bytes 442376 | tf_op jit(solution)/shard_map/ppermute | solution.py:349
  33.3 20.6 %collective-permute-start.19 = (f32[288,128]{1,0:T(8,128)}, f32[288,128]{1,0:T(8,128)S(1)}, u32[]{:S(2)}, u32[]{:S(2)}) collective-permute-start(f32[288,128]{1,0:T(8,128)} %get-tuple-element.39), channel_id=1, source_target_pairs={{0,8},{1,9},{2,10},{3,11},{4,12},{5,13},{6,14},{7,15},{8,0},{9,1},... | collective-permute-start | bytes 442376 | tf_op jit(solution)/shard_map/ppermute | solution.py:349
  34.3 25.2 %collective-permute-start.18 = (f32[288,128]{1,0:T(8,128)}, f32[288,128]{1,0:T(8,128)S(1)}, u32[]{:S(2)}, u32[]{:S(2)}) collective-permute-start(f32[288,128]{1,0:T(8,128)} %get-tuple-element.38), channel_id=1, source_target_pairs={{0,12},{1,13},{2,14},{3,15},{4,8},{5,9},{6,10},{7,11},{8,4},{9,5},... | collective-permute-start | bytes 442376 | tf_op jit(solution)/shard_map/ppermute | solution.py:349
  37.5 1.3 %collective-permute-start.13 = (f32[256,128]{1,0:T(8,128)S(1)}, f32[256,128]{1,0:T(8,128)S(1)}, u32[]{:S(2)}, u32[]{:S(2)}) collective-permute-start(f32[256,128]{1,0:T(8,128)S(1)} %collective-permute-done.12.refs_10_), channel_id=1, source_target_pairs={{0,1},{1,0},{2,3},{3,2},{4,5},{5,4},{6,7},{7,6},{8,9},{9,8},{10,11... | collective-permute-start | bytes 393224 | tf_op jit(solution)/shard_map/ppermute | solution.py:349
  37.5 1.5 %collective-permute-start.17 = (f32[256,128]{1,0:T(8,128)S(1)}, f32[256,128]{1,0:T(8,128)S(1)}, u32[]{:S(2)}, u32[]{:S(2)}) collective-permute-start(f32[256,128]{1,0:T(8,128)S(1)} %collective-permute-done.16.refs_14_), channel_id=1, source_target_pairs={{0,1},{1,0},{2,3},{3,2},{4,5},{5,4},{6,7},{7,6},{8,9},{9,8},{10,11... | collective-permute-start | bytes 393224 | tf_op jit(solution)/shard_map/ppermute | solution.py:349
  39.0 0.9 %copy-start.1 = (f32[256,128]{1,0:T(8,128)S(1)}, f32[256,128]{1,0:T(8,128)}, u32[]{:S(2)}) copy-start(f32[256,128]{1,0:T(8,128)} %get-tuple-element.35.refs_0_) | copy-start | bytes 393220

commit v9 on v7

--- a/solution.py
+++ b/solution.py
@@ -96,6 +96,7 @@
     ids = ids_ref[...]
     plane = lax.broadcasted_iota(jnp.int32, ids.shape, 0)
     owner = (ids // per_owner) ^ dest_ref[...]
+    owner = (owner % (n_sky // 2)) * 2 + owner // (n_sky // 2)
     spot = (owner * planes + plane) * per_owner + ids % per_owner
     pad = jnp.zeros((SUB - planes, bundles), jnp.float32)
     fine = jnp.concatenate([(spot & 15).astype(jnp.float32), pad], axis=0)
@@ -218,33 +219,32 @@
 
 def trace_kernel(n_sky, each, planes, together, me_ref, lens_ref, *refs):
     far = n_sky // NEAR
+    pairs = n_sky // 2
     size = 4 * each + SUB
-    tile_refs, got_refs = refs[:n_sky], refs[n_sky:n_sky + far]
-    shift_ref, matrix_ref, tiles, chosen, rays, places, sems = refs[n_sky + far:]
+    tile_refs, got_refs = refs[:pairs], refs[pairs:pairs + far]
+    shift_ref, matrix_ref, tiles, chosen, rays, places, sems = refs[pairs + far:]
     me = me_ref[0]
     slots = n_sky * each
     rows = tile_refs[0].shape[0]
-    copies = []
+    copies = [
+        pltpu.make_async_copy(tile_ref, tiles.at[pl.ds(k * rows, rows), :], sems.at[0, k])
+        for k, tile_ref in enumerate(tile_refs)
+    ]
     for s in range(n_sky):
         source = me ^ s
         got_ref, first = got_refs[s // NEAR], s % NEAR * size
-        copies.append((
-            pltpu.make_async_copy(
-                got_ref.at[pl.ds(first + 4 * each, SUB), :],
-                places.at[pl.ds(source * SUB, SUB), :],
-                sems.at[0, s]),
-            pltpu.make_async_copy(tile_refs[s], tiles.at[pl.ds(s * rows, rows), :], sems.at[1, s]),
-            pltpu.make_async_copy(
-                got_ref.at[pl.ds(first, 4 * each), :],
-                rays.at[pl.ds(source * 4 * each, 4 * each), :],
-                sems.at[2, s]),
-        ))
-    for kind in range(3):
-        for s in range(n_sky):
-            copies[s][kind].start()
-    for kind in range(3):
-        for s in range(n_sky):
-            copies[s][kind].wait()
+        copies.append(pltpu.make_async_copy(
+            got_ref.at[pl.ds(first + 4 * each, SUB), :],
+            places.at[pl.ds(source * SUB, SUB), :],
+            sems.at[1, s]))
+        copies.append(pltpu.make_async_copy(
+            got_ref.at[pl.ds(first, 4 * each), :],
+            rays.at[pl.ds(source * 4 * each, 4 * each), :],
+            sems.at[2, s]))
+    for copy in copies:
+        copy.start()
+    for copy in copies:
+        copy.wait()
 
     def body(step, carry):
         chains = []
@@ -287,7 +287,7 @@
 
 
 def trace(each, planes, me, lens_weight, tiles, got):
-    n_sky = len(tiles)
+    n_sky = 2 * len(tiles)
     slots = n_sky * each
     rows = tiles[0].shape[0]
     together = 4
@@ -297,13 +297,13 @@
             jax.ShapeDtypeStruct((slots * 4, LANES), jnp.float32),
             jax.ShapeDtypeStruct((slots * 8, LANES), jnp.float32),
         ),
-        in_specs=[pl.BlockSpec(memory_space=pltpu.SMEM)] * 2 + [pl.BlockSpec(memory_space=pl.ANY)] * (n_sky + len(got)),
+        in_specs=[pl.BlockSpec(memory_space=pltpu.SMEM)] * 2 + [pl.BlockSpec(memory_space=pl.ANY)] * (len(tiles) + len(got)),
         out_specs=(
             pl.BlockSpec(memory_space=pltpu.VMEM),
             pl.BlockSpec(memory_space=pltpu.VMEM),
         ),
         scratch_shapes=[
-            pltpu.VMEM((n_sky * rows, LANES), jnp.float32),
+            pltpu.VMEM((len(tiles) * rows, LANES), jnp.float32),
             pltpu.VMEM((planes * together * CHUNKS * SUB, LANES), jnp.float32),
             pltpu.VMEM((slots * 4, LANES), jnp.float32),
             pltpu.SMEM((n_sky * SUB, LANES), jnp.float32),
@@ -316,13 +316,6 @@
 
 def flipped(value, n_sky, bits):
     return lax.ppermute(value, "sky", [(i, i ^ bits) for i in range(n_sky)])
-
-
-def spread(held, n_sky, bits):
-    for bit in bits:
-        for s in [s for s in held if s & (2 * bit - 1) == 0]:
-            if s ^ bit not in held:
-                held[s ^ bit] = flipped(held[s], n_sky, bit)
 
 
 def shards(potential, lens_weight, ray_start, patch_index, destination):
@@ -337,23 +330,26 @@
     flat = ray_start.reshape(bundles, 2, halves, LANES).transpose(0, 2, 1, 3).reshape(bundles * 2 * halves, LANES)
     own, sent = prepare(n_sky, each, me, destination.reshape(1, bundles), patch_index, flat, potential)
     sent = [sent[0]] + [flipped(sent[s], n_sky, s) for s in range(1, NEAR)]
-    held = {0: own}
-    for bit in bits[:2]:
-        held[bit] = flipped(own, n_sky, bit)
-    held[bits[0] ^ bits[1]] = flipped(held[bits[0]], n_sky, bits[1])
-    got = turn(4 * each + SUB, sent)
-    early = [0, bits[0], bits[1]]
-    *got, a, b, c = lax.optimization_barrier((*got, *[held[s] for s in early]))
-    held.update(zip(early, (a, b, c)))
+    across = flipped(own, n_sky, bits[0])
+    across, *sent = lax.optimization_barrier((across, *sent))
+    pair = jnp.concatenate([own, across], axis=0)
+    got = list(turn(4 * each + SUB, sent))
+    held = {0: pair, bits[1]: flipped(pair, n_sky, bits[1])}
+    got[0], held[bits[1]] = lax.optimization_barrier((got[0], held[bits[1]]))
+    for bit in bits[2:-1]:
+        for s in list(held):
+            held[s ^ bit] = flipped(held[s], n_sky, bit)
     got = [got[0]] + [flipped(got[f], n_sky, f * NEAR) for f in range(1, len(got))]
-    spread(held, n_sky, bits[:-1])
     half = len(got) // 2
-    for mid, low in ((half, 0), (half + 1, n_sky // 2)):
-        some = range(low, low + n_sky // 2, 2)
-        got[mid], *evens = lax.optimization_barrier((got[mid], *[held[s] for s in some]))
-        held.update(zip(some, evens))
-    spread(held, n_sky, bits)
-    shift, matrix = trace(each, planes, me, lens_weight, [held[s] for s in range(n_sky)], got)
+    keys = sorted(held)
+    for mids, some in ((list(range(1, half + 1)), keys[:len(keys) // 2]), (list(range(half + 1, len(got))), keys[len(keys) // 2:])):
+        tied = lax.optimization_barrier([got[mid] for mid in mids] + [held[s] for s in some])
+        for mid in mids:
+            got[mid] = tied.pop(0)
+        held.update(zip(some, tied))
+    for s in keys:
+        held[s ^ 1] = flipped(held[s], n_sky, 1)
+    shift, matrix = trace(each, planes, me, lens_weight, [held[s] for s in range(n_sky // 2)], got)
     shift = shift.reshape(slots, halves, 2, LANES).transpose(0, 2, 1, 3).reshape(slots, 2, rays)
     matrix = matrix.reshape(slots, halves, 4, LANES).transpose(0, 2, 1, 3).reshape(slots, 4, rays)
     return shift, matrix

time: 58.9 us -> 61.7 us (1.048)
  waiting for transfers between devices: 14.5 us -> 22 us
  starting transfers between devices: 18.3 us -> 15.4 us
  Pallas kernels: 23.7 us -> 21.6 us
    ppermute x21 -> x14, waiting for transfers between devices: 14.5 us -> 22 us  [flipped(): return lax.ppermute(value, 'sky', [(i, i ^ bits) for i in range(n_sky)])]
    ppermute x21 -> x14, starting transfers between devices: 18.3 us -> 15.4 us  [flipped(): return lax.ppermute(value, 'sky', [(i, i ^ bits) for i in range(n_sky)])]
    pallas_call x1, Pallas kernels: 19.4 us -> 17.2 us  [trace(): pl.pallas_call(functools.partial(trace_kernel, n_sky, each, planes, toget...]
    unnamed x12 -> x11, local copies, waits for them, and re-layouts: 1.58 us -> 1.87 us
  transfers between devices with their start and end apart: 21 -> 14, of which waited for: 10 -> 8; matrix products, arithmetic and copies ran while one was open for 0% -> 2% of each run, Pallas kernels for 3% -> 3%
where the time goes in v9:
time: 61.7 us; the launch traced here: 61.5 us
  waiting for transfers between devices  22 us (36%)
  Pallas kernels  21.6 us (35%)
  starting transfers between devices  15.4 us (25%)
  local copies, waits for them, and re-layouts  1.88 us (3%)
  between operations  0.69 us (1%)
    ppermute x14, waiting for transfers between devices, flipped(): return lax.ppermute(value, 'sky', [(i, i ^ bits) for i in range(n_sky)])  22 us
    pallas_call x1, Pallas kernels, trace(): pl.pallas_call(functools.partial(trace_kernel, n_sky, each, planes, toget...  17.2 us
    ppermute x14, starting transfers between devices, flipped(): return lax.ppermute(value, 'sky', [(i, i ^ bits) for i in range(n_sky)])  15.4 us
    pallas_call x1, Pallas kernels, prepare(): pl.pallas_call(functools.partial(prepare_kernel, n_sky, each), out_shape=...  2.37 us
    pallas_call x1, Pallas kernels, turn(): pl.pallas_call(functools.partial(turn_kernel, size), out_shape=[block] *...  1.96 us
    unnamed x11, local copies, waits for them, and re-layouts  1.87 us
  transfers between devices with their start and end apart: 14, of which 8 were waited for; matrix products, arithmetic and copies ran while one was open for 2% of the time, Pallas kernels for 3%

profile of v9, /device:TPU:0, one launch (start us, length us, event | category | flops | bytes accessed | tf_op | source)
XLA Modules:
  0.0 61.5 jit_solution(3113561953886041335)
XLA Ops:
  0.6 2.4 %prepare.1 = (f32[256,128]{1,0:T(8,128)}, f32[288,128]{1,0:T(8,128)}, f32[288,128]{1,0:T(8,128)}, f32[288,128]{1,0:T(8,128)}, f32[288,128]{1,0:T(8,128)}) custom-call(s32[1]{0:T(128)} %bitcast.me_ref, s32[1,128]{1,0:T(1,128)} %bitcast.18, s32[4,128]{1,0:T(4,128)} %ids_ref.1, f32[512,128]{1,0:T(8,128)} %bitcast.17, f32[4,8,1024]{2,1,0:T(8,128)} %src_ref.1), custom_call_target="tpu_custom_call" | custom-call | tf_op jit(solution)/shard_map/prepare/pallas_call | solution.py:127
  3.0 0.5 collective-permute-start.1
  3.5 2.5 %collective-permute-start.2 = (f32[288,128]{1,0:T(8,128)}, f32[288,128]{1,0:T(8,128)S(1)}, u32[]{:S(2)}, u32[]{:S(2)}) collective-permute-start(f32[288,128]{1,0:T(8,128)} %get-tuple-element.30), channel_id=1, source_target_pairs={{0,2},{1,3},{2,0},{3,1},{4,6},{5,7},{6,4},{7,5},{8,10},{9,11},{10,... | collective-permute-start | bytes 442376 | tf_op jit(solution)/shard_map/ppermute | solution.py:318
  6.0 0.1 collective-permute-start.3
  6.1 2.8 %collective-permute-start = (f32[256,128]{1,0:T(8,128)}, f32[256,128]{1,0:T(8,128)S(1)}, u32[]{:S(2)}, u32[]{:S(2)}) collective-permute-start(f32[256,128]{1,0:T(8,128)} %get-tuple-element.27), channel_id=1, source_target_pairs={{0,8},{1,9},{2,10},{3,11},{4,12},{5,13},{6,14},{7,15},{8,0},{9,1},... | collective-permute-start | bytes 393224 | tf_op jit(solution)/shard_map/ppermute | solution.py:318
  8.9 0.9 %constant_dynamic-update-slice_fusion.1 = f32[512,128]{1,0:T(8,128)S(1)} fusion(f32[256,128]{1,0:T(8,128)} %get-tuple-element.27), kind=kLoop, calls=%fused_computation.1 | loop fusion | bytes 262144
  9.9 6.0 %collective-permute-done = f32[256,128]{1,0:T(8,128)S(1)} collective-permute-done((f32[256,128]{1,0:T(8,128)}, f32[256,128]{1,0:T(8,128)S(1)}, u32[]{:S(2)}, u32[]{:S(2)}) %collective-permute-start) | collective-permute-done | bytes 131104 | tf_op jit(solution)/shard_map/ppermute | solution.py:318
  15.9 0.0 collective-permute-done.1.refs_1_
  15.9 0.0 copy-start.2
  15.9 0.0 collective-permute-done.2.refs_2_
  15.9 0.0 copy-start.3
  15.9 0.0 collective-permute-done.3.refs_3_
  15.9 0.0 copy-start.4
  15.9 0.9 %collective-permute-start.10 = (f32[512,128]{1,0:T(8,128)S(1)}, f32[512,128]{1,0:T(8,128)S(1)}, u32[]{:S(2)}, u32[]{:S(2)}) collective-permute-start(f32[512,128]{1,0:T(8,128)S(1)} %constant_dynamic-update-slice_fusion.refs_0_), channel_id=1, source_target_pairs={{0,4},{1,5},{2,6},{3,7},{4,0},{5,1},{6,2},{7,3},{8,12},{9,13},{10,... | collective-permute-start | bytes 786440 | tf_op jit(solution)/shard_map/ppermute | solution.py:318
  16.8 1.5 %collective-permute-start.6 = (f32[512,128]{1,0:T(8,128)S(1)}, f32[512,128]{1,0:T(8,128)S(1)}, u32[]{:S(2)}, u32[]{:S(2)}) collective-permute-start(f32[512,128]{1,0:T(8,128)S(1)} %constant_dynamic-update-slice_fusion.refs_0_), channel_id=1, source_target_pairs={{0,2},{1,3},{2,0},{3,1},{4,6},{5,7},{6,4},{7,5},{8,10},{9,11},{10,... | collective-permute-start | bytes 786440 | tf_op jit(solution)/shard_map/ppermute | solution.py:318
  18.3 0.0 copy-done.2
  18.3 0.0 copy-done.3
  18.3 0.0 copy-done.4
  18.3 2.0 %turn.1 = (f32[288,128]{1,0:T(8,128)}, f32[288,128]{1,0:T(8,128)}, f32[288,128]{1,0:T(8,128)}, f32[288,128]{1,0:T(8,128)}) custom-call(f32[288,128]{1,0:T(8,128)} %get-tuple-element.32.refs_0_, f32[288,128]{1,0:T(8,128)} %copy-done.2, f32[288,128]{1,0:T(8,128)} %copy-done.3, f32[288,128]{1,0:T(8,128)} %copy-done.4), custom_call_target="tpu_custom_call" | custom-call | tf_op jit(solution)/shard_map/turn/pallas_call | solution.py:147
  20.3 3.5 %collective-permute-done.10.refs_4_ = f32[512,128]{1,0:T(8,128)S(1)} collective-permute-done((f32[512,128]{1,0:T(8,128)S(1)}, f32[512,128]{1,0:T(8,128)S(1)}, u32[]{:S(2)}, u32[]{:S(2)}) %collective-permute-start.10) | collective-permute-done | bytes 262176 | tf_op jit(solution)/shard_map/ppermute | solution.py:318
  23.8 1.4 %collective-permute-start.11 = (f32[512,128]{1,0:T(8,128)S(1)}, f32[512,128]{1,0:T(8,128)S(1)}, u32[]{:S(2)}, u32[]{:S(2)}) collective-permute-start(f32[512,128]{1,0:T(8,128)S(1)} %collective-permute-done.10.refs_4_), channel_id=1, source_target_pairs={{0,2},{1,3},{2,0},{3,1},{4,6},{5,7},{6,4},{7,5},{8,10},{9,11},{10,... | collective-permute-start | bytes 786440 | tf_op jit(solution)/shard_map/ppermute | solution.py:318
  25.2 1.4 %collective-permute-start.4 = (f32[288,128]{1,0:T(8,128)}, f32[288,128]{1,0:T(8,128)S(1)}, u32[]{:S(2)}, u32[]{:S(2)}) collective-permute-start(f32[288,128]{1,0:T(8,128)} %get-tuple-element.36), channel_id=1, source_target_pairs={{0,4},{1,5},{2,6},{3,7},{4,0},{5,1},{6,2},{7,3},{8,12},{9,13},{10,... | collective-permute-start | bytes 442376 | tf_op jit(solution)/shard_map/ppermute | solution.py:318
  26.6 0.0 copy-start.1
  26.6 3.3 %collective-permute-start.5 = (f32[288,128]{1,0:T(8,128)}, f32[288,128]{1,0:T(8,128)S(1)}, u32[]{:S(2)}, u32[]{:S(2)}) collective-permute-start(f32[288,128]{1,0:T(8,128)} %get-tuple-element.37), channel_id=1, source_target_pairs={{0,8},{1,9},{2,10},{3,11},{4,12},{5,13},{6,14},{7,15},{8,0},{9,1},... | collective-permute-start | bytes 442376 | tf_op jit(solution)/shard_map/ppermute | solution.py:318
  29.9 0.0 collective-permute-start.9
  29.9 2.4 %collective-permute-done.4.refs_9_ = f32[288,128]{1,0:T(8,128)S(1)} collective-permute-done((f32[288,128]{1,0:T(8,128)}, f32[288,128]{1,0:T(8,128)S(1)}, u32[]{:S(2)}, u32[]{:S(2)}) %collective-permute-start.4) | collective-permute-done | bytes 147488 | tf_op jit(solution)/shard_map/ppermute | solution.py:318
  32.3 8.4 %collective-permute-done.5.refs_10_ = f32[288,128]{1,0:T(8,128)S(1)} collective-permute-done((f32[288,128]{1,0:T(8,128)}, f32[288,128]{1,0:T(8,128)S(1)}, u32[]{:S(2)}, u32[]{:S(2)}) %collective-permute-start.5) | collective-permute-done | bytes 147488 | tf_op jit(solution)/shard_map/ppermute | solution.py:318
  40.7 0.0 collective-permute-done.6.refs_2_
  40.7 0.0 collective-permute-start.7
  40.7 0.5 collective-permute-start.8
  41.2 0.0 collective-permute-done.9.refs_11_
  41.2 0.0 collective-permute-done.11.refs_6_
  41.2 0.1 collective-permute-start.12
  41.3 0.4 collective-permute-start.13
  41.7 0.5 collective-permute-done.7.refs_1_
  42.2 0.4 collective-permute-done.8.refs_3_
  42.6 0.4 collective-permute-done.12.refs_5_
  43.0 0.4 collective-permute-done.13.refs_7_
  43.4 0.0 copy-done.1
  43.4 0.0 copy-start
  43.4 0.9 %copy-done = f32[288,128]{1,0:T(8,128)S(1)} copy-done((f32[288,128]{1,0:T(8,128)S(1)}, f32[288,128]{1,0:T(8,128)}, u32[]{:S(2)}) %copy-start) | copy-done | bytes 147480
  44.3 17.2 %trace.1 = (f32[1024,128]{1,0:T(8,128)}, f32[2048,128]{1,0:T(8,128)}) custom-call(s32[1]{0:T(128)} %bitcast.me_ref, f32[4]{0:T(128)S(1)} %copy-done.1, f32[512,128]{1,0:T(8,128)S(1)} %constant_dynamic-update-slice_fusion.refs_0_, f32[512,128]{1,0:T(8,128)S(1)} %collective-permute-done.7.refs_1_, f32[512,128]{1,0:T(8,128)S(1)} %collective-permute-done.6.refs_2_, ...), custom_call_target="tpu_custom_call" | custom-call | tf_op jit(solution)/shard_map/trace/pallas_call | solution.py:294
  (1 shorter events, 0.0 us)
Async XLA Ops:
  3.0 12.9 %collective-permute-start.1 = (f32[288,128]{1,0:T(8,128)}, f32[288,128]{1,0:T(8,128)S(1)}, u32[]{:S(2)}, u32[]{:S(2)}) collective-permute-start(f32[288,128]{1,0:T(8,128)} %get-tuple-element.29), channel_id=1, source_target_pairs={{0,1},{1,0},{2,3},{3,2},{4,5},{5,4},{6,7},{7,6},{8,9},{9,8},{10,11... | collective-permute-start | bytes 442376 | tf_op jit(solution)/shard_map/ppermute | solution.py:318
  3.5 12.4 %collective-permute-start.2 = (f32[288,128]{1,0:T(8,128)}, f32[288,128]{1,0:T(8,128)S(1)}, u32[]{:S(2)}, u32[]{:S(2)}) collective-permute-start(f32[288,128]{1,0:T(8,128)} %get-tuple-element.30), channel_id=1, source_target_pairs={{0,2},{1,3},{2,0},{3,1},{4,6},{5,7},{6,4},{7,5},{8,10},{9,11},{10,... | collective-permute-start | bytes 442376 | tf_op jit(solution)/shard_map/ppermute | solution.py:318
  6.0 9.9 %collective-permute-start.3 = (f32[288,128]{1,0:T(8,128)}, f32[288,128]{1,0:T(8,128)S(1)}, u32[]{:S(2)}, u32[]{:S(2)}) collective-permute-start(f32[288,128]{1,0:T(8,128)} %get-tuple-element.31), channel_id=1, source_target_pairs={{0,3},{1,2},{2,1},{3,0},{4,7},{5,6},{6,5},{7,4},{8,11},{9,10},{10,... | collective-permute-start | bytes 442376 | tf_op jit(solution)/shard_map/ppermute | solution.py:318
  6.1 9.7 %collective-permute-start = (f32[256,128]{1,0:T(8,128)}, f32[256,128]{1,0:T(8,128)S(1)}, u32[]{:S(2)}, u32[]{:S(2)}) collective-permute-start(f32[256,128]{1,0:T(8,128)} %get-tuple-element.27), channel_id=1, source_target_pairs={{0,8},{1,9},{2,10},{3,11},{4,12},{5,13},{6,14},{7,15},{8,0},{9,1},... | collective-permute-start | bytes 393224 | tf_op jit(solution)/shard_map/ppermute | solution.py:318
  15.9 2.5 %copy-start.2 = (f32[288,128]{1,0:T(8,128)}, f32[288,128]{1,0:T(8,128)S(1)}, u32[]{:S(2)}) copy-start(f32[288,128]{1,0:T(8,128)S(1)} %collective-permute-done.1.refs_1_) | copy-start | bytes 442372
  15.9 2.5 %copy-start.3 = (f32[288,128]{1,0:T(8,128)}, f32[288,128]{1,0:T(8,128)S(1)}, u32[]{:S(2)}) copy-start(f32[288,128]{1,0:T(8,128)S(1)} %collective-permute-done.2.refs_2_) | copy-start | bytes 442372
  15.9 2.4 %copy-start.4 = (f32[288,128]{1,0:T(8,128)}, f32[288,128]{1,0:T(8,128)S(1)}, u32[]{:S(2)}) copy-start(f32[288,128]{1,0:T(8,128)S(1)} %collective-permute-done.3.refs_3_) | copy-start | bytes 442372
  15.9 7.9 %collective-permute-start.10 = (f32[512,128]{1,0:T(8,128)S(1)}, f32[512,128]{1,0:T(8,128)S(1)}, u32[]{:S(2)}, u32[]{:S(2)}) collective-permute-start(f32[512,128]{1,0:T(8,128)S(1)} %constant_dynamic-update-slice_fusion.refs_0_), channel_id=1, source_target_pairs={{0,4},{1,5},{2,6},{3,7},{4,0},{5,1},{6,2},{7,3},{8,12},{9,13},{10,... | collective-permute-start | bytes 786440 | tf_op jit(solution)/shard_map/ppermute | solution.py:318
  16.8 23.9 %collective-permute-start.6 = (f32[512,128]{1,0:T(8,128)S(1)}, f32[512,128]{1,0:T(8,128)S(1)}, u32[]{:S(2)}, u32[]{:S(2)}) collective-permute-start(f32[512,128]{1,0:T(8,128)S(1)} %constant_dynamic-update-slice_fusion.refs_0_), channel_id=1, source_target_pairs={{0,2},{1,3},{2,0},{3,1},{4,6},{5,7},{6,4},{7,5},{8,10},{9,11},{10,... | collective-permute-start | bytes 786440 | tf_op jit(solution)/shard_map/ppermute | solution.py:318
  23.8 17.4 %collective-permute-start.11 = (f32[512,128]{1,0:T(8,128)S(1)}, f32[512,128]{1,0:T(8,128)S(1)}, u32[]{:S(2)}, u32[]{:S(2)}) collective-permute-start(f32[512,128]{1,0:T(8,128)S(1)} %collective-permute-done.10.refs_4_), channel_id=1, source_target_pairs={{0,2},{1,3},{2,0},{3,1},{4,6},{5,7},{6,4},{7,5},{8,10},{9,11},{10,... | collective-permute-start | bytes 786440 | tf_op jit(solution)/shard_map/ppermute | solution.py:318
  25.2 7.1 %collective-permute-start.4 = (f32[288,128]{1,0:T(8,128)}, f32[288,128]{1,0:T(8,128)S(1)}, u32[]{:S(2)}, u32[]{:S(2)}) collective-permute-start(f32[288,128]{1,0:T(8,128)} %get-tuple-element.36), channel_id=1, source_target_pairs={{0,4},{1,5},{2,6},{3,7},{4,0},{5,1},{6,2},{7,3},{8,12},{9,13},{10,... | collective-permute-start | bytes 442376 | tf_op jit(solution)/shard_map/ppermute | solution.py:318
  26.6 16.8 %copy-start.1 = (f32[4]{0:T(128)S(1)}, f32[4]{0:T(128)}, u32[]{:S(2)}) copy-start(f32[4]{0:T(128)} %lens_ref.1) | copy-start | bytes 52
  26.6 14.1 %collective-permute-start.5 = (f32[288,128]{1,0:T(8,128)}, f32[288,128]{1,0:T(8,128)S(1)}, u32[]{:S(2)}, u32[]{:S(2)}) collective-permute-start(f32[288,128]{1,0:T(8,128)} %get-tuple-element.37), channel_id=1, source_target_pairs={{0,8},{1,9},{2,10},{3,11},{4,12},{5,13},{6,14},{7,15},{8,0},{9,1},... | collective-permute-start | bytes 442376 | tf_op jit(solution)/shard_map/ppermute | solution.py:318
  29.9 11.3 %collective-permute-start.9 = (f32[288,128]{1,0:T(8,128)}, f32[288,128]{1,0:T(8,128)S(1)}, u32[]{:S(2)}, u32[]{:S(2)}) collective-permute-start(f32[288,128]{1,0:T(8,128)} %get-tuple-element.41), channel_id=1, source_target_pairs={{0,12},{1,13},{2,14},{3,15},{4,8},{5,9},{6,10},{7,11},{8,4},{9,5},... | collective-permute-start | bytes 442376 | tf_op jit(solution)/shard_map/ppermute | solution.py:318
  40.7 1.5 %collective-permute-start.7 = (f32[512,128]{1,0:T(8,128)S(1)}, f32[512,128]{1,0:T(8,128)S(1)}, u32[]{:S(2)}, u32[]{:S(2)}) collective-permute-start(f32[512,128]{1,0:T(8,128)S(1)} %constant_dynamic-update-slice_fusion.refs_0_), channel_id=1, source_target_pairs={{0,1},{1,0},{2,3},{3,2},{4,5},{5,4},{6,7},{7,6},{8,9},{9,8},{10,11... | collective-permute-start | bytes 786440 | tf_op jit(solution)/shard_map/ppermute | solution.py:318
  40.7 1.9 %collective-permute-start.8 = (f32[512,128]{1,0:T(8,128)S(1)}, f32[512,128]{1,0:T(8,128)S(1)}, u32[]{:S(2)}, u32[]{:S(2)}) collective-permute-start(f32[512,128]{1,0:T(8,128)S(1)} %collective-permute-done.6.refs_2_), channel_id=1, source_target_pairs={{0,1},{1,0},{2,3},{3,2},{4,5},{5,4},{6,7},{7,6},{8,9},{9,8},{10,11... | collective-permute-start | bytes 786440 | tf_op jit(solution)/shard_map/ppermute | solution.py:318
  41.2 1.8 %collective-permute-start.12 = (f32[512,128]{1,0:T(8,128)S(1)}, f32[512,128]{1,0:T(8,128)S(1)}, u32[]{:S(2)}, u32[]{:S(2)}) collective-permute-start(f32[512,128]{1,0:T(8,128)S(1)} %collective-permute-done.10.refs_4_), channel_id=1, source_target_pairs={{0,1},{1,0},{2,3},{3,2},{4,5},{5,4},{6,7},{7,6},{8,9},{9,8},{10,11... | collective-permute-start | bytes 786440 | tf_op jit(solution)/shard_map/ppermute | solution.py:318
  41.3 2.1 %collective-permute-start.13 = (f32[512,128]{1,0:T(8,128)S(1)}, f32[512,128]{1,0:T(8,128)S(1)}, u32[]{:S(2)}, u32[]{:S(2)}) collective-permute-start(f32[512,128]{1,0:T(8,128)S(1)} %collective-permute-done.11.refs_6_), channel_id=1, source_target_pairs={{0,1},{1,0},{2,3},{3,2},{4,5},{5,4},{6,7},{7,6},{8,9},{9,8},{10,11... | collective-permute-start | bytes 786440 | tf_op jit(solution)/shard_map/ppermute | solution.py:318
  43.4 0.9 %copy-start = (f32[288,128]{1,0:T(8,128)S(1)}, f32[288,128]{1,0:T(8,128)}, u32[]{:S(2)}) copy-start(f32[288,128]{1,0:T(8,128)} %get-tuple-element.46.refs_8_) | copy-start | bytes 442372

commit v10 on v9

--- a/solution.py
+++ b/solution.py
@@ -91,8 +91,8 @@
         if part % 2 == 0:
             sent = jnp.where(found > 0.5, sent, EMPTY)
         for s in range(n_sky):
-            rows = pl.ds(s // NEAR * size + part, each, stride=4)
-            out_refs[s % NEAR][rows, :] = sent[s * each:(s + 1) * each]
+            rows = pl.ds(s % NEAR * size + part, each, stride=4)
+            out_refs[s // NEAR][rows, :] = sent[s * each:(s + 1) * each]
     ids = ids_ref[...]
     plane = lax.broadcasted_iota(jnp.int32, ids.shape, 0)
     owner = (ids // per_owner) ^ dest_ref[...]
@@ -112,7 +112,7 @@
         turn = (LANES - first % LANES) % LANES
         if turn:
             block = pltpu.roll(block, turn, 1)
-        out_refs[s % NEAR][pl.ds(s // NEAR * size + 4 * each, SUB), :] = block
+        out_refs[s // NEAR][pl.ds(s % NEAR * size + 4 * each, SUB), :] = block
 
 
 def prepare_kernel(n_sky, each, me_ref, dest_ref, ids_ref, rays_ref, src_ref, dst_ref, *out_refs):
@@ -122,33 +122,45 @@
 
 def prepare(n_sky, each, me, dest, ids, rays, potential):
     planes, tiles, pixels = potential.shape
-    part = jax.ShapeDtypeStruct((n_sky // NEAR * (4 * each + SUB), LANES), jnp.float32)
+    far = n_sky // NEAR
+    part = jax.ShapeDtypeStruct((NEAR * (4 * each + SUB), LANES), jnp.float32)
     own = jax.ShapeDtypeStruct((planes * tiles * pixels // LANES, LANES), jnp.float32)
     own, *sent = pl.pallas_call(
         functools.partial(prepare_kernel, n_sky, each),
-        out_shape=[own] + [part] * NEAR,
+        out_shape=[own] + [part] * far,
         in_specs=[pl.BlockSpec(memory_space=pltpu.SMEM)] + [pl.BlockSpec(memory_space=pltpu.VMEM)] * 4,
-        out_specs=[pl.BlockSpec(memory_space=pltpu.VMEM)] * (1 + NEAR),
+        out_specs=[pl.BlockSpec(memory_space=pltpu.VMEM)] * (1 + far),
         name="prepare",
     )(me, dest, ids, rays, potential)
     return own, sent
 
 
 def turn_kernel(size, *refs):
+    *refs, sems = refs
     far = len(refs) - NEAR
-    for f in range(far):
-        for c in range(NEAR):
-            refs[NEAR + f][pl.ds(c * size, size), :] = refs[c][pl.ds(f * size, size), :]
+    copies = [
+        pltpu.make_async_copy(
+            refs[f].at[pl.ds(c * size, size), :],
+            refs[far + c].at[pl.ds(f * size, size), :],
+            sems.at[f, c])
+        for f in range(far)
+        for c in range(NEAR)
+    ]
+    for copy in copies:
+        copy.start()
+    for copy in copies:
+        copy.wait()
 
 
 def turn(size, parts):
-    far = parts[0].shape[0] // size
-    block = jax.ShapeDtypeStruct((NEAR * size, LANES), jnp.float32)
+    far = len(parts)
+    block = jax.ShapeDtypeStruct((far * size, LANES), jnp.float32)
     return pl.pallas_call(
         functools.partial(turn_kernel, size),
-        out_shape=[block] * far,
-        in_specs=[pl.BlockSpec(memory_space=pltpu.VMEM)] * NEAR,
-        out_specs=[pl.BlockSpec(memory_space=pltpu.VMEM)] * far,
+        out_shape=[block] * NEAR,
+        in_specs=[pl.BlockSpec(memory_space=pl.ANY)] * far,
+        out_specs=[pl.BlockSpec(memory_space=pltpu.VMEM)] * NEAR,
+        scratch_shapes=[pltpu.SemaphoreType.DMA((far, NEAR))],
         name="turn",
     )(*parts)
 
@@ -218,11 +230,10 @@
 
 
 def trace_kernel(n_sky, each, planes, together, me_ref, lens_ref, *refs):
-    far = n_sky // NEAR
     pairs = n_sky // 2
     size = 4 * each + SUB
-    tile_refs, got_refs = refs[:pairs], refs[pairs:pairs + far]
-    shift_ref, matrix_ref, tiles, chosen, rays, places, sems = refs[pairs + far:]
+    tile_refs, got_refs = refs[:pairs], refs[pairs:pairs + NEAR]
+    shift_ref, matrix_ref, tiles, chosen, rays, places, sems = refs[pairs + NEAR:]
     me = me_ref[0]
     slots = n_sky * each
     rows = tile_refs[0].shape[0]
@@ -232,7 +243,7 @@
     ]
     for s in range(n_sky):
         source = me ^ s
-        got_ref, first = got_refs[s // NEAR], s % NEAR * size
+        got_ref, first = got_refs[s % NEAR], s // NEAR * size
         copies.append(pltpu.make_async_copy(
             got_ref.at[pl.ds(first + 4 * each, SUB), :],
             places.at[pl.ds(source * SUB, SUB), :],
@@ -329,26 +340,20 @@
     bits = [1 << k for k in reversed(range((n_sky - 1).bit_length()))]
     flat = ray_start.reshape(bundles, 2, halves, LANES).transpose(0, 2, 1, 3).reshape(bundles * 2 * halves, LANES)
     own, sent = prepare(n_sky, each, me, destination.reshape(1, bundles), patch_index, flat, potential)
-    sent = [sent[0]] + [flipped(sent[s], n_sky, s) for s in range(1, NEAR)]
     across = flipped(own, n_sky, bits[0])
-    across, *sent = lax.optimization_barrier((across, *sent))
-    pair = jnp.concatenate([own, across], axis=0)
-    got = list(turn(4 * each + SUB, sent))
-    held = {0: pair, bits[1]: flipped(pair, n_sky, bits[1])}
-    got[0], held[bits[1]] = lax.optimization_barrier((got[0], held[bits[1]]))
-    for bit in bits[2:-1]:
+    sent = [sent[0]] + [flipped(sent[f], n_sky, f * NEAR) for f in range(1, len(sent))]
+    held = {0: jnp.concatenate([own, across], axis=0)}
+    for bit in bits[1:-1]:
         for s in list(held):
             held[s ^ bit] = flipped(held[s], n_sky, bit)
-    got = [got[0]] + [flipped(got[f], n_sky, f * NEAR) for f in range(1, len(got))]
-    half = len(got) // 2
+    got = turn(4 * each + SUB, sent)
+    got = [got[0]] + [flipped(got[c], n_sky, c) for c in range(1, NEAR)]
     keys = sorted(held)
-    for mids, some in ((list(range(1, half + 1)), keys[:len(keys) // 2]), (list(range(half + 1, len(got))), keys[len(keys) // 2:])):
-        tied = lax.optimization_barrier([got[mid] for mid in mids] + [held[s] for s in some])
-        for mid in mids:
-            got[mid] = tied.pop(0)
-        held.update(zip(some, tied))
-    for s in keys:
-        held[s ^ 1] = flipped(held[s], n_sky, 1)
+    half = len(keys) // 2
+    for c, some in ((2, keys[:half]), (3, keys[half:])):
+        got[c], *tied = lax.optimization_barrier((got[c], *[held[s] for s in some]))
+        for s, value in zip(some, tied):
+            held[s], held[s ^ 1] = value, flipped(value, n_sky, 1)
     shift, matrix = trace(each, planes, me, lens_weight, [held[s] for s in range(n_sky // 2)], got)
     shift = shift.reshape(slots, halves, 2, LANES).transpose(0, 2, 1, 3).reshape(slots, 2, rays)
     matrix = matrix.reshape(slots, halves, 4, LANES).transpose(0, 2, 1, 3).reshape(slots, 4, rays)

time: 61.7 us -> 64.7 us (1.049)
  waiting for transfers between devices: 22 us -> 23.8 us
  local copies, waits for them, and re-layouts: 1.88 us -> 2.56 us
    ppermute x14, waiting for transfers between devices: 22 us -> 23.8 us  [flipped(): return lax.ppermute(value, 'sky', [(i, i ^ bits) for i in range(n_sky)])]
    unnamed x11 -> x17, local copies, waits for them, and re-layouts: 1.87 us -> 2.55 us
where the time goes in v10:
time: 64.7 us; the launch traced here: 64.5 us
  waiting for transfers between devices  23.8 us (37%)
  Pallas kernels  21.6 us (33%)
  starting transfers between devices  15.8 us (24%)
  local copies, waits for them, and re-layouts  2.56 us (4%)
  between operations  0.71 us (1%)
    ppermute x14, waiting for transfers between devices, flipped(): return lax.ppermute(value, 'sky', [(i, i ^ bits) for i in range(n_sky)])  23.8 us
    pallas_call x1, Pallas kernels, trace(): pl.pallas_call(functools.partial(trace_kernel, n_sky, each, planes, toget...  17.2 us
    ppermute x14, starting transfers between devices, flipped(): return lax.ppermute(value, 'sky', [(i, i ^ bits) for i in range(n_sky)])  15.8 us
    unnamed x17, local copies, waits for them, and re-layouts  2.55 us
    pallas_call x1, Pallas kernels, prepare(): pl.pallas_call(functools.partial(prepare_kernel, n_sky, each), out_shape=...  2.37 us
    pallas_call x1, Pallas kernels, turn(): pl.pallas_call(functools.partial(turn_kernel, size), out_shape=[block] *...  2.01 us
  transfers between devices with their start and end apart: 14, of which 8 were waited for; matrix products, arithmetic and copies ran while one was open for 2% of the time, Pallas kernels for 3%

profile of v10, /device:TPU:0, one launch (start us, length us, event | category | flops | bytes accessed | tf_op | source)
XLA Modules:
  0.0 64.5 jit_solution(15178150290304884295)
XLA Ops:
  0.6 2.4 %prepare.1 = (f32[256,128]{1,0:T(8,128)}, f32[288,128]{1,0:T(8,128)}, f32[288,128]{1,0:T(8,128)}, f32[288,128]{1,0:T(8,128)}, f32[288,128]{1,0:T(8,128)}) custom-call(s32[1]{0:T(128)} %bitcast.me_ref, s32[1,128]{1,0:T(1,128)} %bitcast.18, s32[4,128]{1,0:T(4,128)} %ids_ref.1, f32[512,128]{1,0:T(8,128)} %bitcast.17, f32[4,8,1024]{2,1,0:T(8,128)} %src_ref.1), custom_call_target="tpu_custom_call" | custom-call | tf_op jit(solution)/shard_map/prepare/pallas_call | solution.py:128
  3.0 4.0 %collective-permute-start.4 = (f32[256,128]{1,0:T(8,128)}, f32[256,128]{1,0:T(8,128)S(1)}, u32[]{:S(2)}, u32[]{:S(2)}) collective-permute-start(f32[256,128]{1,0:T(8,128)} %get-tuple-element.24), channel_id=1, source_target_pairs={{0,8},{1,9},{2,10},{3,11},{4,12},{5,13},{6,14},{7,15},{8,0},{9,1},... | collective-permute-start | bytes 393224 | tf_op jit(solution)/shard_map/ppermute | solution.py:329
  7.0 0.0 copy-start.7
  7.0 0.0 copy-start.6
  7.0 1.0 %constant_dynamic-update-slice_fusion.1 = f32[512,128]{1,0:T(8,128)S(1)} fusion(f32[256,128]{1,0:T(8,128)} %get-tuple-element.24), kind=kLoop, calls=%fused_computation.1 | loop fusion | bytes 262144
  8.0 0.0 copy-start.5
  8.0 5.5 %collective-permute-done.4 = f32[256,128]{1,0:T(8,128)S(1)} collective-permute-done((f32[256,128]{1,0:T(8,128)}, f32[256,128]{1,0:T(8,128)S(1)}, u32[]{:S(2)}, u32[]{:S(2)}) %collective-permute-start.4) | collective-permute-done | bytes 131104 | tf_op jit(solution)/shard_map/ppermute | solution.py:329
  13.6 0.9 %collective-permute-start.9 = (f32[512,128]{1,0:T(8,128)S(1)}, f32[512,128]{1,0:T(8,128)S(1)}, u32[]{:S(2)}, u32[]{:S(2)}) collective-permute-start(f32[512,128]{1,0:T(8,128)S(1)} %constant_dynamic-update-slice_fusion.refs_0_), channel_id=1, source_target_pairs={{0,4},{1,5},{2,6},{3,7},{4,0},{5,1},{6,2},{7,3},{8,12},{9,13},{10,... | collective-permute-start | bytes 786440 | tf_op jit(solution)/shard_map/ppermute | solution.py:329
  14.5 0.0 copy-done.7
  14.5 1.2 %collective-permute-start = (f32[288,128]{1,0:T(8,128)S(1)}, f32[288,128]{1,0:T(8,128)S(1)}, u32[]{:S(2)}, u32[]{:S(2)}) collective-permute-start(f32[288,128]{1,0:T(8,128)S(1)} %copy-done.7), channel_id=1, source_target_pairs={{0,4},{1,5},{2,6},{3,7},{4,0},{5,1},{6,2},{7,3},{8,12},{9,13},{10,... | collective-permute-start | bytes 442376 | tf_op jit(solution)/shard_map/ppermute | solution.py:329
  15.7 0.0 copy-done.6
  15.7 2.2 %collective-permute-start.1 = (f32[288,128]{1,0:T(8,128)S(1)}, f32[288,128]{1,0:T(8,128)S(1)}, u32[]{:S(2)}, u32[]{:S(2)}) collective-permute-start(f32[288,128]{1,0:T(8,128)S(1)} %copy-done.6), channel_id=1, source_target_pairs={{0,8},{1,9},{2,10},{3,11},{4,12},{5,13},{6,14},{7,15},{8,0},{9,1},... | collective-permute-start | bytes 442376 | tf_op jit(solution)/shard_map/ppermute | solution.py:329
  17.8 0.0 copy-done.5
  17.8 1.4 %collective-permute-start.2 = (f32[288,128]{1,0:T(8,128)S(1)}, f32[288,128]{1,0:T(8,128)S(1)}, u32[]{:S(2)}, u32[]{:S(2)}) collective-permute-start(f32[288,128]{1,0:T(8,128)S(1)} %copy-done.5), channel_id=1, source_target_pairs={{0,12},{1,13},{2,14},{3,15},{4,8},{5,9},{6,10},{7,11},{8,4},{9,5},... | collective-permute-start | bytes 442376 | tf_op jit(solution)/shard_map/ppermute | solution.py:329
  19.3 1.5 %collective-permute-start.5 = (f32[512,128]{1,0:T(8,128)S(1)}, f32[512,128]{1,0:T(8,128)S(1)}, u32[]{:S(2)}, u32[]{:S(2)}) collective-permute-start(f32[512,128]{1,0:T(8,128)S(1)} %constant_dynamic-update-slice_fusion.refs_0_), channel_id=1, source_target_pairs={{0,2},{1,3},{2,0},{3,1},{4,6},{5,7},{6,4},{7,5},{8,10},{9,11},{10,... | collective-permute-start | bytes 786440 | tf_op jit(solution)/shard_map/ppermute | solution.py:329
  20.8 5.1 %collective-permute-done.9.refs_4_ = f32[512,128]{1,0:T(8,128)S(1)} collective-permute-done((f32[512,128]{1,0:T(8,128)S(1)}, f32[512,128]{1,0:T(8,128)S(1)}, u32[]{:S(2)}, u32[]{:S(2)}) %collective-permute-start.9) | collective-permute-done | bytes 262176 | tf_op jit(solution)/shard_map/ppermute | solution.py:329
  25.9 1.3 %collective-permute-start.10 = (f32[512,128]{1,0:T(8,128)S(1)}, f32[512,128]{1,0:T(8,128)S(1)}, u32[]{:S(2)}, u32[]{:S(2)}) collective-permute-start(f32[512,128]{1,0:T(8,128)S(1)} %collective-permute-done.9.refs_4_), channel_id=1, source_target_pairs={{0,2},{1,3},{2,0},{3,1},{4,6},{5,7},{6,4},{7,5},{8,10},{9,11},{10,... | collective-permute-start | bytes 786440 | tf_op jit(solution)/shard_map/ppermute | solution.py:329
  27.2 0.2 collective-permute-done.refs_1_
  27.4 0.0 copy-start.2
  27.4 0.1 collective-permute-done.1.refs_2_
  27.5 0.0 copy-start.3
  27.5 5.6 %collective-permute-done.2.refs_3_ = f32[288,128]{1,0:T(8,128)S(1)} collective-permute-done((f32[288,128]{1,0:T(8,128)S(1)}, f32[288,128]{1,0:T(8,128)S(1)}, u32[]{:S(2)}, u32[]{:S(2)}) %collective-permute-start.2) | collective-permute-done | bytes 147488 | tf_op jit(solution)/shard_map/ppermute | solution.py:329
  33.1 0.0 copy-start.4
  33.1 0.0 copy-done.2
  33.1 0.0 copy-done.3
  33.1 0.6 copy-done.4
  33.8 2.0 %turn.1 = (f32[288,128]{1,0:T(8,128)}, f32[288,128]{1,0:T(8,128)}, f32[288,128]{1,0:T(8,128)}, f32[288,128]{1,0:T(8,128)}) custom-call(f32[288,128]{1,0:T(8,128)} %get-tuple-element.19.refs_0_, f32[288,128]{1,0:T(8,128)} %copy-done.2, f32[288,128]{1,0:T(8,128)} %copy-done.3, f32[288,128]{1,0:T(8,128)} %copy-done.4), custom_call_target="tpu_custom_call" | custom-call | tf_op jit(solution)/shard_map/turn/pallas_call | solution.py:158
  35.8 1.6 %collective-permute-start.3 = (f32[288,128]{1,0:T(8,128)}, f32[288,128]{1,0:T(8,128)S(1)}, u32[]{:S(2)}, u32[]{:S(2)}) collective-permute-start(f32[288,128]{1,0:T(8,128)} %get-tuple-element.23), channel_id=1, source_target_pairs={{0,2},{1,3},{2,0},{3,1},{4,6},{5,7},{6,4},{7,5},{8,10},{9,11},{10,... | collective-permute-start | bytes 442376 | tf_op jit(solution)/shard_map/ppermute | solution.py:329
  37.4 0.0 collective-permute-start.8
  37.4 4.7 %collective-permute-done.3.refs_10_ = f32[288,128]{1,0:T(8,128)S(1)} collective-permute-done((f32[288,128]{1,0:T(8,128)}, f32[288,128]{1,0:T(8,128)S(1)}, u32[]{:S(2)}, u32[]{:S(2)}) %collective-permute-start.3) | collective-permute-done | bytes 147488 | tf_op jit(solution)/shard_map/ppermute | solution.py:329
  42.1 0.0 collective-permute-done.5.refs_2_
  42.1 0.0 collective-permute-start.6
  42.1 0.5 collective-permute-start.7
  42.6 1.1 %collective-permute-done.8.refs_11_ = f32[288,128]{1,0:T(8,128)S(1)} collective-permute-done((f32[288,128]{1,0:T(8,128)}, f32[288,128]{1,0:T(8,128)S(1)}, u32[]{:S(2)}, u32[]{:S(2)}) %collective-permute-start.8) | collective-permute-done | bytes 147488 | tf_op jit(solution)/shard_map/ppermute | solution.py:329
  43.7 0.0 collective-permute-done.10.refs_6_
  43.7 0.6 collective-permute-start.11
  44.3 0.0 collective-permute-start.12
  44.3 0.0 copy-start.1
  44.3 0.5 collective-permute-start.13
  44.8 1.4 %collective-permute-done.13.refs_9_ = f32[288,128]{1,0:T(8,128)S(1)} collective-permute-done((f32[288,128]{1,0:T(8,128)}, f32[288,128]{1,0:T(8,128)S(1)}, u32[]{:S(2)}, u32[]{:S(2)}) %collective-permute-start.13) | collective-permute-done | bytes 147488 | tf_op jit(solution)/shard_map/ppermute | solution.py:329
  46.3 0.0 collective-permute-done.6.refs_1_
  46.3 0.0 collective-permute-done.7.refs_3_
  46.3 0.0 collective-permute-done.11.refs_5_
  46.3 0.0 collective-permute-done.12.refs_7_
  46.3 0.0 copy-done.1
  46.3 0.0 copy-start
  46.3 0.9 %copy-done = f32[288,128]{1,0:T(8,128)S(1)} copy-done((f32[288,128]{1,0:T(8,128)S(1)}, f32[288,128]{1,0:T(8,128)}, u32[]{:S(2)}) %copy-start) | copy-done | bytes 147480
  47.2 17.2 %trace.1 = (f32[1024,128]{1,0:T(8,128)}, f32[2048,128]{1,0:T(8,128)}) custom-call(s32[1]{0:T(128)} %bitcast.me_ref, f32[4]{0:T(128)S(1)} %copy-done.1, f32[512,128]{1,0:T(8,128)S(1)} %constant_dynamic-update-slice_fusion.refs_0_, f32[512,128]{1,0:T(8,128)S(1)} %collective-permute-done.6.refs_1_, f32[512,128]{1,0:T(8,128)S(1)} %collective-permute-done.5.refs_2_, ...), custom_call_target="tpu_custom_call" | custom-call | tf_op jit(solution)/shard_map/trace/pallas_call | solution.py:305
  (1 shorter events, 0.0 us)
Async XLA Ops:
  3.0 10.5 %collective-permute-start.4 = (f32[256,128]{1,0:T(8,128)}, f32[256,128]{1,0:T(8,128)S(1)}, u32[]{:S(2)}, u32[]{:S(2)}) collective-permute-start(f32[256,128]{1,0:T(8,128)} %get-tuple-element.24), channel_id=1, source_target_pairs={{0,8},{1,9},{2,10},{3,11},{4,12},{5,13},{6,14},{7,15},{8,0},{9,1},... | collective-permute-start | bytes 393224 | tf_op jit(solution)/shard_map/ppermute | solution.py:329
  7.0 7.4 %copy-start.7 = (f32[288,128]{1,0:T(8,128)S(1)}, f32[288,128]{1,0:T(8,128)}, u32[]{:S(2)}) copy-start(f32[288,128]{1,0:T(8,128)} %get-tuple-element.20) | copy-start | bytes 442372
  7.0 8.6 %copy-start.6 = (f32[288,128]{1,0:T(8,128)S(1)}, f32[288,128]{1,0:T(8,128)}, u32[]{:S(2)}) copy-start(f32[288,128]{1,0:T(8,128)} %get-tuple-element.21) | copy-start | bytes 442372
  8.0 9.8 %copy-start.5 = (f32[288,128]{1,0:T(8,128)S(1)}, f32[288,128]{1,0:T(8,128)}, u32[]{:S(2)}) copy-start(f32[288,128]{1,0:T(8,128)} %get-tuple-element.22) | copy-start | bytes 442372
  13.6 12.3 %collective-permute-start.9 = (f32[512,128]{1,0:T(8,128)S(1)}, f32[512,128]{1,0:T(8,128)S(1)}, u32[]{:S(2)}, u32[]{:S(2)}) collective-permute-start(f32[512,128]{1,0:T(8,128)S(1)} %constant_dynamic-update-slice_fusion.refs_0_), channel_id=1, source_target_pairs={{0,4},{1,5},{2,6},{3,7},{4,0},{5,1},{6,2},{7,3},{8,12},{9,13},{10,... | collective-permute-start | bytes 786440 | tf_op jit(solution)/shard_map/ppermute | solution.py:329
  14.5 13.0 %collective-permute-start = (f32[288,128]{1,0:T(8,128)S(1)}, f32[288,128]{1,0:T(8,128)S(1)}, u32[]{:S(2)}, u32[]{:S(2)}) collective-permute-start(f32[288,128]{1,0:T(8,128)S(1)} %copy-done.7), channel_id=1, source_target_pairs={{0,4},{1,5},{2,6},{3,7},{4,0},{5,1},{6,2},{7,3},{8,12},{9,13},{10,... | collective-permute-start | bytes 442376 | tf_op jit(solution)/shard_map/ppermute | solution.py:329
  15.7 11.8 %collective-permute-start.1 = (f32[288,128]{1,0:T(8,128)S(1)}, f32[288,128]{1,0:T(8,128)S(1)}, u32[]{:S(2)}, u32[]{:S(2)}) collective-permute-start(f32[288,128]{1,0:T(8,128)S(1)} %copy-done.6), channel_id=1, source_target_pairs={{0,8},{1,9},{2,10},{3,11},{4,12},{5,13},{6,14},{7,15},{8,0},{9,1},... | collective-permute-start | bytes 442376 | tf_op jit(solution)/shard_map/ppermute | solution.py:329
  17.8 15.3 %collective-permute-start.2 = (f32[288,128]{1,0:T(8,128)S(1)}, f32[288,128]{1,0:T(8,128)S(1)}, u32[]{:S(2)}, u32[]{:S(2)}) collective-permute-start(f32[288,128]{1,0:T(8,128)S(1)} %copy-done.5), channel_id=1, source_target_pairs={{0,12},{1,13},{2,14},{3,15},{4,8},{5,9},{6,10},{7,11},{8,4},{9,5},... | collective-permute-start | bytes 442376 | tf_op jit(solution)/shard_map/ppermute | solution.py:329
  19.3 22.8 %collective-permute-start.5 = (f32[512,128]{1,0:T(8,128)S(1)}, f32[512,128]{1,0:T(8,128)S(1)}, u32[]{:S(2)}, u32[]{:S(2)}) collective-permute-start(f32[512,128]{1,0:T(8,128)S(1)} %constant_dynamic-update-slice_fusion.refs_0_), channel_id=1, source_target_pairs={{0,2},{1,3},{2,0},{3,1},{4,6},{5,7},{6,4},{7,5},{8,10},{9,11},{10,... | collective-permute-start | bytes 786440 | tf_op jit(solution)/shard_map/ppermute | solution.py:329
  25.9 17.9 %collective-permute-start.10 = (f32[512,128]{1,0:T(8,128)S(1)}, f32[512,128]{1,0:T(8,128)S(1)}, u32[]{:S(2)}, u32[]{:S(2)}) collective-permute-start(f32[512,128]{1,0:T(8,128)S(1)} %collective-permute-done.9.refs_4_), channel_id=1, source_target_pairs={{0,2},{1,3},{2,0},{3,1},{4,6},{5,7},{6,4},{7,5},{8,10},{9,11},{10,... | collective-permute-start | bytes 786440 | tf_op jit(solution)/shard_map/ppermute | solution.py:329
  27.4 5.7 %copy-start.2 = (f32[288,128]{1,0:T(8,128)}, f32[288,128]{1,0:T(8,128)S(1)}, u32[]{:S(2)}) copy-start(f32[288,128]{1,0:T(8,128)S(1)} %collective-permute-done.refs_1_) | copy-start | bytes 442372
  27.5 5.6 %copy-start.3 = (f32[288,128]{1,0:T(8,128)}, f32[288,128]{1,0:T(8,128)S(1)}, u32[]{:S(2)}) copy-start(f32[288,128]{1,0:T(8,128)S(1)} %collective-permute-done.1.refs_2_) | copy-start | bytes 442372
  33.1 0.7 %copy-start.4 = (f32[288,128]{1,0:T(8,128)}, f32[288,128]{1,0:T(8,128)S(1)}, u32[]{:S(2)}) copy-start(f32[288,128]{1,0:T(8,128)S(1)} %collective-permute-done.2.refs_3_) | copy-start | bytes 442372
  35.8 6.3 %collective-permute-start.3 = (f32[288,128]{1,0:T(8,128)}, f32[288,128]{1,0:T(8,128)S(1)}, u32[]{:S(2)}, u32[]{:S(2)}) collective-permute-start(f32[288,128]{1,0:T(8,128)} %get-tuple-element.23), channel_id=1, source_target_pairs={{0,2},{1,3},{2,0},{3,1},{4,6},{5,7},{6,4},{7,5},{8,10},{9,11},{10,... | collective-permute-start | bytes 442376 | tf_op jit(solution)/shard_map/ppermute | solution.py:329
  37.4 6.3 %collective-permute-start.8 = (f32[288,128]{1,0:T(8,128)}, f32[288,128]{1,0:T(8,128)S(1)}, u32[]{:S(2)}, u32[]{:S(2)}) collective-permute-start(f32[288,128]{1,0:T(8,128)} %get-tuple-element.27), channel_id=1, source_target_pairs={{0,3},{1,2},{2,1},{3,0},{4,7},{5,6},{6,5},{7,4},{8,11},{9,10},{10,... | collective-permute-start | bytes 442376 | tf_op jit(solution)/shard_map/ppermute | solution.py:329
  42.1 4.2 %collective-permute-start.6 = (f32[512,128]{1,0:T(8,128)S(1)}, f32[512,128]{1,0:T(8,128)S(1)}, u32[]{:S(2)}, u32[]{:S(2)}) collective-permute-start(f32[512,128]{1,0:T(8,128)S(1)} %constant_dynamic-update-slice_fusion.refs_0_), channel_id=1, source_target_pairs={{0,1},{1,0},{2,3},{3,2},{4,5},{5,4},{6,7},{7,6},{8,9},{9,8},{10,11... | collective-permute-start | bytes 786440 | tf_op jit(solution)/shard_map/ppermute | solution.py:329
  42.1 4.2 %collective-permute-start.7 = (f32[512,128]{1,0:T(8,128)S(1)}, f32[512,128]{1,0:T(8,128)S(1)}, u32[]{:S(2)}, u32[]{:S(2)}) collective-permute-start(f32[512,128]{1,0:T(8,128)S(1)} %collective-permute-done.5.refs_2_), channel_id=1, source_target_pairs={{0,1},{1,0},{2,3},{3,2},{4,5},{5,4},{6,7},{7,6},{8,9},{9,8},{10,11... | collective-permute-start | bytes 786440 | tf_op jit(solution)/shard_map/ppermute | solution.py:329
  43.7 2.5 %collective-permute-start.11 = (f32[512,128]{1,0:T(8,128)S(1)}, f32[512,128]{1,0:T(8,128)S(1)}, u32[]{:S(2)}, u32[]{:S(2)}) collective-permute-start(f32[512,128]{1,0:T(8,128)S(1)} %collective-permute-done.9.refs_4_), channel_id=1, source_target_pairs={{0,1},{1,0},{2,3},{3,2},{4,5},{5,4},{6,7},{7,6},{8,9},{9,8},{10,11... | collective-permute-start | bytes 786440 | tf_op jit(solution)/shard_map/ppermute | solution.py:329
  44.3 2.0 %collective-permute-start.12 = (f32[512,128]{1,0:T(8,128)S(1)}, f32[512,128]{1,0:T(8,128)S(1)}, u32[]{:S(2)}, u32[]{:S(2)}) collective-permute-start(f32[512,128]{1,0:T(8,128)S(1)} %collective-permute-done.10.refs_6_), channel_id=1, source_target_pairs={{0,1},{1,0},{2,3},{3,2},{4,5},{5,4},{6,7},{7,6},{8,9},{9,8},{10,11... | collective-permute-start | bytes 786440 | tf_op jit(solution)/shard_map/ppermute | solution.py:329
  44.3 2.0 %copy-start.1 = (f32[4]{0:T(128)S(1)}, f32[4]{0:T(128)}, u32[]{:S(2)}) copy-start(f32[4]{0:T(128)} %lens_ref.1) | copy-start | bytes 52
  44.3 2.0 %collective-permute-start.13 = (f32[288,128]{1,0:T(8,128)}, f32[288,128]{1,0:T(8,128)S(1)}, u32[]{:S(2)}, u32[]{:S(2)}) collective-permute-start(f32[288,128]{1,0:T(8,128)} %get-tuple-element.31), channel_id=1, source_target_pairs={{0,1},{1,0},{2,3},{3,2},{4,5},{5,4},{6,7},{7,6},{8,9},{9,8},{10,11... | collective-permute-start | bytes 442376 | tf_op jit(solution)/shard_map/ppermute | solution.py:329
  46.3 0.9 %copy-start = (f32[288,128]{1,0:T(8,128)S(1)}, f32[288,128]{1,0:T(8,128)}, u32[]{:S(2)}) copy-start(f32[288,128]{1,0:T(8,128)} %get-tuple-element.30.refs_8_) | copy-start | bytes 442372

commit v11 on v7

--- a/solution.py
+++ b/solution.py
@@ -128,6 +128,7 @@
         out_shape=[own] + [part] * NEAR,
         in_specs=[pl.BlockSpec(memory_space=pltpu.SMEM)] + [pl.BlockSpec(memory_space=pltpu.VMEM)] * 4,
         out_specs=[pl.BlockSpec(memory_space=pltpu.VMEM)] * (1 + NEAR),
+        compiler_params=pltpu.CompilerParams(vmem_limit_bytes=16 * 1024 * 1024),
         name="prepare",
     )(me, dest, ids, rays, potential)
     return own, sent
@@ -148,6 +149,7 @@
         out_shape=[block] * far,
         in_specs=[pl.BlockSpec(memory_space=pltpu.VMEM)] * NEAR,
         out_specs=[pl.BlockSpec(memory_space=pltpu.VMEM)] * far,
+        compiler_params=pltpu.CompilerParams(vmem_limit_bytes=4 * 1024 * 1024),
         name="turn",
     )(*parts)
 
@@ -239,10 +241,10 @@
                 rays.at[pl.ds(source * 4 * each, 4 * each), :],
                 sems.at[2, s]),
         ))
-    for kind in range(3):
+    for kind in (1, 0, 2):
         for s in range(n_sky):
             copies[s][kind].start()
-    for kind in range(3):
+    for kind in (0, 2, 1):
         for s in range(n_sky):
             copies[s][kind].wait()
 
@@ -309,7 +311,7 @@
             pltpu.SMEM((n_sky * SUB, LANES), jnp.float32),
             pltpu.SemaphoreType.DMA((3, n_sky)),
         ],
-        compiler_params=pltpu.CompilerParams(vmem_limit_bytes=40 * 1024 * 1024),
+        compiler_params=pltpu.CompilerParams(vmem_limit_bytes=20 * 1024 * 1024),
         name="trace",
     )(me, lens_weight, *tiles, *got)
 

time: 58.9 us -> 56.4 us (0.958)
  Pallas kernels: 23.7 us -> 20.6 us
  local copies, waits for them, and re-layouts: 1.58 us -> 2.53 us
    pallas_call x1, Pallas kernels: 1.98 us -> 0.04 us  [turn(): pl.pallas_call(functools.partial(turn_kernel, size), out_shape=[block] *...]
    pallas_call x1, Pallas kernels: 2.37 us -> 0.55 us  [prepare(): pl.pallas_call(functools.partial(prepare_kernel, n_sky, each), out_shape=...]
    unnamed x12 -> x10, local copies, waits for them, and re-layouts: 1.58 us -> 2.53 us
    pallas_call x1, Pallas kernels: 19.4 us -> 20 us  [trace(): pl.pallas_call(functools.partial(trace_kernel, n_sky, each, planes, toget...]
  transfers between devices with their start and end apart: 21 -> 21, of which waited for: 10 -> 11; matrix products, arithmetic and copies ran while one was open for 0% -> 0% of each run, Pallas kernels for 3% -> 0%
where the time goes in v11:
time: 56.4 us; the launch traced here: 56.2 us
  Pallas kernels  20.6 us (37%)
  starting transfers between devices  18.1 us (32%)
  waiting for transfers between devices  14.3 us (25%)
  local copies, waits for them, and re-layouts  2.53 us (4%)
  between operations  0.68 us (1%)
    pallas_call x1, Pallas kernels, trace(): pl.pallas_call(functools.partial(trace_kernel, n_sky, each, planes, toget...  20 us
    ppermute x21, starting transfers between devices, flipped(): return lax.ppermute(value, 'sky', [(i, i ^ bits) for i in range(n_sky)])  18.1 us
    ppermute x21, waiting for transfers between devices, flipped(): return lax.ppermute(value, 'sky', [(i, i ^ bits) for i in range(n_sky)])  14.3 us
    unnamed x10, local copies, waits for them, and re-layouts  2.53 us
  transfers between devices with their start and end apart: 21, of which 11 were waited for; matrix products, arithmetic and copies ran while one was open for 0% of the time, Pallas kernels for 0%

profile of v11, /device:TPU:0, one launch (start us, length us, event | category | flops | bytes accessed | tf_op | source)
XLA Modules:
  0.0 56.2 jit_solution(1130005849794275006)
XLA Ops:
  0.7 0.7 %copy-done.2 = s32[4,128]{1,0:T(4,128)S(1)} copy-done((s32[4,128]{1,0:T(4,128)S(1)}, s32[4,128]{1,0:T(4,128)}, u32[]{:S(2)}) %copy-start.2) | copy-done | bytes 2072
  1.3 0.9 %copy-done = f32[128,2,256]{2,1,0:T(2,128)S(1)} copy-done((f32[128,2,256]{2,1,0:T(2,128)S(1)}, f32[128,2,256]{2,1,0:T(2,128)}, u32[]{:S(2)}) %copy-start) | copy-done | bytes 262168
  2.3 0.9 %copy-done.1 = f32[4,8,1024]{2,1,0:T(8,128)S(1)} copy-done((f32[4,8,1024]{2,1,0:T(8,128)S(1)}, f32[4,8,1024]{2,1,0:T(8,128)}, u32[]{:S(2)}) %copy-start.1) | copy-done | bytes 131096
  3.2 0.5 prepare.1
  3.7 4.0 %collective-permute-start.3 = (f32[256,128]{1,0:T(8,128)S(1)}, f32[256,128]{1,0:T(8,128)S(1)}, u32[]{:S(2)}, u32[]{:S(2)}) collective-permute-start(f32[256,128]{1,0:T(8,128)S(1)} %get-tuple-element.42.refs_0_), channel_id=1, source_target_pairs={{0,8},{1,9},{2,10},{3,11},{4,12},{5,13},{6,14},{7,15},{8,0},{9,1},... | collective-permute-start | bytes 393224 | tf_op jit(solution)/shard_map/ppermute | solution.py:320
  7.8 0.0 collective-permute-start
  7.8 1.5 %collective-permute-start.1 = (f32[288,128]{1,0:T(8,128)S(1)}, f32[288,128]{1,0:T(8,128)S(1)}, u32[]{:S(2)}, u32[]{:S(2)}) collective-permute-start(f32[288,128]{1,0:T(8,128)S(1)} %get-tuple-element.32), channel_id=1, source_target_pairs={{0,2},{1,3},{2,0},{3,1},{4,6},{5,7},{6,4},{7,5},{8,10},{9,11},{10,... | collective-permute-start | bytes 442376 | tf_op jit(solution)/shard_map/ppermute | solution.py:320
  9.3 0.3 collective-permute-start.2
  9.6 1.6 %collective-permute-start.4 = (f32[256,128]{1,0:T(8,128)S(1)}, f32[256,128]{1,0:T(8,128)S(1)}, u32[]{:S(2)}, u32[]{:S(2)}) collective-permute-start(f32[256,128]{1,0:T(8,128)S(1)} %get-tuple-element.42.refs_0_), channel_id=1, source_target_pairs={{0,4},{1,5},{2,6},{3,7},{4,0},{5,1},{6,2},{7,3},{8,12},{9,13},{10,... | collective-permute-start | bytes 393224 | tf_op jit(solution)/shard_map/ppermute | solution.py:320
  11.2 3.0 %collective-permute-done.3.refs_8_ = f32[256,128]{1,0:T(8,128)S(1)} collective-permute-done((f32[256,128]{1,0:T(8,128)S(1)}, f32[256,128]{1,0:T(8,128)S(1)}, u32[]{:S(2)}, u32[]{:S(2)}) %collective-permute-start.3) | collective-permute-done | bytes 131104 | tf_op jit(solution)/shard_map/ppermute | solution.py:320
  14.2 0.7 %collective-permute-start.14 = (f32[256,128]{1,0:T(8,128)S(1)}, f32[256,128]{1,0:T(8,128)S(1)}, u32[]{:S(2)}, u32[]{:S(2)}) collective-permute-start(f32[256,128]{1,0:T(8,128)S(1)} %collective-permute-done.3.refs_8_), channel_id=1, source_target_pairs={{0,4},{1,5},{2,6},{3,7},{4,0},{5,1},{6,2},{7,3},{8,12},{9,13},{10,... | collective-permute-start | bytes 393224 | tf_op jit(solution)/shard_map/ppermute | solution.py:320
  14.8 0.0 collective-permute-done.refs_1_
  14.8 0.0 collective-permute-done.1.refs_2_
  14.9 2.0 %collective-permute-done.2.refs_3_ = f32[288,128]{1,0:T(8,128)S(1)} collective-permute-done((f32[288,128]{1,0:T(8,128)S(1)}, f32[288,128]{1,0:T(8,128)S(1)}, u32[]{:S(2)}, u32[]{:S(2)}) %collective-permute-start.2) | collective-permute-done | bytes 147488 | tf_op jit(solution)/shard_map/ppermute | solution.py:320
  16.9 0.1 collective-permute-done.4.refs_4_
  17.0 1.5 %collective-permute-start.6 = (f32[256,128]{1,0:T(8,128)S(1)}, f32[256,128]{1,0:T(8,128)S(1)}, u32[]{:S(2)}, u32[]{:S(2)}) collective-permute-start(f32[256,128]{1,0:T(8,128)S(1)} %get-tuple-element.42.refs_0_), channel_id=1, source_target_pairs={{0,2},{1,3},{2,0},{3,1},{4,6},{5,7},{6,4},{7,5},{8,10},{9,11},{10,... | collective-permute-start | bytes 393224 | tf_op jit(solution)/shard_map/ppermute | solution.py:320
  18.5 1.4 %collective-permute-start.5 = (f32[288,128]{1,0:T(8,128)S(1)}, f32[288,128]{1,0:T(8,128)S(1)}, u32[]{:S(2)}, u32[]{:S(2)}) collective-permute-start(f32[288,128]{1,0:T(8,128)S(1)} %get-tuple-element.39), channel_id=1, source_target_pairs={{0,8},{1,9},{2,10},{3,11},{4,12},{5,13},{6,14},{7,15},{8,0},{9,1},... | collective-permute-start | bytes 442376 | tf_op jit(solution)/shard_map/ppermute | solution.py:320
  20.0 2.4 %collective-permute-start.12 = (f32[288,128]{1,0:T(8,128)S(1)}, f32[288,128]{1,0:T(8,128)S(1)}, u32[]{:S(2)}, u32[]{:S(2)}) collective-permute-start(f32[288,128]{1,0:T(8,128)S(1)} %get-tuple-element.46), channel_id=1, source_target_pairs={{0,12},{1,13},{2,14},{3,15},{4,8},{5,9},{6,10},{7,11},{8,4},{9,5},... | collective-permute-start | bytes 442376 | tf_op jit(solution)/shard_map/ppermute | solution.py:320
  22.4 0.5 collective-permute-start.7
  22.9 0.0 collective-permute-done.14.refs_12_
  22.9 1.5 %collective-permute-start.13 = (f32[256,128]{1,0:T(8,128)S(1)}, f32[256,128]{1,0:T(8,128)S(1)}, u32[]{:S(2)}, u32[]{:S(2)}) collective-permute-start(f32[256,128]{1,0:T(8,128)S(1)} %collective-permute-done.3.refs_8_), channel_id=1, source_target_pairs={{0,2},{1,3},{2,0},{3,1},{4,6},{5,7},{6,4},{7,5},{8,10},{9,11},{10,... | collective-permute-start | bytes 393224 | tf_op jit(solution)/shard_map/ppermute | solution.py:320
  24.4 0.0 collective-permute-done.6.refs_2_
  24.4 0.4 collective-permute-start.20
  24.8 4.0 %collective-permute-done.7.refs_6_ = f32[256,128]{1,0:T(8,128)S(1)} collective-permute-done((f32[256,128]{1,0:T(8,128)S(1)}, f32[256,128]{1,0:T(8,128)S(1)}, u32[]{:S(2)}, u32[]{:S(2)}) %collective-permute-start.7) | collective-permute-done | bytes 131104 | tf_op jit(solution)/shard_map/ppermute | solution.py:320
  28.8 0.5 collective-permute-start.15
  29.3 3.2 %collective-permute-done.5.refs_18_ = f32[288,128]{1,0:T(8,128)S(1)} collective-permute-done((f32[288,128]{1,0:T(8,128)S(1)}, f32[288,128]{1,0:T(8,128)S(1)}, u32[]{:S(2)}, u32[]{:S(2)}) %collective-permute-start.5) | collective-permute-done | bytes 147488 | tf_op jit(solution)/shard_map/ppermute | solution.py:320
  32.5 0.0 collective-permute-start.8
  32.5 0.0 collective-permute-done.13.refs_10_
  32.5 0.5 collective-permute-start.9
  33.0 0.0 collective-permute-done.12.refs_19_
  33.0 0.1 collective-permute-start.10
  33.1 0.7 %collective-permute-done.15.refs_14_ = f32[256,128]{1,0:T(8,128)S(1)} collective-permute-done((f32[256,128]{1,0:T(8,128)S(1)}, f32[256,128]{1,0:T(8,128)S(1)}, u32[]{:S(2)}, u32[]{:S(2)}) %collective-permute-start.15) | collective-permute-done | bytes 131104 | tf_op jit(solution)/shard_map/ppermute | solution.py:320
  33.8 0.0 collective-permute-start.11
  33.8 0.3 collective-permute-done.20.refs_17_
  34.1 0.2 collective-permute-start.16
  34.3 0.0 collective-permute-done.8.refs_1_
  34.3 0.3 collective-permute-start.17
  34.6 0.0 collective-permute-done.9.refs_3_
  34.6 0.2 collective-permute-start.18
  34.8 0.0 collective-permute-done.10.refs_5_
  34.8 0.3 collective-permute-start.19
  35.1 0.0 collective-permute-done.11.refs_7_
  35.1 0.3 collective-permute-done.16.refs_9_
  35.5 0.2 collective-permute-done.17.refs_11_
  35.6 0.3 collective-permute-done.18.refs_13_
  36.0 0.2 collective-permute-done.19.refs_15_
  36.2 0.0 copy-done.4
  36.2 20.0 %trace.1 = (f32[1024,128]{1,0:T(8,128)}, f32[2048,128]{1,0:T(8,128)}) custom-call(s32[1]{0:T(128)} %bitcast.me_ref, f32[4]{0:T(128)S(1)} %copy-done.4, f32[256,128]{1,0:T(8,128)S(1)} %get-tuple-element.42.refs_0_, f32[256,128]{1,0:T(8,128)S(1)} %collective-permute-done.8.refs_1_, f32[256,128]{1,0:T(8,128)S(1)} %collective-permute-done.6.refs_2_, ...), custom_call_target="tpu_custom_call" | custom-call | tf_op jit(solution)/shard_map/trace/pallas_call | solution.py:296
  (7 shorter events, 0.1 us)
Async XLA Ops:
  0.6 0.7 %copy-start.2 = (s32[4,128]{1,0:T(4,128)S(1)}, s32[4,128]{1,0:T(4,128)}, u32[]{:S(2)}) copy-start(s32[4,128]{1,0:T(4,128)} %ids_ref.1) | copy-start | bytes 6148
  0.6 0.7 %copy-start.3 = (s32[128,1]{0,1:T(1,128)S(1)}, s32[128,1]{0,1:T(1,128)}, u32[]{:S(2)}) copy-start(s32[128,1]{0,1:T(1,128)} %param.9) | copy-start | bytes 1540
  1.3 1.0 %copy-start = (f32[128,2,256]{2,1,0:T(2,128)S(1)}, f32[128,2,256]{2,1,0:T(2,128)}, u32[]{:S(2)}) copy-start(f32[128,2,256]{2,1,0:T(2,128)} %param.7) | copy-start | bytes 786436
  2.3 0.9 %copy-start.1 = (f32[4,8,1024]{2,1,0:T(8,128)S(1)}, f32[4,8,1024]{2,1,0:T(8,128)}, u32[]{:S(2)}) copy-start(f32[4,8,1024]{2,1,0:T(8,128)} %src_ref.1) | copy-start | bytes 393220
  3.7 10.5 %collective-permute-start.3 = (f32[256,128]{1,0:T(8,128)S(1)}, f32[256,128]{1,0:T(8,128)S(1)}, u32[]{:S(2)}, u32[]{:S(2)}) collective-permute-start(f32[256,128]{1,0:T(8,128)S(1)} %get-tuple-element.42.refs_0_), channel_id=1, source_target_pairs={{0,8},{1,9},{2,10},{3,11},{4,12},{5,13},{6,14},{7,15},{8,0},{9,1},... | collective-permute-start | bytes 393224 | tf_op jit(solution)/shard_map/ppermute | solution.py:320
  7.8 7.1 %collective-permute-start = (f32[288,128]{1,0:T(8,128)S(1)}, f32[288,128]{1,0:T(8,128)S(1)}, u32[]{:S(2)}, u32[]{:S(2)}) collective-permute-start(f32[288,128]{1,0:T(8,128)S(1)} %get-tuple-element.31), channel_id=1, source_target_pairs={{0,1},{1,0},{2,3},{3,2},{4,5},{5,4},{6,7},{7,6},{8,9},{9,8},{10,11... | collective-permute-start | bytes 442376 | tf_op jit(solution)/shard_map/ppermute | solution.py:320
  7.8 7.1 %collective-permute-start.1 = (f32[288,128]{1,0:T(8,128)S(1)}, f32[288,128]{1,0:T(8,128)S(1)}, u32[]{:S(2)}, u32[]{:S(2)}) collective-permute-start(f32[288,128]{1,0:T(8,128)S(1)} %get-tuple-element.32), channel_id=1, source_target_pairs={{0,2},{1,3},{2,0},{3,1},{4,6},{5,7},{6,4},{7,5},{8,10},{9,11},{10,... | collective-permute-start | bytes 442376 | tf_op jit(solution)/shard_map/ppermute | solution.py:320
  9.3 7.5 %collective-permute-start.2 = (f32[288,128]{1,0:T(8,128)S(1)}, f32[288,128]{1,0:T(8,128)S(1)}, u32[]{:S(2)}, u32[]{:S(2)}) collective-permute-start(f32[288,128]{1,0:T(8,128)S(1)} %get-tuple-element.33), channel_id=1, source_target_pairs={{0,3},{1,2},{2,1},{3,0},{4,7},{5,6},{6,5},{7,4},{8,11},{9,10},{10,... | collective-permute-start | bytes 442376 | tf_op jit(solution)/shard_map/ppermute | solution.py:320
  9.6 7.3 %collective-permute-start.4 = (f32[256,128]{1,0:T(8,128)S(1)}, f32[256,128]{1,0:T(8,128)S(1)}, u32[]{:S(2)}, u32[]{:S(2)}) collective-permute-start(f32[256,128]{1,0:T(8,128)S(1)} %get-tuple-element.42.refs_0_), channel_id=1, source_target_pairs={{0,4},{1,5},{2,6},{3,7},{4,0},{5,1},{6,2},{7,3},{8,12},{9,13},{10,... | collective-permute-start | bytes 393224 | tf_op jit(solution)/shard_map/ppermute | solution.py:320
  14.2 8.7 %collective-permute-start.14 = (f32[256,128]{1,0:T(8,128)S(1)}, f32[256,128]{1,0:T(8,128)S(1)}, u32[]{:S(2)}, u32[]{:S(2)}) collective-permute-start(f32[256,128]{1,0:T(8,128)S(1)} %collective-permute-done.3.refs_8_), channel_id=1, source_target_pairs={{0,4},{1,5},{2,6},{3,7},{4,0},{5,1},{6,2},{7,3},{8,12},{9,13},{10,... | collective-permute-start | bytes 393224 | tf_op jit(solution)/shard_map/ppermute | solution.py:320
  17.0 19.2 %copy-start.4 = (f32[4]{0:T(128)S(1)}, f32[4]{0:T(128)}, u32[]{:S(2)}) copy-start(f32[4]{0:T(128)} %lens_ref.1) | copy-start | bytes 52
  17.0 7.4 %collective-permute-start.6 = (f32[256,128]{1,0:T(8,128)S(1)}, f32[256,128]{1,0:T(8,128)S(1)}, u32[]{:S(2)}, u32[]{:S(2)}) collective-permute-start(f32[256,128]{1,0:T(8,128)S(1)} %get-tuple-element.42.refs_0_), channel_id=1, source_target_pairs={{0,2},{1,3},{2,0},{3,1},{4,6},{5,7},{6,4},{7,5},{8,10},{9,11},{10,... | collective-permute-start | bytes 393224 | tf_op jit(solution)/shard_map/ppermute | solution.py:320
  18.5 14.0 %collective-permute-start.5 = (f32[288,128]{1,0:T(8,128)S(1)}, f32[288,128]{1,0:T(8,128)S(1)}, u32[]{:S(2)}, u32[]{:S(2)}) collective-permute-start(f32[288,128]{1,0:T(8,128)S(1)} %get-tuple-element.39), channel_id=1, source_target_pairs={{0,8},{1,9},{2,10},{3,11},{4,12},{5,13},{6,14},{7,15},{8,0},{9,1},... | collective-permute-start | bytes 442376 | tf_op jit(solution)/shard_map/ppermute | solution.py:320
  20.0 13.1 %collective-permute-start.12 = (f32[288,128]{1,0:T(8,128)S(1)}, f32[288,128]{1,0:T(8,128)S(1)}, u32[]{:S(2)}, u32[]{:S(2)}) collective-permute-start(f32[288,128]{1,0:T(8,128)S(1)} %get-tuple-element.46), channel_id=1, source_target_pairs={{0,12},{1,13},{2,14},{3,15},{4,8},{5,9},{6,10},{7,11},{8,4},{9,5},... | collective-permute-start | bytes 442376 | tf_op jit(solution)/shard_map/ppermute | solution.py:320
  22.4 6.4 %collective-permute-start.7 = (f32[256,128]{1,0:T(8,128)S(1)}, f32[256,128]{1,0:T(8,128)S(1)}, u32[]{:S(2)}, u32[]{:S(2)}) collective-permute-start(f32[256,128]{1,0:T(8,128)S(1)} %collective-permute-done.4.refs_4_), channel_id=1, source_target_pairs={{0,2},{1,3},{2,0},{3,1},{4,6},{5,7},{6,4},{7,5},{8,10},{9,11},{10,... | collective-permute-start | bytes 393224 | tf_op jit(solution)/shard_map/ppermute | solution.py:320
  22.9 9.6 %collective-permute-start.13 = (f32[256,128]{1,0:T(8,128)S(1)}, f32[256,128]{1,0:T(8,128)S(1)}, u32[]{:S(2)}, u32[]{:S(2)}) collective-permute-start(f32[256,128]{1,0:T(8,128)S(1)} %collective-permute-done.3.refs_8_), channel_id=1, source_target_pairs={{0,2},{1,3},{2,0},{3,1},{4,6},{5,7},{6,4},{7,5},{8,10},{9,11},{10,... | collective-permute-start | bytes 393224 | tf_op jit(solution)/shard_map/ppermute | solution.py:320
  24.4 9.7 %collective-permute-start.20 = (f32[288,128]{1,0:T(8,128)S(1)}, f32[288,128]{1,0:T(8,128)S(1)}, u32[]{:S(2)}, u32[]{:S(2)}) collective-permute-start(f32[288,128]{1,0:T(8,128)S(1)} %get-tuple-element.53), channel_id=1, source_target_pairs={{0,4},{1,5},{2,6},{3,7},{4,0},{5,1},{6,2},{7,3},{8,12},{9,13},{10,... | collective-permute-start | bytes 442376 | tf_op jit(solution)/shard_map/ppermute | solution.py:320
  28.8 5.0 %collective-permute-start.15 = (f32[256,128]{1,0:T(8,128)S(1)}, f32[256,128]{1,0:T(8,128)S(1)}, u32[]{:S(2)}, u32[]{:S(2)}) collective-permute-start(f32[256,128]{1,0:T(8,128)S(1)} %collective-permute-done.14.refs_12_), channel_id=1, source_target_pairs={{0,2},{1,3},{2,0},{3,1},{4,6},{5,7},{6,4},{7,5},{8,10},{9,11},{10,... | collective-permute-start | bytes 393224 | tf_op jit(solution)/shard_map/ppermute | solution.py:320
  32.5 1.8 %collective-permute-start.8 = (f32[256,128]{1,0:T(8,128)S(1)}, f32[256,128]{1,0:T(8,128)S(1)}, u32[]{:S(2)}, u32[]{:S(2)}) collective-permute-start(f32[256,128]{1,0:T(8,128)S(1)} %get-tuple-element.42.refs_0_), channel_id=1, source_target_pairs={{0,1},{1,0},{2,3},{3,2},{4,5},{5,4},{6,7},{7,6},{8,9},{9,8},{10,11... | collective-permute-start | bytes 393224 | tf_op jit(solution)/shard_map/ppermute | solution.py:320
  32.5 2.1 %collective-permute-start.9 = (f32[256,128]{1,0:T(8,128)S(1)}, f32[256,128]{1,0:T(8,128)S(1)}, u32[]{:S(2)}, u32[]{:S(2)}) collective-permute-start(f32[256,128]{1,0:T(8,128)S(1)} %collective-permute-done.6.refs_2_), channel_id=1, source_target_pairs={{0,1},{1,0},{2,3},{3,2},{4,5},{5,4},{6,7},{7,6},{8,9},{9,8},{10,11... | collective-permute-start | bytes 393224 | tf_op jit(solution)/shard_map/ppermute | solution.py:320
  33.0 1.8 %collective-permute-start.10 = (f32[256,128]{1,0:T(8,128)S(1)}, f32[256,128]{1,0:T(8,128)S(1)}, u32[]{:S(2)}, u32[]{:S(2)}) collective-permute-start(f32[256,128]{1,0:T(8,128)S(1)} %collective-permute-done.4.refs_4_), channel_id=1, source_target_pairs={{0,1},{1,0},{2,3},{3,2},{4,5},{5,4},{6,7},{7,6},{8,9},{9,8},{10,11... | collective-permute-start | bytes 393224 | tf_op jit(solution)/shard_map/ppermute | solution.py:320
  33.8 1.4 %collective-permute-start.11 = (f32[256,128]{1,0:T(8,128)S(1)}, f32[256,128]{1,0:T(8,128)S(1)}, u32[]{:S(2)}, u32[]{:S(2)}) collective-permute-start(f32[256,128]{1,0:T(8,128)S(1)} %collective-permute-done.7.refs_6_), channel_id=1, source_target_pairs={{0,1},{1,0},{2,3},{3,2},{4,5},{5,4},{6,7},{7,6},{8,9},{9,8},{10,11... | collective-permute-start | bytes 393224 | tf_op jit(solution)/shard_map/ppermute | solution.py:320
  34.1 1.3 %collective-permute-start.16 = (f32[256,128]{1,0:T(8,128)S(1)}, f32[256,128]{1,0:T(8,128)S(1)}, u32[]{:S(2)}, u32[]{:S(2)}) collective-permute-start(f32[256,128]{1,0:T(8,128)S(1)} %collective-permute-done.3.refs_8_), channel_id=1, source_target_pairs={{0,1},{1,0},{2,3},{3,2},{4,5},{5,4},{6,7},{7,6},{8,9},{9,8},{10,11... | collective-permute-start | bytes 393224 | tf_op jit(solution)/shard_map/ppermute | solution.py:320
  34.3 1.4 %collective-permute-start.17 = (f32[256,128]{1,0:T(8,128)S(1)}, f32[256,128]{1,0:T(8,128)S(1)}, u32[]{:S(2)}, u32[]{:S(2)}) collective-permute-start(f32[256,128]{1,0:T(8,128)S(1)} %collective-permute-done.13.refs_10_), channel_id=1, source_target_pairs={{0,1},{1,0},{2,3},{3,2},{4,5},{5,4},{6,7},{7,6},{8,9},{9,8},{10,11... | collective-permute-start | bytes 393224 | tf_op jit(solution)/shard_map/ppermute | solution.py:320
  34.6 1.3 %collective-permute-start.18 = (f32[256,128]{1,0:T(8,128)S(1)}, f32[256,128]{1,0:T(8,128)S(1)}, u32[]{:S(2)}, u32[]{:S(2)}) collective-permute-start(f32[256,128]{1,0:T(8,128)S(1)} %collective-permute-done.14.refs_12_), channel_id=1, source_target_pairs={{0,1},{1,0},{2,3},{3,2},{4,5},{5,4},{6,7},{7,6},{8,9},{9,8},{10,11... | collective-permute-start | bytes 393224 | tf_op jit(solution)/shard_map/ppermute | solution.py:320
  34.8 1.4 %collective-permute-start.19 = (f32[256,128]{1,0:T(8,128)S(1)}, f32[256,128]{1,0:T(8,128)S(1)}, u32[]{:S(2)}, u32[]{:S(2)}) collective-permute-start(f32[256,128]{1,0:T(8,128)S(1)} %collective-permute-done.15.refs_14_), channel_id=1, source_target_pairs={{0,1},{1,0},{2,3},{3,2},{4,5},{5,4},{6,7},{7,6},{8,9},{9,8},{10,11... | collective-permute-start | bytes 393224 | tf_op jit(solution)/shard_map/ppermute | solution.py:320

commit v12 on v11

--- a/solution.py
+++ b/solution.py
@@ -128,7 +128,6 @@
         out_shape=[own] + [part] * NEAR,
         in_specs=[pl.BlockSpec(memory_space=pltpu.SMEM)] + [pl.BlockSpec(memory_space=pltpu.VMEM)] * 4,
         out_specs=[pl.BlockSpec(memory_space=pltpu.VMEM)] * (1 + NEAR),
-        compiler_params=pltpu.CompilerParams(vmem_limit_bytes=16 * 1024 * 1024),
         name="prepare",
     )(me, dest, ids, rays, potential)
     return own, sent
@@ -226,27 +225,24 @@
     me = me_ref[0]
     slots = n_sky * each
     rows = tile_refs[0].shape[0]
-    copies = []
+    numbers = []
     for s in range(n_sky):
         source = me ^ s
         got_ref, first = got_refs[s // NEAR], s % NEAR * size
-        copies.append((
-            pltpu.make_async_copy(
-                got_ref.at[pl.ds(first + 4 * each, SUB), :],
-                places.at[pl.ds(source * SUB, SUB), :],
-                sems.at[0, s]),
-            pltpu.make_async_copy(tile_refs[s], tiles.at[pl.ds(s * rows, rows), :], sems.at[1, s]),
-            pltpu.make_async_copy(
-                got_ref.at[pl.ds(first, 4 * each), :],
-                rays.at[pl.ds(source * 4 * each, 4 * each), :],
-                sems.at[2, s]),
-        ))
-    for kind in (1, 0, 2):
-        for s in range(n_sky):
-            copies[s][kind].start()
-    for kind in (0, 2, 1):
-        for s in range(n_sky):
-            copies[s][kind].wait()
+        copy = pltpu.make_async_copy(
+            got_ref.at[pl.ds(first + 4 * each, SUB), :],
+            places.at[pl.ds(source * SUB, SUB), :],
+            sems.at[s])
+        copy.start()
+        numbers.append(copy)
+    for s in range(n_sky):
+        source = me ^ s
+        got_ref, first = got_refs[s // NEAR], s % NEAR * size
+        block = pl.ds(pl.multiple_of(source * (4 * each), SUB), 4 * each)
+        rays[block, :] = got_ref[pl.ds(first, 4 * each), :]
+        tiles[pl.ds(s * rows, rows), :] = tile_refs[s][...]
+    for copy in numbers:
+        copy.wait()
 
     def body(step, carry):
         chains = []
@@ -299,7 +295,7 @@
             jax.ShapeDtypeStruct((slots * 4, LANES), jnp.float32),
             jax.ShapeDtypeStruct((slots * 8, LANES), jnp.float32),
         ),
-        in_specs=[pl.BlockSpec(memory_space=pltpu.SMEM)] * 2 + [pl.BlockSpec(memory_space=pl.ANY)] * (n_sky + len(got)),
+        in_specs=[pl.BlockSpec(memory_space=pltpu.SMEM)] * 2 + [pl.BlockSpec(memory_space=pltpu.VMEM)] * (n_sky + len(got)),
         out_specs=(
             pl.BlockSpec(memory_space=pltpu.VMEM),
             pl.BlockSpec(memory_space=pltpu.VMEM),
@@ -309,7 +305,7 @@
             pltpu.VMEM((planes * together * CHUNKS * SUB, LANES), jnp.float32),
             pltpu.VMEM((slots * 4, LANES), jnp.float32),
             pltpu.SMEM((n_sky * SUB, LANES), jnp.float32),
-            pltpu.SemaphoreType.DMA((3, n_sky)),
+            pltpu.SemaphoreType.DMA((n_sky,)),
         ],
         compiler_params=pltpu.CompilerParams(vmem_limit_bytes=20 * 1024 * 1024),
         name="trace",

time: 56.4 us -> 54.3 us (0.963)
  Pallas kernels: 20.6 us -> 19.2 us
  local copies, waits for them, and re-layouts: 2.53 us -> 1.76 us
    pallas_call x1, Pallas kernels: 20 us -> 16.8 us  [trace(): pl.pallas_call(functools.partial(trace_kernel, n_sky, each, planes, toget...]
    pallas_call x1, Pallas kernels: 0.55 us -> 2.37 us  [prepare(): pl.pallas_call(functools.partial(prepare_kernel, n_sky, each), out_shape=...]
    unnamed x10 -> x6, local copies, waits for them, and re-layouts: 2.53 us -> 1.76 us
  transfers between devices with their start and end apart: 21 -> 21, of which waited for: 11 -> 10; matrix products, arithmetic and copies ran while one was open for 0% -> 0% of each run, Pallas kernels for 0% -> 0%
where the time goes in v12:
time: 54.3 us; the launch traced here: 54.1 us
  Pallas kernels  19.2 us (35%)
  starting transfers between devices  18.2 us (34%)
  waiting for transfers between devices  14.3 us (26%)
  local copies, waits for them, and re-layouts  1.76 us (3%)
  between operations  0.68 us (1%)
    ppermute x21, starting transfers between devices, flipped(): return lax.ppermute(value, 'sky', [(i, i ^ bits) for i in range(n_sky)])  18.2 us
    pallas_call x1, Pallas kernels, trace(): pl.pallas_call(functools.partial(trace_kernel, n_sky, each, planes, toget...  16.8 us
    ppermute x21, waiting for transfers between devices, flipped(): return lax.ppermute(value, 'sky', [(i, i ^ bits) for i in range(n_sky)])  14.3 us
    pallas_call x1, Pallas kernels, prepare(): pl.pallas_call(functools.partial(prepare_kernel, n_sky, each), out_shape=...  2.37 us
    unnamed x6, local copies, waits for them, and re-layouts  1.76 us
  transfers between devices with their start and end apart: 21, of which 10 were waited for; matrix products, arithmetic and copies ran while one was open for 0% of the time, Pallas kernels for 0%

profile of v12, /device:TPU:0, one launch (start us, length us, event | category | flops | bytes accessed | tf_op | source)
XLA Modules:
  0.0 54.1 jit_solution(457900732566356860)
XLA Ops:
  0.6 2.4 %prepare.1 = (f32[256,128]{1,0:T(8,128)}, f32[288,128]{1,0:T(8,128)}, f32[288,128]{1,0:T(8,128)}, f32[288,128]{1,0:T(8,128)}, f32[288,128]{1,0:T(8,128)}) custom-call(s32[1]{0:T(128)} %bitcast.me_ref, s32[1,128]{1,0:T(1,128)} %bitcast.18, s32[4,128]{1,0:T(4,128)} %ids_ref.1, f32[512,128]{1,0:T(8,128)} %bitcast.17, f32[4,8,1024]{2,1,0:T(8,128)} %src_ref.1), custom_call_target="tpu_custom_call" | custom-call | tf_op jit(solution)/shard_map/prepare/pallas_call | solution.py:126
  3.0 4.0 %collective-permute-start.3 = (f32[256,128]{1,0:T(8,128)}, f32[256,128]{1,0:T(8,128)S(1)}, u32[]{:S(2)}, u32[]{:S(2)}) collective-permute-start(f32[256,128]{1,0:T(8,128)} %get-tuple-element.42.refs_0_), channel_id=1, source_target_pairs={{0,8},{1,9},{2,10},{3,11},{4,12},{5,13},{6,14},{7,15},{8,0},{9,1},... | collective-permute-start | bytes 393224 | tf_op jit(solution)/shard_map/ppermute | solution.py:316
  7.0 0.0 collective-permute-start
  7.0 1.5 %collective-permute-start.1 = (f32[288,128]{1,0:T(8,128)}, f32[288,128]{1,0:T(8,128)S(1)}, u32[]{:S(2)}, u32[]{:S(2)}) collective-permute-start(f32[288,128]{1,0:T(8,128)} %get-tuple-element.32), channel_id=1, source_target_pairs={{0,2},{1,3},{2,0},{3,1},{4,6},{5,7},{6,4},{7,5},{8,10},{9,11},{10,... | collective-permute-start | bytes 442376 | tf_op jit(solution)/shard_map/ppermute | solution.py:316
  8.6 0.3 collective-permute-start.2
  8.9 1.6 %collective-permute-start.4 = (f32[256,128]{1,0:T(8,128)}, f32[256,128]{1,0:T(8,128)S(1)}, u32[]{:S(2)}, u32[]{:S(2)}) collective-permute-start(f32[256,128]{1,0:T(8,128)} %get-tuple-element.42.refs_0_), channel_id=1, source_target_pairs={{0,4},{1,5},{2,6},{3,7},{4,0},{5,1},{6,2},{7,3},{8,12},{9,13},{10,... | collective-permute-start | bytes 393224 | tf_op jit(solution)/shard_map/ppermute | solution.py:316
  10.5 3.2 %collective-permute-done.3.refs_8_ = f32[256,128]{1,0:T(8,128)S(1)} collective-permute-done((f32[256,128]{1,0:T(8,128)}, f32[256,128]{1,0:T(8,128)S(1)}, u32[]{:S(2)}, u32[]{:S(2)}) %collective-permute-start.3) | collective-permute-done | bytes 131104 | tf_op jit(solution)/shard_map/ppermute | solution.py:316
  13.7 0.8 %collective-permute-start.14 = (f32[256,128]{1,0:T(8,128)S(1)}, f32[256,128]{1,0:T(8,128)S(1)}, u32[]{:S(2)}, u32[]{:S(2)}) collective-permute-start(f32[256,128]{1,0:T(8,128)S(1)} %collective-permute-done.3.refs_8_), channel_id=1, source_target_pairs={{0,4},{1,5},{2,6},{3,7},{4,0},{5,1},{6,2},{7,3},{8,12},{9,13},{10,... | collective-permute-start | bytes 393224 | tf_op jit(solution)/shard_map/ppermute | solution.py:316
  14.4 0.0 collective-permute-done.refs_1_
  14.4 0.0 collective-permute-done.1.refs_2_
  14.4 1.8 %collective-permute-done.2.refs_3_ = f32[288,128]{1,0:T(8,128)S(1)} collective-permute-done((f32[288,128]{1,0:T(8,128)}, f32[288,128]{1,0:T(8,128)S(1)}, u32[]{:S(2)}, u32[]{:S(2)}) %collective-permute-start.2) | collective-permute-done | bytes 147488 | tf_op jit(solution)/shard_map/ppermute | solution.py:316
  16.3 0.9 %copy-done = f32[288,128]{1,0:T(8,128)S(1)} copy-done((f32[288,128]{1,0:T(8,128)S(1)}, f32[288,128]{1,0:T(8,128)}, u32[]{:S(2)}) %copy-start) | copy-done | bytes 147480
  17.2 0.0 collective-permute-done.4.refs_4_
  17.3 0.0 copy-start.2
  17.3 0.8 %copy-done.1 = f32[256,128]{1,0:T(8,128)S(1)} copy-done((f32[256,128]{1,0:T(8,128)S(1)}, f32[256,128]{1,0:T(8,128)}, u32[]{:S(2)}) %copy-start.1) | copy-done | bytes 131096
  18.1 1.5 %collective-permute-start.6 = (f32[256,128]{1,0:T(8,128)S(1)}, f32[256,128]{1,0:T(8,128)S(1)}, u32[]{:S(2)}, u32[]{:S(2)}) collective-permute-start(f32[256,128]{1,0:T(8,128)S(1)} %copy-done.1), channel_id=1, source_target_pairs={{0,2},{1,3},{2,0},{3,1},{4,6},{5,7},{6,4},{7,5},{8,10},{9,11},{10,... | collective-permute-start | bytes 393224 | tf_op jit(solution)/shard_map/ppermute | solution.py:316
  19.6 1.5 %collective-permute-start.5 = (f32[288,128]{1,0:T(8,128)S(1)}, f32[288,128]{1,0:T(8,128)S(1)}, u32[]{:S(2)}, u32[]{:S(2)}) collective-permute-start(f32[288,128]{1,0:T(8,128)S(1)} %get-tuple-element.39), channel_id=1, source_target_pairs={{0,8},{1,9},{2,10},{3,11},{4,12},{5,13},{6,14},{7,15},{8,0},{9,1},... | collective-permute-start | bytes 442376 | tf_op jit(solution)/shard_map/ppermute | solution.py:316
  21.1 2.4 %collective-permute-start.12 = (f32[288,128]{1,0:T(8,128)S(1)}, f32[288,128]{1,0:T(8,128)S(1)}, u32[]{:S(2)}, u32[]{:S(2)}) collective-permute-start(f32[288,128]{1,0:T(8,128)S(1)} %get-tuple-element.46), channel_id=1, source_target_pairs={{0,12},{1,13},{2,14},{3,15},{4,8},{5,9},{6,10},{7,11},{8,4},{9,5},... | collective-permute-start | bytes 442376 | tf_op jit(solution)/shard_map/ppermute | solution.py:316
  23.6 0.5 collective-permute-start.7
  24.1 0.0 collective-permute-done.14.refs_12_
  24.1 1.5 %collective-permute-start.13 = (f32[256,128]{1,0:T(8,128)S(1)}, f32[256,128]{1,0:T(8,128)S(1)}, u32[]{:S(2)}, u32[]{:S(2)}) collective-permute-start(f32[256,128]{1,0:T(8,128)S(1)} %collective-permute-done.3.refs_8_), channel_id=1, source_target_pairs={{0,2},{1,3},{2,0},{3,1},{4,6},{5,7},{6,4},{7,5},{8,10},{9,11},{10,... | collective-permute-start | bytes 393224 | tf_op jit(solution)/shard_map/ppermute | solution.py:316
  25.6 0.0 collective-permute-done.6.refs_2_
  25.6 0.4 collective-permute-start.20
  26.0 4.0 %collective-permute-done.7.refs_6_ = f32[256,128]{1,0:T(8,128)S(1)} collective-permute-done((f32[256,128]{1,0:T(8,128)S(1)}, f32[256,128]{1,0:T(8,128)S(1)}, u32[]{:S(2)}, u32[]{:S(2)}) %collective-permute-start.7) | collective-permute-done | bytes 131104 | tf_op jit(solution)/shard_map/ppermute | solution.py:316
  30.0 0.5 collective-permute-start.15
  30.5 3.1 %collective-permute-done.5.refs_18_ = f32[288,128]{1,0:T(8,128)S(1)} collective-permute-done((f32[288,128]{1,0:T(8,128)S(1)}, f32[288,128]{1,0:T(8,128)S(1)}, u32[]{:S(2)}, u32[]{:S(2)}) %collective-permute-start.5) | collective-permute-done | bytes 147488 | tf_op jit(solution)/shard_map/ppermute | solution.py:316
  33.6 0.0 collective-permute-start.8
  33.6 0.0 collective-permute-done.13.refs_10_
  33.6 0.5 collective-permute-start.9
  34.1 0.0 collective-permute-done.12.refs_19_
  34.1 0.1 collective-permute-start.10
  34.2 0.7 %collective-permute-done.15.refs_14_ = f32[256,128]{1,0:T(8,128)S(1)} collective-permute-done((f32[256,128]{1,0:T(8,128)S(1)}, f32[256,128]{1,0:T(8,128)S(1)}, u32[]{:S(2)}, u32[]{:S(2)}) %collective-permute-start.15) | collective-permute-done | bytes 131104 | tf_op jit(solution)/shard_map/ppermute | solution.py:316
  34.9 0.0 collective-permute-start.11
  34.9 0.3 collective-permute-done.20.refs_17_
  35.3 0.2 collective-permute-start.16
  35.5 0.0 collective-permute-done.8.refs_1_
  35.5 0.3 collective-permute-start.17
  35.8 0.0 collective-permute-done.9.refs_3_
  35.8 0.2 collective-permute-start.18
  36.0 0.0 collective-permute-done.10.refs_5_
  36.0 0.3 collective-permute-start.19
  36.3 0.0 collective-permute-done.11.refs_7_
  36.3 0.3 collective-permute-done.16.refs_9_
  36.6 0.2 collective-permute-done.17.refs_11_
  36.8 0.3 collective-permute-done.18.refs_13_
  37.1 0.2 collective-permute-done.19.refs_15_
  37.3 0.0 copy-done.2
  37.3 16.8 %trace.1 = (f32[1024,128]{1,0:T(8,128)}, f32[2048,128]{1,0:T(8,128)}) custom-call(s32[1]{0:T(128)} %bitcast.me_ref, f32[4]{0:T(128)S(1)} %copy-done.2, f32[256,128]{1,0:T(8,128)S(1)} %copy-done.1, f32[256,128]{1,0:T(8,128)S(1)} %collective-permute-done.8.refs_1_, f32[256,128]{1,0:T(8,128)S(1)} %collective-permute-done.6.refs_2_, ...), custom_call_target="tpu_custom_call" | custom-call | tf_op jit(solution)/shard_map/trace/pallas_call | solution.py:292
  (3 shorter events, 0.0 us)
Async XLA Ops:
  3.0 10.7 %collective-permute-start.3 = (f32[256,128]{1,0:T(8,128)}, f32[256,128]{1,0:T(8,128)S(1)}, u32[]{:S(2)}, u32[]{:S(2)}) collective-permute-start(f32[256,128]{1,0:T(8,128)} %get-tuple-element.42.refs_0_), channel_id=1, source_target_pairs={{0,8},{1,9},{2,10},{3,11},{4,12},{5,13},{6,14},{7,15},{8,0},{9,1},... | collective-permute-start | bytes 393224 | tf_op jit(solution)/shard_map/ppermute | solution.py:316
  7.0 7.4 %collective-permute-start = (f32[288,128]{1,0:T(8,128)}, f32[288,128]{1,0:T(8,128)S(1)}, u32[]{:S(2)}, u32[]{:S(2)}) collective-permute-start(f32[288,128]{1,0:T(8,128)} %get-tuple-element.31), channel_id=1, source_target_pairs={{0,1},{1,0},{2,3},{3,2},{4,5},{5,4},{6,7},{7,6},{8,9},{9,8},{10,11... | collective-permute-start | bytes 442376 | tf_op jit(solution)/shard_map/ppermute | solution.py:316
  7.0 7.4 %collective-permute-start.1 = (f32[288,128]{1,0:T(8,128)}, f32[288,128]{1,0:T(8,128)S(1)}, u32[]{:S(2)}, u32[]{:S(2)}) collective-permute-start(f32[288,128]{1,0:T(8,128)} %get-tuple-element.32), channel_id=1, source_target_pairs={{0,2},{1,3},{2,0},{3,1},{4,6},{5,7},{6,4},{7,5},{8,10},{9,11},{10,... | collective-permute-start | bytes 442376 | tf_op jit(solution)/shard_map/ppermute | solution.py:316
  8.6 7.7 %collective-permute-start.2 = (f32[288,128]{1,0:T(8,128)}, f32[288,128]{1,0:T(8,128)S(1)}, u32[]{:S(2)}, u32[]{:S(2)}) collective-permute-start(f32[288,128]{1,0:T(8,128)} %get-tuple-element.33), channel_id=1, source_target_pairs={{0,3},{1,2},{2,1},{3,0},{4,7},{5,6},{6,5},{7,4},{8,11},{9,10},{10,... | collective-permute-start | bytes 442376 | tf_op jit(solution)/shard_map/ppermute | solution.py:316
  8.9 8.3 %collective-permute-start.4 = (f32[256,128]{1,0:T(8,128)}, f32[256,128]{1,0:T(8,128)S(1)}, u32[]{:S(2)}, u32[]{:S(2)}) collective-permute-start(f32[256,128]{1,0:T(8,128)} %get-tuple-element.42.refs_0_), channel_id=1, source_target_pairs={{0,4},{1,5},{2,6},{3,7},{4,0},{5,1},{6,2},{7,3},{8,12},{9,13},{10,... | collective-permute-start | bytes 393224 | tf_op jit(solution)/shard_map/ppermute | solution.py:316
  13.7 10.4 %collective-permute-start.14 = (f32[256,128]{1,0:T(8,128)S(1)}, f32[256,128]{1,0:T(8,128)S(1)}, u32[]{:S(2)}, u32[]{:S(2)}) collective-permute-start(f32[256,128]{1,0:T(8,128)S(1)} %collective-permute-done.3.refs_8_), channel_id=1, source_target_pairs={{0,4},{1,5},{2,6},{3,7},{4,0},{5,1},{6,2},{7,3},{8,12},{9,13},{10,... | collective-permute-start | bytes 393224 | tf_op jit(solution)/shard_map/ppermute | solution.py:316
  16.3 0.9 %copy-start = (f32[288,128]{1,0:T(8,128)S(1)}, f32[288,128]{1,0:T(8,128)}, u32[]{:S(2)}) copy-start(f32[288,128]{1,0:T(8,128)} %get-tuple-element.30.refs_0_) | copy-start | bytes 442372
  17.2 0.9 %copy-start.1 = (f32[256,128]{1,0:T(8,128)S(1)}, f32[256,128]{1,0:T(8,128)}, u32[]{:S(2)}) copy-start(f32[256,128]{1,0:T(8,128)} %get-tuple-element.42.refs_0_) | copy-start | bytes 393220
  17.3 20.1 %copy-start.2 = (f32[4]{0:T(128)S(1)}, f32[4]{0:T(128)}, u32[]{:S(2)}) copy-start(f32[4]{0:T(128)} %lens_ref.1) | copy-start | bytes 52
  18.1 7.5 %collective-permute-start.6 = (f32[256,128]{1,0:T(8,128)S(1)}, f32[256,128]{1,0:T(8,128)S(1)}, u32[]{:S(2)}, u32[]{:S(2)}) collective-permute-start(f32[256,128]{1,0:T(8,128)S(1)} %copy-done.1), channel_id=1, source_target_pairs={{0,2},{1,3},{2,0},{3,1},{4,6},{5,7},{6,4},{7,5},{8,10},{9,11},{10,... | collective-permute-start | bytes 393224 | tf_op jit(solution)/shard_map/ppermute | solution.py:316
  19.6 14.0 %collective-permute-start.5 = (f32[288,128]{1,0:T(8,128)S(1)}, f32[288,128]{1,0:T(8,128)S(1)}, u32[]{:S(2)}, u32[]{:S(2)}) collective-permute-start(f32[288,128]{1,0:T(8,128)S(1)} %get-tuple-element.39), channel_id=1, source_target_pairs={{0,8},{1,9},{2,10},{3,11},{4,12},{5,13},{6,14},{7,15},{8,0},{9,1},... | collective-permute-start | bytes 442376 | tf_op jit(solution)/shard_map/ppermute | solution.py:316
  21.1 13.0 %collective-permute-start.12 = (f32[288,128]{1,0:T(8,128)S(1)}, f32[288,128]{1,0:T(8,128)S(1)}, u32[]{:S(2)}, u32[]{:S(2)}) collective-permute-start(f32[288,128]{1,0:T(8,128)S(1)} %get-tuple-element.46), channel_id=1, source_target_pairs={{0,12},{1,13},{2,14},{3,15},{4,8},{5,9},{6,10},{7,11},{8,4},{9,5},... | collective-permute-start | bytes 442376 | tf_op jit(solution)/shard_map/ppermute | solution.py:316
  23.6 6.4 %collective-permute-start.7 = (f32[256,128]{1,0:T(8,128)S(1)}, f32[256,128]{1,0:T(8,128)S(1)}, u32[]{:S(2)}, u32[]{:S(2)}) collective-permute-start(f32[256,128]{1,0:T(8,128)S(1)} %collective-permute-done.4.refs_4_), channel_id=1, source_target_pairs={{0,2},{1,3},{2,0},{3,1},{4,6},{5,7},{6,4},{7,5},{8,10},{9,11},{10,... | collective-permute-start | bytes 393224 | tf_op jit(solution)/shard_map/ppermute | solution.py:316
  24.1 9.5 %collective-permute-start.13 = (f32[256,128]{1,0:T(8,128)S(1)}, f32[256,128]{1,0:T(8,128)S(1)}, u32[]{:S(2)}, u32[]{:S(2)}) collective-permute-start(f32[256,128]{1,0:T(8,128)S(1)} %collective-permute-done.3.refs_8_), channel_id=1, source_target_pairs={{0,2},{1,3},{2,0},{3,1},{4,6},{5,7},{6,4},{7,5},{8,10},{9,11},{10,... | collective-permute-start | bytes 393224 | tf_op jit(solution)/shard_map/ppermute | solution.py:316
  25.6 9.7 %collective-permute-start.20 = (f32[288,128]{1,0:T(8,128)S(1)}, f32[288,128]{1,0:T(8,128)S(1)}, u32[]{:S(2)}, u32[]{:S(2)}) collective-permute-start(f32[288,128]{1,0:T(8,128)S(1)} %get-tuple-element.53), channel_id=1, source_target_pairs={{0,4},{1,5},{2,6},{3,7},{4,0},{5,1},{6,2},{7,3},{8,12},{9,13},{10,... | collective-permute-start | bytes 442376 | tf_op jit(solution)/shard_map/ppermute | solution.py:316
  30.0 5.0 %collective-permute-start.15 = (f32[256,128]{1,0:T(8,128)S(1)}, f32[256,128]{1,0:T(8,128)S(1)}, u32[]{:S(2)}, u32[]{:S(2)}) collective-permute-start(f32[256,128]{1,0:T(8,128)S(1)} %collective-permute-done.14.refs_12_), channel_id=1, source_target_pairs={{0,2},{1,3},{2,0},{3,1},{4,6},{5,7},{6,4},{7,5},{8,10},{9,11},{10,... | collective-permute-start | bytes 393224 | tf_op jit(solution)/shard_map/ppermute | solution.py:316
  33.6 1.9 %collective-permute-start.8 = (f32[256,128]{1,0:T(8,128)S(1)}, f32[256,128]{1,0:T(8,128)S(1)}, u32[]{:S(2)}, u32[]{:S(2)}) collective-permute-start(f32[256,128]{1,0:T(8,128)S(1)} %copy-done.1), channel_id=1, source_target_pairs={{0,1},{1,0},{2,3},{3,2},{4,5},{5,4},{6,7},{7,6},{8,9},{9,8},{10,11... | collective-permute-start | bytes 393224 | tf_op jit(solution)/shard_map/ppermute | solution.py:316
  33.6 2.2 %collective-permute-start.9 = (f32[256,128]{1,0:T(8,128)S(1)}, f32[256,128]{1,0:T(8,128)S(1)}, u32[]{:S(2)}, u32[]{:S(2)}) collective-permute-start(f32[256,128]{1,0:T(8,128)S(1)} %collective-permute-done.6.refs_2_), channel_id=1, source_target_pairs={{0,1},{1,0},{2,3},{3,2},{4,5},{5,4},{6,7},{7,6},{8,9},{9,8},{10,11... | collective-permute-start | bytes 393224 | tf_op jit(solution)/shard_map/ppermute | solution.py:316
  34.1 1.9 %collective-permute-start.10 = (f32[256,128]{1,0:T(8,128)S(1)}, f32[256,128]{1,0:T(8,128)S(1)}, u32[]{:S(2)}, u32[]{:S(2)}) collective-permute-start(f32[256,128]{1,0:T(8,128)S(1)} %collective-permute-done.4.refs_4_), channel_id=1, source_target_pairs={{0,1},{1,0},{2,3},{3,2},{4,5},{5,4},{6,7},{7,6},{8,9},{9,8},{10,11... | collective-permute-start | bytes 393224 | tf_op jit(solution)/shard_map/ppermute | solution.py:316
  34.9 1.4 %collective-permute-start.11 = (f32[256,128]{1,0:T(8,128)S(1)}, f32[256,128]{1,0:T(8,128)S(1)}, u32[]{:S(2)}, u32[]{:S(2)}) collective-permute-start(f32[256,128]{1,0:T(8,128)S(1)} %collective-permute-done.7.refs_6_), channel_id=1, source_target_pairs={{0,1},{1,0},{2,3},{3,2},{4,5},{5,4},{6,7},{7,6},{8,9},{9,8},{10,11... | collective-permute-start | bytes 393224 | tf_op jit(solution)/shard_map/ppermute | solution.py:316
  35.3 1.3 %collective-permute-start.16 = (f32[256,128]{1,0:T(8,128)S(1)}, f32[256,128]{1,0:T(8,128)S(1)}, u32[]{:S(2)}, u32[]{:S(2)}) collective-permute-start(f32[256,128]{1,0:T(8,128)S(1)} %collective-permute-done.3.refs_8_), channel_id=1, source_target_pairs={{0,1},{1,0},{2,3},{3,2},{4,5},{5,4},{6,7},{7,6},{8,9},{9,8},{10,11... | collective-permute-start | bytes 393224 | tf_op jit(solution)/shard_map/ppermute | solution.py:316
  35.5 1.4 %collective-permute-start.17 = (f32[256,128]{1,0:T(8,128)S(1)}, f32[256,128]{1,0:T(8,128)S(1)}, u32[]{:S(2)}, u32[]{:S(2)}) collective-permute-start(f32[256,128]{1,0:T(8,128)S(1)} %collective-permute-done.13.refs_10_), channel_id=1, source_target_pairs={{0,1},{1,0},{2,3},{3,2},{4,5},{5,4},{6,7},{7,6},{8,9},{9,8},{10,11... | collective-permute-start | bytes 393224 | tf_op jit(solution)/shard_map/ppermute | solution.py:316
  35.8 1.3 %collective-permute-start.18 = (f32[256,128]{1,0:T(8,128)S(1)}, f32[256,128]{1,0:T(8,128)S(1)}, u32[]{:S(2)}, u32[]{:S(2)}) collective-permute-start(f32[256,128]{1,0:T(8,128)S(1)} %collective-permute-done.14.refs_12_), channel_id=1, source_target_pairs={{0,1},{1,0},{2,3},{3,2},{4,5},{5,4},{6,7},{7,6},{8,9},{9,8},{10,11... | collective-permute-start | bytes 393224 | tf_op jit(solution)/shard_map/ppermute | solution.py:316
  36.0 1.4 %collective-permute-start.19 = (f32[256,128]{1,0:T(8,128)S(1)}, f32[256,128]{1,0:T(8,128)S(1)}, u32[]{:S(2)}, u32[]{:S(2)}) collective-permute-start(f32[256,128]{1,0:T(8,128)S(1)} %collective-permute-done.15.refs_14_), channel_id=1, source_target_pairs={{0,1},{1,0},{2,3},{3,2},{4,5},{5,4},{6,7},{7,6},{8,9},{9,8},{10,11... | collective-permute-start | bytes 393224 | tf_op jit(solution)/shard_map/ppermute | solution.py:316

commit v13 on v12

--- a/solution.py
+++ b/solution.py
@@ -128,6 +128,7 @@
         out_shape=[own] + [part] * NEAR,
         in_specs=[pl.BlockSpec(memory_space=pltpu.SMEM)] + [pl.BlockSpec(memory_space=pltpu.VMEM)] * 4,
         out_specs=[pl.BlockSpec(memory_space=pltpu.VMEM)] * (1 + NEAR),
+        compiler_params=pltpu.CompilerParams(vmem_limit_bytes=16 * 1024 * 1024),
         name="prepare",
     )(me, dest, ids, rays, potential)
     return own, sent
@@ -347,7 +348,7 @@
     spread(held, n_sky, bits[:-1])
     half = len(got) // 2
     for mid, low in ((half, 0), (half + 1, n_sky // 2)):
-        some = range(low, low + n_sky // 2, 2)
+        some = range(low + n_sky // 2 - 2, low + n_sky // 2, 2)
         got[mid], *evens = lax.optimization_barrier((got[mid], *[held[s] for s in some]))
         held.update(zip(some, evens))
     spread(held, n_sky, bits)

time: 54.3 us -> 55.7 us (1.026)
  waiting for transfers between devices: 14.3 us -> 16.4 us
  Pallas kernels: 19.2 us -> 17.4 us
  local copies, waits for them, and re-layouts: 1.76 us -> 2.53 us
    ppermute x21, waiting for transfers between devices: 14.3 us -> 16.4 us  [flipped(): return lax.ppermute(value, 'sky', [(i, i ^ bits) for i in range(n_sky)])]
    pallas_call x1, Pallas kernels: 2.37 us -> 0.55 us  [prepare(): pl.pallas_call(functools.partial(prepare_kernel, n_sky, each), out_shape=...]
    unnamed x6 -> x10, local copies, waits for them, and re-layouts: 1.76 us -> 2.53 us
where the time goes in v13:
time: 55.7 us; the launch traced here: 55.5 us
  starting transfers between devices  18.5 us (33%)
  Pallas kernels  17.4 us (31%)
  waiting for transfers between devices  16.4 us (29%)
  local copies, waits for them, and re-layouts  2.53 us (5%)
  between operations  0.68 us (1%)
    ppermute x21, starting transfers between devices, flipped(): return lax.ppermute(value, 'sky', [(i, i ^ bits) for i in range(n_sky)])  18.5 us
    pallas_call x1, Pallas kernels, trace(): pl.pallas_call(functools.partial(trace_kernel, n_sky, each, planes, toget...  16.8 us
    ppermute x21, waiting for transfers between devices, flipped(): return lax.ppermute(value, 'sky', [(i, i ^ bits) for i in range(n_sky)])  16.4 us
    unnamed x10, local copies, waits for them, and re-layouts  2.53 us
  transfers between devices with their start and end apart: 21, of which 10 were waited for; matrix products, arithmetic and copies ran while one was open for 0% of the time, Pallas kernels for 0%

profile of v13, /device:TPU:0, one launch (start us, length us, event | category | flops | bytes accessed | tf_op | source)
XLA Modules:
  0.0 55.5 jit_solution(15128451139669874139)
XLA Ops:
  0.6 0.0 copy-start.2
  0.7 0.7 %copy-done.2 = s32[4,128]{1,0:T(4,128)S(1)} copy-done((s32[4,128]{1,0:T(4,128)S(1)}, s32[4,128]{1,0:T(4,128)}, u32[]{:S(2)}) %copy-start.2) | copy-done | bytes 2072
  1.3 0.9 %copy-done = f32[128,2,256]{2,1,0:T(2,128)S(1)} copy-done((f32[128,2,256]{2,1,0:T(2,128)S(1)}, f32[128,2,256]{2,1,0:T(2,128)}, u32[]{:S(2)}) %copy-start) | copy-done | bytes 262168
  2.3 0.9 %copy-done.1 = f32[4,8,1024]{2,1,0:T(8,128)S(1)} copy-done((f32[4,8,1024]{2,1,0:T(8,128)S(1)}, f32[4,8,1024]{2,1,0:T(8,128)}, u32[]{:S(2)}) %copy-start.1) | copy-done | bytes 131096
  3.2 0.5 prepare.1
  3.7 4.0 %collective-permute-start.3 = (f32[256,128]{1,0:T(8,128)S(1)}, f32[256,128]{1,0:T(8,128)S(1)}, u32[]{:S(2)}, u32[]{:S(2)}) collective-permute-start(f32[256,128]{1,0:T(8,128)S(1)} %get-tuple-element.33.refs_0_), channel_id=1, source_target_pairs={{0,8},{1,9},{2,10},{3,11},{4,12},{5,13},{6,14},{7,15},{8,0},{9,1},... | collective-permute-start | bytes 393224 | tf_op jit(solution)/shard_map/ppermute | solution.py:317
  7.8 0.0 collective-permute-start
  7.8 1.5 %collective-permute-start.1 = (f32[288,128]{1,0:T(8,128)S(1)}, f32[288,128]{1,0:T(8,128)S(1)}, u32[]{:S(2)}, u32[]{:S(2)}) collective-permute-start(f32[288,128]{1,0:T(8,128)S(1)} %get-tuple-element.26), channel_id=1, source_target_pairs={{0,2},{1,3},{2,0},{3,1},{4,6},{5,7},{6,4},{7,5},{8,10},{9,11},{10,... | collective-permute-start | bytes 442376 | tf_op jit(solution)/shard_map/ppermute | solution.py:317
  9.3 0.3 collective-permute-start.2
  9.6 1.6 %collective-permute-start.4 = (f32[256,128]{1,0:T(8,128)S(1)}, f32[256,128]{1,0:T(8,128)S(1)}, u32[]{:S(2)}, u32[]{:S(2)}) collective-permute-start(f32[256,128]{1,0:T(8,128)S(1)} %get-tuple-element.33.refs_0_), channel_id=1, source_target_pairs={{0,4},{1,5},{2,6},{3,7},{4,0},{5,1},{6,2},{7,3},{8,12},{9,13},{10,... | collective-permute-start | bytes 393224 | tf_op jit(solution)/shard_map/ppermute | solution.py:317
  11.2 3.0 %collective-permute-done.3.refs_8_ = f32[256,128]{1,0:T(8,128)S(1)} collective-permute-done((f32[256,128]{1,0:T(8,128)S(1)}, f32[256,128]{1,0:T(8,128)S(1)}, u32[]{:S(2)}, u32[]{:S(2)}) %collective-permute-start.3) | collective-permute-done | bytes 131104 | tf_op jit(solution)/shard_map/ppermute | solution.py:317
  14.2 0.7 %collective-permute-start.15 = (f32[256,128]{1,0:T(8,128)S(1)}, f32[256,128]{1,0:T(8,128)S(1)}, u32[]{:S(2)}, u32[]{:S(2)}) collective-permute-start(f32[256,128]{1,0:T(8,128)S(1)} %collective-permute-done.3.refs_8_), channel_id=1, source_target_pairs={{0,4},{1,5},{2,6},{3,7},{4,0},{5,1},{6,2},{7,3},{8,12},{9,13},{10,... | collective-permute-start | bytes 393224 | tf_op jit(solution)/shard_map/ppermute | solution.py:317
  14.8 0.0 collective-permute-done.refs_1_
  14.8 0.0 collective-permute-done.1.refs_2_
  14.9 2.0 %collective-permute-done.2.refs_3_ = f32[288,128]{1,0:T(8,128)S(1)} collective-permute-done((f32[288,128]{1,0:T(8,128)S(1)}, f32[288,128]{1,0:T(8,128)S(1)}, u32[]{:S(2)}, u32[]{:S(2)}) %collective-permute-start.2) | collective-permute-done | bytes 147488 | tf_op jit(solution)/shard_map/ppermute | solution.py:317
  16.9 0.1 collective-permute-done.4.refs_4_
  17.0 1.5 %collective-permute-start.9 = (f32[288,128]{1,0:T(8,128)S(1)}, f32[288,128]{1,0:T(8,128)S(1)}, u32[]{:S(2)}, u32[]{:S(2)}) collective-permute-start(f32[288,128]{1,0:T(8,128)S(1)} %get-tuple-element.35), channel_id=1, source_target_pairs={{0,8},{1,9},{2,10},{3,11},{4,12},{5,13},{6,14},{7,15},{8,0},{9,1},... | collective-permute-start | bytes 442376 | tf_op jit(solution)/shard_map/ppermute | solution.py:317
  18.4 2.4 %collective-permute-start.17 = (f32[288,128]{1,0:T(8,128)S(1)}, f32[288,128]{1,0:T(8,128)S(1)}, u32[]{:S(2)}, u32[]{:S(2)}) collective-permute-start(f32[288,128]{1,0:T(8,128)S(1)} %get-tuple-element.38), channel_id=1, source_target_pairs={{0,12},{1,13},{2,14},{3,15},{4,8},{5,9},{6,10},{7,11},{8,4},{9,5},... | collective-permute-start | bytes 442376 | tf_op jit(solution)/shard_map/ppermute | solution.py:317
  20.9 1.5 %collective-permute-start.6 = (f32[256,128]{1,0:T(8,128)S(1)}, f32[256,128]{1,0:T(8,128)S(1)}, u32[]{:S(2)}, u32[]{:S(2)}) collective-permute-start(f32[256,128]{1,0:T(8,128)S(1)} %get-tuple-element.33.refs_0_), channel_id=1, source_target_pairs={{0,2},{1,3},{2,0},{3,1},{4,6},{5,7},{6,4},{7,5},{8,10},{9,11},{10,... | collective-permute-start | bytes 393224 | tf_op jit(solution)/shard_map/ppermute | solution.py:317
  22.4 0.5 collective-permute-start.10
  22.9 0.0 collective-permute-done.15.refs_12_
  22.9 1.5 %collective-permute-start.18 = (f32[256,128]{1,0:T(8,128)S(1)}, f32[256,128]{1,0:T(8,128)S(1)}, u32[]{:S(2)}, u32[]{:S(2)}) collective-permute-start(f32[256,128]{1,0:T(8,128)S(1)} %collective-permute-done.15.refs_12_), channel_id=1, source_target_pairs={{0,2},{1,3},{2,0},{3,1},{4,6},{5,7},{6,4},{7,5},{8,10},{9,11},{10,... | collective-permute-start | bytes 393224 | tf_op jit(solution)/shard_map/ppermute | solution.py:317
  24.4 2.8 %collective-permute-done.6.refs_2_ = f32[256,128]{1,0:T(8,128)S(1)} collective-permute-done((f32[256,128]{1,0:T(8,128)S(1)}, f32[256,128]{1,0:T(8,128)S(1)}, u32[]{:S(2)}, u32[]{:S(2)}) %collective-permute-start.6) | collective-permute-done | bytes 131104 | tf_op jit(solution)/shard_map/ppermute | solution.py:317
  27.2 0.0 collective-permute-start.20
  27.2 2.8 %collective-permute-done.10.refs_6_ = f32[256,128]{1,0:T(8,128)S(1)} collective-permute-done((f32[256,128]{1,0:T(8,128)S(1)}, f32[256,128]{1,0:T(8,128)S(1)}, u32[]{:S(2)}, u32[]{:S(2)}) %collective-permute-start.10) | collective-permute-done | bytes 131104 | tf_op jit(solution)/shard_map/ppermute | solution.py:317
  30.1 0.0 collective-permute-start.5
  30.1 0.8 %collective-permute-done.9.refs_18_ = f32[288,128]{1,0:T(8,128)S(1)} collective-permute-done((f32[288,128]{1,0:T(8,128)S(1)}, f32[288,128]{1,0:T(8,128)S(1)}, u32[]{:S(2)}, u32[]{:S(2)}) %collective-permute-start.9) | collective-permute-done | bytes 147488 | tf_op jit(solution)/shard_map/ppermute | solution.py:317
  30.9 0.0 collective-permute-start.8
  30.9 0.0 collective-permute-done.17.refs_19_
  30.9 1.5 %collective-permute-start.13 = (f32[256,128]{1,0:T(8,128)S(1)}, f32[256,128]{1,0:T(8,128)S(1)}, u32[]{:S(2)}, u32[]{:S(2)}) collective-permute-start(f32[256,128]{1,0:T(8,128)S(1)} %collective-permute-done.3.refs_8_), channel_id=1, source_target_pairs={{0,2},{1,3},{2,0},{3,1},{4,6},{5,7},{6,4},{7,5},{8,10},{9,11},{10,... | collective-permute-start | bytes 393224 | tf_op jit(solution)/shard_map/ppermute | solution.py:317
  32.5 0.0 collective-permute-done.18.refs_14_
  32.5 0.2 collective-permute-start.12
  32.7 0.0 collective-permute-done.5.refs_1_
  32.7 0.3 collective-permute-start.16
  33.0 0.0 collective-permute-done.8.refs_5_
  33.0 0.2 collective-permute-start.7
  33.2 3.6 %collective-permute-done.13.refs_10_ = f32[256,128]{1,0:T(8,128)S(1)} collective-permute-done((f32[256,128]{1,0:T(8,128)S(1)}, f32[256,128]{1,0:T(8,128)S(1)}, u32[]{:S(2)}, u32[]{:S(2)}) %collective-permute-start.13) | collective-permute-done | bytes 131104 | tf_op jit(solution)/shard_map/ppermute | solution.py:317
  36.8 0.0 collective-permute-start.14
  36.8 0.0 collective-permute-done.12.refs_9_
  36.8 0.5 collective-permute-start.11
  37.3 0.0 collective-permute-done.20.refs_17_
  37.3 0.1 collective-permute-start.19
  37.4 0.0 collective-permute-done.16.refs_13_
  37.4 0.0 collective-permute-done.7.refs_3_
  37.4 0.8 %collective-permute-done.14.refs_11_ = f32[256,128]{1,0:T(8,128)S(1)} collective-permute-done((f32[256,128]{1,0:T(8,128)S(1)}, f32[256,128]{1,0:T(8,128)S(1)}, u32[]{:S(2)}, u32[]{:S(2)}) %collective-permute-start.14) | collective-permute-done | bytes 131104 | tf_op jit(solution)/shard_map/ppermute | solution.py:317
  38.2 0.2 collective-permute-done.11.refs_7_
  38.4 0.3 collective-permute-done.19.refs_15_
  38.7 16.8 %trace.1 = (f32[1024,128]{1,0:T(8,128)}, f32[2048,128]{1,0:T(8,128)}) custom-call(s32[1]{0:T(128)} %bitcast.me_ref, f32[4]{0:T(128)S(1)} %copy-done.4, f32[256,128]{1,0:T(8,128)S(1)} %get-tuple-element.33.refs_0_, f32[256,128]{1,0:T(8,128)S(1)} %collective-permute-done.5.refs_1_, f32[256,128]{1,0:T(8,128)S(1)} %collective-permute-done.6.refs_2_, ...), custom_call_target="tpu_custom_call" | custom-call | tf_op jit(solution)/shard_map/trace/pallas_call | solution.py:293
  (7 shorter events, 0.1 us)
Async XLA Ops:
  0.6 0.7 %copy-start.2 = (s32[4,128]{1,0:T(4,128)S(1)}, s32[4,128]{1,0:T(4,128)}, u32[]{:S(2)}) copy-start(s32[4,128]{1,0:T(4,128)} %ids_ref.1) | copy-start | bytes 6148
  0.6 0.7 %copy-start.3 = (s32[128,1]{0,1:T(1,128)S(1)}, s32[128,1]{0,1:T(1,128)}, u32[]{:S(2)}) copy-start(s32[128,1]{0,1:T(1,128)} %param.9) | copy-start | bytes 1540
  1.3 1.0 %copy-start = (f32[128,2,256]{2,1,0:T(2,128)S(1)}, f32[128,2,256]{2,1,0:T(2,128)}, u32[]{:S(2)}) copy-start(f32[128,2,256]{2,1,0:T(2,128)} %param.7) | copy-start | bytes 786436
  2.3 0.9 %copy-start.1 = (f32[4,8,1024]{2,1,0:T(8,128)S(1)}, f32[4,8,1024]{2,1,0:T(8,128)}, u32[]{:S(2)}) copy-start(f32[4,8,1024]{2,1,0:T(8,128)} %src_ref.1) | copy-start | bytes 393220
  3.7 10.5 %collective-permute-start.3 = (f32[256,128]{1,0:T(8,128)S(1)}, f32[256,128]{1,0:T(8,128)S(1)}, u32[]{:S(2)}, u32[]{:S(2)}) collective-permute-start(f32[256,128]{1,0:T(8,128)S(1)} %get-tuple-element.33.refs_0_), channel_id=1, source_target_pairs={{0,8},{1,9},{2,10},{3,11},{4,12},{5,13},{6,14},{7,15},{8,0},{9,1},... | collective-permute-start | bytes 393224 | tf_op jit(solution)/shard_map/ppermute | solution.py:317
  7.8 7.1 %collective-permute-start = (f32[288,128]{1,0:T(8,128)S(1)}, f32[288,128]{1,0:T(8,128)S(1)}, u32[]{:S(2)}, u32[]{:S(2)}) collective-permute-start(f32[288,128]{1,0:T(8,128)S(1)} %get-tuple-element.25), channel_id=1, source_target_pairs={{0,1},{1,0},{2,3},{3,2},{4,5},{5,4},{6,7},{7,6},{8,9},{9,8},{10,11... | collective-permute-start | bytes 442376 | tf_op jit(solution)/shard_map/ppermute | solution.py:317
  7.8 7.1 %collective-permute-start.1 = (f32[288,128]{1,0:T(8,128)S(1)}, f32[288,128]{1,0:T(8,128)S(1)}, u32[]{:S(2)}, u32[]{:S(2)}) collective-permute-start(f32[288,128]{1,0:T(8,128)S(1)} %get-tuple-element.26), channel_id=1, source_target_pairs={{0,2},{1,3},{2,0},{3,1},{4,6},{5,7},{6,4},{7,5},{8,10},{9,11},{10,... | collective-permute-start | bytes 442376 | tf_op jit(solution)/shard_map/ppermute | solution.py:317
  9.3 7.5 %collective-permute-start.2 = (f32[288,128]{1,0:T(8,128)S(1)}, f32[288,128]{1,0:T(8,128)S(1)}, u32[]{:S(2)}, u32[]{:S(2)}) collective-permute-start(f32[288,128]{1,0:T(8,128)S(1)} %get-tuple-element.27), channel_id=1, source_target_pairs={{0,3},{1,2},{2,1},{3,0},{4,7},{5,6},{6,5},{7,4},{8,11},{9,10},{10,... | collective-permute-start | bytes 442376 | tf_op jit(solution)/shard_map/ppermute | solution.py:317
  9.6 7.3 %collective-permute-start.4 = (f32[256,128]{1,0:T(8,128)S(1)}, f32[256,128]{1,0:T(8,128)S(1)}, u32[]{:S(2)}, u32[]{:S(2)}) collective-permute-start(f32[256,128]{1,0:T(8,128)S(1)} %get-tuple-element.33.refs_0_), channel_id=1, source_target_pairs={{0,4},{1,5},{2,6},{3,7},{4,0},{5,1},{6,2},{7,3},{8,12},{9,13},{10,... | collective-permute-start | bytes 393224 | tf_op jit(solution)/shard_map/ppermute | solution.py:317
  14.2 8.7 %collective-permute-start.15 = (f32[256,128]{1,0:T(8,128)S(1)}, f32[256,128]{1,0:T(8,128)S(1)}, u32[]{:S(2)}, u32[]{:S(2)}) collective-permute-start(f32[256,128]{1,0:T(8,128)S(1)} %collective-permute-done.3.refs_8_), channel_id=1, source_target_pairs={{0,4},{1,5},{2,6},{3,7},{4,0},{5,1},{6,2},{7,3},{8,12},{9,13},{10,... | collective-permute-start | bytes 393224 | tf_op jit(solution)/shard_map/ppermute | solution.py:317
  17.0 21.7 %copy-start.4 = (f32[4]{0:T(128)S(1)}, f32[4]{0:T(128)}, u32[]{:S(2)}) copy-start(f32[4]{0:T(128)} %lens_ref.1) | copy-start | bytes 52
  17.0 13.9 %collective-permute-start.9 = (f32[288,128]{1,0:T(8,128)S(1)}, f32[288,128]{1,0:T(8,128)S(1)}, u32[]{:S(2)}, u32[]{:S(2)}) collective-permute-start(f32[288,128]{1,0:T(8,128)S(1)} %get-tuple-element.35), channel_id=1, source_target_pairs={{0,8},{1,9},{2,10},{3,11},{4,12},{5,13},{6,14},{7,15},{8,0},{9,1},... | collective-permute-start | bytes 442376 | tf_op jit(solution)/shard_map/ppermute | solution.py:317
  18.4 12.5 %collective-permute-start.17 = (f32[288,128]{1,0:T(8,128)S(1)}, f32[288,128]{1,0:T(8,128)S(1)}, u32[]{:S(2)}, u32[]{:S(2)}) collective-permute-start(f32[288,128]{1,0:T(8,128)S(1)} %get-tuple-element.38), channel_id=1, source_target_pairs={{0,12},{1,13},{2,14},{3,15},{4,8},{5,9},{6,10},{7,11},{8,4},{9,5},... | collective-permute-start | bytes 442376 | tf_op jit(solution)/shard_map/ppermute | solution.py:317
  20.9 6.4 %collective-permute-start.6 = (f32[256,128]{1,0:T(8,128)S(1)}, f32[256,128]{1,0:T(8,128)S(1)}, u32[]{:S(2)}, u32[]{:S(2)}) collective-permute-start(f32[256,128]{1,0:T(8,128)S(1)} %get-tuple-element.33.refs_0_), channel_id=1, source_target_pairs={{0,2},{1,3},{2,0},{3,1},{4,6},{5,7},{6,4},{7,5},{8,10},{9,11},{10,... | collective-permute-start | bytes 393224 | tf_op jit(solution)/shard_map/ppermute | solution.py:317
  22.4 7.7 %collective-permute-start.10 = (f32[256,128]{1,0:T(8,128)S(1)}, f32[256,128]{1,0:T(8,128)S(1)}, u32[]{:S(2)}, u32[]{:S(2)}) collective-permute-start(f32[256,128]{1,0:T(8,128)S(1)} %collective-permute-done.4.refs_4_), channel_id=1, source_target_pairs={{0,2},{1,3},{2,0},{3,1},{4,6},{5,7},{6,4},{7,5},{8,10},{9,11},{10,... | collective-permute-start | bytes 393224 | tf_op jit(solution)/shard_map/ppermute | solution.py:317
  22.9 9.5 %collective-permute-start.18 = (f32[256,128]{1,0:T(8,128)S(1)}, f32[256,128]{1,0:T(8,128)S(1)}, u32[]{:S(2)}, u32[]{:S(2)}) collective-permute-start(f32[256,128]{1,0:T(8,128)S(1)} %collective-permute-done.15.refs_12_), channel_id=1, source_target_pairs={{0,2},{1,3},{2,0},{3,1},{4,6},{5,7},{6,4},{7,5},{8,10},{9,11},{10,... | collective-permute-start | bytes 393224 | tf_op jit(solution)/shard_map/ppermute | solution.py:317
  27.2 10.1 %collective-permute-start.20 = (f32[288,128]{1,0:T(8,128)S(1)}, f32[288,128]{1,0:T(8,128)S(1)}, u32[]{:S(2)}, u32[]{:S(2)}) collective-permute-start(f32[288,128]{1,0:T(8,128)S(1)} %get-tuple-element.41), channel_id=1, source_target_pairs={{0,4},{1,5},{2,6},{3,7},{4,0},{5,1},{6,2},{7,3},{8,12},{9,13},{10,... | collective-permute-start | bytes 442376 | tf_op jit(solution)/shard_map/ppermute | solution.py:317
  30.1 2.6 %collective-permute-start.5 = (f32[256,128]{1,0:T(8,128)S(1)}, f32[256,128]{1,0:T(8,128)S(1)}, u32[]{:S(2)}, u32[]{:S(2)}) collective-permute-start(f32[256,128]{1,0:T(8,128)S(1)} %get-tuple-element.33.refs_0_), channel_id=1, source_target_pairs={{0,1},{1,0},{2,3},{3,2},{4,5},{5,4},{6,7},{7,6},{8,9},{9,8},{10,11... | collective-permute-start | bytes 393224 | tf_op jit(solution)/shard_map/ppermute | solution.py:317
  30.9 2.1 %collective-permute-start.8 = (f32[256,128]{1,0:T(8,128)S(1)}, f32[256,128]{1,0:T(8,128)S(1)}, u32[]{:S(2)}, u32[]{:S(2)}) collective-permute-start(f32[256,128]{1,0:T(8,128)S(1)} %collective-permute-done.4.refs_4_), channel_id=1, source_target_pairs={{0,1},{1,0},{2,3},{3,2},{4,5},{5,4},{6,7},{7,6},{8,9},{9,8},{10,11... | collective-permute-start | bytes 393224 | tf_op jit(solution)/shard_map/ppermute | solution.py:317
  30.9 5.9 %collective-permute-start.13 = (f32[256,128]{1,0:T(8,128)S(1)}, f32[256,128]{1,0:T(8,128)S(1)}, u32[]{:S(2)}, u32[]{:S(2)}) collective-permute-start(f32[256,128]{1,0:T(8,128)S(1)} %collective-permute-done.3.refs_8_), channel_id=1, source_target_pairs={{0,2},{1,3},{2,0},{3,1},{4,6},{5,7},{6,4},{7,5},{8,10},{9,11},{10,... | collective-permute-start | bytes 393224 | tf_op jit(solution)/shard_map/ppermute | solution.py:317
  32.5 4.4 %collective-permute-start.12 = (f32[256,128]{1,0:T(8,128)S(1)}, f32[256,128]{1,0:T(8,128)S(1)}, u32[]{:S(2)}, u32[]{:S(2)}) collective-permute-start(f32[256,128]{1,0:T(8,128)S(1)} %collective-permute-done.3.refs_8_), channel_id=1, source_target_pairs={{0,1},{1,0},{2,3},{3,2},{4,5},{5,4},{6,7},{7,6},{8,9},{9,8},{10,11... | collective-permute-start | bytes 393224 | tf_op jit(solution)/shard_map/ppermute | solution.py:317
  32.7 4.7 %collective-permute-start.16 = (f32[256,128]{1,0:T(8,128)S(1)}, f32[256,128]{1,0:T(8,128)S(1)}, u32[]{:S(2)}, u32[]{:S(2)}) collective-permute-start(f32[256,128]{1,0:T(8,128)S(1)} %collective-permute-done.15.refs_12_), channel_id=1, source_target_pairs={{0,1},{1,0},{2,3},{3,2},{4,5},{5,4},{6,7},{7,6},{8,9},{9,8},{10,11... | collective-permute-start | bytes 393224 | tf_op jit(solution)/shard_map/ppermute | solution.py:317
  33.0 4.4 %collective-permute-start.7 = (f32[256,128]{1,0:T(8,128)S(1)}, f32[256,128]{1,0:T(8,128)S(1)}, u32[]{:S(2)}, u32[]{:S(2)}) collective-permute-start(f32[256,128]{1,0:T(8,128)S(1)} %collective-permute-done.6.refs_2_), channel_id=1, source_target_pairs={{0,1},{1,0},{2,3},{3,2},{4,5},{5,4},{6,7},{7,6},{8,9},{9,8},{10,11... | collective-permute-start | bytes 393224 | tf_op jit(solution)/shard_map/ppermute | solution.py:317
  36.8 1.3 %collective-permute-start.14 = (f32[256,128]{1,0:T(8,128)S(1)}, f32[256,128]{1,0:T(8,128)S(1)}, u32[]{:S(2)}, u32[]{:S(2)}) collective-permute-start(f32[256,128]{1,0:T(8,128)S(1)} %collective-permute-done.13.refs_10_), channel_id=1, source_target_pairs={{0,1},{1,0},{2,3},{3,2},{4,5},{5,4},{6,7},{7,6},{8,9},{9,8},{10,11... | collective-permute-start | bytes 393224 | tf_op jit(solution)/shard_map/ppermute | solution.py:317
  36.8 1.5 %collective-permute-start.11 = (f32[256,128]{1,0:T(8,128)S(1)}, f32[256,128]{1,0:T(8,128)S(1)}, u32[]{:S(2)}, u32[]{:S(2)}) collective-permute-start(f32[256,128]{1,0:T(8,128)S(1)} %collective-permute-done.10.refs_6_), channel_id=1, source_target_pairs={{0,1},{1,0},{2,3},{3,2},{4,5},{5,4},{6,7},{7,6},{8,9},{9,8},{10,11... | collective-permute-start | bytes 393224 | tf_op jit(solution)/shard_map/ppermute | solution.py:317
  37.3 1.3 %collective-permute-start.19 = (f32[256,128]{1,0:T(8,128)S(1)}, f32[256,128]{1,0:T(8,128)S(1)}, u32[]{:S(2)}, u32[]{:S(2)}) collective-permute-start(f32[256,128]{1,0:T(8,128)S(1)} %collective-permute-done.18.refs_14_), channel_id=1, source_target_pairs={{0,1},{1,0},{2,3},{3,2},{4,5},{5,4},{6,7},{7,6},{8,9},{9,8},{10,11... | collective-permute-start | bytes 393224 | tf_op jit(solution)/shard_map/ppermute | solution.py:317

commit v14 on v12

--- a/solution.py
+++ b/solution.py
@@ -128,6 +128,7 @@
         out_shape=[own] + [part] * NEAR,
         in_specs=[pl.BlockSpec(memory_space=pltpu.SMEM)] + [pl.BlockSpec(memory_space=pltpu.VMEM)] * 4,
         out_specs=[pl.BlockSpec(memory_space=pltpu.VMEM)] * (1 + NEAR),
+        compiler_params=pltpu.CompilerParams(vmem_limit_bytes=16 * 1024 * 1024),
         name="prepare",
     )(me, dest, ids, rays, potential)
     return own, sent

time: 54.3 us -> 53.2 us (0.980)
  Pallas kernels: 19.2 us -> 17.4 us
  local copies, waits for them, and re-layouts: 1.76 us -> 2.53 us
    pallas_call x1, Pallas kernels: 2.37 us -> 0.55 us  [prepare(): pl.pallas_call(functools.partial(prepare_kernel, n_sky, each), out_shape=...]
    unnamed x6 -> x10, local copies, waits for them, and re-layouts: 1.76 us -> 2.53 us
  transfers between devices with their start and end apart: 21 -> 21, of which waited for: 10 -> 11; matrix products, arithmetic and copies ran while one was open for 0% -> 0% of each run, Pallas kernels for 0% -> 0%
where the time goes in v14:
time: 53.2 us; the launch traced here: 53 us
  starting transfers between devices  18.1 us (34%)
  Pallas kernels  17.4 us (33%)
  waiting for transfers between devices  14.3 us (27%)
  local copies, waits for them, and re-layouts  2.53 us (5%)
  between operations  0.68 us (1%)
    ppermute x21, starting transfers between devices, flipped(): return lax.ppermute(value, 'sky', [(i, i ^ bits) for i in range(n_sky)])  18.1 us
    pallas_call x1, Pallas kernels, trace(): pl.pallas_call(functools.partial(trace_kernel, n_sky, each, planes, toget...  16.8 us
    ppermute x21, waiting for transfers between devices, flipped(): return lax.ppermute(value, 'sky', [(i, i ^ bits) for i in range(n_sky)])  14.3 us
    unnamed x10, local copies, waits for them, and re-layouts  2.53 us
  transfers between devices with their start and end apart: 21, of which 11 were waited for; matrix products, arithmetic and copies ran while one was open for 0% of the time, Pallas kernels for 0%

profile of v14, /device:TPU:0, one launch (start us, length us, event | category | flops | bytes accessed | tf_op | source)
XLA Modules:
  0.0 53.0 jit_solution(17111115308366854017)
XLA Ops:
  0.7 0.7 %copy-done.2 = s32[4,128]{1,0:T(4,128)S(1)} copy-done((s32[4,128]{1,0:T(4,128)S(1)}, s32[4,128]{1,0:T(4,128)}, u32[]{:S(2)}) %copy-start.2) | copy-done | bytes 2072
  1.3 0.9 %copy-done = f32[128,2,256]{2,1,0:T(2,128)S(1)} copy-done((f32[128,2,256]{2,1,0:T(2,128)S(1)}, f32[128,2,256]{2,1,0:T(2,128)}, u32[]{:S(2)}) %copy-start) | copy-done | bytes 262168
  2.3 0.9 %copy-done.1 = f32[4,8,1024]{2,1,0:T(8,128)S(1)} copy-done((f32[4,8,1024]{2,1,0:T(8,128)S(1)}, f32[4,8,1024]{2,1,0:T(8,128)}, u32[]{:S(2)}) %copy-start.1) | copy-done | bytes 131096
  3.2 0.5 %prepare.1 = (f32[256,128]{1,0:T(8,128)S(1)}, f32[288,128]{1,0:T(8,128)S(1)}, f32[288,128]{1,0:T(8,128)S(1)}, f32[288,128]{1,0:T(8,128)S(1)}, f32[288,128]{1,0:T(8,128)S(1)}) custom-call(s32[1]{0:T(128)} %bitcast.me_ref, s32[1,128]{1,0:T(1,128)S(1)} %bitcast.18, s32[4,128]{1,0:T(4,128)S(1)} %copy-done.2, f32[512,128]{1,0:T(8,128)S(1)} %bitcast.17, ...), custom_call_target="tpu_custom_call" | custom-call | tf_op jit(solution)/shard_map/prepare/pallas_call | solution.py:126
  3.7 4.0 %collective-permute-start.3 = (f32[256,128]{1,0:T(8,128)S(1)}, f32[256,128]{1,0:T(8,128)S(1)}, u32[]{:S(2)}, u32[]{:S(2)}) collective-permute-start(f32[256,128]{1,0:T(8,128)S(1)} %get-tuple-element.42.refs_0_), channel_id=1, source_target_pairs={{0,8},{1,9},{2,10},{3,11},{4,12},{5,13},{6,14},{7,15},{8,0},{9,1},... | collective-permute-start | bytes 393224 | tf_op jit(solution)/shard_map/ppermute | solution.py:317
  7.8 0.0 collective-permute-start
  7.8 1.5 %collective-permute-start.1 = (f32[288,128]{1,0:T(8,128)S(1)}, f32[288,128]{1,0:T(8,128)S(1)}, u32[]{:S(2)}, u32[]{:S(2)}) collective-permute-start(f32[288,128]{1,0:T(8,128)S(1)} %get-tuple-element.32), channel_id=1, source_target_pairs={{0,2},{1,3},{2,0},{3,1},{4,6},{5,7},{6,4},{7,5},{8,10},{9,11},{10,... | collective-permute-start | bytes 442376 | tf_op jit(solution)/shard_map/ppermute | solution.py:317
  9.3 0.3 collective-permute-start.2
  9.6 1.6 %collective-permute-start.4 = (f32[256,128]{1,0:T(8,128)S(1)}, f32[256,128]{1,0:T(8,128)S(1)}, u32[]{:S(2)}, u32[]{:S(2)}) collective-permute-start(f32[256,128]{1,0:T(8,128)S(1)} %get-tuple-element.42.refs_0_), channel_id=1, source_target_pairs={{0,4},{1,5},{2,6},{3,7},{4,0},{5,1},{6,2},{7,3},{8,12},{9,13},{10,... | collective-permute-start | bytes 393224 | tf_op jit(solution)/shard_map/ppermute | solution.py:317
  11.2 3.0 %collective-permute-done.3.refs_8_ = f32[256,128]{1,0:T(8,128)S(1)} collective-permute-done((f32[256,128]{1,0:T(8,128)S(1)}, f32[256,128]{1,0:T(8,128)S(1)}, u32[]{:S(2)}, u32[]{:S(2)}) %collective-permute-start.3) | collective-permute-done | bytes 131104 | tf_op jit(solution)/shard_map/ppermute | solution.py:317
  14.2 0.7 %collective-permute-start.14 = (f32[256,128]{1,0:T(8,128)S(1)}, f32[256,128]{1,0:T(8,128)S(1)}, u32[]{:S(2)}, u32[]{:S(2)}) collective-permute-start(f32[256,128]{1,0:T(8,128)S(1)} %collective-permute-done.3.refs_8_), channel_id=1, source_target_pairs={{0,4},{1,5},{2,6},{3,7},{4,0},{5,1},{6,2},{7,3},{8,12},{9,13},{10,... | collective-permute-start | bytes 393224 | tf_op jit(solution)/shard_map/ppermute | solution.py:317
  14.8 0.0 collective-permute-done.refs_1_
  14.8 0.0 collective-permute-done.1.refs_2_
  14.9 2.0 %collective-permute-done.2.refs_3_ = f32[288,128]{1,0:T(8,128)S(1)} collective-permute-done((f32[288,128]{1,0:T(8,128)S(1)}, f32[288,128]{1,0:T(8,128)S(1)}, u32[]{:S(2)}, u32[]{:S(2)}) %collective-permute-start.2) | collective-permute-done | bytes 147488 | tf_op jit(solution)/shard_map/ppermute | solution.py:317
  16.9 0.1 collective-permute-done.4.refs_4_
  17.0 1.5 %collective-permute-start.6 = (f32[256,128]{1,0:T(8,128)S(1)}, f32[256,128]{1,0:T(8,128)S(1)}, u32[]{:S(2)}, u32[]{:S(2)}) collective-permute-start(f32[256,128]{1,0:T(8,128)S(1)} %get-tuple-element.42.refs_0_), channel_id=1, source_target_pairs={{0,2},{1,3},{2,0},{3,1},{4,6},{5,7},{6,4},{7,5},{8,10},{9,11},{10,... | collective-permute-start | bytes 393224 | tf_op jit(solution)/shard_map/ppermute | solution.py:317
  18.5 1.4 %collective-permute-start.5 = (f32[288,128]{1,0:T(8,128)S(1)}, f32[288,128]{1,0:T(8,128)S(1)}, u32[]{:S(2)}, u32[]{:S(2)}) collective-permute-start(f32[288,128]{1,0:T(8,128)S(1)} %get-tuple-element.39), channel_id=1, source_target_pairs={{0,8},{1,9},{2,10},{3,11},{4,12},{5,13},{6,14},{7,15},{8,0},{9,1},... | collective-permute-start | bytes 442376 | tf_op jit(solution)/shard_map/ppermute | solution.py:317
  20.0 2.4 %collective-permute-start.12 = (f32[288,128]{1,0:T(8,128)S(1)}, f32[288,128]{1,0:T(8,128)S(1)}, u32[]{:S(2)}, u32[]{:S(2)}) collective-permute-start(f32[288,128]{1,0:T(8,128)S(1)} %get-tuple-element.46), channel_id=1, source_target_pairs={{0,12},{1,13},{2,14},{3,15},{4,8},{5,9},{6,10},{7,11},{8,4},{9,5},... | collective-permute-start | bytes 442376 | tf_op jit(solution)/shard_map/ppermute | solution.py:317
  22.4 0.5 collective-permute-start.7
  22.9 0.0 collective-permute-done.14.refs_12_
  22.9 1.5 %collective-permute-start.13 = (f32[256,128]{1,0:T(8,128)S(1)}, f32[256,128]{1,0:T(8,128)S(1)}, u32[]{:S(2)}, u32[]{:S(2)}) collective-permute-start(f32[256,128]{1,0:T(8,128)S(1)} %collective-permute-done.3.refs_8_), channel_id=1, source_target_pairs={{0,2},{1,3},{2,0},{3,1},{4,6},{5,7},{6,4},{7,5},{8,10},{9,11},{10,... | collective-permute-start | bytes 393224 | tf_op jit(solution)/shard_map/ppermute | solution.py:317
  24.4 0.0 collective-permute-done.6.refs_2_
  24.4 0.4 collective-permute-start.20
  24.8 4.0 %collective-permute-done.7.refs_6_ = f32[256,128]{1,0:T(8,128)S(1)} collective-permute-done((f32[256,128]{1,0:T(8,128)S(1)}, f32[256,128]{1,0:T(8,128)S(1)}, u32[]{:S(2)}, u32[]{:S(2)}) %collective-permute-start.7) | collective-permute-done | bytes 131104 | tf_op jit(solution)/shard_map/ppermute | solution.py:317
  28.8 0.5 collective-permute-start.15
  29.3 3.2 %collective-permute-done.5.refs_18_ = f32[288,128]{1,0:T(8,128)S(1)} collective-permute-done((f32[288,128]{1,0:T(8,128)S(1)}, f32[288,128]{1,0:T(8,128)S(1)}, u32[]{:S(2)}, u32[]{:S(2)}) %collective-permute-start.5) | collective-permute-done | bytes 147488 | tf_op jit(solution)/shard_map/ppermute | solution.py:317
  32.5 0.0 collective-permute-start.8
  32.5 0.0 collective-permute-done.13.refs_10_
  32.5 0.5 collective-permute-start.9
  33.0 0.0 collective-permute-done.12.refs_19_
  33.0 0.1 collective-permute-start.10
  33.1 0.7 %collective-permute-done.15.refs_14_ = f32[256,128]{1,0:T(8,128)S(1)} collective-permute-done((f32[256,128]{1,0:T(8,128)S(1)}, f32[256,128]{1,0:T(8,128)S(1)}, u32[]{:S(2)}, u32[]{:S(2)}) %collective-permute-start.15) | collective-permute-done | bytes 131104 | tf_op jit(solution)/shard_map/ppermute | solution.py:317
  33.8 0.0 collective-permute-start.11
  33.8 0.3 collective-permute-done.20.refs_17_
  34.1 0.2 collective-permute-start.16
  34.3 0.0 collective-permute-done.8.refs_1_
  34.3 0.3 collective-permute-start.17
  34.6 0.0 collective-permute-done.9.refs_3_
  34.6 0.2 collective-permute-start.18
  34.8 0.0 collective-permute-done.10.refs_5_
  34.8 0.3 collective-permute-start.19
  35.1 0.0 collective-permute-done.11.refs_7_
  35.1 0.3 collective-permute-done.16.refs_9_
  35.5 0.2 collective-permute-done.17.refs_11_
  35.6 0.3 collective-permute-done.18.refs_13_
  36.0 0.2 collective-permute-done.19.refs_15_
  36.2 0.0 copy-done.4
  36.2 16.8 %trace.1 = (f32[1024,128]{1,0:T(8,128)}, f32[2048,128]{1,0:T(8,128)}) custom-call(s32[1]{0:T(128)} %bitcast.me_ref, f32[4]{0:T(128)S(1)} %copy-done.4, f32[256,128]{1,0:T(8,128)S(1)} %get-tuple-element.42.refs_0_, f32[256,128]{1,0:T(8,128)S(1)} %collective-permute-done.8.refs_1_, f32[256,128]{1,0:T(8,128)S(1)} %collective-permute-done.6.refs_2_, ...), custom_call_target="tpu_custom_call" | custom-call | tf_op jit(solution)/shard_map/trace/pallas_call | solution.py:293
  (7 shorter events, 0.1 us)
Async XLA Ops:
  0.6 0.7 %copy-start.2 = (s32[4,128]{1,0:T(4,128)S(1)}, s32[4,128]{1,0:T(4,128)}, u32[]{:S(2)}) copy-start(s32[4,128]{1,0:T(4,128)} %ids_ref.1) | copy-start | bytes 6148
  0.6 0.7 %copy-start.3 = (s32[128,1]{0,1:T(1,128)S(1)}, s32[128,1]{0,1:T(1,128)}, u32[]{:S(2)}) copy-start(s32[128,1]{0,1:T(1,128)} %param.9) | copy-start | bytes 1540
  1.3 1.0 %copy-start = (f32[128,2,256]{2,1,0:T(2,128)S(1)}, f32[128,2,256]{2,1,0:T(2,128)}, u32[]{:S(2)}) copy-start(f32[128,2,256]{2,1,0:T(2,128)} %param.7) | copy-start | bytes 786436
  2.3 0.9 %copy-start.1 = (f32[4,8,1024]{2,1,0:T(8,128)S(1)}, f32[4,8,1024]{2,1,0:T(8,128)}, u32[]{:S(2)}) copy-start(f32[4,8,1024]{2,1,0:T(8,128)} %src_ref.1) | copy-start | bytes 393220
  3.7 10.5 %collective-permute-start.3 = (f32[256,128]{1,0:T(8,128)S(1)}, f32[256,128]{1,0:T(8,128)S(1)}, u32[]{:S(2)}, u32[]{:S(2)}) collective-permute-start(f32[256,128]{1,0:T(8,128)S(1)} %get-tuple-element.42.refs_0_), channel_id=1, source_target_pairs={{0,8},{1,9},{2,10},{3,11},{4,12},{5,13},{6,14},{7,15},{8,0},{9,1},... | collective-permute-start | bytes 393224 | tf_op jit(solution)/shard_map/ppermute | solution.py:317
  7.8 7.1 %collective-permute-start = (f32[288,128]{1,0:T(8,128)S(1)}, f32[288,128]{1,0:T(8,128)S(1)}, u32[]{:S(2)}, u32[]{:S(2)}) collective-permute-start(f32[288,128]{1,0:T(8,128)S(1)} %get-tuple-element.31), channel_id=1, source_target_pairs={{0,1},{1,0},{2,3},{3,2},{4,5},{5,4},{6,7},{7,6},{8,9},{9,8},{10,11... | collective-permute-start | bytes 442376 | tf_op jit(solution)/shard_map/ppermute | solution.py:317
  7.8 7.1 %collective-permute-start.1 = (f32[288,128]{1,0:T(8,128)S(1)}, f32[288,128]{1,0:T(8,128)S(1)}, u32[]{:S(2)}, u32[]{:S(2)}) collective-permute-start(f32[288,128]{1,0:T(8,128)S(1)} %get-tuple-element.32), channel_id=1, source_target_pairs={{0,2},{1,3},{2,0},{3,1},{4,6},{5,7},{6,4},{7,5},{8,10},{9,11},{10,... | collective-permute-start | bytes 442376 | tf_op jit(solution)/shard_map/ppermute | solution.py:317
  9.3 7.5 %collective-permute-start.2 = (f32[288,128]{1,0:T(8,128)S(1)}, f32[288,128]{1,0:T(8,128)S(1)}, u32[]{:S(2)}, u32[]{:S(2)}) collective-permute-start(f32[288,128]{1,0:T(8,128)S(1)} %get-tuple-element.33), channel_id=1, source_target_pairs={{0,3},{1,2},{2,1},{3,0},{4,7},{5,6},{6,5},{7,4},{8,11},{9,10},{10,... | collective-permute-start | bytes 442376 | tf_op jit(solution)/shard_map/ppermute | solution.py:317
  9.6 7.3 %collective-permute-start.4 = (f32[256,128]{1,0:T(8,128)S(1)}, f32[256,128]{1,0:T(8,128)S(1)}, u32[]{:S(2)}, u32[]{:S(2)}) collective-permute-start(f32[256,128]{1,0:T(8,128)S(1)} %get-tuple-element.42.refs_0_), channel_id=1, source_target_pairs={{0,4},{1,5},{2,6},{3,7},{4,0},{5,1},{6,2},{7,3},{8,12},{9,13},{10,... | collective-permute-start | bytes 393224 | tf_op jit(solution)/shard_map/ppermute | solution.py:317
  14.2 8.7 %collective-permute-start.14 = (f32[256,128]{1,0:T(8,128)S(1)}, f32[256,128]{1,0:T(8,128)S(1)}, u32[]{:S(2)}, u32[]{:S(2)}) collective-permute-start(f32[256,128]{1,0:T(8,128)S(1)} %collective-permute-done.3.refs_8_), channel_id=1, source_target_pairs={{0,4},{1,5},{2,6},{3,7},{4,0},{5,1},{6,2},{7,3},{8,12},{9,13},{10,... | collective-permute-start | bytes 393224 | tf_op jit(solution)/shard_map/ppermute | solution.py:317
  17.0 19.2 %copy-start.4 = (f32[4]{0:T(128)S(1)}, f32[4]{0:T(128)}, u32[]{:S(2)}) copy-start(f32[4]{0:T(128)} %lens_ref.1) | copy-start | bytes 52
  17.0 7.4 %collective-permute-start.6 = (f32[256,128]{1,0:T(8,128)S(1)}, f32[256,128]{1,0:T(8,128)S(1)}, u32[]{:S(2)}, u32[]{:S(2)}) collective-permute-start(f32[256,128]{1,0:T(8,128)S(1)} %get-tuple-element.42.refs_0_), channel_id=1, source_target_pairs={{0,2},{1,3},{2,0},{3,1},{4,6},{5,7},{6,4},{7,5},{8,10},{9,11},{10,... | collective-permute-start | bytes 393224 | tf_op jit(solution)/shard_map/ppermute | solution.py:317
  18.5 14.0 %collective-permute-start.5 = (f32[288,128]{1,0:T(8,128)S(1)}, f32[288,128]{1,0:T(8,128)S(1)}, u32[]{:S(2)}, u32[]{:S(2)}) collective-permute-start(f32[288,128]{1,0:T(8,128)S(1)} %get-tuple-element.39), channel_id=1, source_target_pairs={{0,8},{1,9},{2,10},{3,11},{4,12},{5,13},{6,14},{7,15},{8,0},{9,1},... | collective-permute-start | bytes 442376 | tf_op jit(solution)/shard_map/ppermute | solution.py:317
  20.0 13.1 %collective-permute-start.12 = (f32[288,128]{1,0:T(8,128)S(1)}, f32[288,128]{1,0:T(8,128)S(1)}, u32[]{:S(2)}, u32[]{:S(2)}) collective-permute-start(f32[288,128]{1,0:T(8,128)S(1)} %get-tuple-element.46), channel_id=1, source_target_pairs={{0,12},{1,13},{2,14},{3,15},{4,8},{5,9},{6,10},{7,11},{8,4},{9,5},... | collective-permute-start | bytes 442376 | tf_op jit(solution)/shard_map/ppermute | solution.py:317
  22.4 6.4 %collective-permute-start.7 = (f32[256,128]{1,0:T(8,128)S(1)}, f32[256,128]{1,0:T(8,128)S(1)}, u32[]{:S(2)}, u32[]{:S(2)}) collective-permute-start(f32[256,128]{1,0:T(8,128)S(1)} %collective-permute-done.4.refs_4_), channel_id=1, source_target_pairs={{0,2},{1,3},{2,0},{3,1},{4,6},{5,7},{6,4},{7,5},{8,10},{9,11},{10,... | collective-permute-start | bytes 393224 | tf_op jit(solution)/shard_map/ppermute | solution.py:317
  22.9 9.6 %collective-permute-start.13 = (f32[256,128]{1,0:T(8,128)S(1)}, f32[256,128]{1,0:T(8,128)S(1)}, u32[]{:S(2)}, u32[]{:S(2)}) collective-permute-start(f32[256,128]{1,0:T(8,128)S(1)} %collective-permute-done.3.refs_8_), channel_id=1, source_target_pairs={{0,2},{1,3},{2,0},{3,1},{4,6},{5,7},{6,4},{7,5},{8,10},{9,11},{10,... | collective-permute-start | bytes 393224 | tf_op jit(solution)/shard_map/ppermute | solution.py:317
  24.4 9.7 %collective-permute-start.20 = (f32[288,128]{1,0:T(8,128)S(1)}, f32[288,128]{1,0:T(8,128)S(1)}, u32[]{:S(2)}, u32[]{:S(2)}) collective-permute-start(f32[288,128]{1,0:T(8,128)S(1)} %get-tuple-element.53), channel_id=1, source_target_pairs={{0,4},{1,5},{2,6},{3,7},{4,0},{5,1},{6,2},{7,3},{8,12},{9,13},{10,... | collective-permute-start | bytes 442376 | tf_op jit(solution)/shard_map/ppermute | solution.py:317
  28.8 5.0 %collective-permute-start.15 = (f32[256,128]{1,0:T(8,128)S(1)}, f32[256,128]{1,0:T(8,128)S(1)}, u32[]{:S(2)}, u32[]{:S(2)}) collective-permute-start(f32[256,128]{1,0:T(8,128)S(1)} %collective-permute-done.14.refs_12_), channel_id=1, source_target_pairs={{0,2},{1,3},{2,0},{3,1},{4,6},{5,7},{6,4},{7,5},{8,10},{9,11},{10,... | collective-permute-start | bytes 393224 | tf_op jit(solution)/shard_map/ppermute | solution.py:317
  32.5 1.8 %collective-permute-start.8 = (f32[256,128]{1,0:T(8,128)S(1)}, f32[256,128]{1,0:T(8,128)S(1)}, u32[]{:S(2)}, u32[]{:S(2)}) collective-permute-start(f32[256,128]{1,0:T(8,128)S(1)} %get-tuple-element.42.refs_0_), channel_id=1, source_target_pairs={{0,1},{1,0},{2,3},{3,2},{4,5},{5,4},{6,7},{7,6},{8,9},{9,8},{10,11... | collective-permute-start | bytes 393224 | tf_op jit(solution)/shard_map/ppermute | solution.py:317
  32.5 2.1 %collective-permute-start.9 = (f32[256,128]{1,0:T(8,128)S(1)}, f32[256,128]{1,0:T(8,128)S(1)}, u32[]{:S(2)}, u32[]{:S(2)}) collective-permute-start(f32[256,128]{1,0:T(8,128)S(1)} %collective-permute-done.6.refs_2_), channel_id=1, source_target_pairs={{0,1},{1,0},{2,3},{3,2},{4,5},{5,4},{6,7},{7,6},{8,9},{9,8},{10,11... | collective-permute-start | bytes 393224 | tf_op jit(solution)/shard_map/ppermute | solution.py:317
  33.0 1.8 %collective-permute-start.10 = (f32[256,128]{1,0:T(8,128)S(1)}, f32[256,128]{1,0:T(8,128)S(1)}, u32[]{:S(2)}, u32[]{:S(2)}) collective-permute-start(f32[256,128]{1,0:T(8,128)S(1)} %collective-permute-done.4.refs_4_), channel_id=1, source_target_pairs={{0,1},{1,0},{2,3},{3,2},{4,5},{5,4},{6,7},{7,6},{8,9},{9,8},{10,11... | collective-permute-start | bytes 393224 | tf_op jit(solution)/shard_map/ppermute | solution.py:317
  33.8 1.4 %collective-permute-start.11 = (f32[256,128]{1,0:T(8,128)S(1)}, f32[256,128]{1,0:T(8,128)S(1)}, u32[]{:S(2)}, u32[]{:S(2)}) collective-permute-start(f32[256,128]{1,0:T(8,128)S(1)} %collective-permute-done.7.refs_6_), channel_id=1, source_target_pairs={{0,1},{1,0},{2,3},{3,2},{4,5},{5,4},{6,7},{7,6},{8,9},{9,8},{10,11... | collective-permute-start | bytes 393224 | tf_op jit(solution)/shard_map/ppermute | solution.py:317
  34.1 1.3 %collective-permute-start.16 = (f32[256,128]{1,0:T(8,128)S(1)}, f32[256,128]{1,0:T(8,128)S(1)}, u32[]{:S(2)}, u32[]{:S(2)}) collective-permute-start(f32[256,128]{1,0:T(8,128)S(1)} %collective-permute-done.3.refs_8_), channel_id=1, source_target_pairs={{0,1},{1,0},{2,3},{3,2},{4,5},{5,4},{6,7},{7,6},{8,9},{9,8},{10,11... | collective-permute-start | bytes 393224 | tf_op jit(solution)/shard_map/ppermute | solution.py:317
  34.3 1.4 %collective-permute-start.17 = (f32[256,128]{1,0:T(8,128)S(1)}, f32[256,128]{1,0:T(8,128)S(1)}, u32[]{:S(2)}, u32[]{:S(2)}) collective-permute-start(f32[256,128]{1,0:T(8,128)S(1)} %collective-permute-done.13.refs_10_), channel_id=1, source_target_pairs={{0,1},{1,0},{2,3},{3,2},{4,5},{5,4},{6,7},{7,6},{8,9},{9,8},{10,11... | collective-permute-start | bytes 393224 | tf_op jit(solution)/shard_map/ppermute | solution.py:317
  34.6 1.3 %collective-permute-start.18 = (f32[256,128]{1,0:T(8,128)S(1)}, f32[256,128]{1,0:T(8,128)S(1)}, u32[]{:S(2)}, u32[]{:S(2)}) collective-permute-start(f32[256,128]{1,0:T(8,128)S(1)} %collective-permute-done.14.refs_12_), channel_id=1, source_target_pairs={{0,1},{1,0},{2,3},{3,2},{4,5},{5,4},{6,7},{7,6},{8,9},{9,8},{10,11... | collective-permute-start | bytes 393224 | tf_op jit(solution)/shard_map/ppermute | solution.py:317
  34.8 1.4 %collective-permute-start.19 = (f32[256,128]{1,0:T(8,128)S(1)}, f32[256,128]{1,0:T(8,128)S(1)}, u32[]{:S(2)}, u32[]{:S(2)}) collective-permute-start(f32[256,128]{1,0:T(8,128)S(1)} %collective-permute-done.15.refs_14_), channel_id=1, source_target_pairs={{0,1},{1,0},{2,3},{3,2},{4,5},{5,4},{6,7},{7,6},{8,9},{9,8},{10,11... | collective-permute-start | bytes 393224 | tf_op jit(solution)/shard_map/ppermute | solution.py:317

commit v15 on v14

--- a/solution.py
+++ b/solution.py
@@ -222,7 +222,7 @@
     far = n_sky // NEAR
     size = 4 * each + SUB
     tile_refs, got_refs = refs[:n_sky], refs[n_sky:n_sky + far]
-    shift_ref, matrix_ref, tiles, chosen, rays, places, sems = refs[n_sky + far:]
+    shift_out, matrix_out, tiles, chosen, rays, places, shift_ref, matrix_ref, sems, out_sems = refs[n_sky + far:]
     me = me_ref[0]
     slots = n_sky * each
     rows = tile_refs[0].shape[0]
@@ -280,9 +280,27 @@
             shift_ref[pl.ds(base * 4 + 2 * h + 1, SUB, stride=4), :] = jnp.where(used, y - y0, 0.0)
             for e in range(4):
                 matrix_ref[pl.ds(base * 8 + 4 * h + e, SUB, stride=8), :] = jnp.where(used, matrix[e], 0.0)
+        for copy in results(step):
+            copy.start()
         return carry
 
+    def results(step):
+        count = together * SUB
+        return [
+            pltpu.make_async_copy(
+                block.at[pl.ds(step * (count * rows_each), count * rows_each), :],
+                out.at[pl.ds(step * (count * rows_each), count * rows_each), :],
+                out_sems.at[kind, step])
+            for kind, (block, out, rows_each) in enumerate(((shift_ref, shift_out, 4), (matrix_ref, matrix_out, 8)))
+        ]
+
+    def finish(step, carry):
+        for copy in results(step):
+            copy.wait()
+        return carry
+
     lax.fori_loop(0, slots // (SUB * together), body, 0)
+    lax.fori_loop(0, slots // (SUB * together), finish, 0)
 
 
 def trace(each, planes, me, lens_weight, tiles, got):
@@ -298,15 +316,18 @@
         ),
         in_specs=[pl.BlockSpec(memory_space=pltpu.SMEM)] * 2 + [pl.BlockSpec(memory_space=pltpu.VMEM)] * (n_sky + len(got)),
         out_specs=(
-            pl.BlockSpec(memory_space=pltpu.VMEM),
-            pl.BlockSpec(memory_space=pltpu.VMEM),
+            pl.BlockSpec(memory_space=pl.ANY),
+            pl.BlockSpec(memory_space=pl.ANY),
         ),
         scratch_shapes=[
             pltpu.VMEM((n_sky * rows, LANES), jnp.float32),
             pltpu.VMEM((planes * together * CHUNKS * SUB, LANES), jnp.float32),
             pltpu.VMEM((slots * 4, LANES), jnp.float32),
             pltpu.SMEM((n_sky * SUB, LANES), jnp.float32),
+            pltpu.VMEM((slots * 4, LANES), jnp.float32),
+            pltpu.VMEM((slots * 8, LANES), jnp.float32),
             pltpu.SemaphoreType.DMA((n_sky,)),
+            pltpu.SemaphoreType.DMA((2, slots // (SUB * 4))),
         ],
         compiler_params=pltpu.CompilerParams(vmem_limit_bytes=20 * 1024 * 1024),
         name="trace",

time: 53.2 us -> 52.8 us (level)
  no operation moved by 1% of the time
where the time goes in v15:
time: 52.8 us; the launch traced here: 52.6 us
  starting transfers between devices  18.1 us (34%)
  Pallas kernels  17.1 us (32%)
  waiting for transfers between devices  14.3 us (27%)
  local copies, waits for them, and re-layouts  2.53 us (5%)
  between operations  0.68 us (1%)
    ppermute x21, starting transfers between devices, flipped(): return lax.ppermute(value, 'sky', [(i, i ^ bits) for i in range(n_sky)])  18.1 us
    pallas_call x1, Pallas kernels, trace(): pl.pallas_call(functools.partial(trace_kernel, n_sky, each, planes, toget...  16.5 us
    ppermute x21, waiting for transfers between devices, flipped(): return lax.ppermute(value, 'sky', [(i, i ^ bits) for i in range(n_sky)])  14.3 us
    unnamed x10, local copies, waits for them, and re-layouts  2.53 us
  transfers between devices with their start and end apart: 21, of which 11 were waited for; matrix products, arithmetic and copies ran while one was open for 0% of the time, Pallas kernels for 0%

profile of v15, /device:TPU:0, one launch (start us, length us, event | category | flops | bytes accessed | tf_op | source)
XLA Modules:
  0.0 52.6 jit_solution(7809695815656899332)
XLA Ops:
  0.7 0.7 %copy-done.2 = s32[4,128]{1,0:T(4,128)S(1)} copy-done((s32[4,128]{1,0:T(4,128)S(1)}, s32[4,128]{1,0:T(4,128)}, u32[]{:S(2)}) %copy-start.2) | copy-done | bytes 2072
  1.3 0.9 %copy-done = f32[128,2,256]{2,1,0:T(2,128)S(1)} copy-done((f32[128,2,256]{2,1,0:T(2,128)S(1)}, f32[128,2,256]{2,1,0:T(2,128)}, u32[]{:S(2)}) %copy-start) | copy-done | bytes 262168
  2.3 0.9 %copy-done.1 = f32[4,8,1024]{2,1,0:T(8,128)S(1)} copy-done((f32[4,8,1024]{2,1,0:T(8,128)S(1)}, f32[4,8,1024]{2,1,0:T(8,128)}, u32[]{:S(2)}) %copy-start.1) | copy-done | bytes 131096
  3.2 0.5 %prepare.1 = (f32[256,128]{1,0:T(8,128)S(1)}, f32[288,128]{1,0:T(8,128)S(1)}, f32[288,128]{1,0:T(8,128)S(1)}, f32[288,128]{1,0:T(8,128)S(1)}, f32[288,128]{1,0:T(8,128)S(1)}) custom-call(s32[1]{0:T(128)} %bitcast.me_ref, s32[1,128]{1,0:T(1,128)S(1)} %bitcast.18, s32[4,128]{1,0:T(4,128)S(1)} %copy-done.2, f32[512,128]{1,0:T(8,128)S(1)} %bitcast.17, ...), custom_call_target="tpu_custom_call" | custom-call | tf_op jit(solution)/shard_map/prepare/pallas_call | solution.py:126
  3.7 4.0 %collective-permute-start.3 = (f32[256,128]{1,0:T(8,128)S(1)}, f32[256,128]{1,0:T(8,128)S(1)}, u32[]{:S(2)}, u32[]{:S(2)}) collective-permute-start(f32[256,128]{1,0:T(8,128)S(1)} %get-tuple-element.42.refs_0_), channel_id=1, source_target_pairs={{0,8},{1,9},{2,10},{3,11},{4,12},{5,13},{6,14},{7,15},{8,0},{9,1},... | collective-permute-start | bytes 393224 | tf_op jit(solution)/shard_map/ppermute | solution.py:338
  7.8 0.0 collective-permute-start
  7.8 1.5 %collective-permute-start.1 = (f32[288,128]{1,0:T(8,128)S(1)}, f32[288,128]{1,0:T(8,128)S(1)}, u32[]{:S(2)}, u32[]{:S(2)}) collective-permute-start(f32[288,128]{1,0:T(8,128)S(1)} %get-tuple-element.32), channel_id=1, source_target_pairs={{0,2},{1,3},{2,0},{3,1},{4,6},{5,7},{6,4},{7,5},{8,10},{9,11},{10,... | collective-permute-start | bytes 442376 | tf_op jit(solution)/shard_map/ppermute | solution.py:338
  9.3 0.3 collective-permute-start.2
  9.6 1.6 %collective-permute-start.4 = (f32[256,128]{1,0:T(8,128)S(1)}, f32[256,128]{1,0:T(8,128)S(1)}, u32[]{:S(2)}, u32[]{:S(2)}) collective-permute-start(f32[256,128]{1,0:T(8,128)S(1)} %get-tuple-element.42.refs_0_), channel_id=1, source_target_pairs={{0,4},{1,5},{2,6},{3,7},{4,0},{5,1},{6,2},{7,3},{8,12},{9,13},{10,... | collective-permute-start | bytes 393224 | tf_op jit(solution)/shard_map/ppermute | solution.py:338
  11.2 3.0 %collective-permute-done.3.refs_8_ = f32[256,128]{1,0:T(8,128)S(1)} collective-permute-done((f32[256,128]{1,0:T(8,128)S(1)}, f32[256,128]{1,0:T(8,128)S(1)}, u32[]{:S(2)}, u32[]{:S(2)}) %collective-permute-start.3) | collective-permute-done | bytes 131104 | tf_op jit(solution)/shard_map/ppermute | solution.py:338
  14.2 0.7 %collective-permute-start.14 = (f32[256,128]{1,0:T(8,128)S(1)}, f32[256,128]{1,0:T(8,128)S(1)}, u32[]{:S(2)}, u32[]{:S(2)}) collective-permute-start(f32[256,128]{1,0:T(8,128)S(1)} %collective-permute-done.3.refs_8_), channel_id=1, source_target_pairs={{0,4},{1,5},{2,6},{3,7},{4,0},{5,1},{6,2},{7,3},{8,12},{9,13},{10,... | collective-permute-start | bytes 393224 | tf_op jit(solution)/shard_map/ppermute | solution.py:338
  14.8 0.0 collective-permute-done.refs_1_
  14.8 0.0 collective-permute-done.1.refs_2_
  14.9 2.0 %collective-permute-done.2.refs_3_ = f32[288,128]{1,0:T(8,128)S(1)} collective-permute-done((f32[288,128]{1,0:T(8,128)S(1)}, f32[288,128]{1,0:T(8,128)S(1)}, u32[]{:S(2)}, u32[]{:S(2)}) %collective-permute-start.2) | collective-permute-done | bytes 147488 | tf_op jit(solution)/shard_map/ppermute | solution.py:338
  16.9 0.1 collective-permute-done.4.refs_4_
  17.0 1.5 %collective-permute-start.6 = (f32[256,128]{1,0:T(8,128)S(1)}, f32[256,128]{1,0:T(8,128)S(1)}, u32[]{:S(2)}, u32[]{:S(2)}) collective-permute-start(f32[256,128]{1,0:T(8,128)S(1)} %get-tuple-element.42.refs_0_), channel_id=1, source_target_pairs={{0,2},{1,3},{2,0},{3,1},{4,6},{5,7},{6,4},{7,5},{8,10},{9,11},{10,... | collective-permute-start | bytes 393224 | tf_op jit(solution)/shard_map/ppermute | solution.py:338
  18.5 1.4 %collective-permute-start.5 = (f32[288,128]{1,0:T(8,128)S(1)}, f32[288,128]{1,0:T(8,128)S(1)}, u32[]{:S(2)}, u32[]{:S(2)}) collective-permute-start(f32[288,128]{1,0:T(8,128)S(1)} %get-tuple-element.39), channel_id=1, source_target_pairs={{0,8},{1,9},{2,10},{3,11},{4,12},{5,13},{6,14},{7,15},{8,0},{9,1},... | collective-permute-start | bytes 442376 | tf_op jit(solution)/shard_map/ppermute | solution.py:338
  20.0 2.4 %collective-permute-start.12 = (f32[288,128]{1,0:T(8,128)S(1)}, f32[288,128]{1,0:T(8,128)S(1)}, u32[]{:S(2)}, u32[]{:S(2)}) collective-permute-start(f32[288,128]{1,0:T(8,128)S(1)} %get-tuple-element.46), channel_id=1, source_target_pairs={{0,12},{1,13},{2,14},{3,15},{4,8},{5,9},{6,10},{7,11},{8,4},{9,5},... | collective-permute-start | bytes 442376 | tf_op jit(solution)/shard_map/ppermute | solution.py:338
  22.4 0.5 collective-permute-start.7
  22.9 0.0 collective-permute-done.14.refs_12_
  22.9 1.5 %collective-permute-start.13 = (f32[256,128]{1,0:T(8,128)S(1)}, f32[256,128]{1,0:T(8,128)S(1)}, u32[]{:S(2)}, u32[]{:S(2)}) collective-permute-start(f32[256,128]{1,0:T(8,128)S(1)} %collective-permute-done.3.refs_8_), channel_id=1, source_target_pairs={{0,2},{1,3},{2,0},{3,1},{4,6},{5,7},{6,4},{7,5},{8,10},{9,11},{10,... | collective-permute-start | bytes 393224 | tf_op jit(solution)/shard_map/ppermute | solution.py:338
  24.4 0.0 collective-permute-done.6.refs_2_
  24.4 0.4 collective-permute-start.20
  24.8 4.0 %collective-permute-done.7.refs_6_ = f32[256,128]{1,0:T(8,128)S(1)} collective-permute-done((f32[256,128]{1,0:T(8,128)S(1)}, f32[256,128]{1,0:T(8,128)S(1)}, u32[]{:S(2)}, u32[]{:S(2)}) %collective-permute-start.7) | collective-permute-done | bytes 131104 | tf_op jit(solution)/shard_map/ppermute | solution.py:338
  28.8 0.5 collective-permute-start.15
  29.3 3.2 %collective-permute-done.5.refs_18_ = f32[288,128]{1,0:T(8,128)S(1)} collective-permute-done((f32[288,128]{1,0:T(8,128)S(1)}, f32[288,128]{1,0:T(8,128)S(1)}, u32[]{:S(2)}, u32[]{:S(2)}) %collective-permute-start.5) | collective-permute-done | bytes 147488 | tf_op jit(solution)/shard_map/ppermute | solution.py:338
  32.5 0.0 collective-permute-start.8
  32.5 0.0 collective-permute-done.13.refs_10_
  32.5 0.5 collective-permute-start.9
  33.0 0.0 collective-permute-done.12.refs_19_
  33.0 0.1 collective-permute-start.10
  33.1 0.7 %collective-permute-done.15.refs_14_ = f32[256,128]{1,0:T(8,128)S(1)} collective-permute-done((f32[256,128]{1,0:T(8,128)S(1)}, f32[256,128]{1,0:T(8,128)S(1)}, u32[]{:S(2)}, u32[]{:S(2)}) %collective-permute-start.15) | collective-permute-done | bytes 131104 | tf_op jit(solution)/shard_map/ppermute | solution.py:338
  33.8 0.0 collective-permute-start.11
  33.8 0.3 collective-permute-done.20.refs_17_
  34.1 0.2 collective-permute-start.16
  34.3 0.0 collective-permute-done.8.refs_1_
  34.3 0.3 collective-permute-start.17
  34.6 0.0 collective-permute-done.9.refs_3_
  34.6 0.2 collective-permute-start.18
  34.8 0.0 collective-permute-done.10.refs_5_
  34.8 0.3 collective-permute-start.19
  35.1 0.0 collective-permute-done.11.refs_7_
  35.1 0.3 collective-permute-done.16.refs_9_
  35.5 0.2 collective-permute-done.17.refs_11_
  35.6 0.3 collective-permute-done.18.refs_13_
  36.0 0.2 collective-permute-done.19.refs_15_
  36.2 0.0 copy-done.4
  36.2 16.5 %trace.1 = (f32[1024,128]{1,0:T(8,128)}, f32[2048,128]{1,0:T(8,128)}) custom-call(s32[1]{0:T(128)} %bitcast.me_ref, f32[4]{0:T(128)S(1)} %copy-done.4, f32[256,128]{1,0:T(8,128)S(1)} %get-tuple-element.42.refs_0_, f32[256,128]{1,0:T(8,128)S(1)} %collective-permute-done.8.refs_1_, f32[256,128]{1,0:T(8,128)S(1)} %collective-permute-done.6.refs_2_, ...), custom_call_target="tpu_custom_call" | custom-call | tf_op jit(solution)/shard_map/trace/pallas_call | solution.py:311
  (7 shorter events, 0.1 us)
Async XLA Ops:
  0.6 0.7 %copy-start.2 = (s32[4,128]{1,0:T(4,128)S(1)}, s32[4,128]{1,0:T(4,128)}, u32[]{:S(2)}) copy-start(s32[4,128]{1,0:T(4,128)} %ids_ref.1) | copy-start | bytes 6148
  0.6 0.7 %copy-start.3 = (s32[128,1]{0,1:T(1,128)S(1)}, s32[128,1]{0,1:T(1,128)}, u32[]{:S(2)}) copy-start(s32[128,1]{0,1:T(1,128)} %param.9) | copy-start | bytes 1540
  1.3 1.0 %copy-start = (f32[128,2,256]{2,1,0:T(2,128)S(1)}, f32[128,2,256]{2,1,0:T(2,128)}, u32[]{:S(2)}) copy-start(f32[128,2,256]{2,1,0:T(2,128)} %param.7) | copy-start | bytes 786436
  2.3 0.9 %copy-start.1 = (f32[4,8,1024]{2,1,0:T(8,128)S(1)}, f32[4,8,1024]{2,1,0:T(8,128)}, u32[]{:S(2)}) copy-start(f32[4,8,1024]{2,1,0:T(8,128)} %src_ref.1) | copy-start | bytes 393220
  3.7 10.5 %collective-permute-start.3 = (f32[256,128]{1,0:T(8,128)S(1)}, f32[256,128]{1,0:T(8,128)S(1)}, u32[]{:S(2)}, u32[]{:S(2)}) collective-permute-start(f32[256,128]{1,0:T(8,128)S(1)} %get-tuple-element.42.refs_0_), channel_id=1, source_target_pairs={{0,8},{1,9},{2,10},{3,11},{4,12},{5,13},{6,14},{7,15},{8,0},{9,1},... | collective-permute-start | bytes 393224 | tf_op jit(solution)/shard_map/ppermute | solution.py:338
  7.8 7.1 %collective-permute-start = (f32[288,128]{1,0:T(8,128)S(1)}, f32[288,128]{1,0:T(8,128)S(1)}, u32[]{:S(2)}, u32[]{:S(2)}) collective-permute-start(f32[288,128]{1,0:T(8,128)S(1)} %get-tuple-element.31), channel_id=1, source_target_pairs={{0,1},{1,0},{2,3},{3,2},{4,5},{5,4},{6,7},{7,6},{8,9},{9,8},{10,11... | collective-permute-start | bytes 442376 | tf_op jit(solution)/shard_map/ppermute | solution.py:338
  7.8 7.1 %collective-permute-start.1 = (f32[288,128]{1,0:T(8,128)S(1)}, f32[288,128]{1,0:T(8,128)S(1)}, u32[]{:S(2)}, u32[]{:S(2)}) collective-permute-start(f32[288,128]{1,0:T(8,128)S(1)} %get-tuple-element.32), channel_id=1, source_target_pairs={{0,2},{1,3},{2,0},{3,1},{4,6},{5,7},{6,4},{7,5},{8,10},{9,11},{10,... | collective-permute-start | bytes 442376 | tf_op jit(solution)/shard_map/ppermute | solution.py:338
  9.3 7.5 %collective-permute-start.2 = (f32[288,128]{1,0:T(8,128)S(1)}, f32[288,128]{1,0:T(8,128)S(1)}, u32[]{:S(2)}, u32[]{:S(2)}) collective-permute-start(f32[288,128]{1,0:T(8,128)S(1)} %get-tuple-element.33), channel_id=1, source_target_pairs={{0,3},{1,2},{2,1},{3,0},{4,7},{5,6},{6,5},{7,4},{8,11},{9,10},{10,... | collective-permute-start | bytes 442376 | tf_op jit(solution)/shard_map/ppermute | solution.py:338
  9.6 7.3 %collective-permute-start.4 = (f32[256,128]{1,0:T(8,128)S(1)}, f32[256,128]{1,0:T(8,128)S(1)}, u32[]{:S(2)}, u32[]{:S(2)}) collective-permute-start(f32[256,128]{1,0:T(8,128)S(1)} %get-tuple-element.42.refs_0_), channel_id=1, source_target_pairs={{0,4},{1,5},{2,6},{3,7},{4,0},{5,1},{6,2},{7,3},{8,12},{9,13},{10,... | collective-permute-start | bytes 393224 | tf_op jit(solution)/shard_map/ppermute | solution.py:338
  14.2 8.7 %collective-permute-start.14 = (f32[256,128]{1,0:T(8,128)S(1)}, f32[256,128]{1,0:T(8,128)S(1)}, u32[]{:S(2)}, u32[]{:S(2)}) collective-permute-start(f32[256,128]{1,0:T(8,128)S(1)} %collective-permute-done.3.refs_8_), channel_id=1, source_target_pairs={{0,4},{1,5},{2,6},{3,7},{4,0},{5,1},{6,2},{7,3},{8,12},{9,13},{10,... | collective-permute-start | bytes 393224 | tf_op jit(solution)/shard_map/ppermute | solution.py:338
  17.0 19.2 %copy-start.4 = (f32[4]{0:T(128)S(1)}, f32[4]{0:T(128)}, u32[]{:S(2)}) copy-start(f32[4]{0:T(128)} %lens_ref.1) | copy-start | bytes 52
  17.0 7.4 %collective-permute-start.6 = (f32[256,128]{1,0:T(8,128)S(1)}, f32[256,128]{1,0:T(8,128)S(1)}, u32[]{:S(2)}, u32[]{:S(2)}) collective-permute-start(f32[256,128]{1,0:T(8,128)S(1)} %get-tuple-element.42.refs_0_), channel_id=1, source_target_pairs={{0,2},{1,3},{2,0},{3,1},{4,6},{5,7},{6,4},{7,5},{8,10},{9,11},{10,... | collective-permute-start | bytes 393224 | tf_op jit(solution)/shard_map/ppermute | solution.py:338
  18.5 14.0 %collective-permute-start.5 = (f32[288,128]{1,0:T(8,128)S(1)}, f32[288,128]{1,0:T(8,128)S(1)}, u32[]{:S(2)}, u32[]{:S(2)}) collective-permute-start(f32[288,128]{1,0:T(8,128)S(1)} %get-tuple-element.39), channel_id=1, source_target_pairs={{0,8},{1,9},{2,10},{3,11},{4,12},{5,13},{6,14},{7,15},{8,0},{9,1},... | collective-permute-start | bytes 442376 | tf_op jit(solution)/shard_map/ppermute | solution.py:338
  20.0 13.1 %collective-permute-start.12 = (f32[288,128]{1,0:T(8,128)S(1)}, f32[288,128]{1,0:T(8,128)S(1)}, u32[]{:S(2)}, u32[]{:S(2)}) collective-permute-start(f32[288,128]{1,0:T(8,128)S(1)} %get-tuple-element.46), channel_id=1, source_target_pairs={{0,12},{1,13},{2,14},{3,15},{4,8},{5,9},{6,10},{7,11},{8,4},{9,5},... | collective-permute-start | bytes 442376 | tf_op jit(solution)/shard_map/ppermute | solution.py:338
  22.4 6.4 %collective-permute-start.7 = (f32[256,128]{1,0:T(8,128)S(1)}, f32[256,128]{1,0:T(8,128)S(1)}, u32[]{:S(2)}, u32[]{:S(2)}) collective-permute-start(f32[256,128]{1,0:T(8,128)S(1)} %collective-permute-done.4.refs_4_), channel_id=1, source_target_pairs={{0,2},{1,3},{2,0},{3,1},{4,6},{5,7},{6,4},{7,5},{8,10},{9,11},{10,... | collective-permute-start | bytes 393224 | tf_op jit(solution)/shard_map/ppermute | solution.py:338
  22.9 9.6 %collective-permute-start.13 = (f32[256,128]{1,0:T(8,128)S(1)}, f32[256,128]{1,0:T(8,128)S(1)}, u32[]{:S(2)}, u32[]{:S(2)}) collective-permute-start(f32[256,128]{1,0:T(8,128)S(1)} %collective-permute-done.3.refs_8_), channel_id=1, source_target_pairs={{0,2},{1,3},{2,0},{3,1},{4,6},{5,7},{6,4},{7,5},{8,10},{9,11},{10,... | collective-permute-start | bytes 393224 | tf_op jit(solution)/shard_map/ppermute | solution.py:338
  24.4 9.7 %collective-permute-start.20 = (f32[288,128]{1,0:T(8,128)S(1)}, f32[288,128]{1,0:T(8,128)S(1)}, u32[]{:S(2)}, u32[]{:S(2)}) collective-permute-start(f32[288,128]{1,0:T(8,128)S(1)} %get-tuple-element.53), channel_id=1, source_target_pairs={{0,4},{1,5},{2,6},{3,7},{4,0},{5,1},{6,2},{7,3},{8,12},{9,13},{10,... | collective-permute-start | bytes 442376 | tf_op jit(solution)/shard_map/ppermute | solution.py:338
  28.8 5.0 %collective-permute-start.15 = (f32[256,128]{1,0:T(8,128)S(1)}, f32[256,128]{1,0:T(8,128)S(1)}, u32[]{:S(2)}, u32[]{:S(2)}) collective-permute-start(f32[256,128]{1,0:T(8,128)S(1)} %collective-permute-done.14.refs_12_), channel_id=1, source_target_pairs={{0,2},{1,3},{2,0},{3,1},{4,6},{5,7},{6,4},{7,5},{8,10},{9,11},{10,... | collective-permute-start | bytes 393224 | tf_op jit(solution)/shard_map/ppermute | solution.py:338
  32.5 1.8 %collective-permute-start.8 = (f32[256,128]{1,0:T(8,128)S(1)}, f32[256,128]{1,0:T(8,128)S(1)}, u32[]{:S(2)}, u32[]{:S(2)}) collective-permute-start(f32[256,128]{1,0:T(8,128)S(1)} %get-tuple-element.42.refs_0_), channel_id=1, source_target_pairs={{0,1},{1,0},{2,3},{3,2},{4,5},{5,4},{6,7},{7,6},{8,9},{9,8},{10,11... | collective-permute-start | bytes 393224 | tf_op jit(solution)/shard_map/ppermute | solution.py:338
  32.5 2.1 %collective-permute-start.9 = (f32[256,128]{1,0:T(8,128)S(1)}, f32[256,128]{1,0:T(8,128)S(1)}, u32[]{:S(2)}, u32[]{:S(2)}) collective-permute-start(f32[256,128]{1,0:T(8,128)S(1)} %collective-permute-done.6.refs_2_), channel_id=1, source_target_pairs={{0,1},{1,0},{2,3},{3,2},{4,5},{5,4},{6,7},{7,6},{8,9},{9,8},{10,11... | collective-permute-start | bytes 393224 | tf_op jit(solution)/shard_map/ppermute | solution.py:338
  33.0 1.8 %collective-permute-start.10 = (f32[256,128]{1,0:T(8,128)S(1)}, f32[256,128]{1,0:T(8,128)S(1)}, u32[]{:S(2)}, u32[]{:S(2)}) collective-permute-start(f32[256,128]{1,0:T(8,128)S(1)} %collective-permute-done.4.refs_4_), channel_id=1, source_target_pairs={{0,1},{1,0},{2,3},{3,2},{4,5},{5,4},{6,7},{7,6},{8,9},{9,8},{10,11... | collective-permute-start | bytes 393224 | tf_op jit(solution)/shard_map/ppermute | solution.py:338
  33.8 1.4 %collective-permute-start.11 = (f32[256,128]{1,0:T(8,128)S(1)}, f32[256,128]{1,0:T(8,128)S(1)}, u32[]{:S(2)}, u32[]{:S(2)}) collective-permute-start(f32[256,128]{1,0:T(8,128)S(1)} %collective-permute-done.7.refs_6_), channel_id=1, source_target_pairs={{0,1},{1,0},{2,3},{3,2},{4,5},{5,4},{6,7},{7,6},{8,9},{9,8},{10,11... | collective-permute-start | bytes 393224 | tf_op jit(solution)/shard_map/ppermute | solution.py:338
  34.1 1.3 %collective-permute-start.16 = (f32[256,128]{1,0:T(8,128)S(1)}, f32[256,128]{1,0:T(8,128)S(1)}, u32[]{:S(2)}, u32[]{:S(2)}) collective-permute-start(f32[256,128]{1,0:T(8,128)S(1)} %collective-permute-done.3.refs_8_), channel_id=1, source_target_pairs={{0,1},{1,0},{2,3},{3,2},{4,5},{5,4},{6,7},{7,6},{8,9},{9,8},{10,11... | collective-permute-start | bytes 393224 | tf_op jit(solution)/shard_map/ppermute | solution.py:338
  34.3 1.4 %collective-permute-start.17 = (f32[256,128]{1,0:T(8,128)S(1)}, f32[256,128]{1,0:T(8,128)S(1)}, u32[]{:S(2)}, u32[]{:S(2)}) collective-permute-start(f32[256,128]{1,0:T(8,128)S(1)} %collective-permute-done.13.refs_10_), channel_id=1, source_target_pairs={{0,1},{1,0},{2,3},{3,2},{4,5},{5,4},{6,7},{7,6},{8,9},{9,8},{10,11... | collective-permute-start | bytes 393224 | tf_op jit(solution)/shard_map/ppermute | solution.py:338
  34.6 1.3 %collective-permute-start.18 = (f32[256,128]{1,0:T(8,128)S(1)}, f32[256,128]{1,0:T(8,128)S(1)}, u32[]{:S(2)}, u32[]{:S(2)}) collective-permute-start(f32[256,128]{1,0:T(8,128)S(1)} %collective-permute-done.14.refs_12_), channel_id=1, source_target_pairs={{0,1},{1,0},{2,3},{3,2},{4,5},{5,4},{6,7},{7,6},{8,9},{9,8},{10,11... | collective-permute-start | bytes 393224 | tf_op jit(solution)/shard_map/ppermute | solution.py:338
  34.8 1.4 %collective-permute-start.19 = (f32[256,128]{1,0:T(8,128)S(1)}, f32[256,128]{1,0:T(8,128)S(1)}, u32[]{:S(2)}, u32[]{:S(2)}) collective-permute-start(f32[256,128]{1,0:T(8,128)S(1)} %collective-permute-done.15.refs_14_), channel_id=1, source_target_pairs={{0,1},{1,0},{2,3},{3,2},{4,5},{5,4},{6,7},{7,6},{8,9},{9,8},{10,11... | collective-permute-start | bytes 393224 | tf_op jit(solution)/shard_map/ppermute | solution.py:338

commit v16 on v15

--- a/solution.py
+++ b/solution.py
@@ -362,9 +362,9 @@
         held[bit] = flipped(own, n_sky, bit)
     held[bits[0] ^ bits[1]] = flipped(held[bits[0]], n_sky, bits[1])
     got = turn(4 * each + SUB, sent)
-    early = [0, bits[0], bits[1]]
-    *got, a, b, c = lax.optimization_barrier((*got, *[held[s] for s in early]))
-    held.update(zip(early, (a, b, c)))
+    early = [0, bits[0]]
+    *got, a, b = lax.optimization_barrier((*got, *[held[s] for s in early]))
+    held.update(zip(early, (a, b)))
     got = [got[0]] + [flipped(got[f], n_sky, f * NEAR) for f in range(1, len(got))]
     spread(held, n_sky, bits[:-1])
     half = len(got) // 2

time: 52.8 us -> 52.4 us (level)
  waiting for transfers between devices: 14.3 us -> 13.2 us
  starting transfers between devices: 18.1 us -> 18.7 us
    ppermute x21, waiting for transfers between devices: 14.3 us -> 13.2 us  [flipped(): return lax.ppermute(value, 'sky', [(i, i ^ bits) for i in range(n_sky)])]
    ppermute x21, starting transfers between devices: 18.1 us -> 18.7 us  [flipped(): return lax.ppermute(value, 'sky', [(i, i ^ bits) for i in range(n_sky)])]
  transfers between devices with their start and end apart: 21 -> 21, of which waited for: 11 -> 10; matrix products, arithmetic and copies ran while one was open for 0% -> 0% of each run, Pallas kernels for 0% -> 0%
where the time goes in v16:
time: 52.4 us; the launch traced here: 52.2 us
  starting transfers between devices  18.7 us (36%)
  Pallas kernels  17.1 us (33%)
  waiting for transfers between devices  13.2 us (25%)
  local copies, waits for them, and re-layouts  2.53 us (5%)
  between operations  0.7 us (1%)
    ppermute x21, starting transfers between devices, flipped(): return lax.ppermute(value, 'sky', [(i, i ^ bits) for i in range(n_sky)])  18.7 us
    pallas_call x1, Pallas kernels, trace(): pl.pallas_call(functools.partial(trace_kernel, n_sky, each, planes, toget...  16.5 us
    ppermute x21, waiting for transfers between devices, flipped(): return lax.ppermute(value, 'sky', [(i, i ^ bits) for i in range(n_sky)])  13.2 us
    unnamed x10, local copies, waits for them, and re-layouts  2.53 us
  transfers between devices with their start and end apart: 21, of which 10 were waited for; matrix products, arithmetic and copies ran while one was open for 0% of the time, Pallas kernels for 0%

profile of v16, /device:TPU:0, one launch (start us, length us, event | category | flops | bytes accessed | tf_op | source)
XLA Modules:
  0.0 52.2 jit_solution(11256659907714332605)
XLA Ops:
  0.7 0.7 %copy-done.2 = s32[4,128]{1,0:T(4,128)S(1)} copy-done((s32[4,128]{1,0:T(4,128)S(1)}, s32[4,128]{1,0:T(4,128)}, u32[]{:S(2)}) %copy-start.2) | copy-done | bytes 2072
  1.3 0.9 %copy-done = f32[128,2,256]{2,1,0:T(2,128)S(1)} copy-done((f32[128,2,256]{2,1,0:T(2,128)S(1)}, f32[128,2,256]{2,1,0:T(2,128)}, u32[]{:S(2)}) %copy-start) | copy-done | bytes 262168
  2.3 0.9 %copy-done.1 = f32[4,8,1024]{2,1,0:T(8,128)S(1)} copy-done((f32[4,8,1024]{2,1,0:T(8,128)S(1)}, f32[4,8,1024]{2,1,0:T(8,128)}, u32[]{:S(2)}) %copy-start.1) | copy-done | bytes 131096
  3.2 0.5 %prepare.1 = (f32[256,128]{1,0:T(8,128)S(1)}, f32[288,128]{1,0:T(8,128)S(1)}, f32[288,128]{1,0:T(8,128)S(1)}, f32[288,128]{1,0:T(8,128)S(1)}, f32[288,128]{1,0:T(8,128)S(1)}) custom-call(s32[1]{0:T(128)} %bitcast.me_ref, s32[1,128]{1,0:T(1,128)S(1)} %bitcast.18, s32[4,128]{1,0:T(4,128)S(1)} %copy-done.2, f32[512,128]{1,0:T(8,128)S(1)} %bitcast.17, ...), custom_call_target="tpu_custom_call" | custom-call | tf_op jit(solution)/shard_map/prepare/pallas_call | solution.py:126
  3.7 3.0 %collective-permute-start.6 = (f32[256,128]{1,0:T(8,128)S(1)}, f32[256,128]{1,0:T(8,128)S(1)}, u32[]{:S(2)}, u32[]{:S(2)}) collective-permute-start(f32[256,128]{1,0:T(8,128)S(1)} %get-tuple-element.40.refs_0_), channel_id=1, source_target_pairs={{0,4},{1,5},{2,6},{3,7},{4,0},{5,1},{6,2},{7,3},{8,12},{9,13},{10,... | collective-permute-start | bytes 393224 | tf_op jit(solution)/shard_map/ppermute | solution.py:338
  6.8 0.0 collective-permute-start
  6.8 1.5 %collective-permute-start.1 = (f32[288,128]{1,0:T(8,128)S(1)}, f32[288,128]{1,0:T(8,128)S(1)}, u32[]{:S(2)}, u32[]{:S(2)}) collective-permute-start(f32[288,128]{1,0:T(8,128)S(1)} %get-tuple-element.31), channel_id=1, source_target_pairs={{0,2},{1,3},{2,0},{3,1},{4,6},{5,7},{6,4},{7,5},{8,10},{9,11},{10,... | collective-permute-start | bytes 442376 | tf_op jit(solution)/shard_map/ppermute | solution.py:338
  8.3 0.3 collective-permute-start.2
  8.6 2.6 %collective-permute-start.3 = (f32[256,128]{1,0:T(8,128)S(1)}, f32[256,128]{1,0:T(8,128)S(1)}, u32[]{:S(2)}, u32[]{:S(2)}) collective-permute-start(f32[256,128]{1,0:T(8,128)S(1)} %get-tuple-element.40.refs_0_), channel_id=1, source_target_pairs={{0,8},{1,9},{2,10},{3,11},{4,12},{5,13},{6,14},{7,15},{8,0},{9,1},... | collective-permute-start | bytes 393224 | tf_op jit(solution)/shard_map/ppermute | solution.py:338
  11.2 0.0 collective-permute-done.6.refs_4_
  11.2 1.5 %collective-permute-start.7 = (f32[256,128]{1,0:T(8,128)S(1)}, f32[256,128]{1,0:T(8,128)S(1)}, u32[]{:S(2)}, u32[]{:S(2)}) collective-permute-start(f32[256,128]{1,0:T(8,128)S(1)} %collective-permute-done.6.refs_4_), channel_id=1, source_target_pairs={{0,2},{1,3},{2,0},{3,1},{4,6},{5,7},{6,4},{7,5},{8,10},{9,11},{10,... | collective-permute-start | bytes 393224 | tf_op jit(solution)/shard_map/ppermute | solution.py:338
  12.7 5.2 %collective-permute-done.3.refs_8_ = f32[256,128]{1,0:T(8,128)S(1)} collective-permute-done((f32[256,128]{1,0:T(8,128)S(1)}, f32[256,128]{1,0:T(8,128)S(1)}, u32[]{:S(2)}, u32[]{:S(2)}) %collective-permute-start.3) | collective-permute-done | bytes 131104 | tf_op jit(solution)/shard_map/ppermute | solution.py:338
  18.0 0.0 collective-permute-start.14
  18.0 0.0 collective-permute-done.refs_1_
  18.0 0.0 collective-permute-done.1.refs_2_
  18.0 0.0 collective-permute-done.2.refs_3_
  18.0 0.0 copy-start.4
  18.0 3.1 %collective-permute-start.4 = (f32[288,128]{1,0:T(8,128)S(1)}, f32[288,128]{1,0:T(8,128)S(1)}, u32[]{:S(2)}, u32[]{:S(2)}) collective-permute-start(f32[288,128]{1,0:T(8,128)S(1)} %get-tuple-element.38), channel_id=1, source_target_pairs={{0,8},{1,9},{2,10},{3,11},{4,12},{5,13},{6,14},{7,15},{8,0},{9,1},... | collective-permute-start | bytes 442376 | tf_op jit(solution)/shard_map/ppermute | solution.py:338
  21.2 1.3 %collective-permute-start.12 = (f32[288,128]{1,0:T(8,128)S(1)}, f32[288,128]{1,0:T(8,128)S(1)}, u32[]{:S(2)}, u32[]{:S(2)}) collective-permute-start(f32[288,128]{1,0:T(8,128)S(1)} %get-tuple-element.44), channel_id=1, source_target_pairs={{0,12},{1,13},{2,14},{3,15},{4,8},{5,9},{6,10},{7,11},{8,4},{9,5},... | collective-permute-start | bytes 442376 | tf_op jit(solution)/shard_map/ppermute | solution.py:338
  22.5 1.6 %collective-permute-start.5 = (f32[256,128]{1,0:T(8,128)S(1)}, f32[256,128]{1,0:T(8,128)S(1)}, u32[]{:S(2)}, u32[]{:S(2)}) collective-permute-start(f32[256,128]{1,0:T(8,128)S(1)} %get-tuple-element.40.refs_0_), channel_id=1, source_target_pairs={{0,2},{1,3},{2,0},{3,1},{4,6},{5,7},{6,4},{7,5},{8,10},{9,11},{10,... | collective-permute-start | bytes 393224 | tf_op jit(solution)/shard_map/ppermute | solution.py:338
  24.0 0.0 collective-permute-done.7.refs_6_
  24.0 0.5 collective-permute-start.13
  24.5 0.7 %collective-permute-done.14.refs_12_ = f32[256,128]{1,0:T(8,128)S(1)} collective-permute-done((f32[256,128]{1,0:T(8,128)S(1)}, f32[256,128]{1,0:T(8,128)S(1)}, u32[]{:S(2)}, u32[]{:S(2)}) %collective-permute-start.14) | collective-permute-done | bytes 131104 | tf_op jit(solution)/shard_map/ppermute | solution.py:338
  25.3 0.0 collective-permute-start.20
  25.3 3.1 %collective-permute-done.5.refs_2_ = f32[256,128]{1,0:T(8,128)S(1)} collective-permute-done((f32[256,128]{1,0:T(8,128)S(1)}, f32[256,128]{1,0:T(8,128)S(1)}, u32[]{:S(2)}, u32[]{:S(2)}) %collective-permute-start.5) | collective-permute-done | bytes 131104 | tf_op jit(solution)/shard_map/ppermute | solution.py:338
  28.4 1.6 %collective-permute-start.15 = (f32[256,128]{1,0:T(8,128)S(1)}, f32[256,128]{1,0:T(8,128)S(1)}, u32[]{:S(2)}, u32[]{:S(2)}) collective-permute-start(f32[256,128]{1,0:T(8,128)S(1)} %collective-permute-done.14.refs_12_), channel_id=1, source_target_pairs={{0,2},{1,3},{2,0},{3,1},{4,6},{5,7},{6,4},{7,5},{8,10},{9,11},{10,... | collective-permute-start | bytes 393224 | tf_op jit(solution)/shard_map/ppermute | solution.py:338
  30.0 2.3 %collective-permute-done.4.refs_18_ = f32[288,128]{1,0:T(8,128)S(1)} collective-permute-done((f32[288,128]{1,0:T(8,128)S(1)}, f32[288,128]{1,0:T(8,128)S(1)}, u32[]{:S(2)}, u32[]{:S(2)}) %collective-permute-start.4) | collective-permute-done | bytes 147488 | tf_op jit(solution)/shard_map/ppermute | solution.py:338
  32.3 0.0 collective-permute-start.8
  32.3 0.0 collective-permute-done.13.refs_10_
  32.3 0.5 collective-permute-start.9
  32.8 0.0 collective-permute-done.12.refs_19_
  32.8 0.1 collective-permute-start.10
  32.9 0.5 collective-permute-done.15.refs_14_
  33.4 0.0 collective-permute-start.11
  33.4 0.3 collective-permute-done.20.refs_17_
  33.7 0.2 collective-permute-start.16
  33.9 0.0 collective-permute-done.8.refs_1_
  33.9 0.3 collective-permute-start.17
  34.2 0.0 collective-permute-done.9.refs_3_
  34.2 0.2 collective-permute-start.18
  34.4 0.0 collective-permute-done.10.refs_5_
  34.4 0.3 collective-permute-start.19
  34.7 0.0 collective-permute-done.11.refs_7_
  34.7 0.3 collective-permute-done.16.refs_9_
  35.0 0.2 collective-permute-done.17.refs_11_
  35.2 0.3 collective-permute-done.18.refs_13_
  35.6 0.2 collective-permute-done.19.refs_15_
  35.8 16.5 %trace.1 = (f32[1024,128]{1,0:T(8,128)}, f32[2048,128]{1,0:T(8,128)}) custom-call(s32[1]{0:T(128)} %bitcast.me_ref, f32[4]{0:T(128)S(1)} %copy-done.4, f32[256,128]{1,0:T(8,128)S(1)} %get-tuple-element.40.refs_0_, f32[256,128]{1,0:T(8,128)S(1)} %collective-permute-done.8.refs_1_, f32[256,128]{1,0:T(8,128)S(1)} %collective-permute-done.5.refs_2_, ...), custom_call_target="tpu_custom_call" | custom-call | tf_op jit(solution)/shard_map/trace/pallas_call | solution.py:311
  (7 shorter events, 0.1 us)
Async XLA Ops:
  0.6 0.7 %copy-start.2 = (s32[4,128]{1,0:T(4,128)S(1)}, s32[4,128]{1,0:T(4,128)}, u32[]{:S(2)}) copy-start(s32[4,128]{1,0:T(4,128)} %ids_ref.1) | copy-start | bytes 6148
  0.6 0.7 %copy-start.3 = (s32[128,1]{0,1:T(1,128)S(1)}, s32[128,1]{0,1:T(1,128)}, u32[]{:S(2)}) copy-start(s32[128,1]{0,1:T(1,128)} %param.9) | copy-start | bytes 1540
  1.3 1.0 %copy-start = (f32[128,2,256]{2,1,0:T(2,128)S(1)}, f32[128,2,256]{2,1,0:T(2,128)}, u32[]{:S(2)}) copy-start(f32[128,2,256]{2,1,0:T(2,128)} %param.7) | copy-start | bytes 786436
  2.3 0.9 %copy-start.1 = (f32[4,8,1024]{2,1,0:T(8,128)S(1)}, f32[4,8,1024]{2,1,0:T(8,128)}, u32[]{:S(2)}) copy-start(f32[4,8,1024]{2,1,0:T(8,128)} %src_ref.1) | copy-start | bytes 393220
  3.7 7.5 %collective-permute-start.6 = (f32[256,128]{1,0:T(8,128)S(1)}, f32[256,128]{1,0:T(8,128)S(1)}, u32[]{:S(2)}, u32[]{:S(2)}) collective-permute-start(f32[256,128]{1,0:T(8,128)S(1)} %get-tuple-element.40.refs_0_), channel_id=1, source_target_pairs={{0,4},{1,5},{2,6},{3,7},{4,0},{5,1},{6,2},{7,3},{8,12},{9,13},{10,... | collective-permute-start | bytes 393224 | tf_op jit(solution)/shard_map/ppermute | solution.py:338
  6.8 11.2 %collective-permute-start = (f32[288,128]{1,0:T(8,128)S(1)}, f32[288,128]{1,0:T(8,128)S(1)}, u32[]{:S(2)}, u32[]{:S(2)}) collective-permute-start(f32[288,128]{1,0:T(8,128)S(1)} %get-tuple-element.30), channel_id=1, source_target_pairs={{0,1},{1,0},{2,3},{3,2},{4,5},{5,4},{6,7},{7,6},{8,9},{9,8},{10,11... | collective-permute-start | bytes 442376 | tf_op jit(solution)/shard_map/ppermute | solution.py:338
  6.8 11.2 %collective-permute-start.1 = (f32[288,128]{1,0:T(8,128)S(1)}, f32[288,128]{1,0:T(8,128)S(1)}, u32[]{:S(2)}, u32[]{:S(2)}) collective-permute-start(f32[288,128]{1,0:T(8,128)S(1)} %get-tuple-element.31), channel_id=1, source_target_pairs={{0,2},{1,3},{2,0},{3,1},{4,6},{5,7},{6,4},{7,5},{8,10},{9,11},{10,... | collective-permute-start | bytes 442376 | tf_op jit(solution)/shard_map/ppermute | solution.py:338
  8.3 9.7 %collective-permute-start.2 = (f32[288,128]{1,0:T(8,128)S(1)}, f32[288,128]{1,0:T(8,128)S(1)}, u32[]{:S(2)}, u32[]{:S(2)}) collective-permute-start(f32[288,128]{1,0:T(8,128)S(1)} %get-tuple-element.32), channel_id=1, source_target_pairs={{0,3},{1,2},{2,1},{3,0},{4,7},{5,6},{6,5},{7,4},{8,11},{9,10},{10,... | collective-permute-start | bytes 442376 | tf_op jit(solution)/shard_map/ppermute | solution.py:338
  8.6 9.3 %collective-permute-start.3 = (f32[256,128]{1,0:T(8,128)S(1)}, f32[256,128]{1,0:T(8,128)S(1)}, u32[]{:S(2)}, u32[]{:S(2)}) collective-permute-start(f32[256,128]{1,0:T(8,128)S(1)} %get-tuple-element.40.refs_0_), channel_id=1, source_target_pairs={{0,8},{1,9},{2,10},{3,11},{4,12},{5,13},{6,14},{7,15},{8,0},{9,1},... | collective-permute-start | bytes 393224 | tf_op jit(solution)/shard_map/ppermute | solution.py:338
  11.2 12.8 %collective-permute-start.7 = (f32[256,128]{1,0:T(8,128)S(1)}, f32[256,128]{1,0:T(8,128)S(1)}, u32[]{:S(2)}, u32[]{:S(2)}) collective-permute-start(f32[256,128]{1,0:T(8,128)S(1)} %collective-permute-done.6.refs_4_), channel_id=1, source_target_pairs={{0,2},{1,3},{2,0},{3,1},{4,6},{5,7},{6,4},{7,5},{8,10},{9,11},{10,... | collective-permute-start | bytes 393224 | tf_op jit(solution)/shard_map/ppermute | solution.py:338
  18.0 7.3 %collective-permute-start.14 = (f32[256,128]{1,0:T(8,128)S(1)}, f32[256,128]{1,0:T(8,128)S(1)}, u32[]{:S(2)}, u32[]{:S(2)}) collective-permute-start(f32[256,128]{1,0:T(8,128)S(1)} %collective-permute-done.3.refs_8_), channel_id=1, source_target_pairs={{0,4},{1,5},{2,6},{3,7},{4,0},{5,1},{6,2},{7,3},{8,12},{9,13},{10,... | collective-permute-start | bytes 393224 | tf_op jit(solution)/shard_map/ppermute | solution.py:338
  18.0 17.7 %copy-start.4 = (f32[4]{0:T(128)S(1)}, f32[4]{0:T(128)}, u32[]{:S(2)}) copy-start(f32[4]{0:T(128)} %lens_ref.1) | copy-start | bytes 52
  18.0 14.2 %collective-permute-start.4 = (f32[288,128]{1,0:T(8,128)S(1)}, f32[288,128]{1,0:T(8,128)S(1)}, u32[]{:S(2)}, u32[]{:S(2)}) collective-permute-start(f32[288,128]{1,0:T(8,128)S(1)} %get-tuple-element.38), channel_id=1, source_target_pairs={{0,8},{1,9},{2,10},{3,11},{4,12},{5,13},{6,14},{7,15},{8,0},{9,1},... | collective-permute-start | bytes 442376 | tf_op jit(solution)/shard_map/ppermute | solution.py:338
  21.2 11.6 %collective-permute-start.12 = (f32[288,128]{1,0:T(8,128)S(1)}, f32[288,128]{1,0:T(8,128)S(1)}, u32[]{:S(2)}, u32[]{:S(2)}) collective-permute-start(f32[288,128]{1,0:T(8,128)S(1)} %get-tuple-element.44), channel_id=1, source_target_pairs={{0,12},{1,13},{2,14},{3,15},{4,8},{5,9},{6,10},{7,11},{8,4},{9,5},... | collective-permute-start | bytes 442376 | tf_op jit(solution)/shard_map/ppermute | solution.py:338
  22.5 5.9 %collective-permute-start.5 = (f32[256,128]{1,0:T(8,128)S(1)}, f32[256,128]{1,0:T(8,128)S(1)}, u32[]{:S(2)}, u32[]{:S(2)}) collective-permute-start(f32[256,128]{1,0:T(8,128)S(1)} %get-tuple-element.40.refs_0_), channel_id=1, source_target_pairs={{0,2},{1,3},{2,0},{3,1},{4,6},{5,7},{6,4},{7,5},{8,10},{9,11},{10,... | collective-permute-start | bytes 393224 | tf_op jit(solution)/shard_map/ppermute | solution.py:338
  24.0 8.2 %collective-permute-start.13 = (f32[256,128]{1,0:T(8,128)S(1)}, f32[256,128]{1,0:T(8,128)S(1)}, u32[]{:S(2)}, u32[]{:S(2)}) collective-permute-start(f32[256,128]{1,0:T(8,128)S(1)} %collective-permute-done.3.refs_8_), channel_id=1, source_target_pairs={{0,2},{1,3},{2,0},{3,1},{4,6},{5,7},{6,4},{7,5},{8,10},{9,11},{10,... | collective-permute-start | bytes 393224 | tf_op jit(solution)/shard_map/ppermute | solution.py:338
  25.3 8.4 %collective-permute-start.20 = (f32[288,128]{1,0:T(8,128)S(1)}, f32[288,128]{1,0:T(8,128)S(1)}, u32[]{:S(2)}, u32[]{:S(2)}) collective-permute-start(f32[288,128]{1,0:T(8,128)S(1)} %get-tuple-element.51), channel_id=1, source_target_pairs={{0,4},{1,5},{2,6},{3,7},{4,0},{5,1},{6,2},{7,3},{8,12},{9,13},{10,... | collective-permute-start | bytes 442376 | tf_op jit(solution)/shard_map/ppermute | solution.py:338
  28.4 5.0 %collective-permute-start.15 = (f32[256,128]{1,0:T(8,128)S(1)}, f32[256,128]{1,0:T(8,128)S(1)}, u32[]{:S(2)}, u32[]{:S(2)}) collective-permute-start(f32[256,128]{1,0:T(8,128)S(1)} %collective-permute-done.14.refs_12_), channel_id=1, source_target_pairs={{0,2},{1,3},{2,0},{3,1},{4,6},{5,7},{6,4},{7,5},{8,10},{9,11},{10,... | collective-permute-start | bytes 393224 | tf_op jit(solution)/shard_map/ppermute | solution.py:338
  32.3 1.6 %collective-permute-start.8 = (f32[256,128]{1,0:T(8,128)S(1)}, f32[256,128]{1,0:T(8,128)S(1)}, u32[]{:S(2)}, u32[]{:S(2)}) collective-permute-start(f32[256,128]{1,0:T(8,128)S(1)} %get-tuple-element.40.refs_0_), channel_id=1, source_target_pairs={{0,1},{1,0},{2,3},{3,2},{4,5},{5,4},{6,7},{7,6},{8,9},{9,8},{10,11... | collective-permute-start | bytes 393224 | tf_op jit(solution)/shard_map/ppermute | solution.py:338
  32.3 1.9 %collective-permute-start.9 = (f32[256,128]{1,0:T(8,128)S(1)}, f32[256,128]{1,0:T(8,128)S(1)}, u32[]{:S(2)}, u32[]{:S(2)}) collective-permute-start(f32[256,128]{1,0:T(8,128)S(1)} %collective-permute-done.5.refs_2_), channel_id=1, source_target_pairs={{0,1},{1,0},{2,3},{3,2},{4,5},{5,4},{6,7},{7,6},{8,9},{9,8},{10,11... | collective-permute-start | bytes 393224 | tf_op jit(solution)/shard_map/ppermute | solution.py:338
  32.8 1.6 %collective-permute-start.10 = (f32[256,128]{1,0:T(8,128)S(1)}, f32[256,128]{1,0:T(8,128)S(1)}, u32[]{:S(2)}, u32[]{:S(2)}) collective-permute-start(f32[256,128]{1,0:T(8,128)S(1)} %collective-permute-done.6.refs_4_), channel_id=1, source_target_pairs={{0,1},{1,0},{2,3},{3,2},{4,5},{5,4},{6,7},{7,6},{8,9},{9,8},{10,11... | collective-permute-start | bytes 393224 | tf_op jit(solution)/shard_map/ppermute | solution.py:338
  33.4 1.4 %collective-permute-start.11 = (f32[256,128]{1,0:T(8,128)S(1)}, f32[256,128]{1,0:T(8,128)S(1)}, u32[]{:S(2)}, u32[]{:S(2)}) collective-permute-start(f32[256,128]{1,0:T(8,128)S(1)} %collective-permute-done.7.refs_6_), channel_id=1, source_target_pairs={{0,1},{1,0},{2,3},{3,2},{4,5},{5,4},{6,7},{7,6},{8,9},{9,8},{10,11... | collective-permute-start | bytes 393224 | tf_op jit(solution)/shard_map/ppermute | solution.py:338
  33.7 1.3 %collective-permute-start.16 = (f32[256,128]{1,0:T(8,128)S(1)}, f32[256,128]{1,0:T(8,128)S(1)}, u32[]{:S(2)}, u32[]{:S(2)}) collective-permute-start(f32[256,128]{1,0:T(8,128)S(1)} %collective-permute-done.3.refs_8_), channel_id=1, source_target_pairs={{0,1},{1,0},{2,3},{3,2},{4,5},{5,4},{6,7},{7,6},{8,9},{9,8},{10,11... | collective-permute-start | bytes 393224 | tf_op jit(solution)/shard_map/ppermute | solution.py:338
  33.9 1.3 %collective-permute-start.17 = (f32[256,128]{1,0:T(8,128)S(1)}, f32[256,128]{1,0:T(8,128)S(1)}, u32[]{:S(2)}, u32[]{:S(2)}) collective-permute-start(f32[256,128]{1,0:T(8,128)S(1)} %collective-permute-done.13.refs_10_), channel_id=1, source_target_pairs={{0,1},{1,0},{2,3},{3,2},{4,5},{5,4},{6,7},{7,6},{8,9},{9,8},{10,11... | collective-permute-start | bytes 393224 | tf_op jit(solution)/shard_map/ppermute | solution.py:338
  34.2 1.3 %collective-permute-start.18 = (f32[256,128]{1,0:T(8,128)S(1)}, f32[256,128]{1,0:T(8,128)S(1)}, u32[]{:S(2)}, u32[]{:S(2)}) collective-permute-start(f32[256,128]{1,0:T(8,128)S(1)} %collective-permute-done.14.refs_12_), channel_id=1, source_target_pairs={{0,1},{1,0},{2,3},{3,2},{4,5},{5,4},{6,7},{7,6},{8,9},{9,8},{10,11... | collective-permute-start | bytes 393224 | tf_op jit(solution)/shard_map/ppermute | solution.py:338
  34.4 1.3 %collective-permute-start.19 = (f32[256,128]{1,0:T(8,128)S(1)}, f32[256,128]{1,0:T(8,128)S(1)}, u32[]{:S(2)}, u32[]{:S(2)}) collective-permute-start(f32[256,128]{1,0:T(8,128)S(1)} %collective-permute-done.15.refs_14_), channel_id=1, source_target_pairs={{0,1},{1,0},{2,3},{3,2},{4,5},{5,4},{6,7},{7,6},{8,9},{9,8},{10,11... | collective-permute-start | bytes 393224 | tf_op jit(solution)/shard_map/ppermute | solution.py:338

commit v17 on v16

--- a/solution.py
+++ b/solution.py
@@ -362,9 +362,9 @@
         held[bit] = flipped(own, n_sky, bit)
     held[bits[0] ^ bits[1]] = flipped(held[bits[0]], n_sky, bits[1])
     got = turn(4 * each + SUB, sent)
-    early = [0, bits[0]]
-    *got, a, b = lax.optimization_barrier((*got, *[held[s] for s in early]))
-    held.update(zip(early, (a, b)))
+    early = [0]
+    *got, a = lax.optimization_barrier((*got, *[held[s] for s in early]))
+    held.update(zip(early, (a,)))
     got = [got[0]] + [flipped(got[f], n_sky, f * NEAR) for f in range(1, len(got))]
     spread(held, n_sky, bits[:-1])
     half = len(got) // 2

time: 52.4 us -> 52.8 us (level)
  waiting for transfers between devices: 13.2 us -> 14.1 us
    ppermute x21, waiting for transfers between devices: 13.2 us -> 14.1 us  [flipped(): return lax.ppermute(value, 'sky', [(i, i ^ bits) for i in range(n_sky)])]
where the time goes in v17:
time: 52.8 us; the launch traced here: 52.6 us
  starting transfers between devices  18.2 us (34%)
  Pallas kernels  17.1 us (32%)
  waiting for transfers between devices  14.1 us (27%)
  local copies, waits for them, and re-layouts  2.53 us (5%)
  between operations  0.69 us (1%)
    ppermute x21, starting transfers between devices, flipped(): return lax.ppermute(value, 'sky', [(i, i ^ bits) for i in range(n_sky)])  18.2 us
    pallas_call x1, Pallas kernels, trace(): pl.pallas_call(functools.partial(trace_kernel, n_sky, each, planes, toget...  16.5 us
    ppermute x21, waiting for transfers between devices, flipped(): return lax.ppermute(value, 'sky', [(i, i ^ bits) for i in range(n_sky)])  14.1 us
    unnamed x10, local copies, waits for them, and re-layouts  2.53 us
  transfers between devices with their start and end apart: 21, of which 10 were waited for; matrix products, arithmetic and copies ran while one was open for 0% of the time, Pallas kernels for 0%

profile of v17, /device:TPU:0, one launch (start us, length us, event | category | flops | bytes accessed | tf_op | source)
XLA Modules:
  0.0 52.6 jit_solution(4965705035833817947)
XLA Ops:
  0.7 0.7 %copy-done.2 = s32[4,128]{1,0:T(4,128)S(1)} copy-done((s32[4,128]{1,0:T(4,128)S(1)}, s32[4,128]{1,0:T(4,128)}, u32[]{:S(2)}) %copy-start.2) | copy-done | bytes 2072
  1.3 0.9 %copy-done = f32[128,2,256]{2,1,0:T(2,128)S(1)} copy-done((f32[128,2,256]{2,1,0:T(2,128)S(1)}, f32[128,2,256]{2,1,0:T(2,128)}, u32[]{:S(2)}) %copy-start) | copy-done | bytes 262168
  2.3 0.9 %copy-done.1 = f32[4,8,1024]{2,1,0:T(8,128)S(1)} copy-done((f32[4,8,1024]{2,1,0:T(8,128)S(1)}, f32[4,8,1024]{2,1,0:T(8,128)}, u32[]{:S(2)}) %copy-start.1) | copy-done | bytes 131096
  3.2 0.5 %prepare.1 = (f32[256,128]{1,0:T(8,128)S(1)}, f32[288,128]{1,0:T(8,128)S(1)}, f32[288,128]{1,0:T(8,128)S(1)}, f32[288,128]{1,0:T(8,128)S(1)}, f32[288,128]{1,0:T(8,128)S(1)}) custom-call(s32[1]{0:T(128)} %bitcast.me_ref, s32[1,128]{1,0:T(1,128)S(1)} %bitcast.18, s32[4,128]{1,0:T(4,128)S(1)} %copy-done.2, f32[512,128]{1,0:T(8,128)S(1)} %bitcast.17, ...), custom_call_target="tpu_custom_call" | custom-call | tf_op jit(solution)/shard_map/prepare/pallas_call | solution.py:126
  3.7 4.0 %collective-permute-start.12 = (f32[256,128]{1,0:T(8,128)S(1)}, f32[256,128]{1,0:T(8,128)S(1)}, u32[]{:S(2)}, u32[]{:S(2)}) collective-permute-start(f32[256,128]{1,0:T(8,128)S(1)} %get-tuple-element.39.refs_0_), channel_id=1, source_target_pairs={{0,8},{1,9},{2,10},{3,11},{4,12},{5,13},{6,14},{7,15},{8,0},{9,1},... | collective-permute-start | bytes 393224 | tf_op jit(solution)/shard_map/ppermute | solution.py:338
  7.8 0.0 collective-permute-start
  7.8 1.5 %collective-permute-start.1 = (f32[288,128]{1,0:T(8,128)S(1)}, f32[288,128]{1,0:T(8,128)S(1)}, u32[]{:S(2)}, u32[]{:S(2)}) collective-permute-start(f32[288,128]{1,0:T(8,128)S(1)} %get-tuple-element.30), channel_id=1, source_target_pairs={{0,2},{1,3},{2,0},{3,1},{4,6},{5,7},{6,4},{7,5},{8,10},{9,11},{10,... | collective-permute-start | bytes 442376 | tf_op jit(solution)/shard_map/ppermute | solution.py:338
  9.3 0.3 collective-permute-start.2
  9.6 1.6 %collective-permute-start.5 = (f32[256,128]{1,0:T(8,128)S(1)}, f32[256,128]{1,0:T(8,128)S(1)}, u32[]{:S(2)}, u32[]{:S(2)}) collective-permute-start(f32[256,128]{1,0:T(8,128)S(1)} %get-tuple-element.39.refs_0_), channel_id=1, source_target_pairs={{0,4},{1,5},{2,6},{3,7},{4,0},{5,1},{6,2},{7,3},{8,12},{9,13},{10,... | collective-permute-start | bytes 393224 | tf_op jit(solution)/shard_map/ppermute | solution.py:338
  11.2 3.0 %collective-permute-done.12.refs_8_ = f32[256,128]{1,0:T(8,128)S(1)} collective-permute-done((f32[256,128]{1,0:T(8,128)S(1)}, f32[256,128]{1,0:T(8,128)S(1)}, u32[]{:S(2)}, u32[]{:S(2)}) %collective-permute-start.12) | collective-permute-done | bytes 131104 | tf_op jit(solution)/shard_map/ppermute | solution.py:338
  14.2 0.7 %collective-permute-start.14 = (f32[256,128]{1,0:T(8,128)S(1)}, f32[256,128]{1,0:T(8,128)S(1)}, u32[]{:S(2)}, u32[]{:S(2)}) collective-permute-start(f32[256,128]{1,0:T(8,128)S(1)} %collective-permute-done.12.refs_8_), channel_id=1, source_target_pairs={{0,4},{1,5},{2,6},{3,7},{4,0},{5,1},{6,2},{7,3},{8,12},{9,13},{10,... | collective-permute-start | bytes 393224 | tf_op jit(solution)/shard_map/ppermute | solution.py:338
  14.8 2.1 %collective-permute-done.5.refs_4_ = f32[256,128]{1,0:T(8,128)S(1)} collective-permute-done((f32[256,128]{1,0:T(8,128)S(1)}, f32[256,128]{1,0:T(8,128)S(1)}, u32[]{:S(2)}, u32[]{:S(2)}) %collective-permute-start.5) | collective-permute-done | bytes 131104 | tf_op jit(solution)/shard_map/ppermute | solution.py:338
  17.0 1.5 %collective-permute-start.6 = (f32[256,128]{1,0:T(8,128)S(1)}, f32[256,128]{1,0:T(8,128)S(1)}, u32[]{:S(2)}, u32[]{:S(2)}) collective-permute-start(f32[256,128]{1,0:T(8,128)S(1)} %collective-permute-done.5.refs_4_), channel_id=1, source_target_pairs={{0,2},{1,3},{2,0},{3,1},{4,6},{5,7},{6,4},{7,5},{8,10},{9,11},{10,... | collective-permute-start | bytes 393224 | tf_op jit(solution)/shard_map/ppermute | solution.py:338
  18.5 0.0 collective-permute-done.refs_1_
  18.5 0.0 collective-permute-done.1.refs_2_
  18.5 0.0 collective-permute-done.2.refs_3_
  18.6 0.0 copy-start.4
  18.6 1.4 %collective-permute-start.3 = (f32[288,128]{1,0:T(8,128)S(1)}, f32[288,128]{1,0:T(8,128)S(1)}, u32[]{:S(2)}, u32[]{:S(2)}) collective-permute-start(f32[288,128]{1,0:T(8,128)S(1)} %get-tuple-element.37), channel_id=1, source_target_pairs={{0,8},{1,9},{2,10},{3,11},{4,12},{5,13},{6,14},{7,15},{8,0},{9,1},... | collective-permute-start | bytes 442376 | tf_op jit(solution)/shard_map/ppermute | solution.py:338
  20.0 1.2 %collective-permute-start.11 = (f32[288,128]{1,0:T(8,128)S(1)}, f32[288,128]{1,0:T(8,128)S(1)}, u32[]{:S(2)}, u32[]{:S(2)}) collective-permute-start(f32[288,128]{1,0:T(8,128)S(1)} %get-tuple-element.43), channel_id=1, source_target_pairs={{0,12},{1,13},{2,14},{3,15},{4,8},{5,9},{6,10},{7,11},{8,4},{9,5},... | collective-permute-start | bytes 442376 | tf_op jit(solution)/shard_map/ppermute | solution.py:338
  21.1 1.3 %collective-permute-start.4 = (f32[256,128]{1,0:T(8,128)S(1)}, f32[256,128]{1,0:T(8,128)S(1)}, u32[]{:S(2)}, u32[]{:S(2)}) collective-permute-start(f32[256,128]{1,0:T(8,128)S(1)} %get-tuple-element.39.refs_0_), channel_id=1, source_target_pairs={{0,2},{1,3},{2,0},{3,1},{4,6},{5,7},{6,4},{7,5},{8,10},{9,11},{10,... | collective-permute-start | bytes 393224 | tf_op jit(solution)/shard_map/ppermute | solution.py:338
  22.4 0.0 collective-permute-done.14.refs_12_
  22.4 0.8 %collective-permute-start.13 = (f32[256,128]{1,0:T(8,128)S(1)}, f32[256,128]{1,0:T(8,128)S(1)}, u32[]{:S(2)}, u32[]{:S(2)}) collective-permute-start(f32[256,128]{1,0:T(8,128)S(1)} %collective-permute-done.12.refs_8_), channel_id=1, source_target_pairs={{0,2},{1,3},{2,0},{3,1},{4,6},{5,7},{6,4},{7,5},{8,10},{9,11},{10,... | collective-permute-start | bytes 393224 | tf_op jit(solution)/shard_map/ppermute | solution.py:338
  23.2 0.0 collective-permute-done.6.refs_6_
  23.2 1.0 %collective-permute-start.20 = (f32[288,128]{1,0:T(8,128)S(1)}, f32[288,128]{1,0:T(8,128)S(1)}, u32[]{:S(2)}, u32[]{:S(2)}) collective-permute-start(f32[288,128]{1,0:T(8,128)S(1)} %get-tuple-element.49), channel_id=1, source_target_pairs={{0,4},{1,5},{2,6},{3,7},{4,0},{5,1},{6,2},{7,3},{8,12},{9,13},{10,... | collective-permute-start | bytes 442376 | tf_op jit(solution)/shard_map/ppermute | solution.py:338
  24.2 3.3 %collective-permute-done.4.refs_2_ = f32[256,128]{1,0:T(8,128)S(1)} collective-permute-done((f32[256,128]{1,0:T(8,128)S(1)}, f32[256,128]{1,0:T(8,128)S(1)}, u32[]{:S(2)}, u32[]{:S(2)}) %collective-permute-start.4) | collective-permute-done | bytes 131104 | tf_op jit(solution)/shard_map/ppermute | solution.py:338
  27.5 1.2 %collective-permute-start.15 = (f32[256,128]{1,0:T(8,128)S(1)}, f32[256,128]{1,0:T(8,128)S(1)}, u32[]{:S(2)}, u32[]{:S(2)}) collective-permute-start(f32[256,128]{1,0:T(8,128)S(1)} %collective-permute-done.14.refs_12_), channel_id=1, source_target_pairs={{0,2},{1,3},{2,0},{3,1},{4,6},{5,7},{6,4},{7,5},{8,10},{9,11},{10,... | collective-permute-start | bytes 393224 | tf_op jit(solution)/shard_map/ppermute | solution.py:338
  28.8 2.8 %collective-permute-done.3.refs_18_ = f32[288,128]{1,0:T(8,128)S(1)} collective-permute-done((f32[288,128]{1,0:T(8,128)S(1)}, f32[288,128]{1,0:T(8,128)S(1)}, u32[]{:S(2)}, u32[]{:S(2)}) %collective-permute-start.3) | collective-permute-done | bytes 147488 | tf_op jit(solution)/shard_map/ppermute | solution.py:338
  31.6 0.0 collective-permute-start.7
  31.6 0.0 collective-permute-done.13.refs_10_
  31.6 0.5 collective-permute-start.8
  32.1 0.0 collective-permute-done.11.refs_19_
  32.1 0.1 collective-permute-start.9
  32.2 0.3 collective-permute-done.15.refs_14_
  32.5 0.1 collective-permute-start.10
  32.6 1.4 %collective-permute-done.20.refs_17_ = f32[288,128]{1,0:T(8,128)S(1)} collective-permute-done((f32[288,128]{1,0:T(8,128)S(1)}, f32[288,128]{1,0:T(8,128)S(1)}, u32[]{:S(2)}, u32[]{:S(2)}) %collective-permute-start.20) | collective-permute-done | bytes 147488 | tf_op jit(solution)/shard_map/ppermute | solution.py:338
  34.0 0.0 collective-permute-start.16
  34.0 0.0 collective-permute-done.7.refs_1_
  34.0 0.5 collective-permute-start.17
  34.6 0.0 collective-permute-done.8.refs_3_
  34.6 0.1 collective-permute-start.18
  34.6 0.0 collective-permute-done.9.refs_5_
  34.6 0.4 collective-permute-start.19
  35.1 0.0 collective-permute-done.10.refs_7_
  35.1 0.3 collective-permute-done.16.refs_9_
  35.4 0.2 collective-permute-done.17.refs_11_
  35.6 0.3 collective-permute-done.18.refs_13_
  35.9 0.2 collective-permute-done.19.refs_15_
  36.1 16.5 %trace.1 = (f32[1024,128]{1,0:T(8,128)}, f32[2048,128]{1,0:T(8,128)}) custom-call(s32[1]{0:T(128)} %bitcast.me_ref, f32[4]{0:T(128)S(1)} %copy-done.4, f32[256,128]{1,0:T(8,128)S(1)} %get-tuple-element.39.refs_0_, f32[256,128]{1,0:T(8,128)S(1)} %collective-permute-done.7.refs_1_, f32[256,128]{1,0:T(8,128)S(1)} %collective-permute-done.4.refs_2_, ...), custom_call_target="tpu_custom_call" | custom-call | tf_op jit(solution)/shard_map/trace/pallas_call | solution.py:311
  (7 shorter events, 0.1 us)
Async XLA Ops:
  0.6 0.7 %copy-start.2 = (s32[4,128]{1,0:T(4,128)S(1)}, s32[4,128]{1,0:T(4,128)}, u32[]{:S(2)}) copy-start(s32[4,128]{1,0:T(4,128)} %ids_ref.1) | copy-start | bytes 6148
  0.6 0.7 %copy-start.3 = (s32[128,1]{0,1:T(1,128)S(1)}, s32[128,1]{0,1:T(1,128)}, u32[]{:S(2)}) copy-start(s32[128,1]{0,1:T(1,128)} %param.9) | copy-start | bytes 1540
  1.3 1.0 %copy-start = (f32[128,2,256]{2,1,0:T(2,128)S(1)}, f32[128,2,256]{2,1,0:T(2,128)}, u32[]{:S(2)}) copy-start(f32[128,2,256]{2,1,0:T(2,128)} %param.7) | copy-start | bytes 786436
  2.3 0.9 %copy-start.1 = (f32[4,8,1024]{2,1,0:T(8,128)S(1)}, f32[4,8,1024]{2,1,0:T(8,128)}, u32[]{:S(2)}) copy-start(f32[4,8,1024]{2,1,0:T(8,128)} %src_ref.1) | copy-start | bytes 393220
  3.7 10.5 %collective-permute-start.12 = (f32[256,128]{1,0:T(8,128)S(1)}, f32[256,128]{1,0:T(8,128)S(1)}, u32[]{:S(2)}, u32[]{:S(2)}) collective-permute-start(f32[256,128]{1,0:T(8,128)S(1)} %get-tuple-element.39.refs_0_), channel_id=1, source_target_pairs={{0,8},{1,9},{2,10},{3,11},{4,12},{5,13},{6,14},{7,15},{8,0},{9,1},... | collective-permute-start | bytes 393224 | tf_op jit(solution)/shard_map/ppermute | solution.py:338
  7.8 10.8 %collective-permute-start = (f32[288,128]{1,0:T(8,128)S(1)}, f32[288,128]{1,0:T(8,128)S(1)}, u32[]{:S(2)}, u32[]{:S(2)}) collective-permute-start(f32[288,128]{1,0:T(8,128)S(1)} %get-tuple-element.29), channel_id=1, source_target_pairs={{0,1},{1,0},{2,3},{3,2},{4,5},{5,4},{6,7},{7,6},{8,9},{9,8},{10,11... | collective-permute-start | bytes 442376 | tf_op jit(solution)/shard_map/ppermute | solution.py:338
  7.8 10.8 %collective-permute-start.1 = (f32[288,128]{1,0:T(8,128)S(1)}, f32[288,128]{1,0:T(8,128)S(1)}, u32[]{:S(2)}, u32[]{:S(2)}) collective-permute-start(f32[288,128]{1,0:T(8,128)S(1)} %get-tuple-element.30), channel_id=1, source_target_pairs={{0,2},{1,3},{2,0},{3,1},{4,6},{5,7},{6,4},{7,5},{8,10},{9,11},{10,... | collective-permute-start | bytes 442376 | tf_op jit(solution)/shard_map/ppermute | solution.py:338
  9.3 9.2 %collective-permute-start.2 = (f32[288,128]{1,0:T(8,128)S(1)}, f32[288,128]{1,0:T(8,128)S(1)}, u32[]{:S(2)}, u32[]{:S(2)}) collective-permute-start(f32[288,128]{1,0:T(8,128)S(1)} %get-tuple-element.31), channel_id=1, source_target_pairs={{0,3},{1,2},{2,1},{3,0},{4,7},{5,6},{6,5},{7,4},{8,11},{9,10},{10,... | collective-permute-start | bytes 442376 | tf_op jit(solution)/shard_map/ppermute | solution.py:338
  9.6 7.3 %collective-permute-start.5 = (f32[256,128]{1,0:T(8,128)S(1)}, f32[256,128]{1,0:T(8,128)S(1)}, u32[]{:S(2)}, u32[]{:S(2)}) collective-permute-start(f32[256,128]{1,0:T(8,128)S(1)} %get-tuple-element.39.refs_0_), channel_id=1, source_target_pairs={{0,4},{1,5},{2,6},{3,7},{4,0},{5,1},{6,2},{7,3},{8,12},{9,13},{10,... | collective-permute-start | bytes 393224 | tf_op jit(solution)/shard_map/ppermute | solution.py:338
  14.2 8.2 %collective-permute-start.14 = (f32[256,128]{1,0:T(8,128)S(1)}, f32[256,128]{1,0:T(8,128)S(1)}, u32[]{:S(2)}, u32[]{:S(2)}) collective-permute-start(f32[256,128]{1,0:T(8,128)S(1)} %collective-permute-done.12.refs_8_), channel_id=1, source_target_pairs={{0,4},{1,5},{2,6},{3,7},{4,0},{5,1},{6,2},{7,3},{8,12},{9,13},{10,... | collective-permute-start | bytes 393224 | tf_op jit(solution)/shard_map/ppermute | solution.py:338
  17.0 6.2 %collective-permute-start.6 = (f32[256,128]{1,0:T(8,128)S(1)}, f32[256,128]{1,0:T(8,128)S(1)}, u32[]{:S(2)}, u32[]{:S(2)}) collective-permute-start(f32[256,128]{1,0:T(8,128)S(1)} %collective-permute-done.5.refs_4_), channel_id=1, source_target_pairs={{0,2},{1,3},{2,0},{3,1},{4,6},{5,7},{6,4},{7,5},{8,10},{9,11},{10,... | collective-permute-start | bytes 393224 | tf_op jit(solution)/shard_map/ppermute | solution.py:338
  18.6 17.5 %copy-start.4 = (f32[4]{0:T(128)S(1)}, f32[4]{0:T(128)}, u32[]{:S(2)}) copy-start(f32[4]{0:T(128)} %lens_ref.1) | copy-start | bytes 52
  18.6 13.0 %collective-permute-start.3 = (f32[288,128]{1,0:T(8,128)S(1)}, f32[288,128]{1,0:T(8,128)S(1)}, u32[]{:S(2)}, u32[]{:S(2)}) collective-permute-start(f32[288,128]{1,0:T(8,128)S(1)} %get-tuple-element.37), channel_id=1, source_target_pairs={{0,8},{1,9},{2,10},{3,11},{4,12},{5,13},{6,14},{7,15},{8,0},{9,1},... | collective-permute-start | bytes 442376 | tf_op jit(solution)/shard_map/ppermute | solution.py:338
  20.0 12.1 %collective-permute-start.11 = (f32[288,128]{1,0:T(8,128)S(1)}, f32[288,128]{1,0:T(8,128)S(1)}, u32[]{:S(2)}, u32[]{:S(2)}) collective-permute-start(f32[288,128]{1,0:T(8,128)S(1)} %get-tuple-element.43), channel_id=1, source_target_pairs={{0,12},{1,13},{2,14},{3,15},{4,8},{5,9},{6,10},{7,11},{8,4},{9,5},... | collective-permute-start | bytes 442376 | tf_op jit(solution)/shard_map/ppermute | solution.py:338
  21.1 6.4 %collective-permute-start.4 = (f32[256,128]{1,0:T(8,128)S(1)}, f32[256,128]{1,0:T(8,128)S(1)}, u32[]{:S(2)}, u32[]{:S(2)}) collective-permute-start(f32[256,128]{1,0:T(8,128)S(1)} %get-tuple-element.39.refs_0_), channel_id=1, source_target_pairs={{0,2},{1,3},{2,0},{3,1},{4,6},{5,7},{6,4},{7,5},{8,10},{9,11},{10,... | collective-permute-start | bytes 393224 | tf_op jit(solution)/shard_map/ppermute | solution.py:338
  22.4 9.2 %collective-permute-start.13 = (f32[256,128]{1,0:T(8,128)S(1)}, f32[256,128]{1,0:T(8,128)S(1)}, u32[]{:S(2)}, u32[]{:S(2)}) collective-permute-start(f32[256,128]{1,0:T(8,128)S(1)} %collective-permute-done.12.refs_8_), channel_id=1, source_target_pairs={{0,2},{1,3},{2,0},{3,1},{4,6},{5,7},{6,4},{7,5},{8,10},{9,11},{10,... | collective-permute-start | bytes 393224 | tf_op jit(solution)/shard_map/ppermute | solution.py:338
  23.2 10.9 %collective-permute-start.20 = (f32[288,128]{1,0:T(8,128)S(1)}, f32[288,128]{1,0:T(8,128)S(1)}, u32[]{:S(2)}, u32[]{:S(2)}) collective-permute-start(f32[288,128]{1,0:T(8,128)S(1)} %get-tuple-element.49), channel_id=1, source_target_pairs={{0,4},{1,5},{2,6},{3,7},{4,0},{5,1},{6,2},{7,3},{8,12},{9,13},{10,... | collective-permute-start | bytes 442376 | tf_op jit(solution)/shard_map/ppermute | solution.py:338
  27.5 5.0 %collective-permute-start.15 = (f32[256,128]{1,0:T(8,128)S(1)}, f32[256,128]{1,0:T(8,128)S(1)}, u32[]{:S(2)}, u32[]{:S(2)}) collective-permute-start(f32[256,128]{1,0:T(8,128)S(1)} %collective-permute-done.14.refs_12_), channel_id=1, source_target_pairs={{0,2},{1,3},{2,0},{3,1},{4,6},{5,7},{6,4},{7,5},{8,10},{9,11},{10,... | collective-permute-start | bytes 393224 | tf_op jit(solution)/shard_map/ppermute | solution.py:338
  31.6 2.5 %collective-permute-start.7 = (f32[256,128]{1,0:T(8,128)S(1)}, f32[256,128]{1,0:T(8,128)S(1)}, u32[]{:S(2)}, u32[]{:S(2)}) collective-permute-start(f32[256,128]{1,0:T(8,128)S(1)} %get-tuple-element.39.refs_0_), channel_id=1, source_target_pairs={{0,1},{1,0},{2,3},{3,2},{4,5},{5,4},{6,7},{7,6},{8,9},{9,8},{10,11... | collective-permute-start | bytes 393224 | tf_op jit(solution)/shard_map/ppermute | solution.py:338
  31.6 3.0 %collective-permute-start.8 = (f32[256,128]{1,0:T(8,128)S(1)}, f32[256,128]{1,0:T(8,128)S(1)}, u32[]{:S(2)}, u32[]{:S(2)}) collective-permute-start(f32[256,128]{1,0:T(8,128)S(1)} %collective-permute-done.4.refs_2_), channel_id=1, source_target_pairs={{0,1},{1,0},{2,3},{3,2},{4,5},{5,4},{6,7},{7,6},{8,9},{9,8},{10,11... | collective-permute-start | bytes 393224 | tf_op jit(solution)/shard_map/ppermute | solution.py:338
  32.1 2.6 %collective-permute-start.9 = (f32[256,128]{1,0:T(8,128)S(1)}, f32[256,128]{1,0:T(8,128)S(1)}, u32[]{:S(2)}, u32[]{:S(2)}) collective-permute-start(f32[256,128]{1,0:T(8,128)S(1)} %collective-permute-done.5.refs_4_), channel_id=1, source_target_pairs={{0,1},{1,0},{2,3},{3,2},{4,5},{5,4},{6,7},{7,6},{8,9},{9,8},{10,11... | collective-permute-start | bytes 393224 | tf_op jit(solution)/shard_map/ppermute | solution.py:338
  32.5 2.6 %collective-permute-start.10 = (f32[256,128]{1,0:T(8,128)S(1)}, f32[256,128]{1,0:T(8,128)S(1)}, u32[]{:S(2)}, u32[]{:S(2)}) collective-permute-start(f32[256,128]{1,0:T(8,128)S(1)} %collective-permute-done.6.refs_6_), channel_id=1, source_target_pairs={{0,1},{1,0},{2,3},{3,2},{4,5},{5,4},{6,7},{7,6},{8,9},{9,8},{10,11... | collective-permute-start | bytes 393224 | tf_op jit(solution)/shard_map/ppermute | solution.py:338
  34.0 1.3 %collective-permute-start.16 = (f32[256,128]{1,0:T(8,128)S(1)}, f32[256,128]{1,0:T(8,128)S(1)}, u32[]{:S(2)}, u32[]{:S(2)}) collective-permute-start(f32[256,128]{1,0:T(8,128)S(1)} %collective-permute-done.12.refs_8_), channel_id=1, source_target_pairs={{0,1},{1,0},{2,3},{3,2},{4,5},{5,4},{6,7},{7,6},{8,9},{9,8},{10,11... | collective-permute-start | bytes 393224 | tf_op jit(solution)/shard_map/ppermute | solution.py:338
  34.0 1.5 %collective-permute-start.17 = (f32[256,128]{1,0:T(8,128)S(1)}, f32[256,128]{1,0:T(8,128)S(1)}, u32[]{:S(2)}, u32[]{:S(2)}) collective-permute-start(f32[256,128]{1,0:T(8,128)S(1)} %collective-permute-done.13.refs_10_), channel_id=1, source_target_pairs={{0,1},{1,0},{2,3},{3,2},{4,5},{5,4},{6,7},{7,6},{8,9},{9,8},{10,11... | collective-permute-start | bytes 393224 | tf_op jit(solution)/shard_map/ppermute | solution.py:338
  34.6 1.3 %collective-permute-start.18 = (f32[256,128]{1,0:T(8,128)S(1)}, f32[256,128]{1,0:T(8,128)S(1)}, u32[]{:S(2)}, u32[]{:S(2)}) collective-permute-start(f32[256,128]{1,0:T(8,128)S(1)} %collective-permute-done.14.refs_12_), channel_id=1, source_target_pairs={{0,1},{1,0},{2,3},{3,2},{4,5},{5,4},{6,7},{7,6},{8,9},{9,8},{10,11... | collective-permute-start | bytes 393224 | tf_op jit(solution)/shard_map/ppermute | solution.py:338
  34.6 1.5 %collective-permute-start.19 = (f32[256,128]{1,0:T(8,128)S(1)}, f32[256,128]{1,0:T(8,128)S(1)}, u32[]{:S(2)}, u32[]{:S(2)}) collective-permute-start(f32[256,128]{1,0:T(8,128)S(1)} %collective-permute-done.15.refs_14_), channel_id=1, source_target_pairs={{0,1},{1,0},{2,3},{3,2},{4,5},{5,4},{6,7},{7,6},{8,9},{9,8},{10,11... | collective-permute-start | bytes 393224 | tf_op jit(solution)/shard_map/ppermute | solution.py:338
